TPU v7x, 32 devices: a whole 2x2x4 slice. The times are simulated.
32 devices in a mesh: dp: 4 (over z), tm: 2 (over x), pos: 4 (over y, core).
Axes of the slice: x: 2, y: 2, z: 4, core: 2. Of those that a mesh axis runs over, the one named last changes fastest.
Arguments:
- tokens: bfloat16 [8, 16, 196, 768], P('dp', 'tm', 'pos'), may hold values from -6 to 6
- cotangent: bfloat16 [8, 16, 196, 768], P('dp', 'tm', 'pos'), may hold values from -6 to 6
- frame_counts: int32 [8], P('dp'), may hold values from 1 to 16, as said below
- weight_in: float32 [768, 9984], P('dp')
- weight_out: float32 [3072, 768], P('dp'), may hold values from -0.109375 to 0.109375
- vectors: float32 [768, 18], P('dp')
- moment_in: float32 [768, 9984], P('dp'), may hold values from -0.00048828125 to 0.00048828125
- moment_out: float32 [3072, 768], P('dp'), may hold values from -0.00048828125 to 0.00048828125
- moment_vec: float32 [768, 18], P('dp'), may hold values from -0.00048828125 to 0.00048828125
- square_in: float32 [768, 9984], P('dp'), may hold values from 9.959334e-11 to 3.9837336e-10
- square_out: float32 [3072, 768], P('dp'), may hold values from 9.959334e-11 to 3.9837336e-10
- square_vec: float32 [768, 18], P('dp'), may hold values from 9.959334e-11 to 3.9837336e-10
Outputs:
- block_out: bfloat16 [8, 16, 196, 768], P('dp', 'tm', 'pos')
- input_grad: float32 [8, 16, 196, 768], P('dp', 'tm', 'pos')
- grad_norm: float32 [], replicated
- new_in: float32 [768, 9984], P('dp')
- new_out: float32 [3072, 768], P('dp')
- new_vec: float32 [768, 18], P('dp')
- first_in: float32 [768, 9984], P('dp')
- first_out: float32 [3072, 768], P('dp')
- first_vec: float32 [768, 18], P('dp')
- second_in: float32 [768, 9984], P('dp')
- second_out: float32 [3072, 768], P('dp')
- second_vec: float32 [768, 18], P('dp')
- bias_down_grad: float32 [768], P('dp')
Inputs may be any that keep to these rules, and one draw needn't show every extreme that they name: `frame_counts`: among the 2 clips of each index of dp (consecutive rows of one device) one has 16 frames.
All inputs are finite; a program needn't handle non-finite values.
Results may differ from a plain program's by a relative error of at most 0.019.
Values may be sent and summed in bfloat16 or wider, within the bound.
No kernel may reach another device: no remote copies, remote signals or barrier semaphores. Data moves between devices by JAX's collectives and lax.ppermute only.
A program may use at most 320 MiB of HBM per device.

v0:
```python
import jax
import jax.numpy as jnp
from jax import lax
from jax.sharding import PartitionSpec as P

HEADS = 12
HD = 64
D = 768
FF = 3072
MB = 2
STEP = 10


NORM_EPSILON = 1e-06
CLIP_NORM = 1.0
LEARN_RATE = 0.03
LEARN_RATE_VEC = 0.25
BETA_FIRST = 0.9
BETA_SECOND = 0.999
ADAM_EPSILON = 1e-08
WEIGHT_DECAY = 0.05
MASKED_SCORE = -1e30
TIME_FORMS = ("cfphd,cgphd->cphfg", "cphfg,cgphd->cfphd", "cphfg,cfphd->cgphd")
SPACE_FORMS = ("cfphd,cfqhd->cfhpq", "cfhpq,cfqhd->cfphd", "cfhpq,cfphd->cfqhd")


def layer_norm(inputs, gain, shift):
    centre = jnp.mean(inputs, axis=-1, keepdims=True)
    centred = inputs - centre
    variance = jnp.mean(centred * centred, axis=-1, keepdims=True)
    return centred * lax.rsqrt(variance + NORM_EPSILON) * gain + shift


def gelu_exact(inputs):
    return jax.nn.gelu(inputs, approximate=False)


def project(inputs, weight):
    return jnp.einsum("...i,ij->...j", inputs, weight, preferred_element_type=jnp.float32)


def project_back(grads, weight):
    return jnp.einsum("...j,ij->...i", grads, weight, preferred_element_type=jnp.float32)


def weight_grad(left, right):
    flat_left = left.reshape(-1, left.shape[-1])
    flat_right = right.reshape(-1, right.shape[-1])
    return jnp.dot(flat_left.T, flat_right, preferred_element_type=jnp.float32)


def row_total(grads):
    return jnp.sum(grads.astype(jnp.float32).reshape(-1, grads.shape[-1]), axis=0)


def with_heads(inputs):
    return inputs.reshape(inputs.shape[:-1] + (HEADS, HD))


def merge_heads(inputs):
    return inputs.reshape(inputs.shape[:-2] + (D,))


def attend_forward(queries, keys, values, forms, key_mask):
    scores = jnp.einsum(
        forms[0], with_heads(queries), with_heads(keys), preferred_element_type=jnp.float32
    ) * HD ** (-0.5)
    if key_mask is not None:
        scores = jnp.where(key_mask, scores, MASKED_SCORE)
    probs = jax.nn.softmax(scores, axis=-1)
    log_total = jax.nn.logsumexp(scores, axis=-1)
    probs_low = probs.astype(jnp.bfloat16)
    mixed = jnp.einsum(forms[1], probs_low, with_heads(values), preferred_element_type=jnp.float32)
    return (merge_heads(mixed), probs, probs_low, log_total)


def attend_backward(grad_out, queries, keys, values, forms, probs, probs_low):
    grad_heads = with_heads(grad_out)
    grad_probs = jnp.einsum(
        forms[0], grad_heads, with_heads(values), preferred_element_type=jnp.float32
    )
    weighted = jnp.sum(probs * grad_probs, axis=-1)
    grad_scores = (probs * (grad_probs - weighted[..., None])).astype(jnp.bfloat16)
    scale = HD ** (-0.5)
    grad_queries = (
        jnp.einsum(forms[1], grad_scores, with_heads(keys), preferred_element_type=jnp.float32)
        * scale
    )
    grad_keys = (
        jnp.einsum(forms[2], grad_scores, with_heads(queries), preferred_element_type=jnp.float32)
        * scale
    )
    grad_values = jnp.einsum(forms[2], probs_low, grad_heads, preferred_element_type=jnp.float32)
    return (merge_heads(grad_queries), merge_heads(grad_keys), merge_heads(grad_values), weighted)


def micro_step(inputs_low, cot_low, counts, gathered, first_frame, frames_all):
    w_all, w_down, vec_low = gathered
    params = vec_low.astype(jnp.float32)
    frames_here = inputs_low.shape[1]
    key_valid = jnp.arange(frames_all, dtype=jnp.int32)[None, :] < counts[:, None]
    key_mask = key_valid[:, None, None, None, :]
    own_frames = (first_frame + jnp.arange(frames_here, dtype=jnp.int32))[None, :] < counts[:, None]
    inputs = inputs_low.astype(jnp.float32)
    normed, time_norm_back = jax.vjp(layer_norm, inputs, params[:, 0], params[:, 1])
    time_in = normed.astype(jnp.bfloat16)
    mixed = project(time_in, w_all[:, : 3 * D])
    time_queries = (mixed[..., :D] + params[:, 2]).astype(jnp.bfloat16)
    time_keys = mixed[..., D : 2 * D].astype(jnp.bfloat16)
    time_values = (mixed[..., 2 * D :] + params[:, 3]).astype(jnp.bfloat16)
    keys_all, values_all = (
        lax.all_gather(time_keys, "tm", axis=1, tiled=True),
        lax.all_gather(time_values, "tm", axis=1, tiled=True),
    )
    attended, time_probs, time_low, time_total = attend_forward(
        time_queries, keys_all, values_all, TIME_FORMS, key_mask
    )
    time_attn = attended.astype(jnp.bfloat16)
    time_proj = (project(time_attn, w_all[:, 3 * D : 4 * D]) + params[:, 4]).astype(jnp.bfloat16)
    after_time = inputs + (project(time_proj, w_all[:, 4 * D : 5 * D]) + params[:, 5])
    normed, space_norm_back = jax.vjp(layer_norm, after_time, params[:, 6], params[:, 7])
    space_in = normed.astype(jnp.bfloat16)
    mixed = project(space_in, w_all[:, 5 * D : 8 * D])
    space_queries = (mixed[..., :D] + params[:, 8]).astype(jnp.bfloat16)
    space_keys = mixed[..., D : 2 * D].astype(jnp.bfloat16)
    space_values = (mixed[..., 2 * D :] + params[:, 9]).astype(jnp.bfloat16)
    frame_keys, frame_values = (
        lax.all_gather(space_keys, "pos", axis=2, tiled=True),
        lax.all_gather(space_values, "pos", axis=2, tiled=True),
    )
    attended, space_probs, space_low, space_total = attend_forward(
        space_queries, frame_keys, frame_values, SPACE_FORMS, None
    )
    space_attn = attended.astype(jnp.bfloat16)
    after_space = after_time + (project(space_attn, w_all[:, 8 * D : 9 * D]) + params[:, 10])
    normed, mlp_norm_back = jax.vjp(layer_norm, after_space, params[:, 11], params[:, 12])
    mlp_in = normed.astype(jnp.bfloat16)
    bias_up = params[:, 13:17].T.reshape(FF)
    hidden_pre = project(mlp_in, w_all[:, 9 * D :]) + bias_up
    activated, gelu_back = jax.vjp(gelu_exact, hidden_pre)
    hidden_low = activated.astype(jnp.bfloat16)
    block_out = after_space + (project(hidden_low, w_down) + params[:, 17])
    grad_out = cot_low.astype(jnp.float32) * own_frames.astype(jnp.float32)[:, :, None, None]
    grad_top = grad_out.astype(jnp.bfloat16)
    grad_bias_down = row_total(grad_top)
    grad_down = weight_grad(hidden_low, grad_top)
    grad_hidden = gelu_back(project_back(grad_top, w_down))[0].astype(jnp.bfloat16)
    grad_bias_up = row_total(grad_hidden)
    grad_up = weight_grad(mlp_in, grad_hidden)
    grad_norm_in, grad_gain_m, grad_shift_m = mlp_norm_back(
        project_back(grad_hidden, w_all[:, 9 * D :])
    )
    grad_space = grad_out + grad_norm_in
    grad_branch = grad_space.astype(jnp.bfloat16)
    grad_bias_os = row_total(grad_branch)
    grad_out_space = weight_grad(space_attn, grad_branch)
    grad_attn = project_back(grad_branch, w_all[:, 8 * D : 9 * D]).astype(jnp.bfloat16)
    grad_q, grad_k, grad_v, space_weighted = attend_backward(
        grad_attn, space_queries, frame_keys, frame_values, SPACE_FORMS, space_probs, space_low
    )
    grad_k, grad_v = (
        lax.psum_scatter(
            grad_k.astype(jnp.bfloat16), "pos", scatter_dimension=2, tiled=True
        ).astype(jnp.float32),
        lax.psum_scatter(
            grad_v.astype(jnp.bfloat16), "pos", scatter_dimension=2, tiled=True
        ).astype(jnp.float32),
    )
    grad_qkv = jnp.concatenate(
        [grad_q.astype(jnp.bfloat16), grad_k.astype(jnp.bfloat16), grad_v.astype(jnp.bfloat16)],
        axis=-1,
    )
    grad_bias_qs = row_total(grad_qkv[..., :D])
    grad_bias_vs = row_total(grad_qkv[..., 2 * D :])
    grad_qkv_space = weight_grad(space_in, grad_qkv)
    grad_norm_in, grad_gain_s, grad_shift_s = space_norm_back(
        project_back(grad_qkv, w_all[:, 5 * D : 8 * D])
    )
    grad_time = grad_space + grad_norm_in
    grad_branch = grad_time.astype(jnp.bfloat16)
    grad_bias_fc = row_total(grad_branch)
    grad_fc = weight_grad(time_proj, grad_branch)
    grad_proj = project_back(grad_branch, w_all[:, 4 * D : 5 * D]).astype(jnp.bfloat16)
    grad_bias_ot = row_total(grad_proj)
    grad_out_time = weight_grad(time_attn, grad_proj)
    grad_attn = project_back(grad_proj, w_all[:, 3 * D : 4 * D]).astype(jnp.bfloat16)
    grad_q, grad_k, grad_v, time_weighted = attend_backward(
        grad_attn, time_queries, keys_all, values_all, TIME_FORMS, time_probs, time_low
    )
    grad_k, grad_v = (
        lax.psum_scatter(grad_k.astype(jnp.bfloat16), "tm", scatter_dimension=1, tiled=True).astype(
            jnp.float32
        ),
        lax.psum_scatter(grad_v.astype(jnp.bfloat16), "tm", scatter_dimension=1, tiled=True).astype(
            jnp.float32
        ),
    )
    grad_qkv = jnp.concatenate(
        [grad_q.astype(jnp.bfloat16), grad_k.astype(jnp.bfloat16), grad_v.astype(jnp.bfloat16)],
        axis=-1,
    )
    grad_bias_qt = row_total(grad_qkv[..., :D])
    grad_bias_vt = row_total(grad_qkv[..., 2 * D :])
    grad_qkv_time = weight_grad(time_in, grad_qkv)
    grad_norm_in, grad_gain_t, grad_shift_t = time_norm_back(
        project_back(grad_qkv, w_all[:, : 3 * D])
    )
    grad_inputs = grad_time + grad_norm_in
    grad_in = jnp.concatenate(
        [grad_qkv_time, grad_out_time, grad_fc, grad_qkv_space, grad_out_space, grad_up], axis=1
    )
    columns = [
        grad_gain_t,
        grad_shift_t,
        grad_bias_qt,
        grad_bias_vt,
        grad_bias_ot,
        grad_bias_fc,
        grad_gain_s,
        grad_shift_s,
        grad_bias_qs,
        grad_bias_vs,
        grad_bias_os,
        grad_gain_m,
        grad_shift_m,
    ]
    up_columns = grad_bias_up.reshape(4, D)
    columns = columns + [up_columns[0], up_columns[1], up_columns[2], up_columns[3], grad_bias_down]
    grad_vec = jnp.stack(columns, axis=1)
    return (block_out.astype(jnp.bfloat16), grad_inputs, (grad_in, grad_down, grad_vec))


def reduce_grads(grads):
    summed = (
        lax.psum_scatter(
            grads[0].astype(jnp.bfloat16), "dp", scatter_dimension=0, tiled=True
        ).astype(jnp.float32),
        lax.psum_scatter(
            grads[1].astype(jnp.bfloat16), "dp", scatter_dimension=0, tiled=True
        ).astype(jnp.float32),
        lax.psum_scatter(
            grads[2].astype(jnp.bfloat16), "dp", scatter_dimension=0, tiled=True
        ).astype(jnp.float32),
    )
    return (
        lax.psum(summed[0].astype(jnp.bfloat16), ("tm", "pos")).astype(jnp.float32),
        lax.psum(summed[1].astype(jnp.bfloat16), ("tm", "pos")).astype(jnp.float32),
        lax.psum(summed[2].astype(jnp.bfloat16), ("tm", "pos")).astype(jnp.float32),
    )


def add_all(first_set, second_set):
    return (
        first_set[0] + second_set[0],
        first_set[1] + second_set[1],
        first_set[2] + second_set[2],
    )


def adam_update(weight, grad, moment, square, decay, factor, rate):
    grad = grad * factor
    moment = BETA_FIRST * moment + (1.0 - BETA_FIRST) * grad
    square = BETA_SECOND * square + (1.0 - BETA_SECOND) * grad * grad
    moment_hat = moment / (1.0 - BETA_FIRST**STEP)
    square_hat = square / (1.0 - BETA_SECOND**STEP)
    fresh = weight - rate * (moment_hat / (jnp.sqrt(square_hat) + ADAM_EPSILON) + decay * weight)
    return (fresh, moment, square)


def shards(
    tokens,
    cotangent,
    frame_counts,
    weight_in,
    weight_out,
    vectors,
    moment_in,
    moment_out,
    moment_vec,
    square_in,
    square_out,
    square_vec,
):
    frames_here = tokens.shape[1]
    frames_all = frames_here * lax.axis_size("tm")
    first_frame = lax.axis_index("tm") * frames_here
    per_micro = tokens.shape[0] // MB
    low_in = weight_in.astype(jnp.bfloat16)
    low_out = weight_out.astype(jnp.bfloat16)
    low_vec = vectors.astype(jnp.bfloat16)
    shard_sums = None
    outputs = []
    input_grads = []
    for micro_index in range(MB):
        gathered = (
            lax.all_gather(low_in, "dp", axis=0, tiled=True),
            lax.all_gather(low_out, "dp", axis=0, tiled=True),
            lax.all_gather(low_vec, "dp", axis=0, tiled=True),
        )
        start = micro_index * per_micro
        stop = start + per_micro
        block_part, grad_part, grads = micro_step(
            tokens[start:stop],
            cotangent[start:stop],
            frame_counts[start:stop],
            gathered,
            first_frame,
            frames_all,
        )
        outputs.append(block_part)
        input_grads.append(grad_part)
        reduced = reduce_grads(grads)
        shard_sums = reduced if shard_sums is None else add_all(shard_sums, reduced)
    local_square = (
        jnp.sum(shard_sums[0] * shard_sums[0])
        + jnp.sum(shard_sums[1] * shard_sums[1])
        + jnp.sum(shard_sums[2] * shard_sums[2])
    )
    total_square = lax.psum(local_square, "dp")
    grad_norm = jnp.sqrt(total_square)
    factor = CLIP_NORM / jnp.maximum(grad_norm, CLIP_NORM)
    new_in, first_in, second_in = adam_update(
        weight_in, shard_sums[0], moment_in, square_in, WEIGHT_DECAY, factor, LEARN_RATE
    )
    new_out, first_out, second_out = adam_update(
        weight_out, shard_sums[1], moment_out, square_out, WEIGHT_DECAY, factor, LEARN_RATE
    )
    new_vec, first_vec, second_vec = adam_update(
        vectors, shard_sums[2], moment_vec, square_vec, 0.0, factor, LEARN_RATE_VEC
    )
    bias_down_grad = shard_sums[2][:, 17] * factor
    block_out = jnp.concatenate(outputs, axis=0)
    input_grad = jnp.concatenate(input_grads, axis=0)
    return (
        block_out,
        input_grad,
        grad_norm,
        new_in,
        new_out,
        new_vec,
        first_in,
        first_out,
        first_vec,
        second_in,
        second_out,
        second_vec,
        bias_down_grad,
    )


def solution(mesh):
    return jax.shard_map(
        shards,
        mesh=mesh,
        in_specs=(
            P("dp", "tm", "pos", None),
            P("dp", "tm", "pos", None),
            P("dp"),
            P("dp", None),
            P("dp", None),
            P("dp", None),
            P("dp", None),
            P("dp", None),
            P("dp", None),
            P("dp", None),
            P("dp", None),
            P("dp", None),
        ),
        out_specs=(
            P("dp", "tm", "pos", None),
            P("dp", "tm", "pos", None),
            P(),
            P("dp", None),
            P("dp", None),
            P("dp", None),
            P("dp", None),
            P("dp", None),
            P("dp", None),
            P("dp", None),
            P("dp", None),
            P("dp", None),
            P("dp"),
        ),
        check_vma=False,
    )
```

profile of v0, /device:TPU:0, one launch (start us, length us, event | category | flops | bytes accessed | tf_op | source)
XLA Modules:
  0.0 1884.6 jit_solution(1536857085414580778)
XLA Ops:
  7.2 5.5 convert_element_type.673
  13.4 14.7 all-gather
  30.7 248.1 %all-gather.12.cloned.1.call-done = bf16[768,9984]{1,0:T(8,128)(2,1)} async-done(((bf16[192,9984]{1,0:T(8,128)(2,1)}), bf16[768,9984]{1,0:T(8,128)(2,1)}) %all-gather.12.cloned.1.call-update) | async-done | bytes 15335440 | tf_op jit(solution)/shard_map/all_gather | solution.py:296
  300.1 6.4 all-gather.16.cloned.1.call-done
  311.3 5.4 fusion.279
  316.7 15.0 all-gather.14.cloned.1.call-done
  331.7 4.8 reshape.1432
  344.3 12.5 all-gather.26.cloned.1.call-done
  366.3 6.2 fusion.278
  372.6 9.3 all-gather.24.cloned.1.call-done
  432.5 4.9 copy.263
  444.7 13.7 all-gather.18.cloned.1.call-done
  458.4 4.9 copy.261
  463.3 4.8 fusion.91
  476.7 7.7 all-gather.30.cloned.1.call-done
  484.3 4.9 copy.278
  496.6 14.3 all-gather.28.cloned.1.call-done
  510.9 5.3 copy.276
  516.2 4.8 fusion.92
  529.2 4.9 fusion.141
  534.1 10.4 fusion.131
  546.9 26.8 %multiply_convert_fusion.5 = (bf16[8,49,3072]{2,1,0:T(8,128)(2,1)}, f32[8,49,3072]{2,1,0:T(8,128)}, bf16[8,49,3072]{2,1,0:T(8,128)(2,1)}, f32[8,49,3072]{2,1,0:T(8,128)}) fusion(f32[8,49,3072]{2,1,0:T(8,128)S(1)} %get-tuple-element.187, f32[3072]{0:T(1024)S(1)} %add.472, u8[49,3072]{1,0:T(8,128)(4,1)S(1)} %get-tuple-element.66, ...), kind=kLoop, calls=%fused_computation.54 | loop fusion | flops 169795584 | bytes 24698880 | tf_op jit(solution)/shard_map/convert_element_type | solution.py:141
  573.7 28.6 %all-gather.22.cloned.1.call-done = bf16[3072,768]{1,0:T(8,128)(2,1)} async-done(((bf16[768,768]{1,0:T(8,128)(2,1)}), bf16[3072,768]{1,0:T(8,128)(2,1)}) %all-gather.22.cloned.1.call-update) | async-done | bytes 4718608 | tf_op jit(solution)/shard_map/all_gather | solution.py:297
  602.3 10.3 fusion.290
  612.6 6.4 fusion.289
  619.2 8.8 fusion.294
  627.9 6.5 fusion.115
  645.3 6.3 convolution_convert_fusion
  651.6 4.9 copy.312
  656.5 6.3 multiply_reduce_fusion.1
  670.9 4.9 copy.310
  685.3 6.3 convolution_convert_fusion.1
  691.6 4.9 copy.289
  696.5 7.0 multiply_reduce_fusion.2
  711.5 4.9 copy.287
  738.7 21.7 %reduce-scatter.21.cloned.1.call-done = bf16[1,8,49,768]{3,1,0,2:T(8,128)(2,1)} async-done(((bf16[1,8,196,768]{3,1,0,2:T(8,128)(2,1)}), bf16[1,8,49,768]{3,1,0,2:T(8,128)(2,1)}) %reduce-scatter.21.cloned.1.call-update) | async-done | bytes 602128 | tf_op jit(solution)/shard_map/reduce_scatter | solution.py:165
  762.5 5.6 fusion.117
  768.1 28.3 %reduce-scatter.19.cloned.1.call-done = bf16[1,8,49,768]{3,1,0,2:T(8,128)(2,1)} async-done(((bf16[1,8,196,768]{3,1,0,2:T(8,128)(2,1)}), bf16[1,8,49,768]{3,1,0,2:T(8,128)(2,1)}) %reduce-scatter.19.cloned.1.call-update) | async-done | bytes 602128 | tf_op jit(solution)/shard_map/reduce_scatter | solution.py:162
  797.6 6.7 fusion.114
  814.3 5.0 multiply_reduce_fusion.5
  824.8 4.9 reshape.1493
  829.8 5.1 convert_bitcast_fusion
  837.3 4.9 reshape.1494
  868.8 5.1 convert_bitcast_fusion.1
  877.9 6.9 bitcast_convert_fusion
  897.2 5.8 fusion.20
  937.8 5.9 fusion.18
  951.8 4.8 fusion.22
  962.0 4.8 fusion.112
  966.8 5.7 fusion.105
  983.2 38.9 %reduce-scatter.41.cloned.1.call-done = bf16[768,768]{1,0:T(8,128)(2,1)} async-done(((bf16[3072,768]{1,0:T(8,128)(2,1)}), bf16[768,768]{1,0:T(8,128)(2,1)}) %reduce-scatter.41.cloned.1.call-update) | async-done | bytes 1179664 | tf_op jit(solution)/shard_map/reduce_scatter | solution.py:238
  1022.1 88.5 %reduce-scatter.39.cloned.1.call-done = bf16[768,768]{1,0:T(8,128)(2,1)} async-done(((bf16[3072,768]{1,0:T(8,128)(2,1)}), bf16[768,768]{1,0:T(8,128)(2,1)}) %reduce-scatter.39.cloned.1.call-update) | async-done | bytes 1179664 | tf_op jit(solution)/shard_map/reduce_scatter | solution.py:238
  1110.6 259.2 %reduce-scatter.37.cloned.1.call-done = bf16[192,9984]{1,0:T(8,128)(2,1)} async-done(((bf16[768,9984]{1,0:T(8,128)(2,1)}), bf16[192,9984]{1,0:T(8,128)(2,1)}) %reduce-scatter.37.cloned.1.call-update) | async-done | bytes 3833872 | tf_op jit(solution)/shard_map/reduce_scatter | solution.py:235
  1369.8 259.8 %reduce-scatter.35.cloned.1.call-done = bf16[192,9984]{1,0:T(8,128)(2,1)} async-done(((bf16[768,9984]{1,0:T(8,128)(2,1)}), bf16[192,9984]{1,0:T(8,128)(2,1)}) %reduce-scatter.35.cloned.1.call-update) | async-done | bytes 3833872 | tf_op jit(solution)/shard_map/reduce_scatter | solution.py:235
  1630.4 5.6 fusion.122
  1636.1 4.9 fusion.121
  1644.9 7.5 reduce-scatter.43.cloned.1.call-done
  1653.3 19.5 %reduce-scatter.45.cloned.1.call-done = bf16[192,18]{1,0:T(8,128)(2,1)} async-done(((bf16[768,18]{1,0:T(8,128)(2,1)}), bf16[192,18]{1,0:T(8,128)(2,1)}) %reduce-scatter.45.cloned.1.call-update) | async-done | bytes 6928
  1673.7 23.7 %all-reduce = (bf16[192,18]{0,1:T(8,128)(2,1)S(1)}, bf16[192,18]{0,1:T(8,128)(2,1)S(1)}) all-reduce(bf16[192,18]{0,1:T(8,128)(2,1)S(1)} %copy.365, bf16[192,18]{0,1:T(8,128)(2,1)S(1)} %copy.363), channel_id=1, replica_groups=mesh['dp'=4,'tm'=2,'pos'=4] {'tm','pos'}, use_global_device_ids=true, to_apply=%region_87.88 | all-reduce | flops 6912 | bytes 27648 | tf_op jit(solution)/shard_map/psum | solution.py:248
  1698.0 123.3 %all-reduce.4.cloned.1.call-done = (bf16[192,9984]{1,0:T(8,128)(2,1)}, bf16[192,9984]{1,0:T(8,128)(2,1)}, bf16[768,768]{1,0:T(8,128)(2,1)}, bf16[768,768]{1,0:T(8,128)(2,1)}) async-done(((bf16[192,9984]{1,0:T(8,128)(2,1)}, bf16[192,9984]{1,0:T(8,128)(2,1)}, bf16[768,768]{1,0:T(8,128)(2,1)}, bf16[768,768]{1,0:T(8,128)(2,1)}), (bf16[192,9984]{1,0:T(8,128)(2,1)}, bf16[192,9984]{1,0:T(8,128)(2,1)}, ...) | async-done | bytes 10027024 | tf_op jit(solution)/shard_map/psum | solution.py:246
  1824.1 5.8 multiply_reduce_fusion
  1834.1 12.2 psum.55
  1848.2 8.1 multiply_subtract_fusion.1
  1856.3 20.5 %multiply_subtract_fusion = (f32[192,9984]{1,0:T(8,128)}, f32[192,9984]{1,0:T(8,128)}, f32[192,9984]{1,0:T(8,128)}) fusion(f32[192,9984]{1,0:T(8,128)} %param.15, f32[]{:T(128)S(6)} %div.236, bf16[192,9984]{1,0:T(8,128)(2,1)} %get-tuple-element.101, bf16[192,9984]{1,0:T(8,128)(2,1)} %get-tuple-element.102, f32[192,9984]{1,0:T(8,128)} %param.18, ...), kind=kLoop, calls=%fused_computation.12 | loop fusion | flops 36421632 | bytes 53673988 | tf_op jit(solution)/shard_map/sub | solution.py:266
  (593 shorter events, 324.2 us)
Async XLA Ops:
  7.2 271.6 %all-gather.12.cloned.1.call-start = ((), (), s32[]{:S(2)}) async-start(), calls=%async_computation.14 | async-start | bytes 19169280 | tf_op jit(solution)/shard_map/all_gather | solution.py:296
  12.7 16.2 copy-start.62
  12.7 293.9 %all-gather.16.cloned.1.call-start = ((), (), s32[]{:S(2)}) async-start(), calls=%async_computation.16 | async-start | bytes 1806336 | tf_op jit(solution)/shard_map/all_gather | solution.py:112
  28.9 371.6 %copy-start.94 = (f32[768]{0:T(1024)}, f32[768]{0:T(1024)S(1)}, u32[]{:S(2)}) copy-start(f32[768]{0:T(1024)S(1)} %get-tuple-element.88) | copy-start | bytes 9220
  28.9 505.2 %copy-start.144 = (f32[768]{0:T(1024)}, f32[768]{0:T(1024)S(1)}, u32[]{:S(2)}) copy-start(f32[768]{0:T(1024)S(1)} %get-tuple-element.82) | copy-start | bytes 9220
  28.9 605.6 %copy-start.126 = (f32[768]{0:T(1024)}, f32[768]{0:T(1024)S(1)}, u32[]{:S(2)}) copy-start(f32[768]{0:T(1024)S(1)} %get-tuple-element.83) | copy-start | bytes 9220
  29.0 334.5 %copy-start.2 = (bf16[1,8,49,768]{3,1,2,0:T(8,128)(2,1)}, bf16[1,8,49,768]{3,1,2,0:T(8,128)(2,1)S(1)}, u32[]{:S(2)}) copy-start(bf16[1,8,49,768]{3,1,2,0:T(8,128)(2,1)S(1)} %get-tuple-element.140) | copy-start | bytes 1806340
  29.0 368.3 %copy-start.4 = (bf16[1,8,49,768]{3,1,2,0:T(8,128)(2,1)}, bf16[1,8,49,768]{3,1,2,0:T(8,128)(2,1)S(1)}, u32[]{:S(2)}) copy-start(bf16[1,8,49,768]{3,1,2,0:T(8,128)(2,1)S(1)} %get-tuple-element.141) | copy-start | bytes 1806340
  29.3 253.0 %copy-start.90 = (f32[8,49]{1,0:T(8,128)}, f32[8,49]{1,0:T(8,128)S(1)}, u32[]{:S(2)}) copy-start(f32[8,49]{1,0:T(8,128)S(1)} %broadcast_multiply_fusion.5) | copy-start | bytes 4708
  29.7 252.7 %copy-start.114 = (f32[8,49]{1,0:T(8,128)}, f32[8,49]{1,0:T(8,128)S(1)}, u32[]{:S(2)}) copy-start(f32[8,49]{1,0:T(8,128)S(1)} %fusion.109) | copy-start | bytes 4708
  29.7 252.7 %copy-start.104 = (f32[8,49]{1,0:T(8,128)}, f32[8,49]{1,0:T(8,128)S(1)}, u32[]{:S(2)}) copy-start(f32[8,49]{1,0:T(8,128)S(1)} %broadcast_multiply_fusion.2) | copy-start | bytes 4708
  30.0 252.3 %copy-start.116 = (f32[8,49]{1,0:T(8,128)}, f32[8,49]{1,0:T(8,128)S(1)}, u32[]{:S(2)}) copy-start(f32[8,49]{1,0:T(8,128)S(1)} %fusion.111) | copy-start | bytes 4708
  30.1 252.3 %copy-start.92 = (f32[8,49]{1,0:T(8,128)}, f32[8,49]{1,0:T(8,128)S(1)}, u32[]{:S(2)}) copy-start(f32[8,49]{1,0:T(8,128)S(1)} %fusion.228) | copy-start | bytes 4708
  30.1 252.3 %copy-start.108 = (f32[8,49]{1,0:T(8,128)}, f32[8,49]{1,0:T(8,128)S(1)}, u32[]{:S(2)}) copy-start(f32[8,49]{1,0:T(8,128)S(1)} %fusion.231) | copy-start | bytes 4708
  285.1 46.6 %all-gather.14.cloned.1.call-start = ((), (), s32[]{:S(2)}) async-start(), calls=%async_computation.15 | async-start | bytes 1806336 | tf_op jit(solution)/shard_map/all_gather | solution.py:113
  291.2 65.6 %all-gather.26.cloned.1.call-start = ((), (), s32[]{:S(2)}) async-start(), calls=%async_computation.21 | async-start | bytes 1806336 | tf_op jit(solution)/shard_map/all_gather | solution.py:112
  293.5 88.4 %all-gather.24.cloned.1.call-start = ((), (), s32[]{:S(2)}) async-start(), calls=%async_computation.20 | async-start | bytes 1806336 | tf_op jit(solution)/shard_map/all_gather | solution.py:113
  299.6 132.8 %all-gather.20.cloned.1.call-start = ((), (), s32[]{:S(2)}) async-start(), calls=%async_computation.18 | async-start | bytes 3010560 | tf_op jit(solution)/shard_map/all_gather | solution.py:128
  316.7 23.5 %copy-start.86 = (f32[49,12,8]{2,1,0:T(8,128)}, f32[49,12,8]{2,1,0:T(8,128)S(1)}, u32[]{:S(2)}) copy-start(f32[49,12,8]{2,1,0:T(8,128)S(1)} %get-tuple-element.173) | copy-start | bytes 56452
  344.3 19.2 %copy-start.82 = (bf16[8,49,768]{2,0,1:T(8,128)(2,1)}, bf16[8,49,768]{2,0,1:T(8,128)(2,1)S(1)}, u32[]{:S(2)}) copy-start(bf16[8,49,768]{2,0,1:T(8,128)(2,1)S(1)} %convert_element_type.680) | copy-start | bytes 1806340
  366.0 34.6 %copy-start.96 = (f32[8,49]{1,0:T(8,128)}, f32[8,49]{1,0:T(8,128)S(1)}, u32[]{:S(2)}) copy-start(f32[8,49]{1,0:T(8,128)S(1)} %broadcast_multiply_fusion.4) | copy-start | bytes 4708
  366.3 34.3 %copy-start.98 = (f32[8,49]{1,0:T(8,128)}, f32[8,49]{1,0:T(8,128)S(1)}, u32[]{:S(2)}) copy-start(f32[8,49]{1,0:T(8,128)S(1)} %fusion.229) | copy-start | bytes 4708
  401.1 6.9 copy-start.80
  407.9 50.5 %all-gather.18.cloned.1.call-start = ((), (), s32[]{:S(2)}) async-start(), calls=%async_computation.17 | async-start | bytes 3010560 | tf_op jit(solution)/shard_map/all_gather | solution.py:129
  414.3 70.0 %all-gather.30.cloned.1.call-start = ((), (), s32[]{:S(2)}) async-start(), calls=%async_computation.23 | async-start | bytes 3010560 | tf_op jit(solution)/shard_map/all_gather | solution.py:128
  416.7 94.2 %all-gather.28.cloned.1.call-start = ((), (), s32[]{:S(2)}) async-start(), calls=%async_computation.22 | async-start | bytes 3010560 | tf_op jit(solution)/shard_map/all_gather | solution.py:129
  417.4 184.9 %all-gather.22.cloned.1.call-start = ((), (), s32[]{:S(2)}) async-start(), calls=%async_computation.19 | async-start | bytes 5898240 | tf_op jit(solution)/shard_map/all_gather | solution.py:297
  420.3 314.2 %reduce-scatter.29.cloned.1.call-start = ((), (), s32[]{:S(2)}) async-start(), calls=%async_computation.29 | async-start | bytes 3010560 | tf_op jit(solution)/shard_map/reduce_scatter | solution.py:165
  423.9 420.6 %copy-start.34 = (bf16[1,8,49,768]{3,1,2,0:T(8,128)(2,1)}, bf16[1,8,49,768]{3,1,2,0:T(8,128)(2,1)S(1)}, u32[]{:S(2)}) copy-start(bf16[1,8,49,768]{3,1,2,0:T(8,128)(2,1)S(1)} %get-tuple-element.138) | copy-start | bytes 1806340
  475.2 159.3 %copy-start.110 = (f32[8,49]{1,0:T(8,128)}, f32[8,49]{1,0:T(8,128)S(1)}, u32[]{:S(2)}) copy-start(f32[8,49]{1,0:T(8,128)S(1)} %broadcast_multiply_fusion.3) | copy-start | bytes 4708
  476.7 157.8 %copy-start.128 = (f32[8,49]{1,0:T(8,128)}, f32[8,49]{1,0:T(8,128)S(1)}, u32[]{:S(2)}) copy-start(f32[8,49]{1,0:T(8,128)S(1)} %fusion.230) | copy-start | bytes 4708
  528.1 106.5 %copy-start.112 = (f32[8,49]{1,0:T(8,128)}, f32[8,49]{1,0:T(8,128)S(1)}, u32[]{:S(2)}) copy-start(f32[8,49]{1,0:T(8,128)S(1)} %broadcast_multiply_fusion) | copy-start | bytes 4708
  528.4 106.2 %copy-start.130 = (f32[8,49]{1,0:T(8,128)}, f32[8,49]{1,0:T(8,128)S(1)}, u32[]{:S(2)}) copy-start(f32[8,49]{1,0:T(8,128)S(1)} %fusion.233) | copy-start | bytes 4708
  534.1 10.4 copy-start.23
  612.6 6.6 copy-start.22
  619.2 8.8 copy-start.11
  619.2 8.8 copy-start.14
  656.5 80.1 %reduce-scatter.27.cloned.1.call-start = ((), (), s32[]{:S(2)}) async-start(), calls=%async_computation.28 | async-start | bytes 3010560 | tf_op jit(solution)/shard_map/reduce_scatter | solution.py:162
  675.9 84.6 %reduce-scatter.21.cloned.1.call-start = ((), (), s32[]{:S(2)}) async-start(), calls=%async_computation.25 | async-start | bytes 3010560 | tf_op jit(solution)/shard_map/reduce_scatter | solution.py:165
  696.5 99.9 %reduce-scatter.19.cloned.1.call-start = ((), (), s32[]{:S(2)}) async-start(), calls=%async_computation.24 | async-start | bytes 3010560 | tf_op jit(solution)/shard_map/reduce_scatter | solution.py:162
  716.4 180.7 %reduce-scatter.31.cloned.1.call-start = ((), (), s32[]{:S(2)}) async-start(), calls=%async_computation.30 | async-start | bytes 2064384 | tf_op jit(solution)/shard_map/reduce_scatter | solution.py:191
  734.4 28.0 %copy-start.95 = (f32[768]{0:T(1024)S(1)}, f32[768]{0:T(1024)}, u32[]{:S(2)}) copy-start(f32[768]{0:T(1024)} %copy-done.94) | copy-start | bytes 9220
  734.4 28.0 %copy-start.107 = (f32[8,49]{1,0:T(8,128)S(1)}, f32[8,49]{1,0:T(8,128)}, u32[]{:S(2)}) copy-start(f32[8,49]{1,0:T(8,128)} %copy-done.106) | copy-start | bytes 4708
  762.5 35.1 %copy-start.97 = (f32[8,49]{1,0:T(8,128)S(1)}, f32[8,49]{1,0:T(8,128)}, u32[]{:S(2)}) copy-start(f32[8,49]{1,0:T(8,128)} %copy-done.96) | copy-start | bytes 4708
  762.5 35.1 %copy-start.123 = (f32[8,49]{1,0:T(8,128)S(1)}, f32[8,49]{1,0:T(8,128)}, u32[]{:S(2)}) copy-start(f32[8,49]{1,0:T(8,128)} %copy-done.122) | copy-start | bytes 4708
  797.6 6.7 copy-start.69
  797.6 6.7 copy-start.8
  797.6 6.7 copy-start.31
  797.6 6.7 copy-start.37
  829.7 67.4 %reduce-scatter.33.cloned.1.call-start = ((), (), s32[]{:S(2)}) async-start(), calls=%async_computation.31 | async-start | bytes 2064384 | tf_op jit(solution)/shard_map/reduce_scatter | solution.py:194
  844.4 93.3 %reduce-scatter.23.cloned.1.call-start = ((), (), s32[]{:S(2)}) async-start(), calls=%async_computation.26 | async-start | bytes 2064384 | tf_op jit(solution)/shard_map/reduce_scatter | solution.py:191
  868.7 69.0 %reduce-scatter.25.cloned.1.call-start = ((), (), s32[]{:S(2)}) async-start(), calls=%async_computation.27 | async-start | bytes 2064384 | tf_op jit(solution)/shard_map/reduce_scatter | solution.py:194
  877.8 144.3 %reduce-scatter.41.cloned.1.call-start = ((), (), s32[]{:S(2)}) async-start(), calls=%async_computation.35 | async-start | bytes 5898240 | tf_op jit(solution)/shard_map/reduce_scatter | solution.py:238
  884.8 225.9 %reduce-scatter.39.cloned.1.call-start = ((), (), s32[]{:S(2)}) async-start(), calls=%async_computation.34 | async-start | bytes 5898240 | tf_op jit(solution)/shard_map/reduce_scatter | solution.py:238
  891.5 478.3 %reduce-scatter.37.cloned.1.call-start = ((), (), s32[]{:S(2)}) async-start(), calls=%async_computation.33 | async-start | bytes 19169280 | tf_op jit(solution)/shard_map/reduce_scatter | solution.py:235
  918.2 711.5 %reduce-scatter.35.cloned.1.call-start = ((), (), s32[]{:S(2)}) async-start(), calls=%async_computation.32 | async-start | bytes 19169280 | tf_op jit(solution)/shard_map/reduce_scatter | solution.py:235
  956.6 695.8 %reduce-scatter.43.cloned.1.call-start = ((), (), s32[]{:S(2)}) async-start(), calls=%async_computation.36 | async-start | bytes 245760
  966.8 7.3 copy-start.115
  972.6 6.5 copy-start.58
  977.3 695.5 %reduce-scatter.45.cloned.1.call-start = ((), (), s32[]{:S(2)}) async-start(), calls=%async_computation.37 | async-start | bytes 245760
  983.2 838.1 %all-reduce.4.cloned.1.call-start = ((), (), s32[]{:S(2)}) async-start(), calls=%async_computation.38 | async-start | bytes 20054016 | tf_op jit(solution)/shard_map/psum | solution.py:246
  1831.9 15.1 copy-start.101
  1831.9 15.1 copy-start.124
  1831.9 15.1 copy-start.125
  (124 other events, 391.2 us)
Sparse Core Ops, SparseCore 0:
  12.8 265.8 all-gather.11
  285.3 21.2 all-gather.15
  308.7 23.0 all-gather.13
  333.7 23.0 all-gather.25
  358.8 23.0 all-gather.23
  408.1 24.3 all-gather.19
  434.0 24.3 all-gather.17
  460.0 24.3 all-gather.29
  486.5 24.3 all-gather.27
  512.9 89.4 all-gather.21
  656.6 31.8 reduce-scatter.28
  691.1 33.3 reduce-scatter.26
  727.0 33.3 reduce-scatter.20
  763.0 33.3 reduce-scatter.18
  829.9 23.8 reduce-scatter.30
  856.6 23.9 reduce-scatter.32
  883.3 23.9 reduce-scatter.22
  910.0 23.9 reduce-scatter.24
  936.8 85.2 reduce-scatter.40
  1024.9 85.7 reduce-scatter.38
  1113.0 256.7 reduce-scatter.36
  1372.3 257.3 reduce-scatter.34
  1631.9 20.4 reduce-scatter.42
  1655.2 17.5 reduce-scatter.44
  1676.9 144.3 all-reduce.3
where the time goes:
time: 1890 us; the launch traced here: 1880 us
  waiting for transfers between devices  1210 us (64%)
  matrix products  283 us (15%)
  local copies, waits for them, and re-layouts  194 us (10%)
  other arithmetic  128 us (7%)
  blocking collectives  50.6 us (3%)
  between operations  20.5 us (1%)
    reduce_scatter x2, waiting for transfers between devices, reduce_grads(): lax.psum_scatter(grads[0].astype(jnp.bfloat16), 'dp', scatter_dimension=0...  519 us
    all_gather x1, waiting for transfers between devices, shards(): lax.all_gather(low_in, 'dp', axis=0, tiled=True)  248 us
    reduce_scatter x2, waiting for transfers between devices, reduce_grads(): lax.psum_scatter(grads[1].astype(jnp.bfloat16), 'dp', scatter_dimension=0...  127 us
    psum x1, waiting for transfers between devices, reduce_grads(): lax.psum(summed[0].astype(jnp.bfloat16), ('tm', 'pos')).astype(jnp.float32)  123 us
    dot_general x14, matrix products, project_back(): jnp.einsum('...j,ij->...i', grads, weight, preferred_element_type=jnp.flo...  70.1 us
    dot_general x14, matrix products, project(): jnp.einsum('...i,ij->...j', inputs, weight, preferred_element_type=jnp.fl...  54.1 us
    dot_general x14, matrix products, weight_grad(): return jnp.dot(flat_left.T, flat_right, preferred_element_type=jnp.float32)  53.2 us
    another operation x15, local copies, waits for them, and re-layouts  47.5 us
  transfers between devices with their start and end apart: 25, of which 19 were waited for; matrix products, arithmetic and copies ran while one was open for 22% of the time, Pallas kernels for 0%

commit v1 on v0

v1 whole, which is shorter than its diff:
```python
import functools

import jax
import jax.numpy as jnp
from jax import lax
from jax.experimental import pallas as pl
from jax.experimental.pallas import tpu as pltpu
from jax.sharding import PartitionSpec as P

HEADS = 12
HD = 64
D = 768
FF = 3072
STEP = 10

NORM_EPSILON = 1e-06
CLIP_NORM = 1.0
LEARN_RATE = 0.03
LEARN_RATE_VEC = 0.25
BETA_FIRST = 0.9
BETA_SECOND = 0.999
ADAM_EPSILON = 1e-08
WEIGHT_DECAY = 0.05
MASKED_SCORE = -1e30
SCALE = HD ** (-0.5)

F32 = jnp.float32
BF16 = jnp.bfloat16
PAIR = 2 * HD
PAIRS = D // PAIR
NB = 256
ROWB = 112
VMEM_LIMIT = 56 * 1024 * 1024
SMALL_VMEM = 24 * 1024 * 1024

G_T, B_T, C_T, E_T, O_T, F_T, G_S, B_S, C_S, E_S, O_S, G_M, B_M, U_1, U_2 = (
    0, 1, 2, 3, 4, 5, 6, 7, 8, 9, 10, 11, 12, 13, 17,
)


COUNT_AT, T_AT, P_AT, Z_AT, C_AT, Q_AT = 0, 1, 2, 3, 4, 5
A_AT, B_AT, PAIR_AT, ODD_AT = 13, 14, 15, 16
OTHERS = (1, 3, 2)
PIECE = 48
VROWS = 24


def dot_nn(a, b):
    return lax.dot_general(a, b, (((1,), (0,)), ((), ())), preferred_element_type=F32)


def dot_nt(a, b):
    return lax.dot_general(a, b, (((1,), (1,)), ((), ())), preferred_element_type=F32)


def dot_tn(a, b):
    return lax.dot_general(a, b, (((0,), (0,)), ((), ())), preferred_element_type=F32)


def loop(count, body, unroll=1):
    def step(i, carry):
        body(i)
        return carry

    lax.fori_loop(0, count, step, 0, unroll=unroll)


def block(i, size):
    return pl.ds(pl.multiple_of(i * size, size), size)


def row_blocks(rows, body):
    loop(rows // ROWB, lambda i: body(pl.ds(pl.multiple_of(i * ROWB, 16), ROWB)))


def col_blocks(cols, body):
    loop(cols // NB, lambda i: body(block(i, NB)))


LANES = 128
TILES = D // LANES


def put_slot(xs, s, slots, value):
    for j in range(TILES):
        xs[j, pl.ds(s, value.shape[0], stride=slots), :] = value[:, j * LANES : (j + 1) * LANES]


def get_slot(xs, s, slots, count):
    return jnp.concatenate([xs[j, pl.ds(s, count, stride=slots), :] for j in range(TILES)], axis=1)


def get_rows(xs, r):
    return jnp.concatenate([xs[j, r, :] for j in range(TILES)], axis=1)


def put_rows(xs, r, value):
    for j in range(TILES):
        xs[j, r, :] = value[:, j * LANES : (j + 1) * LANES]


def put_cols(xs, i, value):
    per = NB // LANES
    for j in range(per):
        xs[i * per + j] = value[:, j * LANES : (j + 1) * LANES]


def normalise(x):
    centred = x - jnp.mean(x, axis=-1, keepdims=True)
    variance = jnp.mean(centred * centred, axis=-1, keepdims=True)
    inverse = lax.rsqrt(variance + NORM_EPSILON)
    return centred * inverse, inverse


def norm_back(x, grad, gain):
    z_hat, inverse = normalise(x)
    h = grad * gain
    first = jnp.mean(h, axis=-1, keepdims=True)
    second = jnp.mean(h * z_hat, axis=-1, keepdims=True)
    dz = inverse * (h - first - z_hat * second)
    return dz, jnp.sum(grad * z_hat, axis=0, keepdims=True), jnp.sum(grad, axis=0, keepdims=True)


def softmax_rows(scores):
    top = jnp.max(scores, axis=-1, keepdims=True)
    e = jnp.exp(scores - top)
    return e * (1.0 / jnp.sum(e, axis=-1, keepdims=True))


def head_masks():
    lane = lax.broadcasted_iota(jnp.int32, (1, PAIR), 1)
    return [(lane < HD).astype(BF16), (lane >= HD).astype(BF16)]


def gelu_parts(a):
    z = jnp.abs(a) * 0.7071067811865476
    t = 1.0 / (1.0 + 0.3275911 * z)
    e = jnp.exp(-z * z)
    poly = t * (0.254829592 + t * (-0.284496736 + t * (1.421413741 + t * (-1.453152027 + t * 1.061405429))))
    tail = 0.5 * poly * e
    phi_low = jnp.where(a < 0.0, tail, 1.0 - tail)
    return a * phi_low, phi_low + a * (0.3989422804014327 * e)


class Weight:
    def __init__(self, cols, rows=D, whole=None, shard=None, blocks=None, pieces=(), offset=0, tall=False):
        self.rows, self.cols, self.whole, self.offset, self.tall = rows, cols, whole, offset, tall
        self.blocks = blocks
        self.arrays = [whole] if whole is not None else [shard, *pieces]

    def scratch(self):
        count = 1 if self.whole is not None else len(self.blocks) + 8 * len(OTHERS)
        return [pltpu.VMEM((self.rows, self.cols), BF16), pltpu.SemaphoreType.DMA((count,))]

    def copies(self, refs, scal, dst, sems):
        if self.whole is not None:
            return [pltpu.make_async_copy(refs[0], dst, sems.at[0])]
        shard = self.rows // 4
        z, c = scal[Z_AT], scal[C_AT]
        own_rows = pl.ds(pl.multiple_of(z * shard, 16), shard)
        out, at = [], 0
        for first, size in self.blocks:
            if self.tall:
                src, to = refs[0].at[first : first + size, :], dst.at[own_rows, :]
            else:
                src, to = refs[0].at[:, first : first + size], dst.at[own_rows, at : at + size]
            at += size
            out.append(pltpu.make_async_copy(src, to, sems.at[len(out)]))
        width = self.cols if self.tall else self.cols // 2
        for k in range(8):
            half = c if k < 4 else 1 - c
            quarter = scal[Q_AT + k]
            for j, m in enumerate(OTHERS):
                row = jnp.bitwise_xor(z, m) * shard + quarter * PIECE
                col = 0
                if self.tall:
                    row = row + half * (shard // 2)
                else:
                    col = pl.multiple_of(half * width, 128)
                src = refs[1 + k].at[j, :, self.offset : self.offset + width]
                to = dst.at[pl.ds(pl.multiple_of(row, 16), PIECE), pl.ds(col, width)]
                out.append(pltpu.make_async_copy(src, to, sems.at[len(out)]))
        return out


class Loaded:
    def __init__(self, ref, copies):
        self.ref, self.copies, self.waited = ref, copies, False

    def get(self):
        if not self.waited:
            for c in self.copies:
                c.wait()
            self.waited = True
        return self.ref


def sds(shape, dtype):
    return jax.ShapeDtypeStruct(shape, dtype)


def cost(microseconds):
    return pl.CostEstimate(flops=int(microseconds * 1e9), bytes_accessed=0, transcendentals=0)


COSTS = {
    "time_in": 12, "time_attn": 11, "time_mid": 9, "space_in": 10, "space_mid": 15, "cot": 3, "cut": 3, "join": 3,
    "mlp": 50, "mlp_out": 14, "space_back": 22, "space_out": 17, "time_proj": 14, "time_attn_back": 28, "time_out": 20,
}


def call(kernel, scal, ins, weights, outs, scratch=(), after=()):
    n_in, n_out, n_scr = len(ins), len(outs), len(scratch)
    arrays = [a for w in weights for a in w.arrays]

    def body(scal_ref, *refs):
        in_refs, refs = refs[:n_in], refs[n_in:]
        array_refs, refs = refs[: len(arrays)], refs[len(arrays) + len(after) :]
        out_refs, refs = refs[:n_out], refs[n_out:]
        own, refs = refs[:n_scr], refs[n_scr:]
        loaded, at = [], 0
        for i, w in enumerate(weights):
            dst, sems = refs[2 * i : 2 * i + 2]
            copies = w.copies(array_refs[at : at + len(w.arrays)], scal_ref, dst, sems)
            at += len(w.arrays)
            for c in copies:
                c.start()
            loaded.append(Loaded(dst, copies))
        kernel(scal_ref, *in_refs, *loaded, *out_refs, *own)
        for w in loaded:
            w.get()

    in_vmem = pl.BlockSpec(memory_space=pltpu.VMEM)
    name = getattr(kernel, "func", kernel).__name__.removesuffix("_kernel")
    return pl.pallas_call(
        body,
        name=name,
        out_shape=tuple(outs),
        in_specs=[pl.BlockSpec(memory_space=pltpu.SMEM)]
        + [in_vmem] * n_in
        + [pl.BlockSpec(memory_space=pl.ANY)] * (len(arrays) + len(after)),
        out_specs=tuple(in_vmem for _ in outs),
        scratch_shapes=list(scratch) + [x for w in weights for x in w.scratch()],
        compiler_params=pltpu.CompilerParams(vmem_limit_bytes=VMEM_LIMIT),
        cost_estimate=cost(COSTS[name]),
    )(scal, *ins, *arrays, *after)


def grad_cols(width, body):
    loop(width // NB, lambda i: body(pl.multiple_of(i * NB, NB), NB))
    if width % NB:
        body(width - width % NB, width % NB)


def weight_grad(left_t, right, scal, mine, theirs):
    width = mine.shape[1]
    for out, half in ((theirs, 1 - scal[C_AT]), (mine, scal[C_AT])):

        def body(at, size, out=out, half=half):
            c = pl.ds(pl.multiple_of(half * width + at, 128), size)
            out[:, pl.ds(at, size)] = dot_nn(left_t[...], right[:, c]).astype(BF16)

        grad_cols(width, body)


def time_mask(scal, slots):
    row = lax.broadcasted_iota(jnp.int32, (ROWB, ROWB), 0)
    col = lax.broadcasted_iota(jnp.int32, (ROWB, ROWB), 1)
    frame = jnp.bitwise_xor(col % slots, scal[T_AT] * (slots // 2))
    return (row // slots == col // slots) & (frame < scal[COUNT_AT])


def project_qkv(h, w, par, q_row, v_row, out):
    for part, row in enumerate((q_row, None, v_row)):

        def cols(i, part=part, row=row):
            c = pl.ds(pl.multiple_of(part * D + i * NB, NB), NB)
            value = dot_nn(h[...], w[:, c])
            if row is not None:
                value = value + par[row : row + 1, block(i, NB)]
            out[:, c] = value.astype(BF16)

        loop(D // NB, cols)


def time_in_kernel(scal, own, peer, w_load, vec_load, x_out, h_out, qkv_out, par, xs):
    half, here = own.shape[0], own.shape[1]
    slots = 2 * half
    for s in range(slots):
        src = own if s < half else peer
        put_slot(xs, s, slots, src[s % half].astype(F32))
    vec = vec_load.get()
    par[...] = vec[:, :LANES].astype(F32).T[:VROWS, :]
    gain, shift = par[G_T : G_T + 1, :], par[B_T : B_T + 1, :]

    def rows(r):
        x = get_rows(xs, r)
        x_out[r, :] = x.astype(BF16)
        h_out[r, :] = (normalise(x)[0] * gain + shift).astype(BF16)

    row_blocks(xs.shape[1], rows)
    project_qkv(h_out, w_load.get(), par, C_T, E_T, qkv_out)


def time_attn_kernel(slots, scal, qkv, y_out):
    mask = time_mask(scal, slots)
    masks = head_masks()

    def group(r):
        for j in range(PAIRS):
            q = qkv[r, j * PAIR : (j + 1) * PAIR]
            k = qkv[r, D + j * PAIR : D + (j + 1) * PAIR]
            v = qkv[r, 2 * D + j * PAIR : 2 * D + (j + 1) * PAIR]
            y = 0.0
            for h in range(2):
                s = jnp.where(mask, dot_nt(q * masks[h], k) * SCALE, MASKED_SCORE)
                y += dot_nn(softmax_rows(s).astype(BF16), v * masks[h])
            y_out[r, j * PAIR : (j + 1) * PAIR] = y.astype(BF16)

    row_blocks(y_out.shape[0], group)


def time_mid_kernel(scal, y, x, par, w_load, z_out, b0, b1, b2, b3, xs):
    here, per = b0.shape[1], b0.shape[0]
    slots = 4 * per
    w = w_load.get()

    def proj(i):
        c = block(i, NB)
        z_out[:, c] = (dot_nn(y[...], w[:, c]) + par[O_T : O_T + 1, c]).astype(BF16)

    loop(D // NB, proj)

    def after(i):
        c = block(i, NB)
        fc = dot_nn(z_out[...], w[:, pl.ds(pl.multiple_of(D + i * NB, NB), NB)])
        put_cols(xs, i, x[:, c].astype(F32) + (fc + par[F_T : F_T + 1, c]))

    loop(D // NB, after)
    for r, out in enumerate((b0, b1, b2, b3)):
        first = jnp.bitwise_xor(scal[P_AT], r) * per
        for i in range(per):
            out[i] = get_slot(xs, first + i, slots, here).astype(BF16)


def fill_space(blocks, xs):
    per, here = blocks[0].shape[0], blocks[0].shape[1]
    whole = here * len(blocks)
    for f in range(per):
        for r, b in enumerate(blocks):
            xs[f * whole + r * here : f * whole + (r + 1) * here, :] = b[f].astype(F32)


def cot_kernel(scal, b0, b1, b2, b3, dy_out, xs):
    per, here = b0.shape[0], b0.shape[1]
    fill_space((b0, b1, b2, b3), xs)
    whole = 4 * here
    rows = xs.shape[0]
    row = lax.broadcasted_iota(jnp.int32, (rows, 1), 0)
    slot = scal[P_AT] * per
    weight = jnp.zeros((rows, 1), F32)
    for f in range(per):
        frame = jnp.bitwise_xor(slot + f, scal[T_AT] * (2 * per))
        live = (frame < scal[COUNT_AT]).astype(F32)
        weight = jnp.where((row >= f * whole) & (row < (f + 1) * whole), live, weight)
    dy_out[...] = (xs[...] * weight).astype(BF16)


def cut_kernel(scal, own, peer, b0, b1, b2, b3):
    half, per = own.shape[0], b0.shape[0]
    for r, out in enumerate((b0, b1, b2, b3)):
        first = jnp.bitwise_xor(scal[P_AT], r) * per
        for i in range(per):
            for src, low in ((own, 0), (peer, half)):

                @pl.when((first >= low) & (first < low + half))
                def put(src=src, low=low):
                    out[i] = src[first - low + i]


def join_kernel(scal, b0, b1, b2, b3, own, peer):
    half, per = own.shape[0], b0.shape[0]
    for r, src in enumerate((b0, b1, b2, b3)):
        first = jnp.bitwise_xor(scal[P_AT], r) * per
        for i in range(per):
            for out, low in ((own, 0), (peer, half)):

                @pl.when((first >= low) & (first < low + half))
                def put(out=out, low=low):
                    out[first - low + i] = src[i]


def space_in_kernel(scal, b0, b1, b2, b3, par, w_load, x_out, h_out, qkv_out, xs):
    fill_space((b0, b1, b2, b3), xs)
    gain, shift = par[G_S : G_S + 1, :], par[B_S : B_S + 1, :]

    def rows(r):
        x = xs[r, :]
        x_out[r, :] = x.astype(BF16)
        h_out[r, :] = (normalise(x)[0] * gain + shift).astype(BF16)

    row_blocks(xs.shape[0], rows)
    project_qkv(h_out, w_load.get(), par, C_S, E_S, qkv_out)


def space_windows(rows, per):
    whole = rows // per
    step = whole // 16 * 16
    width = rows - step * (per - 1)
    return whole, step, width


def space_mid_kernel(per, scal, qkv, x, par, w_load, y_out, x2_out, m_out, ys):
    rows = x.shape[0]
    whole, step, width = space_windows(rows, per)
    masks = head_masks()
    ys[...] = jnp.zeros_like(ys)
    key = lax.broadcasted_iota(jnp.int32, (1, width), 1)
    query = lax.broadcasted_iota(jnp.int32, (width, 1), 0)

    def frame(f):
        r = pl.ds(pl.multiple_of(f * step, 16), width)
        first = f * (whole - step)
        keys = (key >= first) & (key < first + whole)
        queries = ((query >= first) & (query < first + whole)).astype(F32)
        for j in range(PAIRS):
            q = qkv[r, j * PAIR : (j + 1) * PAIR]
            k = qkv[r, D + j * PAIR : D + (j + 1) * PAIR]
            v = qkv[r, 2 * D + j * PAIR : 2 * D + (j + 1) * PAIR]
            y = 0.0
            for h in range(2):
                s = jnp.where(keys, dot_nt(q * masks[h], k) * SCALE, MASKED_SCORE)
                y += dot_nn(softmax_rows(s).astype(BF16), v * masks[h])
            ys[r, j * PAIR : (j + 1) * PAIR] += y * queries

    loop(per, frame)
    y_out[...] = ys[...].astype(BF16)
    w = w_load.get()

    def proj(i):
        c = block(i, NB)
        x2_out[:, c] = x[:, c].astype(F32) + (dot_nn(y_out[...], w[:, c]) + par[O_S : O_S + 1, c])

    loop(D // NB, proj)
    gain, shift = par[G_M : G_M + 1, :], par[B_M : B_M + 1, :]

    def norm(r):
        m_out[r, :] = (normalise(x2_out[r, :])[0] * gain + shift).astype(BF16)

    row_blocks(rows, norm)


def mlp_kernel(scal, m, dy, par, w1_load, w2_load, x3_out, dm_out, dw1, dw1_their, dw2, dw2_their, dup, es, das, mt):
    mt[...] = m[...].T
    w1, w2 = w1_load.get(), w2_load.get()

    def hidden(i):
        c = block(i, D)
        a = dot_nn(m[...], w1[:, c]) + par[pl.ds(U_1 + i, 1), :]
        g = dot_nt(dy[...], w2[c, :])
        value, slope = gelu_parts(a)
        da = (g * slope).astype(BF16)
        es[:, c] = value.astype(BF16)
        das[:, c] = da
        dup[pl.ds(i, 1), :] = jnp.sum(da.astype(F32), axis=0, keepdims=True)

    loop(FF // D, hidden)
    weight_grad(mt, das, scal, dw1, dw1_their)
    rows = D // 4

    def down(i):
        value = dot_tn(es[:, block(i, D)], dy[...]).astype(BF16)
        for j in range(4):
            part, to = value[j * rows : (j + 1) * rows, :], slice(j % 2 * D, (j % 2 + 1) * D)

            @pl.when(scal[C_AT] == j // 2)
            def keep(part=part, to=to):
                dw2[block(i, rows), to] = part

            @pl.when(scal[C_AT] != j // 2)
            def send(part=part, to=to):
                dw2_their[block(i, rows), to] = part

    loop(FF // D, down)

    def outs(c):
        x3_out[:, c] = dot_nn(es[...], w2[:, c])
        dm_out[:, c] = dot_nt(das[...], w1[c, :])

    col_blocks(D, outs)


def mlp_out_kernel(per, scal, x2, x3, dm, dy, y, par, w_load, dx2_out, dys_out, dw, dw_their, dvec, b0, b1, b2, b3, xs, yt):
    rows = x2.shape[0]
    here = b0.shape[1]
    gain = par[G_M : G_M + 1, :]
    dvec[...] = jnp.zeros_like(dvec)
    yt[...] = y[...].T

    def back(r):
        xs[r, :] = x2[r, :] + (x3[r, :] + par[U_2 : U_2 + 1, :])
        dz, dg, db = norm_back(x2[r, :], dm[r, :], gain)
        g = dy[r, :].astype(F32)
        dx2 = g + dz
        dx2_out[r, :] = dx2
        low = dx2.astype(BF16)
        dys_out[r, :] = low
        dvec[0:1, :] += dg
        dvec[1:2, :] += db
        dvec[2:3, :] += jnp.sum(g, axis=0, keepdims=True)
        dvec[3:4, :] += jnp.sum(low.astype(F32), axis=0, keepdims=True)

    row_blocks(rows, back)
    for f in range(per):
        for r, out in enumerate((b0, b1, b2, b3)):
            first = f * 4 * here + r * here
            out[f] = xs[first : first + here, :].astype(BF16)

    weight_grad(yt, dys_out, scal, dw, dw_their)
    w = w_load.get()

    def proj(i):
        c = block(i, NB)
        xs[:, c] = dot_nt(dys_out[...], w[c, :])

    loop(D // NB, proj)
    dys_out[...] = xs[...].astype(BF16)


def space_back_kernel(per, scal, qkv, dy, dqkv_out, dvec, acc):
    rows = dy.shape[0]
    whole, step, width = space_windows(rows, per)
    masks = head_masks()
    acc[...] = jnp.zeros_like(acc)
    key = lax.broadcasted_iota(jnp.int32, (1, width), 1)
    query = lax.broadcasted_iota(jnp.int32, (width, 1), 0)

    def frame(f):
        r = pl.ds(pl.multiple_of(f * step, 16), width)
        first = f * (whole - step)
        keys = (key >= first) & (key < first + whole)
        queries = ((query >= first) & (query < first + whole)).astype(F32)
        for j in range(PAIRS):
            cq = slice(j * PAIR, (j + 1) * PAIR)
            ck = slice(D + j * PAIR, D + (j + 1) * PAIR)
            cv = slice(2 * D + j * PAIR, 2 * D + (j + 1) * PAIR)
            q, k, v, g = qkv[r, cq], qkv[r, ck], qkv[r, cv], dy[r, cq]
            dq = dk = dv = 0.0
            for h in range(2):
                qm, km, gm = q * masks[h], k * masks[h], g * masks[h]
                s = jnp.where(keys, dot_nt(qm, k) * SCALE, MASKED_SCORE)
                p = softmax_rows(s) * queries
                dp = dot_nt(gm, v)
                ds = (p * (dp - jnp.sum(p * dp, axis=-1, keepdims=True))).astype(BF16)
                dq += dot_nn(ds, km)
                dk += dot_tn(ds, qm)
                dv += dot_tn(p.astype(BF16), gm)
            acc[r, cq] += dq * SCALE
            acc[r, ck] += dk * SCALE
            acc[r, cv] += dv

    loop(per, frame)
    low = acc[...].astype(BF16)
    dqkv_out[...] = low
    dvec[...] = jnp.zeros_like(dvec)
    dvec[0:1, :] = jnp.sum(dqkv_out[:, :D].astype(F32), axis=0, keepdims=True)
    dvec[1:2, :] = jnp.sum(dqkv_out[:, 2 * D :].astype(F32), axis=0, keepdims=True)


def space_out_kernel(per, scal, dqkv, h, x, dx2, par, w_load, dw, dw_their, dvec, b0, b1, b2, b3, xs, ht):
    rows = x.shape[0]
    here = b0.shape[1]
    ht[...] = h[...].T
    weight_grad(ht, dqkv, scal, dw, dw_their)
    w = w_load.get()

    def proj(c):
        xs[:, c] = dot_nt(dqkv[...], w[c, :])

    col_blocks(D, proj)
    gain = par[G_S : G_S + 1, :]
    dvec[...] = jnp.zeros_like(dvec)

    def back(r):
        dz, dg, db = norm_back(x[r, :].astype(F32), xs[r, :], gain)
        xs[r, :] = dx2[r, :] + dz
        dvec[0:1, :] += dg
        dvec[1:2, :] += db

    row_blocks(rows, back)
    for f in range(per):
        for r, out in enumerate((b0, b1, b2, b3)):
            first = f * 4 * here + r * here
            out[f] = xs[first : first + here, :].astype(BF16)


def time_proj_kernel(scal, b0, b1, b2, b3, y, z, w_load, dx1_out, dy_out, dw, dw_their, dvec, xs, zt, dz):
    per, here = b0.shape[0], b0.shape[1]
    slots = 4 * per
    for r, src in enumerate((b0, b1, b2, b3)):
        first = jnp.bitwise_xor(scal[P_AT], r) * per
        for i in range(per):
            put_slot(xs, first + i, slots, src[i].astype(F32))
    dvec[...] = jnp.zeros_like(dvec)

    def gather_rows(r):
        value = get_rows(xs, r)
        dx1_out[r, :] = value.astype(BF16)
        dvec[0:1, :] += jnp.sum(value, axis=0, keepdims=True)

    row_blocks(xs.shape[1], gather_rows)
    w = w_load.get()

    def proj_f(i):
        c = block(i, NB)
        dz[:, c] = dot_nt(dx1_out[...], w[c, D:]).astype(BF16)

    loop(D // NB, proj_f)

    def proj_o(i):
        c = block(i, NB)
        dy_out[:, c] = dot_nt(dz[...], w[c, :D]).astype(BF16)

    loop(D // NB, proj_o)
    dvec[1:2, :] = jnp.sum(dz[...].astype(F32), axis=0, keepdims=True)

    def put_grad(half, left, right):
        zt[...] = left[...].T

        def cols(out):
            def body(i):
                out[:, block(i, NB)] = dot_nn(zt[...], right[:, block(i, NB)]).astype(BF16)

            loop(D // NB, body)

        pl.when(scal[C_AT] == half)(lambda: cols(dw))
        pl.when(scal[C_AT] != half)(lambda: cols(dw_their))

    put_grad(1, z, dx1_out)
    put_grad(0, y, dz)


def time_attn_back_kernel(slots, scal, qkv, dys, dqkv_out, dvec):
    mask = time_mask(scal, slots)
    masks = head_masks()

    def group(rr):
        for j in range(PAIRS):
            cq = slice(j * PAIR, (j + 1) * PAIR)
            ck = slice(D + j * PAIR, D + (j + 1) * PAIR)
            cv = slice(2 * D + j * PAIR, 2 * D + (j + 1) * PAIR)
            q, k, v, g = qkv[rr, cq], qkv[rr, ck], qkv[rr, cv], dys[rr, cq]
            dq = dk = dv = 0.0
            for hh in range(2):
                qm, km, gm = q * masks[hh], k * masks[hh], g * masks[hh]
                s = jnp.where(mask, dot_nt(qm, k) * SCALE, MASKED_SCORE)
                p = softmax_rows(s)
                dp = dot_nt(gm, v)
                ds = (p * (dp - jnp.sum(p * dp, axis=-1, keepdims=True))).astype(BF16)
                dq += dot_nn(ds, km)
                dk += dot_tn(ds, qm)
                dv += dot_tn(p.astype(BF16), gm)
            dqkv_out[rr, cq] = (dq * SCALE).astype(BF16)
            dqkv_out[rr, ck] = (dk * SCALE).astype(BF16)
            dqkv_out[rr, cv] = dv.astype(BF16)

    row_blocks(dys.shape[0], group)
    dvec[...] = jnp.zeros_like(dvec)
    dvec[0:1, :] = jnp.sum(dqkv_out[:, :D].astype(F32), axis=0, keepdims=True)
    dvec[1:2, :] = jnp.sum(dqkv_out[:, 2 * D :].astype(F32), axis=0, keepdims=True)


def time_out_kernel(
    scal, dqkv, h, x, dx1, par, v_t, v_a, v_n, v_s, v_m, v_u, w_load, own, peer, dw, dw_their, vec, dvec, xs, ht, vs
):
    half, here = own.shape[0], own.shape[1]
    slots = 2 * half
    w = w_load.get()

    def proj(i):
        put_cols(xs, i, dot_nt(dqkv[...], w[block(i, NB), :]))

    loop(D // NB, proj)
    gain = par[G_T : G_T + 1, :]
    dvec[...] = jnp.zeros_like(dvec)

    def back(r):
        dz, dg, db = norm_back(x[r, :].astype(F32), get_rows(xs, r), gain)
        put_rows(xs, r, dx1[r, :].astype(F32) + dz)
        dvec[0:1, :] += dg
        dvec[1:2, :] += db

    row_blocks(xs.shape[1], back)
    for s in range(slots):
        v = get_slot(xs, s, slots, here)
        if s < half:
            own[s] = v
        else:
            peer[s - half] = v.astype(BF16)
    vs[...] = jnp.zeros_like(vs)
    for at, (src, row, count) in enumerate(
        (
            (dvec, 0, 2), (None, 0, 0), (v_a, 0, 2), (None, 0, 0), (v_t, 1, 1), (v_t, 0, 1), (v_n, 0, 2), (None, 0, 0),
            (v_s, 0, 2), (None, 0, 0), (v_m, 3, 1), (v_m, 0, 2), (None, 0, 0), (None, 0, 0), (None, 0, 0), (None, 0, 0),
            (None, 0, 0), (v_m, 2, 1),
        )
    ):
        if src is not None:
            vs[at : at + count, :] = src[row : row + count, :]
    vs[U_1 : U_1 + FF // D, :] = v_u[: FF // D, :]
    vec[...] = vs[...].T.astype(BF16)
    ht[...] = h[...].T
    weight_grad(ht, dqkv, scal, dw, dw_their)


def add_split_kernel(packs, n_after, sel_at, scal, *refs):
    n = len(packs)
    send, keep = refs[2 * n + n_after], refs[2 * n + n_after + 1]
    sel = scal[sel_at]
    for i, (offset, width) in enumerate(packs):
        mine, other = refs[i], refs[n + i]
        for out, which in ((send, 1 - sel), (keep, sel)):
            value = mine[0, which].astype(F32) + other[0, which].astype(F32)
            out[0, :, offset : offset + width] = value.astype(BF16)


def add_split(scal, sel_at, mine, other, packs, rows, after=()):
    n = mine[0].shape[0]
    out = sds((n, rows, sum(w for _, w in packs)), BF16)

    def spec(a):
        return pl.BlockSpec((1,) + a.shape[1:], lambda i: (i, 0, 0, 0))

    return pl.pallas_call(
        functools.partial(add_split_kernel, packs, len(after), sel_at),
        grid=(n,),
        out_shape=(out, out),
        in_specs=[pl.BlockSpec(memory_space=pltpu.SMEM)]
        + [spec(a) for a in [*mine, *other]]
        + [pl.BlockSpec(memory_space=pl.ANY)] * len(after),
        out_specs=tuple(pl.BlockSpec((1, *out.shape[1:]), lambda i: (i, 0, 0)) for _ in range(2)),
        compiler_params=pltpu.CompilerParams(vmem_limit_bytes=SMALL_VMEM),
        cost_estimate=cost(2),
    )(scal, *mine, *other, *after)


def adam_update(weight, grad, moment, square, decay, factor, rate):
    grad = grad * factor
    moment = BETA_FIRST * moment + (1.0 - BETA_FIRST) * grad
    square = BETA_SECOND * square + (1.0 - BETA_SECOND) * grad * grad
    moment_hat = moment * (1.0 / (1.0 - BETA_FIRST**STEP))
    square_hat = square * (1.0 / (1.0 - BETA_SECOND**STEP))
    fresh = weight - rate * (moment_hat / (jnp.sqrt(square_hat) + ADAM_EPSILON) + decay * weight)
    return (fresh, moment, square)


PLANE = ("tm", "pos")
EVERY = ("dp", "tm", "pos")


def pos_permute(a, r):
    n = lax.axis_size("pos")
    return lax.ppermute(a, "pos", [(i, i ^ r) for i in range(n)]) if r else a


def tm_permute(a):
    n = lax.axis_size("tm")
    return lax.ppermute(a, "tm", [(i, n - 1 - i) for i in range(n)])


def grid_permute(a, move):
    pairs = []
    for z in range(4):
        for x in range(2):
            for p in range(4):
                zz, xx, pp = move(z, x, p)
                pairs.append(((z * 2 + x) * 4 + p, (zz * 2 + xx) * 4 + pp))
    return lax.ppermute(a, EVERY, pairs)


def next_plane(a):
    return grid_permute(a, lambda z, x, p: (z ^ 1, x, p))


def far_plane(a):
    return grid_permute(a, lambda z, x, p: (z ^ 3, x, p))


def first_side(a):
    return grid_permute(a, lambda z, x, p: (z, x, p ^ 2) if p & 1 else (z, x ^ 1, p))


def second_side(a):
    return grid_permute(a, lambda z, x, p: (z, x ^ 1, p) if p & 1 else (z, x, p ^ 2))


def other_core(a):
    return grid_permute(a, lambda z, x, p: (z, x, p ^ 1))


def spread_plane(part):
    side = first_side(part)
    far, both = second_side(part), second_side(side)
    own = [part, side, far, both]
    return own + [other_core(a) for a in own]


def once(value, *others):
    return lax.optimization_barrier((value, *others))[0]


def gather_lines(piece):
    near = next_plane(piece)
    return [near, far_plane(piece), far_plane(near)]


class Group:
    def __init__(self, scal, members):
        self.scal, self.members, self.packs, at = scal, members, [], 0
        for mine, _ in members:
            self.packs.append((at, mine.shape[1]))
            at += mine.shape[1]
        self.width = at
        self.received = [other_core(t) for _, t in members]

    def add(self, mine, theirs):
        self.members = self.members + [(mine, theirs)]
        self.packs.append((self.width, mine.shape[1]))
        self.width += mine.shape[1]
        self.received = self.received + [other_core(theirs)]

    def chip(self, *after):
        mine = [m.reshape(4, 2, -1, m.shape[1]) for m, _ in self.members]
        other = [r.reshape(4, 2, -1, r.shape[1]) for r in self.received]
        self.send, self.keep = add_split(self.scal, A_AT, mine, other, self.packs, 2 * PIECE, after)
        self.received = first_side(self.send)

    def step(self, sel, shape, rows, move, after):
        shape = (*shape, self.width)
        self.send, self.keep = add_split(
            self.scal, sel, [self.keep.reshape(shape)], [self.received.reshape(shape)], [(0, self.width)], rows, after
        )
        self.received = move(self.send)

    def side(self, *after):
        self.step(B_AT, (4, 2, PIECE), PIECE, second_side, after)

    def plane(self, *after):
        self.step(PAIR_AT, (1, 2, 2 * PIECE), 2 * PIECE, far_plane, after)

    def pair(self, *after):
        self.step(ODD_AT, (1, 2, PIECE), PIECE, next_plane, after)

    def total(self):
        return (self.keep[0].astype(F32) + self.received[0].astype(F32)).astype(BF16)


def adam_kernel(jobs, n_arrays, scal, factor, *refs):
    arrays, refs = refs[:n_arrays], refs[n_arrays:]
    ins, outs, grads, sems = refs[:9], refs[9:19], refs[19:22], refs[22]
    step, scale = pl.program_id(0), factor[0]

    @pl.when(step == 0)
    def bring():
        copies = []
        for start, offset, width, to_grad, firsts in jobs:
            for k in range(8):
                half = scal[C_AT] if k < 4 else 1 - scal[C_AT]
                quarter = scal[Q_AT + k] * PIECE
                each = width // len(firsts)
                for j, (low, high) in enumerate(firsts):
                    src = arrays[start + k].at[:, offset + j * each : offset + (j + 1) * each]
                    if to_grad == 1:
                        rows = pl.ds(pl.multiple_of(low + half * (high - low) + quarter, 16), PIECE)
                        to = grads[1].at[rows, :]
                    else:
                        rows = pl.ds(pl.multiple_of(quarter, 16), PIECE)
                        to = grads[to_grad].at[rows, pl.ds(pl.multiple_of(low + half * (high - low), 128), each)]
                    copies.append(pltpu.make_async_copy(src, to, sems.at[len(copies)]))
        for c in copies:
            c.start()
        for c in copies:
            c.wait()
        g = grads[2][:, :LANES].astype(F32).T[: ins[6].shape[0], :]
        fresh = adam_update(ins[6][...], g, ins[7][...], ins[8][...], 0.0, scale, LEARN_RATE_VEC)
        for out, value in zip(outs[6:9], fresh):
            out[...] = value
        outs[9][...] = g[U_2 : U_2 + 1, :] * scale

    for i, grad in enumerate(grads[:2]):
        weight, moment, square = ins[3 * i : 3 * i + 3]
        size = weight.shape[0]
        g = grad[pl.ds(pl.multiple_of(step * size, 16), size), :].astype(F32)
        fresh = adam_update(weight[...], g, moment[...], square[...], WEIGHT_DECAY, scale, LEARN_RATE)
        for out, value in zip(outs[3 * i : 3 * i + 3], fresh):
            out[...] = value


def adam_all(scal, factor, arrays, jobs, blocks, wide, tall, vec):
    anywhere = pl.BlockSpec(memory_space=pl.ANY)
    smem = pl.BlockSpec(memory_space=pltpu.SMEM)
    both = [*wide, *tall]
    specs = [pl.BlockSpec((v.shape[0] // blocks, v.shape[1]), lambda i: (i, 0)) for v in both]
    specs += [pl.BlockSpec(v.shape, lambda i: (0, 0)) for v in vec]
    both = both + list(vec)
    shard = vec[0].shape[1]
    return pl.pallas_call(
        functools.partial(adam_kernel, jobs, len(arrays)),
        grid=(blocks,),
        out_shape=tuple(sds(v.shape, F32) for v in both) + (sds((1, shard), F32),),
        in_specs=[smem, smem] + [anywhere] * len(arrays) + specs,
        out_specs=(*specs, pl.BlockSpec((1, shard), lambda i: (0, 0))),
        scratch_shapes=[
            pltpu.VMEM(wide[0].shape, BF16),
            pltpu.VMEM(tall[0].shape, BF16),
            pltpu.VMEM((shard, 2 * LANES), BF16),
            pltpu.SemaphoreType.DMA((sum(8 * len(j[4]) for j in jobs),)),
        ],
        compiler_params=pltpu.CompilerParams(vmem_limit_bytes=VMEM_LIMIT),
        cost_estimate=cost(25),
    )(scal, factor, *arrays, *both)


def shards(
    tokens,
    cotangent,
    frame_counts,
    weight_in,
    weight_out,
    vectors,
    moment_in,
    moment_out,
    moment_vec,
    square_in,
    square_out,
    square_vec,
):
    clips, half, here, _ = tokens.shape
    tm, n_pos, n_dp = lax.axis_size("tm"), lax.axis_size("pos"), lax.axis_size("dp")
    slots = half * tm
    per = slots // n_pos
    rows = slots * here
    t, p, z = lax.axis_index("tm"), lax.axis_index("pos"), lax.axis_index("dp")
    count = lax.dynamic_index_in_dim(frame_counts, t, keepdims=False)
    line = n_dp == 4
    core = p % 2 if line else 0
    a = jnp.where(core == 0, t, p // 2)
    b = jnp.where(core == 0, p // 2, t)
    quarters = [2 * a + b, 2 * (1 - a) + b, 2 * a + 1 - b, 2 * (1 - a) + 1 - b]
    quarters += [2 * b + a, 2 * (1 - b) + a, 2 * b + 1 - a, 2 * (1 - b) + 1 - a]
    scal = jnp.stack([count, t, p, z, core, *quarters, a, b, z // 2, z % 2]).astype(jnp.int32)

    own_tokens, peer_tokens, own_cot, peer_cot = (
        lax.dynamic_index_in_dim(v, at, keepdims=False) for v in (tokens, cotangent) for at in (t, 1 - t)
    )
    low_in, low_out = weight_in.astype(BF16), weight_out.astype(BF16)
    vec_low = jnp.pad(vectors.astype(BF16), ((0, 0), (0, LANES - vectors.shape[1])))
    vec_low = jnp.concatenate([vec_low, vec_low], axis=1)

    spans = {"at": (0, 3 * D), "ot": (3 * D, 2 * D), "as": (5 * D, 3 * D), "os": (8 * D, D)}

    def whole(low, *after):
        part = low.shape[0] // (tm * n_pos)
        mine = once(lax.dynamic_slice_in_dim(low, (t * n_pos + p) * part, part, axis=0), *after)
        return lax.all_gather(mine, EVERY, axis=0, tiled=True)

    blk = sds((per, here, D), BF16)
    act = sds((rows, D), BF16)
    wide = sds((rows, 3 * D), BF16)
    full = sds((rows, D), F32)
    par_out = sds((VROWS, D), F32)
    vec_out = sds((8, D), F32)
    scr = pltpu.VMEM((rows, D), F32)
    scr_tiled = pltpu.VMEM((TILES, rows, LANES), F32)
    scr_low = pltpu.VMEM((rows, D), BF16)
    scr_hidden = pltpu.VMEM((rows, FF), BF16)
    scr_t = pltpu.VMEM((D, rows), BF16)

    def halves(cols, height=D):
        return [sds((height, cols), BF16)] * 2

    after_in = after_attn = after_mid = after_space = ()
    if line:
        quarter = lax.dynamic_slice_in_dim(weight_in, quarters[0] * PIECE, PIECE, axis=0)
        vec_quarter = lax.dynamic_slice_in_dim(vec_low[:, :LANES], quarters[0] * PIECE, PIECE, axis=0)

        def half_of(first, width):
            return lax.dynamic_slice_in_dim(quarter, first + core * (width // 2), width // 2, axis=1).astype(BF16)

        def lines(piece, near):
            return [near, far_plane(piece), far_plane(near)]

        def sides(first):
            return first_side(first), second_side(first)

        def cores(group):
            return group + [other_core(v) for v in group]

        piece_0 = jnp.concatenate([half_of(*spans["at"]), vec_quarter], axis=1)
        near_0 = next_plane(piece_0)
        lines_0 = lines(piece_0, near_0)
        peer_tokens = tm_permute(peer_tokens)
        piece_1 = half_of(*spans["ot"])
        piece_2 = jnp.concatenate([half_of(*spans[name]) for name in ("as", "os")], axis=1)
        first_0 = jnp.stack(
            once(lines_0, peer_tokens, low_in, low_out, vec_low, own_tokens, scal, piece_1, piece_2)
        )
        side_0, far_0 = sides(first_0)
        up_all, down_all = whole(low_in[:, 9 * D :], first_0), whole(low_out, first_0)
        piece_1 = once(piece_1, first_0)
        near_1 = next_plane(piece_1)
        both_0 = second_side(side_0)
        lines_1 = lines(once(piece_1, far_0, near_1), once(near_1, far_0))
        group_0 = cores([first_0, side_0, far_0, both_0])
        peer_cot = tm_permute(once(peer_cot, both_0))
        first_1 = jnp.stack(once(lines_1, both_0))
        side_1, far_1 = sides(first_1)
        near_2 = next_plane(once(piece_2, first_1))
        w_at = Weight(3 * D, shard=low_in, blocks=[spans["at"]], pieces=group_0)
        w_vec = Weight(2 * LANES, shard=vec_low, blocks=[(0, 2 * LANES)], pieces=group_0, offset=3 * D // 2)
        after_in = (first_1,)
    else:
        peer_tokens, peer_cot = tm_permute(peer_tokens), tm_permute(peer_cot)

        w_at, w_ot, w_as, w_os = (
            Weight(width, whole=whole(low_in[:, first : first + width])) for first, width in spans.values()
        )
        up_all, down_all = whole(low_in[:, 9 * D :]), whole(low_out)
        w_vec = Weight(2 * LANES, whole=lax.all_gather(vec_low, "dp", axis=0, tiled=True))

    x, h_t, qkv_t, par = call(
        time_in_kernel, scal, [own_tokens, peer_tokens], [w_at, w_vec], [act, act, wide, par_out], [scr_tiled], after_in
    )
    if line:
        both_1 = second_side(once(side_1, h_t))
        lines_2 = lines(once(piece_2, h_t, near_2), once(near_2, h_t))
        after_attn = (near_2, side_1, peer_cot)
    (y_t,) = call(functools.partial(time_attn_kernel, slots), scal, [qkv_t], [], [act], [], after_attn)
    if line:
        group_1 = cores(once([first_1, side_1, far_1, both_1], y_t))
        w_ot = Weight(2 * D, shard=low_in, blocks=[spans["ot"]], pieces=group_1)
        first_2 = jnp.stack(once(lines_2, y_t))
        side_2, far_2 = sides(first_2)
        after_mid = (first_2,)
    z_t, *x1 = call(time_mid_kernel, scal, [y_t, x, par], [w_ot], [act, blk, blk, blk, blk], [scr_tiled], after_mid)
    x1 = [pos_permute(v, r) for r, v in enumerate(x1)]
    cot = call(cut_kernel, scal, [own_cot, peer_cot], [], [blk] * 4, [], (z_t,))
    if line:
        both_2 = second_side(once(side_2, z_t))
        group_2 = cores([first_2, side_2, far_2, both_2])
        w_as = Weight(3 * D, shard=low_in, blocks=[spans["as"]], pieces=group_2)
        w_os = Weight(D, shard=low_in, blocks=[spans["os"]], pieces=group_2, offset=3 * D // 2)
        after_space = (cot[0],)

    x1, h_s, qkv_s = call(space_in_kernel, scal, [*x1, par], [w_as], [act, act, wide], [scr], after_space)
    cot = [pos_permute(once(v, h_s), r) for r, v in enumerate(cot)]
    y_s, x2, m = call(
        functools.partial(space_mid_kernel, per), scal, [qkv_s, x1, par], [w_os], [act, full, act], [scr]
    )
    (dy,) = call(cot_kernel, scal, cot, [], [act], [scr], (m,))

    x3, dm, g_1, g_1t, g_2, g_2t, v_u = call(
        mlp_kernel,
        scal,
        [m, dy, par],
        [Weight(FF, whole=up_all), Weight(D, rows=FF, whole=down_all)],
        [full, full, *halves(FF // 2), *halves(FF // 2), vec_out],
        [scr_hidden, scr_hidden, scr_t],
    )
    if line:
        group_a = Group(scal, [(g_1, g_1t), (g_2, g_2t)])
    dx2, dys, g_os, g_ost, v_m, *out = call(
        functools.partial(mlp_out_kernel, per),
        scal,
        [x2, x3, dm, dy, y_s, par],
        [w_os],
        [full, act, *halves(D // 2), vec_out, blk, blk, blk, blk],
        [scr, scr_t],
    )

    wait = ()
    if line:
        group_a.chip(v_m)
        wait = (group_a.send,)
    dqkv_s, v_s = call(
        functools.partial(space_back_kernel, per),
        scal,
        [qkv_s, dys],
        [],
        [wide, vec_out],
        [pltpu.VMEM((rows, 3 * D), F32)],
        wait,
    )
    g_as, g_ast, v_n, *dx1 = call(
        functools.partial(space_out_kernel, per),
        scal,
        [dqkv_s, h_s, x1, dx2, par],
        [w_as],
        [*halves(3 * D // 2), vec_out, blk, blk, blk, blk],
        [scr, scr_t],
    )
    dx1 = [pos_permute(v, r) for r, v in enumerate(dx1)]

    if line:
        group_s = Group(scal, [(g_os, g_ost), (g_as, g_ast)])
        group_a.side(*dx1[1:])
        wait = (group_a.send,)
    dx1, dy_t, g_ot, g_ott, v_t = call(
        time_proj_kernel,
        scal,
        [*dx1, y_t, z_t],
        [w_ot],
        [act, act, *halves(D), vec_out],
        [scr_tiled, scr_t, scr_low],
        wait,
    )
    if line:
        group_s.add(g_ot, g_ott)
        group_a.plane(v_t)
        group_s.chip(group_a.send)
        wait = (group_s.send,)
    out = [pos_permute(once(v, v_t), r) for r, v in enumerate(out)]
    dqkv_t, v_a = call(
        functools.partial(time_attn_back_kernel, slots), scal, [qkv_t, dy_t], [], [wide, vec_out], [], wait
    )
    out_own, out_peer = call(join_kernel, scal, out, [], [sds((half, here, D), BF16)] * 2, [], (v_a,))
    if line:
        group_s.side(v_a)
        group_a.pair(v_a)
        wait = (group_s.send, group_a.send, out_own)
    out_peer = tm_permute(out_peer)
    mine = (jnp.arange(clips, dtype=jnp.int32) == t)[:, None, None, None]
    grad_own, grad_peer, g_at, g_att, g_vec, _ = call(
        time_out_kernel,
        scal,
        [dqkv_t, h_t, x, dx1, par, v_t, v_a, v_n, v_s, v_m, v_u],
        [w_at],
        [
            sds((half, here, D), F32),
            sds((half, here, D), BF16),
            *halves(3 * D // 2),
            sds((D, LANES), BF16),
            vec_out,
        ],
        [scr_tiled, scr_t, pltpu.VMEM((LANES, D), F32)],
        wait,
    )
    if line:
        group_t = Group(scal, [(g_at, g_att), (g_vec, g_vec)])
        group_t.chip()
        group_s.plane(group_t.send)
        sum_a = group_a.total()
        group_t.side()
        group_s.pair(group_t.send)
        group_t.plane()
        sum_s = group_s.total()
        parts = spread_plane(once(sum_a, group_t.send)) + spread_plane(once(sum_s, group_t.send))
        grad_peer = once(grad_peer, group_t.send)
        block_out = once(jnp.where(mine, out_own[None], out_peer[None]), group_t.send)
        group_t.pair()
        sum_t = group_t.total()
        sums = [sum_a, sum_s, sum_t]
        parts = [*parts, *spread_plane(sum_t)]
    else:
        block_out = jnp.where(mine, out_own[None], out_peer[None])
    grad_peer = tm_permute(grad_peer).astype(F32)
    input_grad = jnp.where(mine, grad_own[None], grad_peer[None])

    if line:
        square_sums = []
        for total in sums[:-1]:
            total = total.astype(F32)
            square_sums.append(jnp.sum(total * total))
        last = sums[-1].astype(F32)
        vec_at = group_t.width - LANES
        alone = jnp.where(core == 0, last[:, vec_at:], 0.0)
        square_sums += [jnp.sum(last[:, :vec_at] * last[:, :vec_at]), jnp.sum(alone * alone)]
        total_square = jnp.broadcast_to(sum(square_sums), (8, LANES))
        for move in (next_plane, far_plane, first_side, second_side, other_core):
            total_square = total_square + move(total_square)
        total_square = total_square[0, 0]
    else:
        g_in = jnp.concatenate([g_at, g_att, g_ot, g_ott, g_as, g_ast, g_os, g_ost, g_1, g_1t], axis=1)
        g_out = jnp.concatenate([g_2, g_2t], axis=1).reshape(4, D // 4, 4, D).transpose(0, 2, 1, 3).reshape(FF, D)
        g_vec = g_vec[:, : vectors.shape[1]]

        def reduced(grad):
            mine_rows = lax.psum_scatter(grad, "dp", scatter_dimension=0, tiled=True)
            return lax.psum(mine_rows, PLANE).astype(F32)

        g_in, g_out, g_vec = reduced(g_in), reduced(g_out), reduced(g_vec)
        local_square = jnp.sum(g_in * g_in) + jnp.sum(g_out * g_out) + jnp.sum(g_vec * g_vec)
        total_square = lax.psum(local_square, "dp")

    grad_norm = jnp.sqrt(total_square)
    factor = CLIP_NORM / jnp.maximum(grad_norm, CLIP_NORM)
    wide_in, tall_in = (weight_in, moment_in, square_in), (weight_out, moment_out, square_out)
    vec_in = (vectors, moment_vec, square_vec)
    if line:

        def span(name):
            first, width = spans[name]
            return ((first, first + width // 2),)

        shard = weight_out.shape[0]
        jobs = [
            (0, *group_a.packs[0], 0, ((9 * D, 9 * D + FF // 2),)),
            (0, *group_a.packs[1], 1, ((0, shard // 2), (shard // 4, shard // 4 * 3))),
        ]
        for name, (offset, width) in zip(("os", "as", "ot"), group_s.packs):
            jobs.append((8, offset, width, 0, span(name)))
        jobs.append((16, *group_t.packs[0], 0, span("at")))
        jobs.append((16, *group_t.packs[1], 2, ((0, LANES),)))
        fresh = adam_all(scal, factor.reshape(1), parts, jobs, 12, wide_in, tall_in, [v.T for v in vec_in])
        *fresh, new_v, first_v, second_v, bias_down = fresh
        fresh += [new_v.T, first_v.T, second_v.T]
        bias_down_grad = bias_down.reshape(-1)
    else:
        fresh = [
            *adam_update(weight_in, g_in, moment_in, square_in, WEIGHT_DECAY, factor, LEARN_RATE),
            *adam_update(weight_out, g_out, moment_out, square_out, WEIGHT_DECAY, factor, LEARN_RATE),
            *adam_update(vectors, g_vec, moment_vec, square_vec, 0.0, factor, LEARN_RATE_VEC),
        ]
        bias_down_grad = g_vec[:, U_2] * factor
    new_in, first_in, second_in, new_out, first_out, second_out, new_vec, first_vec, second_vec = fresh
    return (
        block_out,
        input_grad,
        grad_norm,
        new_in,
        new_out,
        new_vec,
        first_in,
        first_out,
        first_vec,
        second_in,
        second_out,
        second_vec,
        bias_down_grad,
    )


def solution(mesh):
    acts, rows = P("dp", "tm", "pos", None), P("dp", None)
    return jax.shard_map(
        shards,
        mesh=mesh,
        in_specs=(acts, acts, P("dp"), *[rows] * 9),
        out_specs=(acts, acts, P(), *[rows] * 9, P("dp")),
        check_vma=False,
    )
```

time: 1890 us -> 554 us (0.29)
  waiting for transfers between devices: 1210 us -> 125 us
  matrix products: 283 us -> 0 us
  Pallas kernels: 0 us -> 269 us
  local copies, waits for them, and re-layouts: 194 us -> 29.8 us
  other arithmetic: 128 us -> 18.8 us
  starting transfers between devices: 2.52 us -> 82.7 us
  blocking collectives: 50.6 us -> 0 us
    reduce_scatter x12 -> x0, waiting for transfers between devices: 697 us -> none  [the longest x2 519 us: reduce_grads(): lax.psum_scatter(grads[0].astype(jnp.bfloat16), 'dp', scatter_dimension=0...]
    all_gather x10 -> x2, waiting for transfers between devices: 358 us -> 0.01 us  [whole(): return lax.all_gather(mine, EVERY, axis=0, tiled=True)]
    dot_general x64 -> x0, matrix products: 271 us -> none  [the longest x14 70.1 us: project_back(): jnp.einsum('...j,ij->...i', grads, weight, preferred_element_type=jnp.flo...]
    pallas_call x0 -> x28, Pallas kernels: none -> 269 us  [the longest x15 224 us: call(): pl.pallas_call(body, name=name, out_shape=tuple(outs), in_specs=[pl.Block...]
    ppermute x0 -> x91, waiting for transfers between devices: none -> 125 us  [the longest x75 88 us: grid_permute(): return lax.ppermute(a, EVERY, pairs)]
    psum x1 -> x0, waiting for transfers between devices: 123 us -> none  [reduce_grads(): lax.psum(summed[0].astype(jnp.bfloat16), ('tm', 'pos')).astype(jnp.float32)]
    ppermute x0 -> x91, starting transfers between devices: none -> 82.6 us  [the longest x75 69.2 us: grid_permute(): return lax.ppermute(a, EVERY, pairs)]
    convert_element_type x30 -> x1, local copies, waits for them, and re-layouts: 72 us -> 0.13 us  [shards(): vectors.astype(BF16)]
  transfers between devices with their start and end apart: 25 -> 93, of which waited for: 19 -> 30; matrix products, arithmetic and copies ran while one was open for 22% -> 6% of each run, Pallas kernels for 0% -> 31%
where the time goes in v1:
time: 554 us; the launch traced here: 545 us
  Pallas kernels  269 us (49%)
  waiting for transfers between devices  125 us (23%)
  starting transfers between devices  82.7 us (15%)
  local copies, waits for them, and re-layouts  29.8 us (5%)
  between operations  20.1 us (4%)
  other arithmetic  18.8 us (3%)
    pallas_call x15, Pallas kernels, call(): pl.pallas_call(body, name=name, out_shape=tuple(outs), in_specs=[pl.Block...  224 us
    ppermute x75, waiting for transfers between devices, grid_permute(): return lax.ppermute(a, EVERY, pairs)  88 us
    ppermute x75, starting transfers between devices, grid_permute(): return lax.ppermute(a, EVERY, pairs)  69.2 us
    ppermute x12, waiting for transfers between devices, pos_permute(): return lax.ppermute(a, 'pos', [(i, i ^ r) for i in range(n)]) if r else a  28.9 us
    pallas_call x1, Pallas kernels, adam_all(): pl.pallas_call(functools.partial(adam_kernel, jobs, len(arrays)), grid=(b...  28.6 us
    pallas_call x12, Pallas kernels, add_split(): pl.pallas_call(functools.partial(add_split_kernel, packs, len(after), sel...  16.8 us
    unnamed x186, local copies, waits for them, and re-layouts  13.1 us
  transfers between devices with their start and end apart: 93, of which 30 were waited for; matrix products, arithmetic and copies ran while one was open for 6% of the time, Pallas kernels for 31%

profile of v1, /device:TPU:0, one launch (start us, length us, event | category | flops | bytes accessed | tf_op | source)
XLA Modules:
  0.0 545.2 jit_solution(5756411867603886879)
XLA Ops:
  7.2 2.2 dynamic-slice_bitcast_fusion.1
  9.4 2.9 collective-permute-start
  14.3 3.6 collective-permute-start.2
  19.6 4.4 collective-permute-done.1
  26.3 5.6 %convert_element_type.76.refs_2_.refs_3_.refs_5_.refs_6_.refs_11_ = bf16[192,9984]{1,0:T(8,128)(2,1)} convert(f32[192,9984]{1,0:T(8,128)} %refs_24_.1) | non-fusion elementwise | flops 1916928 | bytes 11501568 | tf_op jit(solution)/shard_map/convert_element_type | solution.py:956
  32.5 1.7 dynamic_slice.64
  37.6 1.7 constant_dynamic-slice_fusion
  41.5 2.0 collective-permute-start.5
  43.4 10.3 %collective-permute-done.4.refs_4_.refs_13_ = bf16[3,48,1280]{2,1,0:T(8,128)(2,1)S(1)} collective-permute-done((bf16[3,48,1280]{2,1,0:T(8,128)(2,1)S(1)}, bf16[3,48,1280]{2,1,0:T(8,128)(2,1)S(1)}, u32[]{:S(2)}, u32[]{:S(2)}) %collective-permute-start.4) | collective-permute-done | bytes 368672 | tf_op jit(solution)/shard_map/ppermute | solution.py:778
  54.5 6.8 %collective-permute-done.6.refs_6_.refs_15_ = bf16[3,48,1280]{2,1,0:T(8,128)(2,1)S(1)} collective-permute-done((bf16[3,48,1280]{2,1,0:T(8,128)(2,1)S(1)}, bf16[3,48,1280]{2,1,0:T(8,128)(2,1)S(1)}, u32[]{:S(2)}, u32[]{:S(2)}) %collective-permute-start.6) | collective-permute-done | bytes 368672 | tf_op jit(solution)/shard_map/ppermute | solution.py:778
  61.3 2.3 collective-permute-start.13
  63.5 4.3 collective-permute-done.13
  67.8 3.2 collective-permute-start.12
  71.1 2.0 copy.46.refs_1_
  73.2 1.8 collective-permute-done.12
  79.5 12.2 %time_in.1 = (bf16[784,768]{1,0:T(8,128)(2,1)}, bf16[784,768]{1,0:T(8,128)(2,1)}, bf16[784,2304]{1,0:T(8,128)(2,1)}, f32[24,768]{1,0:T(8,128)}) custom-call(s32[17]{0:T(128)} %stack.104.scal_ref.scal, bf16[8,49,768]{2,1,0:T(8,128)(2,1)} %bitcast.115, bf16[8,49,768]{2,1,0:T(8,128)(2,1)} %copy.46.refs_1_, ...), custom_call_target="tpu_custom_call" | custom-call | flops 12000000000 | tf_op jit(solution)/shard_map/time_in/pallas_call | solution.py:235
  91.7 3.0 collective-permute-start.24
  96.8 7.8 %collective-permute-done.16 = bf16[8,49,768]{2,0,1:T(8,128)(2,1)S(1)} collective-permute-done((bf16[8,49,768]{2,0,1:T(8,128)(2,1)S(1)}, bf16[8,49,768]{2,0,1:T(8,128)(2,1)S(1)}, u32[]{:S(2)}, u32[]{:S(2)}) %collective-permute-start.16) | collective-permute-done | bytes 602144 | tf_op jit(solution)/shard_map/ppermute | solution.py:768
  105.6 10.8 %time_attn.1.refs_0_.refs_4_ = bf16[784,768]{1,0:T(8,128)(2,1)} custom-call(s32[17]{0:T(128)} %stack.104.scal_ref.scal, bf16[784,2304]{1,0:T(8,128)(2,1)} %get-tuple-element.150.refs_0_, bf16[48,1536]{1,0:T(8,128)(2,1)} %copy-done.37, bf16[3,48,768]{2,1,0:T(8,128)(2,1)} %copy-done.73, bf16[8,49,768]{2,1,0:T(8,128)(2,1)} %copy.47.refs_3_.refs_1_), custom_call_target="tpu_custom_call" | custom-call | flops 11000000512 | tf_op jit(solution)/shard_map/time_attn/pallas_call | solution.py:235
  118.5 1.7 collective-permute-start.29
  121.5 9.0 %time_mid.1 = (bf16[784,768]{1,0:T(8,128)(2,1)}, bf16[4,49,768]{2,1,0:T(8,128)(2,1)}, bf16[4,49,768]{2,1,0:T(8,128)(2,1)}, bf16[4,49,768]{2,1,0:T(8,128)(2,1)}, bf16[4,49,768]{2,1,0:T(8,128)(2,1)}) custom-call(s32[17]{0:T(128)} %stack.104.scal_ref.scal, bf16[784,768]{1,0:T(8,128)(2,1)} %time_attn.1.refs_0_.refs_4_, ...), custom_call_target="tpu_custom_call" | custom-call | flops 8999999488 | tf_op jit(solution)/shard_map/time_mid/pallas_call | solution.py:235
  134.4 5.7 %collective-permute-done.30.refs_9_.refs_7_.refs_10_ = bf16[3,48,1536]{2,1,0:T(8,128)(2,1)S(1)} collective-permute-done((bf16[3,48,1536]{2,1,0:T(8,128)(2,1)S(1)}, bf16[3,48,1536]{2,1,0:T(8,128)(2,1)S(1)}, u32[]{:S(2)}, u32[]{:S(2)}) %collective-permute-start.30) | collective-permute-done | bytes 442400 | tf_op jit(solution)/shard_map/ppermute | solution.py:778
  142.9 3.1 cut.1
  146.1 7.4 %collective-permute-done.26.refs_2_ = bf16[4,49,768]{2,1,0:T(8,128)(2,1)S(1)} collective-permute-done((bf16[4,49,768]{2,1,0:T(8,128)(2,1)}, bf16[4,49,768]{2,1,0:T(8,128)(2,1)S(1)}, u32[]{:S(2)}, u32[]{:S(2)}) %collective-permute-start.26) | collective-permute-done | bytes 301088 | tf_op jit(solution)/shard_map/ppermute | solution.py:763
  153.4 6.3 %collective-permute-done.27.refs_3_ = bf16[4,49,768]{2,1,0:T(8,128)(2,1)S(1)} collective-permute-done((bf16[4,49,768]{2,1,0:T(8,128)(2,1)}, bf16[4,49,768]{2,1,0:T(8,128)(2,1)S(1)}, u32[]{:S(2)}, u32[]{:S(2)}) %collective-permute-start.27) | collective-permute-done | bytes 301088 | tf_op jit(solution)/shard_map/ppermute | solution.py:763
  160.9 10.3 %space_in.1 = (bf16[784,768]{1,0:T(8,128)(2,1)}, bf16[784,768]{1,0:T(8,128)(2,1)}, bf16[784,2304]{1,0:T(8,128)(2,1)}) custom-call(s32[17]{0:T(128)} %stack.104.scal_ref.scal, bf16[4,49,768]{2,1,0:T(8,128)(2,1)} %get-tuple-element.166.refs_0_, bf16[4,49,768]{2,1,0:T(8,128)(2,1)} %copy-done.60, bf16[4,49,768]{2,1,0:T(8,128)(2,1)} %copy-done.64, ...), custom_call_target="tpu_custom_call" | custom-call | flops 10000000000 | tf_op jit(solution)/shard_map/space_in/pallas_call | solution.py:235
  173.1 14.7 %space_mid.1 = (bf16[784,768]{1,0:T(8,128)(2,1)}, f32[784,768]{1,0:T(8,128)}, bf16[784,768]{1,0:T(8,128)(2,1)}) custom-call(s32[17]{0:T(128)} %stack.104.scal_ref.scal, bf16[784,2304]{1,0:T(8,128)(2,1)} %get-tuple-element.173.refs_0_, bf16[784,768]{1,0:T(8,128)(2,1)} %get-tuple-element.174.refs_1_.refs_2_, ...), custom_call_target="tpu_custom_call" | custom-call | flops 15000000512 | tf_op jit(solution)/shard_map/space_mid/pallas_call | solution.py:235
  189.0 2.8 cot.1.refs_1_.refs_3_
  191.8 43.7 %mlp.1 = (f32[784,768]{1,0:T(8,128)}, f32[784,768]{1,0:T(8,128)}, bf16[768,1536]{1,0:T(8,128)(2,1)}, bf16[768,1536]{1,0:T(8,128)(2,1)}, bf16[768,1536]{1,0:T(8,1...) custom-call(s32[17]{0:T(128)} %stack.104.scal_ref.scal, bf16[784,768]{1,0:T(8,128)(2,1)} %get-tuple-element.176.refs_4_.refs_0_, ...), custom_call_target="tpu_custom_call" | custom-call | flops 49999998976 | tf_op jit(solution)/shard_map/mlp/pallas_call | solution.py:235
  236.3 13.2 %mlp_out.1 = (f32[784,768]{1,0:T(8,128)}, bf16[784,768]{1,0:T(8,128)(2,1)}, bf16[768,384]{1,0:T(8,128)(2,1)}, bf16[768,384]{1,0:T(8,128)(2,1)}, f32[8,768]{1,0:T...) custom-call(s32[17]{0:T(128)} %stack.104.scal_ref.scal, ...), custom_call_target="tpu_custom_call" | custom-call | flops 14000000000 | tf_op jit(solution)/shard_map/mlp_out/pallas_call | solution.py:235
  250.2 4.2 shard_map.219
  257.3 21.6 %space_back.1 = (bf16[784,2304]{1,0:T(8,128)(2,1)}, f32[8,768]{1,0:T(8,128)}) custom-call(s32[17]{0:T(128)} %stack.104.scal_ref.scal, bf16[784,2304]{1,0:T(8,128)(2,1)} %get-tuple-element.173.refs_0_, bf16[784,768]{1,0:T(8,128)(2,1)} %get-tuple-element.191.refs_1_, bf16[4,96,3072]{2,1,0:T(8,128)(2,1)} %get-tuple-element.197.refs_2_), custom_call_target="tpu_custom_call" | custom-call | flops 22000001024 | tf_op jit(solution)/shard_map/space_back/pallas_call | solution.py:235
  279.0 17.8 %space_out.1 = (bf16[768,1152]{1,0:T(8,128)(2,1)}, bf16[768,1152]{1,0:T(8,128)(2,1)}, f32[8,768]{1,0:T(8,128)}, bf16[4,49,768]{2,1,0:T(8,128)(2,1)}, bf16[4,49,7...) custom-call(s32[17]{0:T(128)} %stack.104.scal_ref.scal, ...), custom_call_target="tpu_custom_call" | custom-call | flops 16999999488 | tf_op jit(solution)/shard_map/space_out/pallas_call | solution.py:235
  299.3 9.0 %collective-permute-done.41.refs_3_.refs_2_ = bf16[4,49,768]{2,1,0:T(8,128)(2,1)S(1)} collective-permute-done((bf16[4,49,768]{2,1,0:T(8,128)(2,1)}, bf16[4,49,768]{2,1,0:T(8,128)(2,1)S(1)}, u32[]{:S(2)}, u32[]{:S(2)}) %collective-permute-start.41) | collective-permute-done | bytes 301088 | tf_op jit(solution)/shard_map/ppermute | solution.py:763
  308.2 5.9 %collective-permute-done.42.refs_4_.refs_3_ = bf16[4,49,768]{2,1,0:T(8,128)(2,1)S(1)} collective-permute-done((bf16[4,49,768]{2,1,0:T(8,128)(2,1)}, bf16[4,49,768]{2,1,0:T(8,128)(2,1)S(1)}, u32[]{:S(2)}, u32[]{:S(2)}) %collective-permute-start.42) | collective-permute-done | bytes 301088 | tf_op jit(solution)/shard_map/ppermute | solution.py:763
  314.1 2.3 shard_map.220
  318.4 13.9 %time_proj.1 = (bf16[784,768]{1,0:T(8,128)(2,1)}, bf16[784,768]{1,0:T(8,128)(2,1)}, bf16[768,768]{1,0:T(8,128)(2,1)}, bf16[768,768]{1,0:T(8,128)(2,1)}, f32[8,768]{1,0:T(8,128)}) custom-call(s32[17]{0:T(128)} %stack.104.scal_ref.scal, bf16[4,49,768]{2,1,0:T(8,128)(2,1)} %get-tuple-element.200.refs_0_, bf16[4,49,768]{2,1,0:T(8,128)(2,1)} %copy-done.16, ...), custom_call_target="tpu_custom_call" | custom-call | flops 14000000000 | tf_op jit(solution)/shard_map/time_proj/pallas_call | solution.py:235
  337.6 2.5 collective-permute-start.53
  341.5 1.7 collective-permute-start.52
  343.2 28.1 %time_attn_back.1 = (bf16[784,2304]{1,0:T(8,128)(2,1)}, f32[8,768]{1,0:T(8,128)}) custom-call(s32[17]{0:T(128)} %stack.104.scal_ref.scal, bf16[784,2304]{1,0:T(8,128)(2,1)} %get-tuple-element.150.refs_0_, bf16[784,768]{1,0:T(8,128)(2,1)} %get-tuple-element.214.refs_1_, bf16[4,96,2304]{2,1,0:T(8,128)(2,1)} %copy-done.13), custom_call_target="tpu_custom_call" | custom-call | flops 28000000000 | tf_op jit(solution)/shard_map/time_attn_back/pallas_call | solution.py:235
  371.4 2.7 join.1
  374.8 2.7 shard_map.223
  378.4 19.8 %time_out.1 = (f32[8,49,768]{2,1,0:T(8,128)}, bf16[8,49,768]{2,1,0:T(8,128)(2,1)}, bf16[768,1152]{1,0:T(8,128)(2,1)}, bf16[768,1152]{1,0:T(8,128)(2,1)}, bf16[768,128]{1,0:T(8,128)(2,1)}, /*index=5*/f32[8,768]{1,0:T(8,128)}) custom-call(s32[17]{0:T(128)} %stack.104.scal_ref.scal, bf16[784,2304]{1,0:T(8,128)(2,1)} %get-tuple-element.227.refs_0_, ...), custom_call_target="tpu_custom_call" | custom-call | flops 20000000000 | tf_op jit(solution)/shard_map/time_out/pallas_call | solution.py:235
  399.6 2.9 collective-permute-done.55
  407.2 7.6 %collective-permute-done.60 = bf16[4,48,2304]{2,1,0:T(8,128)(2,1)S(1)} collective-permute-done((bf16[4,48,2304]{2,1,0:T(8,128)(2,1)S(1)}, bf16[4,48,2304]{2,1,0:T(8,128)(2,1)S(1)}, u32[]{:S(2)}, u32[]{:S(2)}) %collective-permute-start.60) | collective-permute-done | bytes 884768 | tf_op jit(solution)/shard_map/ppermute | solution.py:778
  416.5 4.9 collective-permute-done.56
  424.4 2.8 collective-permute-done.61
  427.8 7.0 %collective-permute-start.62 = (bf16[1,48,2304]{2,1,0:T(8,128)(2,1)S(1)}, bf16[1,48,2304]{2,1,0:T(8,128)(2,1)S(1)}, u32[]{:S(2)}, u32[]{:S(2)}) collective-permute-start(bf16[1,48,2304]{2,1,0:T(8,128)(2,1)S(1)} %get-tuple-element.253), channel_id=1, source_target_pairs={{0,8},{1,9},{2,10},{3,11},{4,12},{5,13},{6,14},{7,15},{8,0},{9,1},... | collective-permute-start | bytes 663560 | tf_op jit(solution)/shard_map/ppermute | solution.py:778
  435.5 1.7 collective-permute-start.63
  437.9 8.3 %collective-permute-done.63 = bf16[1,96,1280]{2,1,0:T(8,128)(2,1)S(1)} collective-permute-done((bf16[1,96,1280]{2,1,0:T(8,128)(2,1)S(1)}, bf16[1,96,1280]{2,1,0:T(8,128)(2,1)S(1)}, u32[]{:S(2)}, u32[]{:S(2)}) %collective-permute-start.63) | collective-permute-done | bytes 245792 | tf_op jit(solution)/shard_map/ppermute | solution.py:778
  450.0 2.1 collective-permute-done.64
  457.7 2.3 collective-permute-start.78
  464.0 1.7 collective-permute-start.77
  465.7 2.3 collective-permute-done.66
  468.8 13.1 %collective-permute-done.77.refs_9_ = bf16[48,2304]{1,0:T(8,128)(2,1)S(1)} collective-permute-done((bf16[48,2304]{1,0:T(8,128)(2,1)S(1)}, bf16[48,2304]{1,0:T(8,128)(2,1)S(1)}, u32[]{:S(2)}, u32[]{:S(2)}) %collective-permute-start.77) | collective-permute-done | bytes 221216 | tf_op jit(solution)/shard_map/ppermute | solution.py:778
  481.9 1.7 collective-permute-start.67
  483.7 1.9 collective-permute-done.67
  485.5 1.8 collective-permute-start.68
  487.6 1.6 collective-permute-done.68
  489.2 1.7 collective-permute-start.79
  493.1 2.4 collective-permute-done.79.refs_11_
  495.5 2.5 collective-permute-start.72
  505.6 1.7 broadcast_select_fusion
  508.2 28.6 %shard_map.231 = (f32[192,9984]{1,0:T(8,128)}, f32[192,9984]{1,0:T(8,128)}, f32[192,9984]{1,0:T(8,128)}, f32[768,768]{1,0:T(8,128)}, f32[768,768]{1,0:T(8,128)},...) custom-call(s32[17]{0:T(128)} %stack.104.scal_ref.scal, ...), custom_call_target="tpu_custom_call" | custom-call | flops 24999999488 | tf_op jit(solution)/shard_map/pallas_call | solution.py:907
  (385 shorter events, 86.5 us)
Async XLA Ops:
  7.2 184.6 %all-gather.5.cloned.1.call-start = ((), (), s32[]{:S(2)}) async-start(), calls=%async_computation.1 | async-start | bytes 4866048 | tf_op jit(solution)/shard_map/all_gather | solution.py:965
  9.4 29.9 %collective-permute-start = (bf16[8,49,768]{2,0,1:T(8,128)(2,1)}, bf16[8,49,768]{2,0,1:T(8,128)(2,1)}, u32[]{:S(2)}, u32[]{:S(2)}) collective-permute-start(bf16[8,49,768]{2,0,1:T(8,128)(2,1)} %get-tuple-element.279), channel_id=1, source_target_pairs={{0,4},{4,0},{1,5},{5,1},{2,6},{6,2},{3,7},{7,3},{8,12},{12,8},{9,1... | collective-permute-start | bytes 1806344 | tf_op jit(solution)/shard_map/ppermute | solution.py:768
  14.3 24.9 %collective-permute-start.2 = (bf16[48,1280]{1,0:T(8,128)(2,1)}, bf16[48,1280]{1,0:T(8,128)(2,1)}, u32[]{:S(2)}, u32[]{:S(2)}) collective-permute-start(bf16[48,1280]{1,0:T(8,128)(2,1)} %pad_maximum_fusion.4), channel_id=1, source_target_pairs={{0,24},{1,25},{2,26},{3,27},{4,28},{5,29},{6,30},{7,31},{8,16},{9,... | collective-permute-start | bytes 368648 | tf_op jit(solution)/shard_map/ppermute | solution.py:778
  24.1 15.2 %collective-permute-start.3 = (bf16[48,1280]{1,0:T(8,128)(2,1)}, bf16[48,1280]{1,0:T(8,128)(2,1)}, u32[]{:S(2)}, u32[]{:S(2)}) collective-permute-start(bf16[48,1280]{1,0:T(8,128)(2,1)} %collective-permute-done.1), channel_id=1, source_target_pairs={{0,24},{1,25},{2,26},{3,27},{4,28},{5,29},{6,30},{7,31},{8,16},{9,... | collective-permute-start | bytes 368648 | tf_op jit(solution)/shard_map/ppermute | solution.py:778
  40.5 151.3 %all-gather.3.cloned.1.call-start = ((), (), s32[]{:S(2)}) async-start(), calls=%async_computation | async-start | bytes 4866048 | tf_op jit(solution)/shard_map/all_gather | solution.py:965
  41.3 12.4 %collective-permute-start.4 = (bf16[3,48,1280]{2,1,0:T(8,128)(2,1)S(1)}, bf16[3,48,1280]{2,1,0:T(8,128)(2,1)S(1)}, u32[]{:S(2)}, u32[]{:S(2)}) collective-permute-start(bf16[3,48,1280]{2,1,0:T(8,128)(2,1)S(1)} %pad_maximum_fusion.1.refs_3_.refs_12_), channel_id=1, source_target_pairs={{0,4},{1,3},{2,6},{3,1},{4,0},{5,7},{6,2},{7,5},{8,12},{9,11},{10,... | collective-permute-start | bytes 1105928 | tf_op jit(solution)/shard_map/ppermute | solution.py:778
  41.5 12.5 %collective-permute-start.5 = (bf16[3,48,1280]{2,1,0:T(8,128)(2,1)S(1)}, bf16[3,48,1280]{2,1,0:T(8,128)(2,1)S(1)}, u32[]{:S(2)}, u32[]{:S(2)}) collective-permute-start(bf16[3,48,1280]{2,1,0:T(8,128)(2,1)S(1)} %pad_maximum_fusion.1.refs_3_.refs_12_), channel_id=1, source_target_pairs={{0,2},{1,5},{2,0},{3,7},{4,6},{5,1},{6,4},{7,3},{8,10},{9,13},{10,... | collective-permute-start | bytes 1105928 | tf_op jit(solution)/shard_map/ppermute | solution.py:778
  53.7 7.5 %collective-permute-start.6 = (bf16[3,48,1280]{2,1,0:T(8,128)(2,1)S(1)}, bf16[3,48,1280]{2,1,0:T(8,128)(2,1)S(1)}, u32[]{:S(2)}, u32[]{:S(2)}) collective-permute-start(bf16[3,48,1280]{2,1,0:T(8,128)(2,1)S(1)} %collective-permute-done.4.refs_4_.refs_13_), channel_id=1, source_target_pairs={{0,2},{1,5},{2,0},{3,7},{4,6},{5,1},{6,4},{7,3},{8,10},{9,13},{10,... | collective-permute-start | bytes 1105928 | tf_op jit(solution)/shard_map/ppermute | solution.py:778
  53.8 7.5 %collective-permute-start.11 = (bf16[48,768]{1,0:T(8,128)(2,1)S(1)}, bf16[48,768]{1,0:T(8,128)(2,1)S(1)}, u32[]{:S(2)}, u32[]{:S(2)}) collective-permute-start(bf16[48,768]{1,0:T(8,128)(2,1)S(1)} %copy-done.40), channel_id=1, source_target_pairs={{0,8},{1,9},{2,10},{3,11},{4,12},{5,13},{6,14},{7,15},{8,0},{9,1},... | collective-permute-start | bytes 221192 | tf_op jit(solution)/shard_map/ppermute | solution.py:778
  53.8 22.1 %collective-permute-start.7 = (bf16[3,48,1280]{2,1,0:T(8,128)(2,1)S(1)}, bf16[3,48,1280]{2,1,0:T(8,128)(2,1)S(1)}, u32[]{:S(2)}, u32[]{:S(2)}) collective-permute-start(bf16[3,48,1280]{2,1,0:T(8,128)(2,1)S(1)} %pad_maximum_fusion.1.refs_3_.refs_12_), channel_id=1, source_target_pairs={{0,1},{1,0},{2,3},{3,2},{4,5},{5,4},{6,7},{7,6},{8,9},{9,8},{10,11... | collective-permute-start | bytes 1105928 | tf_op jit(solution)/shard_map/ppermute | solution.py:778
  53.9 22.6 %collective-permute-start.9 = (bf16[3,48,1280]{2,1,0:T(8,128)(2,1)S(1)}, bf16[3,48,1280]{2,1,0:T(8,128)(2,1)S(1)}, u32[]{:S(2)}, u32[]{:S(2)}) collective-permute-start(bf16[3,48,1280]{2,1,0:T(8,128)(2,1)S(1)} %collective-permute-done.5.refs_5_.refs_14_), channel_id=1, source_target_pairs={{0,1},{1,0},{2,3},{3,2},{4,5},{5,4},{6,7},{7,6},{8,9},{9,8},{10,11... | collective-permute-start | bytes 1105928 | tf_op jit(solution)/shard_map/ppermute | solution.py:778
  54.4 23.6 %collective-permute-start.8 = (bf16[3,48,1280]{2,1,0:T(8,128)(2,1)S(1)}, bf16[3,48,1280]{2,1,0:T(8,128)(2,1)S(1)}, u32[]{:S(2)}, u32[]{:S(2)}) collective-permute-start(bf16[3,48,1280]{2,1,0:T(8,128)(2,1)S(1)} %collective-permute-done.4.refs_4_.refs_13_), channel_id=1, source_target_pairs={{0,1},{1,0},{2,3},{3,2},{4,5},{5,4},{6,7},{7,6},{8,9},{9,8},{10,11... | collective-permute-start | bytes 1105928 | tf_op jit(solution)/shard_map/ppermute | solution.py:778
  61.3 16.9 %collective-permute-start.10 = (bf16[3,48,1280]{2,1,0:T(8,128)(2,1)S(1)}, bf16[3,48,1280]{2,1,0:T(8,128)(2,1)S(1)}, u32[]{:S(2)}, u32[]{:S(2)}) collective-permute-start(bf16[3,48,1280]{2,1,0:T(8,128)(2,1)S(1)} %collective-permute-done.6.refs_6_.refs_15_), channel_id=1, source_target_pairs={{0,1},{1,0},{2,3},{3,2},{4,5},{5,4},{6,7},{7,6},{8,9},{9,8},{10,11... | collective-permute-start | bytes 1105928 | tf_op jit(solution)/shard_map/ppermute | solution.py:778
  67.8 7.1 %collective-permute-start.12 = (bf16[48,768]{1,0:T(8,128)(2,1)S(1)}, bf16[48,768]{1,0:T(8,128)(2,1)S(1)}, u32[]{:S(2)}, u32[]{:S(2)}) collective-permute-start(bf16[48,768]{1,0:T(8,128)(2,1)S(1)} %copy-done.40), channel_id=1, source_target_pairs={{0,24},{1,25},{2,26},{3,27},{4,28},{5,29},{6,30},{7,31},{8,16},{9,... | collective-permute-start | bytes 221192 | tf_op jit(solution)/shard_map/ppermute | solution.py:778
  75.6 40.8 %collective-permute-start.17 = (bf16[3,48,768]{2,1,0:T(8,128)(2,1)}, bf16[3,48,768]{2,1,0:T(8,128)(2,1)S(1)}, u32[]{:S(2)}, u32[]{:S(2)}) collective-permute-start(bf16[3,48,768]{2,1,0:T(8,128)(2,1)} %pad_maximum_fusion.2.refs_20_.refs_4_.refs_7_), channel_id=1, source_target_pairs={{0,2},{1,5},{2,0},{3,7},{4,6},{5,1},{6,4},{7,3},{8,10},{9,13},{10,... | collective-permute-start | bytes 663560 | tf_op jit(solution)/shard_map/ppermute | solution.py:778
  75.9 15.8 %collective-permute-start.15 = (bf16[3,48,768]{2,1,0:T(8,128)(2,1)}, bf16[3,48,768]{2,1,0:T(8,128)(2,1)S(1)}, u32[]{:S(2)}, u32[]{:S(2)}) collective-permute-start(bf16[3,48,768]{2,1,0:T(8,128)(2,1)} %pad_maximum_fusion.2.refs_20_.refs_4_.refs_7_), channel_id=1, source_target_pairs={{0,4},{1,3},{2,6},{3,1},{4,0},{5,7},{6,2},{7,5},{8,12},{9,11},{10,... | collective-permute-start | bytes 663560 | tf_op jit(solution)/shard_map/ppermute | solution.py:778
  76.6 15.1 %collective-permute-start.14 = (bf16[48,1536]{1,0:T(8,128)(2,1)S(1)}, bf16[48,1536]{1,0:T(8,128)(2,1)S(1)}, u32[]{:S(2)}, u32[]{:S(2)}) collective-permute-start(bf16[48,1536]{1,0:T(8,128)(2,1)S(1)} %copy-done.38), channel_id=1, source_target_pairs={{0,8},{1,9},{2,10},{3,11},{4,12},{5,13},{6,14},{7,15},{8,0},{9,1},... | collective-permute-start | bytes 442376 | tf_op jit(solution)/shard_map/ppermute | solution.py:778
  78.0 26.6 %collective-permute-start.16 = (bf16[8,49,768]{2,0,1:T(8,128)(2,1)S(1)}, bf16[8,49,768]{2,0,1:T(8,128)(2,1)S(1)}, u32[]{:S(2)}, u32[]{:S(2)}) collective-permute-start(bf16[8,49,768]{2,0,1:T(8,128)(2,1)S(1)} %get-tuple-element.152), channel_id=1, source_target_pairs={{0,4},{4,0},{1,5},{5,1},{2,6},{6,2},{3,7},{7,3},{8,12},{12,8},{9,1... | collective-permute-start | bytes 1806344 | tf_op jit(solution)/shard_map/ppermute | solution.py:768
  91.7 24.7 %collective-permute-start.24 = (bf16[48,1536]{1,0:T(8,128)(2,1)S(1)}, bf16[48,1536]{1,0:T(8,128)(2,1)S(1)}, u32[]{:S(2)}, u32[]{:S(2)}) collective-permute-start(bf16[48,1536]{1,0:T(8,128)(2,1)S(1)} %collective-permute-done.14.refs_1_), channel_id=1, source_target_pairs={{0,24},{1,25},{2,26},{3,27},{4,28},{5,29},{6,30},{7,31},{8,16},{9,... | collective-permute-start | bytes 442376 | tf_op jit(solution)/shard_map/ppermute | solution.py:778
  94.8 21.6 %collective-permute-start.23 = (bf16[48,1536]{1,0:T(8,128)(2,1)S(1)}, bf16[48,1536]{1,0:T(8,128)(2,1)S(1)}, u32[]{:S(2)}, u32[]{:S(2)}) collective-permute-start(bf16[48,1536]{1,0:T(8,128)(2,1)S(1)} %copy-done.38), channel_id=1, source_target_pairs={{0,24},{1,25},{2,26},{3,27},{4,28},{5,29},{6,30},{7,31},{8,16},{9,... | collective-permute-start | bytes 442376 | tf_op jit(solution)/shard_map/ppermute | solution.py:778
  95.6 20.8 %collective-permute-start.18 = (bf16[3,48,768]{2,1,0:T(8,128)(2,1)S(1)}, bf16[3,48,768]{2,1,0:T(8,128)(2,1)S(1)}, u32[]{:S(2)}, u32[]{:S(2)}) collective-permute-start(bf16[3,48,768]{2,1,0:T(8,128)(2,1)S(1)} %collective-permute-done.15.refs_2_.refs_5_.refs_8_), channel_id=1, source_target_pairs={{0,2},{1,5},{2,0},{3,7},{4,6},{5,1},{6,4},{7,3},{8,10},{9,13},{10,... | collective-permute-start | bytes 663560 | tf_op jit(solution)/shard_map/ppermute | solution.py:778
  118.5 15.4 %collective-permute-start.29 = (bf16[3,48,1536]{2,1,0:T(8,128)(2,1)S(1)}, bf16[3,48,1536]{2,1,0:T(8,128)(2,1)S(1)}, u32[]{:S(2)}, u32[]{:S(2)}) collective-permute-start(bf16[3,48,1536]{2,1,0:T(8,128)(2,1)S(1)} %pad_maximum_fusion.refs_12_.refs_6_.refs_4_.refs_7_), channel_id=1, source_target_pairs={{0,2},{1,5},{2,0},{3,7},{4,6},{5,1},{6,4},{7,3},{8,10},{9,13},{10,... | collective-permute-start | bytes 1327112 | tf_op jit(solution)/shard_map/ppermute | solution.py:778
  120.1 11.6 %collective-permute-start.28 = (bf16[3,48,1536]{2,1,0:T(8,128)(2,1)S(1)}, bf16[3,48,1536]{2,1,0:T(8,128)(2,1)S(1)}, u32[]{:S(2)}, u32[]{:S(2)}) collective-permute-start(bf16[3,48,1536]{2,1,0:T(8,128)(2,1)S(1)} %pad_maximum_fusion.refs_12_.refs_6_.refs_4_.refs_7_), channel_id=1, source_target_pairs={{0,4},{1,3},{2,6},{3,1},{4,0},{5,7},{6,2},{7,5},{8,12},{9,11},{10,... | collective-permute-start | bytes 1327112 | tf_op jit(solution)/shard_map/ppermute | solution.py:778
  131.8 8.3 %collective-permute-start.30 = (bf16[3,48,1536]{2,1,0:T(8,128)(2,1)S(1)}, bf16[3,48,1536]{2,1,0:T(8,128)(2,1)S(1)}, u32[]{:S(2)}, u32[]{:S(2)}) collective-permute-start(bf16[3,48,1536]{2,1,0:T(8,128)(2,1)S(1)} %collective-permute-done.28.refs_7_.refs_5_.refs_8_), channel_id=1, source_target_pairs={{0,2},{1,5},{2,0},{3,7},{4,6},{5,1},{6,4},{7,3},{8,10},{9,13},{10,... | collective-permute-start | bytes 1327112 | tf_op jit(solution)/shard_map/ppermute | solution.py:778
  133.3 6.8 %collective-permute-start.31 = (bf16[3,48,1536]{2,1,0:T(8,128)(2,1)}, bf16[3,48,1536]{2,1,0:T(8,128)(2,1)S(1)}, u32[]{:S(2)}, u32[]{:S(2)}) collective-permute-start(bf16[3,48,1536]{2,1,0:T(8,128)(2,1)} %copy-done.33), channel_id=1, source_target_pairs={{0,1},{1,0},{2,3},{3,2},{4,5},{5,4},{6,7},{7,6},{8,9},{9,8},{10,11... | collective-permute-start | bytes 1327112 | tf_op jit(solution)/shard_map/ppermute | solution.py:778
  133.3 8.4 %collective-permute-start.25 = (bf16[4,49,768]{2,1,0:T(8,128)(2,1)}, bf16[4,49,768]{2,1,0:T(8,128)(2,1)S(1)}, u32[]{:S(2)}, u32[]{:S(2)}) collective-permute-start(bf16[4,49,768]{2,1,0:T(8,128)(2,1)} %get-tuple-element.167), channel_id=1, source_target_pairs={{0,1},{1,0},{2,3},{3,2},{4,5},{5,4},{6,7},{7,6},{8,9},{9,8},{10,11... | collective-permute-start | bytes 903176 | tf_op jit(solution)/shard_map/ppermute | solution.py:763
  133.8 25.9 %collective-permute-start.32 = (bf16[3,48,1536]{2,1,0:T(8,128)(2,1)S(1)}, bf16[3,48,1536]{2,1,0:T(8,128)(2,1)S(1)}, u32[]{:S(2)}, u32[]{:S(2)}) collective-permute-start(bf16[3,48,1536]{2,1,0:T(8,128)(2,1)S(1)} %collective-permute-done.28.refs_7_.refs_5_.refs_8_), channel_id=1, source_target_pairs={{0,1},{1,0},{2,3},{3,2},{4,5},{5,4},{6,7},{7,6},{8,9},{9,8},{10,11... | collective-permute-start | bytes 1327112 | tf_op jit(solution)/shard_map/ppermute | solution.py:778
  133.9 25.8 %collective-permute-start.33 = (bf16[3,48,1536]{2,1,0:T(8,128)(2,1)S(1)}, bf16[3,48,1536]{2,1,0:T(8,128)(2,1)S(1)}, u32[]{:S(2)}, u32[]{:S(2)}) collective-permute-start(bf16[3,48,1536]{2,1,0:T(8,128)(2,1)S(1)} %collective-permute-done.29.refs_8_.refs_6_.refs_9_), channel_id=1, source_target_pairs={{0,1},{1,0},{2,3},{3,2},{4,5},{5,4},{6,7},{7,6},{8,9},{9,8},{10,11... | collective-permute-start | bytes 1327112 | tf_op jit(solution)/shard_map/ppermute | solution.py:778
  140.1 19.6 %collective-permute-start.34 = (bf16[3,48,1536]{2,1,0:T(8,128)(2,1)S(1)}, bf16[3,48,1536]{2,1,0:T(8,128)(2,1)S(1)}, u32[]{:S(2)}, u32[]{:S(2)}) collective-permute-start(bf16[3,48,1536]{2,1,0:T(8,128)(2,1)S(1)} %collective-permute-done.30.refs_9_.refs_7_.refs_10_), channel_id=1, source_target_pairs={{0,1},{1,0},{2,3},{3,2},{4,5},{5,4},{6,7},{7,6},{8,9},{9,8},{10,11... | collective-permute-start | bytes 1327112 | tf_op jit(solution)/shard_map/ppermute | solution.py:778
  140.2 13.2 %collective-permute-start.26 = (bf16[4,49,768]{2,1,0:T(8,128)(2,1)}, bf16[4,49,768]{2,1,0:T(8,128)(2,1)S(1)}, u32[]{:S(2)}, u32[]{:S(2)}) collective-permute-start(bf16[4,49,768]{2,1,0:T(8,128)(2,1)} %get-tuple-element.168), channel_id=1, source_target_pairs={{0,2},{1,3},{2,0},{3,1},{4,6},{5,7},{6,4},{7,5},{8,10},{9,11},{10,... | collective-permute-start | bytes 903176 | tf_op jit(solution)/shard_map/ppermute | solution.py:763
  141.7 18.0 %collective-permute-start.27 = (bf16[4,49,768]{2,1,0:T(8,128)(2,1)}, bf16[4,49,768]{2,1,0:T(8,128)(2,1)S(1)}, u32[]{:S(2)}, u32[]{:S(2)}) collective-permute-start(bf16[4,49,768]{2,1,0:T(8,128)(2,1)} %get-tuple-element.169), channel_id=1, source_target_pairs={{0,3},{1,2},{2,1},{3,0},{4,7},{5,6},{6,5},{7,4},{8,11},{9,10},{10,... | collective-permute-start | bytes 903176 | tf_op jit(solution)/shard_map/ppermute | solution.py:763
  171.1 16.7 %collective-permute-start.35 = (bf16[4,49,768]{2,1,0:T(8,128)(2,1)S(1)}, bf16[4,49,768]{2,1,0:T(8,128)(2,1)S(1)}, u32[]{:S(2)}, u32[]{:S(2)}) collective-permute-start(bf16[4,49,768]{2,1,0:T(8,128)(2,1)S(1)} %copy-done.63), channel_id=1, source_target_pairs={{0,1},{1,0},{2,3},{3,2},{4,5},{5,4},{6,7},{7,6},{8,9},{9,8},{10,11... | collective-permute-start | bytes 903176 | tf_op jit(solution)/shard_map/ppermute | solution.py:763
  171.6 16.3 %collective-permute-start.36 = (bf16[4,49,768]{2,1,0:T(8,128)(2,1)S(1)}, bf16[4,49,768]{2,1,0:T(8,128)(2,1)S(1)}, u32[]{:S(2)}, u32[]{:S(2)}) collective-permute-start(bf16[4,49,768]{2,1,0:T(8,128)(2,1)S(1)} %copy-done.62), channel_id=1, source_target_pairs={{0,2},{1,3},{2,0},{3,1},{4,6},{5,7},{6,4},{7,5},{8,10},{9,11},{10,... | collective-permute-start | bytes 903176 | tf_op jit(solution)/shard_map/ppermute | solution.py:763
  172.9 15.4 %collective-permute-start.37 = (bf16[4,49,768]{2,1,0:T(8,128)(2,1)S(1)}, bf16[4,49,768]{2,1,0:T(8,128)(2,1)S(1)}, u32[]{:S(2)}, u32[]{:S(2)}) collective-permute-start(bf16[4,49,768]{2,1,0:T(8,128)(2,1)S(1)} %copy-done.61), channel_id=1, source_target_pairs={{0,3},{1,2},{2,1},{3,0},{4,7},{5,6},{6,5},{7,4},{8,11},{9,10},{10,... | collective-permute-start | bytes 903176 | tf_op jit(solution)/shard_map/ppermute | solution.py:763
  235.5 13.9 %collective-permute-start.38 = (bf16[768,1536]{1,0:T(8,128)(2,1)}, bf16[768,1536]{1,0:T(8,128)(2,1)S(1)}, u32[]{:S(2)}, u32[]{:S(2)}) collective-permute-start(bf16[768,1536]{1,0:T(8,128)(2,1)} %get-tuple-element.194), channel_id=1, source_target_pairs={{0,1},{1,0},{2,3},{3,2},{4,5},{5,4},{6,7},{7,6},{8,9},{9,8},{10,11... | collective-permute-start | bytes 7077896 | tf_op jit(solution)/shard_map/ppermute | solution.py:778
  236.2 13.3 %collective-permute-start.39 = (bf16[768,1536]{1,0:T(8,128)(2,1)}, bf16[768,1536]{1,0:T(8,128)(2,1)}, u32[]{:S(2)}, u32[]{:S(2)}) collective-permute-start(bf16[768,1536]{1,0:T(8,128)(2,1)} %get-tuple-element.195), channel_id=1, source_target_pairs={{0,1},{1,0},{2,3},{3,2},{4,5},{5,4},{6,7},{7,6},{8,9},{9,8},{10,11... | collective-permute-start | bytes 7077896 | tf_op jit(solution)/shard_map/ppermute | solution.py:778
  255.9 58.3 %collective-permute-start.43 = (bf16[4,96,3072]{2,1,0:T(8,128)(2,1)}, bf16[4,96,3072]{2,1,0:T(8,128)(2,1)S(1)}, u32[]{:S(2)}, u32[]{:S(2)}) collective-permute-start(bf16[4,96,3072]{2,1,0:T(8,128)(2,1)} %get-tuple-element.197.refs_2_), channel_id=1, source_target_pairs={{0,4},{1,3},{2,6},{3,1},{4,0},{5,7},{6,2},{7,5},{8,12},{9,11},{10,... | collective-permute-start | bytes 7077896 | tf_op jit(solution)/shard_map/ppermute | solution.py:778
  297.1 11.1 %collective-permute-start.41 = (bf16[4,49,768]{2,1,0:T(8,128)(2,1)}, bf16[4,49,768]{2,1,0:T(8,128)(2,1)S(1)}, u32[]{:S(2)}, u32[]{:S(2)}) collective-permute-start(bf16[4,49,768]{2,1,0:T(8,128)(2,1)} %get-tuple-element.202), channel_id=1, source_target_pairs={{0,2},{1,3},{2,0},{3,1},{4,6},{5,7},{6,4},{7,5},{8,10},{9,11},{10,... | collective-permute-start | bytes 903176 | tf_op jit(solution)/shard_map/ppermute | solution.py:763
  297.5 16.6 %collective-permute-start.42 = (bf16[4,49,768]{2,1,0:T(8,128)(2,1)}, bf16[4,49,768]{2,1,0:T(8,128)(2,1)S(1)}, u32[]{:S(2)}, u32[]{:S(2)}) collective-permute-start(bf16[4,49,768]{2,1,0:T(8,128)(2,1)} %get-tuple-element.203), channel_id=1, source_target_pairs={{0,3},{1,2},{2,1},{3,0},{4,7},{5,6},{6,5},{7,4},{8,11},{9,10},{10,... | collective-permute-start | bytes 903176 | tf_op jit(solution)/shard_map/ppermute | solution.py:763
  298.7 38.9 %collective-permute-start.48 = (bf16[768,1152]{1,0:T(8,128)(2,1)}, bf16[768,1152]{1,0:T(8,128)(2,1)S(1)}, u32[]{:S(2)}, u32[]{:S(2)}) collective-permute-start(bf16[768,1152]{1,0:T(8,128)(2,1)} %get-tuple-element.219), channel_id=1, source_target_pairs={{0,1},{1,0},{2,3},{3,2},{4,5},{5,4},{6,7},{7,6},{8,9},{9,8},{10,11... | collective-permute-start | bytes 5308424 | tf_op jit(solution)/shard_map/ppermute | solution.py:778
  317.5 16.4 %collective-permute-start.50 = (bf16[4,48,3072]{2,1,0:T(8,128)(2,1)}, bf16[4,48,3072]{2,1,0:T(8,128)(2,1)S(1)}, u32[]{:S(2)}, u32[]{:S(2)}) collective-permute-start(bf16[4,48,3072]{2,1,0:T(8,128)(2,1)} %get-tuple-element.205.refs_15_), channel_id=1, source_target_pairs={{0,2},{1,5},{2,0},{3,7},{4,6},{5,1},{6,4},{7,3},{8,10},{9,13},{10,... | collective-permute-start | bytes 3538952 | tf_op jit(solution)/shard_map/ppermute | solution.py:778
  332.3 7.7 %collective-permute-start.49 = (bf16[768,768]{1,0:T(8,128)(2,1)}, bf16[768,768]{1,0:T(8,128)(2,1)S(1)}, u32[]{:S(2)}, u32[]{:S(2)}) collective-permute-start(bf16[768,768]{1,0:T(8,128)(2,1)} %get-tuple-element.220), channel_id=1, source_target_pairs={{0,1},{1,0},{2,3},{3,2},{4,5},{5,4},{6,7},{7,6},{8,9},{9,8},{10,11... | collective-permute-start | bytes 3538952 | tf_op jit(solution)/shard_map/ppermute | solution.py:778
  332.9 38.4 %collective-permute-start.44 = (bf16[4,49,768]{2,1,0:T(8,128)(2,1)S(1)}, bf16[4,49,768]{2,1,0:T(8,128)(2,1)}, u32[]{:S(2)}, u32[]{:S(2)}) collective-permute-start(bf16[4,49,768]{2,1,0:T(8,128)(2,1)S(1)} %copy-done.59), channel_id=1, source_target_pairs={{0,1},{1,0},{2,3},{3,2},{4,5},{5,4},{6,7},{7,6},{8,9},{9,8},{10,11... | collective-permute-start | bytes 903176 | tf_op jit(solution)/shard_map/ppermute | solution.py:763
  333.9 37.4 %collective-permute-start.45 = (bf16[4,49,768]{2,1,0:T(8,128)(2,1)S(1)}, bf16[4,49,768]{2,1,0:T(8,128)(2,1)}, u32[]{:S(2)}, u32[]{:S(2)}) collective-permute-start(bf16[4,49,768]{2,1,0:T(8,128)(2,1)S(1)} %copy-done.58), channel_id=1, source_target_pairs={{0,2},{1,3},{2,0},{3,1},{4,6},{5,7},{6,4},{7,5},{8,10},{9,11},{10,... | collective-permute-start | bytes 903176 | tf_op jit(solution)/shard_map/ppermute | solution.py:763
  336.5 34.8 %collective-permute-start.46 = (bf16[4,49,768]{2,1,0:T(8,128)(2,1)S(1)}, bf16[4,49,768]{2,1,0:T(8,128)(2,1)}, u32[]{:S(2)}, u32[]{:S(2)}) collective-permute-start(bf16[4,49,768]{2,1,0:T(8,128)(2,1)S(1)} %copy-done.57), channel_id=1, source_target_pairs={{0,3},{1,2},{2,1},{3,0},{4,7},{5,6},{6,5},{7,4},{8,11},{9,10},{10,... | collective-permute-start | bytes 903176 | tf_op jit(solution)/shard_map/ppermute | solution.py:763
  337.6 36.5 %collective-permute-start.53 = (bf16[1,96,3072]{2,1,0:T(8,128)(2,1)S(1)}, bf16[1,96,3072]{2,1,0:T(8,128)(2,1)S(1)}, u32[]{:S(2)}, u32[]{:S(2)}) collective-permute-start(bf16[1,96,3072]{2,1,0:T(8,128)(2,1)S(1)} %get-tuple-element.222.refs_6_), channel_id=1, source_target_pairs={{0,24},{1,25},{2,26},{3,27},{4,28},{5,29},{6,30},{7,31},{8,16},{9,... | collective-permute-start | bytes 1769480 | tf_op jit(solution)/shard_map/ppermute | solution.py:778
  341.5 33.2 %collective-permute-start.52 = (bf16[4,96,2304]{2,1,0:T(8,128)(2,1)S(1)}, bf16[4,96,2304]{2,1,0:T(8,128)(2,1)}, u32[]{:S(2)}, u32[]{:S(2)}) collective-permute-start(bf16[4,96,2304]{2,1,0:T(8,128)(2,1)S(1)} %get-tuple-element.223.refs_2_), channel_id=1, source_target_pairs={{0,4},{1,3},{2,6},{3,1},{4,0},{5,7},{6,2},{7,5},{8,12},{9,11},{10,... | collective-permute-start | bytes 5308424 | tf_op jit(solution)/shard_map/ppermute | solution.py:778
  398.8 16.0 %collective-permute-start.60 = (bf16[4,48,2304]{2,1,0:T(8,128)(2,1)S(1)}, bf16[4,48,2304]{2,1,0:T(8,128)(2,1)S(1)}, u32[]{:S(2)}, u32[]{:S(2)}) collective-permute-start(bf16[4,48,2304]{2,1,0:T(8,128)(2,1)S(1)} %copy-done.15), channel_id=1, source_target_pairs={{0,2},{1,5},{2,0},{3,7},{4,6},{5,1},{6,4},{7,3},{8,10},{9,13},{10,... | collective-permute-start | bytes 2654216 | tf_op jit(solution)/shard_map/ppermute | solution.py:778
  406.0 15.5 %collective-permute-start.56 = (bf16[4,96,1280]{2,1,0:T(8,128)(2,1)S(1)}, bf16[4,96,1280]{2,1,0:T(8,128)(2,1)S(1)}, u32[]{:S(2)}, u32[]{:S(2)}) collective-permute-start(bf16[4,96,1280]{2,1,0:T(8,128)(2,1)S(1)} %get-tuple-element.240.refs_2_), channel_id=1, source_target_pairs={{0,4},{1,3},{2,6},{3,1},{4,0},{5,7},{6,2},{7,5},{8,12},{9,11},{10,... | collective-permute-start | bytes 2949128 | tf_op jit(solution)/shard_map/ppermute | solution.py:778
  415.6 11.6 %collective-permute-start.61 = (bf16[1,96,2304]{2,1,0:T(8,128)(2,1)S(1)}, bf16[1,96,2304]{2,1,0:T(8,128)(2,1)S(1)}, u32[]{:S(2)}, u32[]{:S(2)}) collective-permute-start(bf16[1,96,2304]{2,1,0:T(8,128)(2,1)S(1)} %get-tuple-element.251), channel_id=1, source_target_pairs={{0,24},{1,25},{2,26},{3,27},{4,28},{5,29},{6,30},{7,31},{8,16},{9,... | collective-permute-start | bytes 1327112 | tf_op jit(solution)/shard_map/ppermute | solution.py:778
  422.3 12.5 %collective-permute-start.57 = (bf16[4,48,1280]{2,1,0:T(8,128)(2,1)S(1)}, bf16[4,48,1280]{2,1,0:T(8,128)(2,1)S(1)}, u32[]{:S(2)}, u32[]{:S(2)}) collective-permute-start(bf16[4,48,1280]{2,1,0:T(8,128)(2,1)S(1)} %get-tuple-element.242.refs_2_), channel_id=1, source_target_pairs={{0,2},{1,5},{2,0},{3,7},{4,6},{5,1},{6,4},{7,3},{8,10},{9,13},{10,... | collective-permute-start | bytes 1474568 | tf_op jit(solution)/shard_map/ppermute | solution.py:778
  423.3 36.9 %collective-permute-start.51 = (bf16[8,49,768]{2,0,1:T(8,128)(2,1)S(1)}, bf16[8,49,768]{2,0,1:T(8,128)(2,1)S(1)}, u32[]{:S(2)}, u32[]{:S(2)}) collective-permute-start(bf16[8,49,768]{2,0,1:T(8,128)(2,1)S(1)} %copy.51), channel_id=1, source_target_pairs={{0,4},{4,0},{1,5},{5,1},{2,6},{6,2},{3,7},{7,3},{8,12},{12,8},{9,1... | collective-permute-start | bytes 1806344 | tf_op jit(solution)/shard_map/ppermute | solution.py:768
  424.4 12.8 %collective-permute-start.59 = (bf16[1,48,3072]{2,1,0:T(8,128)(2,1)S(1)}, bf16[1,48,3072]{2,1,0:T(8,128)(2,1)S(1)}, u32[]{:S(2)}, u32[]{:S(2)}) collective-permute-start(bf16[1,48,3072]{2,1,0:T(8,128)(2,1)S(1)} %copy-done.20), channel_id=1, source_target_pairs={{0,8},{1,9},{2,10},{3,11},{4,12},{5,13},{6,14},{7,15},{8,0},{9,1},... | collective-permute-start | bytes 884744 | tf_op jit(solution)/shard_map/ppermute | solution.py:778
  427.8 20.1 %collective-permute-start.62 = (bf16[1,48,2304]{2,1,0:T(8,128)(2,1)S(1)}, bf16[1,48,2304]{2,1,0:T(8,128)(2,1)S(1)}, u32[]{:S(2)}, u32[]{:S(2)}) collective-permute-start(bf16[1,48,2304]{2,1,0:T(8,128)(2,1)S(1)} %get-tuple-element.253), channel_id=1, source_target_pairs={{0,8},{1,9},{2,10},{3,11},{4,12},{5,13},{6,14},{7,15},{8,0},{9,1},... | collective-permute-start | bytes 663560 | tf_op jit(solution)/shard_map/ppermute | solution.py:778
  435.5 10.7 %collective-permute-start.63 = (bf16[1,96,1280]{2,1,0:T(8,128)(2,1)S(1)}, bf16[1,96,1280]{2,1,0:T(8,128)(2,1)S(1)}, u32[]{:S(2)}, u32[]{:S(2)}) collective-permute-start(bf16[1,96,1280]{2,1,0:T(8,128)(2,1)S(1)} %get-tuple-element.243), channel_id=1, source_target_pairs={{0,24},{1,25},{2,26},{3,27},{4,28},{5,29},{6,30},{7,31},{8,16},{9,... | collective-permute-start | bytes 737288 | tf_op jit(solution)/shard_map/ppermute | solution.py:778
  460.2 25.4 %collective-permute-start.73 = (bf16[48,3072]{1,0:T(8,128)(2,1)S(1)}, bf16[48,3072]{1,0:T(8,128)(2,1)S(1)}, u32[]{:S(2)}, u32[]{:S(2)}) collective-permute-start(bf16[48,3072]{1,0:T(8,128)(2,1)S(1)} %get-tuple-element.257.refs_0_), channel_id=1, source_target_pairs={{0,1},{1,0},{2,3},{3,2},{4,5},{5,4},{6,7},{7,6},{8,9},{9,8},{10,11... | collective-permute-start | bytes 884744 | tf_op jit(solution)/shard_map/ppermute | solution.py:778
  460.3 27.1 %collective-permute-start.71 = (bf16[48,3072]{1,0:T(8,128)(2,1)S(1)}, bf16[48,3072]{1,0:T(8,128)(2,1)S(1)}, u32[]{:S(2)}, u32[]{:S(2)}) collective-permute-start(bf16[48,3072]{1,0:T(8,128)(2,1)S(1)} %get-tuple-element.257.refs_0_), channel_id=1, source_target_pairs={{0,2},{1,5},{2,0},{3,7},{4,6},{5,1},{6,4},{7,3},{8,10},{9,13},{10,... | collective-permute-start | bytes 884744 | tf_op jit(solution)/shard_map/ppermute | solution.py:778
  461.3 37.6 %collective-permute-start.58 = (bf16[8,49,768]{2,0,1:T(8,128)(2,1)S(1)}, bf16[8,49,768]{2,0,1:T(8,128)(2,1)S(1)}, u32[]{:S(2)}, u32[]{:S(2)}) collective-permute-start(bf16[8,49,768]{2,0,1:T(8,128)(2,1)S(1)} %copy.53), channel_id=1, source_target_pairs={{0,4},{4,0},{1,5},{5,1},{2,6},{6,2},{3,7},{7,3},{8,12},{12,8},{9,1... | collective-permute-start | bytes 1806344 | tf_op jit(solution)/shard_map/ppermute | solution.py:768
  464.0 17.9 %collective-permute-start.77 = (bf16[48,2304]{1,0:T(8,128)(2,1)S(1)}, bf16[48,2304]{1,0:T(8,128)(2,1)S(1)}, u32[]{:S(2)}, u32[]{:S(2)}) collective-permute-start(bf16[48,2304]{1,0:T(8,128)(2,1)S(1)} %get-tuple-element.258.refs_8_), channel_id=1, source_target_pairs={{0,4},{1,3},{2,6},{3,1},{4,0},{5,7},{6,2},{7,5},{8,12},{9,11},{10,... | collective-permute-start | bytes 663560 | tf_op jit(solution)/shard_map/ppermute | solution.py:778
  468.0 23.0 %collective-permute-start.70 = (bf16[48,3072]{1,0:T(8,128)(2,1)S(1)}, bf16[48,3072]{1,0:T(8,128)(2,1)}, u32[]{:S(2)}, u32[]{:S(2)}) collective-permute-start(bf16[48,3072]{1,0:T(8,128)(2,1)S(1)} %get-tuple-element.257.refs_0_), channel_id=1, source_target_pairs={{0,4},{1,3},{2,6},{3,1},{4,0},{5,7},{6,2},{7,5},{8,12},{9,11},{10,... | collective-permute-start | bytes 884744 | tf_op jit(solution)/shard_map/ppermute | solution.py:778
  485.5 6.8 %collective-permute-start.82 = (bf16[48,2304]{1,0:T(8,128)(2,1)S(1)}, bf16[48,2304]{1,0:T(8,128)(2,1)S(1)}, u32[]{:S(2)}, u32[]{:S(2)}) collective-permute-start(bf16[48,2304]{1,0:T(8,128)(2,1)S(1)} %collective-permute-done.78.refs_10_), channel_id=1, source_target_pairs={{0,1},{1,0},{2,3},{3,2},{4,5},{5,4},{6,7},{7,6},{8,9},{9,8},{10,11... | collective-permute-start | bytes 663560 | tf_op jit(solution)/shard_map/ppermute | solution.py:778
  493.1 11.7 %collective-permute-start.74 = (bf16[48,3072]{1,0:T(8,128)(2,1)}, bf16[48,3072]{1,0:T(8,128)(2,1)}, u32[]{:S(2)}, u32[]{:S(2)}) collective-permute-start(bf16[48,3072]{1,0:T(8,128)(2,1)} %collective-permute-done.70.refs_1_), channel_id=1, source_target_pairs={{0,1},{1,0},{2,3},{3,2},{4,5},{5,4},{6,7},{7,6},{8,9},{9,8},{10,11... | collective-permute-start | bytes 884744 | tf_op jit(solution)/shard_map/ppermute | solution.py:778
  495.5 9.4 %collective-permute-start.72 = (bf16[48,3072]{1,0:T(8,128)(2,1)}, bf16[48,3072]{1,0:T(8,128)(2,1)}, u32[]{:S(2)}, u32[]{:S(2)}) collective-permute-start(bf16[48,3072]{1,0:T(8,128)(2,1)} %collective-permute-done.70.refs_1_), channel_id=1, source_target_pairs={{0,2},{1,5},{2,0},{3,7},{4,6},{5,1},{6,4},{7,3},{8,10},{9,13},{10,... | collective-permute-start | bytes 884744 | tf_op jit(solution)/shard_map/ppermute | solution.py:778
  498.9 6.7 %collective-permute-start.86 = (bf16[48,1280]{1,0:T(8,128)(2,1)S(1)}, bf16[48,1280]{1,0:T(8,128)(2,1)}, u32[]{:S(2)}, u32[]{:S(2)}) collective-permute-start(bf16[48,1280]{1,0:T(8,128)(2,1)S(1)} %collective-permute-done.84.refs_17_), channel_id=1, source_target_pairs={{0,2},{1,5},{2,0},{3,7},{4,6},{5,1},{6,4},{7,3},{8,10},{9,13},{10,... | collective-permute-start | bytes 368648 | tf_op jit(solution)/shard_map/ppermute | solution.py:778
  (123 other events, 1044.7 us)
Sparse Core Ops, SparseCore 0:
  40.6 73.2 all-gather.4
  116.9 63.9 all-gather.2

commit v2 on v1

--- a/solution.py
+++ b/solution.py
@@ -30,8 +30,11 @@
 PAIRS = D // PAIR
 NB = 256
 ROWB = 112
+WINDOW = 128
 VMEM_LIMIT = 56 * 1024 * 1024
-SMALL_VMEM = 24 * 1024 * 1024
+SMALL_VMEM = 16 * 1024 * 1024
+SPARE_VMEM = 4 * 1024 * 1024
+ADAM_VMEM = 20 * 1024 * 1024
 
 G_T, B_T, C_T, E_T, O_T, F_T, G_S, B_S, C_S, E_S, O_S, G_M, B_M, U_1, U_2 = (
     0, 1, 2, 3, 4, 5, 6, 7, 8, 9, 10, 11, 12, 13, 17,
@@ -119,12 +122,6 @@
     second = jnp.mean(h * z_hat, axis=-1, keepdims=True)
     dz = inverse * (h - first - z_hat * second)
     return dz, jnp.sum(grad * z_hat, axis=0, keepdims=True), jnp.sum(grad, axis=0, keepdims=True)
-
-
-def softmax_rows(scores):
-    top = jnp.max(scores, axis=-1, keepdims=True)
-    e = jnp.exp(scores - top)
-    return e * (1.0 / jnp.sum(e, axis=-1, keepdims=True))
 
 
 def head_masks():
@@ -143,8 +140,8 @@
 
 
 class Weight:
-    def __init__(self, cols, rows=D, whole=None, shard=None, blocks=None, pieces=(), offset=0, tall=False):
-        self.rows, self.cols, self.whole, self.offset, self.tall = rows, cols, whole, offset, tall
+    def __init__(self, cols, rows=D, whole=None, shard=None, blocks=None, pieces=(), offset=0):
+        self.rows, self.cols, self.whole, self.offset = rows, cols, whole, offset
         self.blocks = blocks
         self.arrays = [whole] if whole is not None else [shard, *pieces]
 
@@ -154,29 +151,22 @@
 
     def copies(self, refs, scal, dst, sems):
         if self.whole is not None:
-            return [pltpu.make_async_copy(refs[0], dst, sems.at[0])]
+            return [pltpu.make_async_copy(refs[0].at[:, self.offset : self.offset + self.cols], dst, sems.at[0])]
         shard = self.rows // 4
         z, c = scal[Z_AT], scal[C_AT]
         own_rows = pl.ds(pl.multiple_of(z * shard, 16), shard)
         out, at = [], 0
         for first, size in self.blocks:
-            if self.tall:
-                src, to = refs[0].at[first : first + size, :], dst.at[own_rows, :]
-            else:
-                src, to = refs[0].at[:, first : first + size], dst.at[own_rows, at : at + size]
+            src, to = refs[0].at[:, first : first + size], dst.at[own_rows, at : at + size]
             at += size
             out.append(pltpu.make_async_copy(src, to, sems.at[len(out)]))
-        width = self.cols if self.tall else self.cols // 2
+        width = self.cols // 2
         for k in range(8):
             half = c if k < 4 else 1 - c
             quarter = scal[Q_AT + k]
             for j, m in enumerate(OTHERS):
                 row = jnp.bitwise_xor(z, m) * shard + quarter * PIECE
-                col = 0
-                if self.tall:
-                    row = row + half * (shard // 2)
-                else:
-                    col = pl.multiple_of(half * width, 128)
+                col = pl.multiple_of(half * width, 128)
                 src = refs[1 + k].at[j, :, self.offset : self.offset + width]
                 to = dst.at[pl.ds(pl.multiple_of(row, 16), PIECE), pl.ds(col, width)]
                 out.append(pltpu.make_async_copy(src, to, sems.at[len(out)]))
@@ -203,18 +193,16 @@
     return pl.CostEstimate(flops=int(microseconds * 1e9), bytes_accessed=0, transcendentals=0)
 
 
-COSTS = {
-    "time_in": 12, "time_attn": 11, "time_mid": 9, "space_in": 10, "space_mid": 15, "cot": 3, "cut": 3, "join": 3,
-    "mlp": 50, "mlp_out": 14, "space_back": 22, "space_out": 17, "time_proj": 14, "time_attn_back": 28, "time_out": 20,
-}
-
-
-def call(kernel, scal, ins, weights, outs, scratch=(), after=()):
+COSTS = {"join": 20, "cut": 20, "cot": 20}
+
+
+def call(kernel, scal, ins, weights, outs, scratch=(), after=(), anywhere=(), left=()):
     n_in, n_out, n_scr = len(ins), len(outs), len(scratch)
     arrays = [a for w in weights for a in w.arrays]
+    n_left = len(left)
 
     def body(scal_ref, *refs):
-        in_refs, refs = refs[:n_in], refs[n_in:]
+        in_refs, refs = refs[: n_in + n_left], refs[n_in + n_left :]
         array_refs, refs = refs[: len(arrays)], refs[len(arrays) + len(after) :]
         out_refs, refs = refs[:n_out], refs[n_out:]
         own, refs = refs[:n_scr], refs[n_scr:]
@@ -231,6 +219,15 @@
             w.get()
 
     in_vmem = pl.BlockSpec(memory_space=pltpu.VMEM)
+    def padded(v):
+        lead = 1
+        for n in v.shape[:-2]:
+            lead *= n
+        return lead * (-(-v.shape[-2] // 16) * 16) * (-(-v.shape[-1] // LANES) * LANES) * jnp.dtype(v.dtype).itemsize
+
+    held = [v for v in scratch if v.dtype in (BF16, F32)]
+    used = sum(padded(v) for v in held) + sum(w.rows * w.cols * 2 for w in weights)
+    limit = used + SPARE_VMEM
     name = getattr(kernel, "func", kernel).__name__.removesuffix("_kernel")
     return pl.pallas_call(
         body,
@@ -238,12 +235,13 @@
         out_shape=tuple(outs),
         in_specs=[pl.BlockSpec(memory_space=pltpu.SMEM)]
         + [in_vmem] * n_in
+        + [pl.BlockSpec(memory_space=pltpu.HBM)] * n_left
         + [pl.BlockSpec(memory_space=pl.ANY)] * (len(arrays) + len(after)),
-        out_specs=tuple(in_vmem for _ in outs),
+        out_specs=tuple(pl.BlockSpec(memory_space=pltpu.HBM) if i in anywhere else in_vmem for i in range(n_out)),
         scratch_shapes=list(scratch) + [x for w in weights for x in w.scratch()],
-        compiler_params=pltpu.CompilerParams(vmem_limit_bytes=VMEM_LIMIT),
-        cost_estimate=cost(COSTS[name]),
-    )(scal, *ins, *arrays, *after)
+        compiler_params=pltpu.CompilerParams(vmem_limit_bytes=limit),
+        cost_estimate=cost(COSTS.get(name, 0)),
+    )(scal, *ins, *left, *arrays, *after)
 
 
 def grad_cols(width, body):
@@ -263,11 +261,64 @@
         grad_cols(width, body)
 
 
-def time_mask(scal, slots):
-    row = lax.broadcasted_iota(jnp.int32, (ROWB, ROWB), 0)
-    col = lax.broadcasted_iota(jnp.int32, (ROWB, ROWB), 1)
-    frame = jnp.bitwise_xor(col % slots, scal[T_AT] * (slots // 2))
-    return (row // slots == col // slots) & (frame < scal[COUNT_AT])
+def stack_heads(a, masks):
+    return jnp.concatenate([a * masks[0], a * masks[1]], axis=0)
+
+
+def softmax_cols(scores):
+    e = jnp.exp(scores - jnp.max(scores, axis=0, keepdims=True))
+    return e * (1.0 / jnp.sum(e, axis=0, keepdims=True))
+
+
+def pair_cols(j):
+    return [slice(part * D + j * PAIR, part * D + (j + 1) * PAIR) for part in range(3)]
+
+
+def pair_probs(q, kk, bias):
+    size = q.shape[0]
+    s = dot_nt(kk, q)
+    return [softmax_cols(s[h * size : (h + 1) * size] + bias) for h in range(2)]
+
+
+def pair_forward(q, k, v, bias, masks):
+    p = pair_probs(q * BF16(SCALE), stack_heads(k, masks), bias)
+    return dot_tn(jnp.concatenate(p, axis=0).astype(BF16), stack_heads(v, masks))
+
+
+def pair_backward(q, k, v, g, bias, masks, valid=None):
+    size = q.shape[0]
+    q = q * BF16(SCALE)
+    kk, vv = stack_heads(k, masks), stack_heads(v, masks)
+    p = pair_probs(q, kk, bias)
+    dp = dot_nt(vv, g)
+    ds = []
+    for h in range(2):
+        if valid is not None:
+            p[h] = p[h] * valid
+        d = dp[h * size : (h + 1) * size]
+        ds.append(p[h] * (d - jnp.sum(p[h] * d, axis=0, keepdims=True)))
+    ds = jnp.concatenate(ds, axis=0).astype(BF16)
+    pp = jnp.concatenate(p, axis=0).astype(BF16)
+    dq = dot_tn(ds, kk) * SCALE
+    dk, dv = dot_nn(ds, q), dot_nn(pp, g)
+    first = lax.broadcasted_iota(jnp.int32, (1, PAIR), 1) < HD
+    return dq, jnp.where(first, dk[:size], dk[size:]), jnp.where(first, dv[:size], dv[size:])
+
+
+def time_bias(scal, slots, size):
+    row = lax.broadcasted_iota(jnp.int32, (size, size), 0)
+    col = lax.broadcasted_iota(jnp.int32, (size, size), 1)
+    frame = jnp.bitwise_xor(row % slots, scal[T_AT] * (slots // 2))
+    return jnp.where((row // slots == col // slots) & (frame < scal[COUNT_AT]), 0.0, MASKED_SCORE)
+
+
+def time_windows(rows, slots, scal, body):
+    masks = head_masks()
+    bias = time_bias(scal, slots, WINDOW)
+    loop(rows // WINDOW, lambda i: body(block(i, WINDOW), bias, masks))
+    left = rows % WINDOW
+    if left:
+        body(pl.ds(rows - left, left), time_bias(scal, slots, left), masks)
 
 
 def project_qkv(h, w, par, q_row, v_row, out):
@@ -303,21 +354,12 @@
 
 
 def time_attn_kernel(slots, scal, qkv, y_out):
-    mask = time_mask(scal, slots)
-    masks = head_masks()
-
-    def group(r):
+    def body(r, bias, masks):
         for j in range(PAIRS):
-            q = qkv[r, j * PAIR : (j + 1) * PAIR]
-            k = qkv[r, D + j * PAIR : D + (j + 1) * PAIR]
-            v = qkv[r, 2 * D + j * PAIR : 2 * D + (j + 1) * PAIR]
-            y = 0.0
-            for h in range(2):
-                s = jnp.where(mask, dot_nt(q * masks[h], k) * SCALE, MASKED_SCORE)
-                y += dot_nn(softmax_rows(s).astype(BF16), v * masks[h])
-            y_out[r, j * PAIR : (j + 1) * PAIR] = y.astype(BF16)
-
-    row_blocks(y_out.shape[0], group)
+            cq, ck, cv = pair_cols(j)
+            y_out[r, cq] = pair_forward(qkv[r, cq], qkv[r, ck], qkv[r, cv], bias, masks).astype(BF16)
+
+    time_windows(y_out.shape[0], slots, scal, body)
 
 
 def time_mid_kernel(scal, y, x, par, w_load, z_out, b0, b1, b2, b3, xs):
@@ -410,28 +452,26 @@
     return whole, step, width
 
 
+def space_frame(f, rows, per):
+    whole, step, width = space_windows(rows, per)
+    first = f * (whole - step)
+    row = lax.broadcasted_iota(jnp.int32, (width, 1), 0)
+    col = lax.broadcasted_iota(jnp.int32, (1, width), 1)
+    by_row, by_col = (row >= first) & (row < first + whole), (col >= first) & (col < first + whole)
+    r = pl.ds(pl.multiple_of(f * step, 16), width)
+    return r, jnp.where(by_row, 0.0, MASKED_SCORE), by_col.astype(F32), by_row.astype(F32)
+
+
 def space_mid_kernel(per, scal, qkv, x, par, w_load, y_out, x2_out, m_out, ys):
     rows = x.shape[0]
-    whole, step, width = space_windows(rows, per)
     masks = head_masks()
     ys[...] = jnp.zeros_like(ys)
-    key = lax.broadcasted_iota(jnp.int32, (1, width), 1)
-    query = lax.broadcasted_iota(jnp.int32, (width, 1), 0)
 
     def frame(f):
-        r = pl.ds(pl.multiple_of(f * step, 16), width)
-        first = f * (whole - step)
-        keys = (key >= first) & (key < first + whole)
-        queries = ((query >= first) & (query < first + whole)).astype(F32)
+        r, bias, _, valid = space_frame(f, rows, per)
         for j in range(PAIRS):
-            q = qkv[r, j * PAIR : (j + 1) * PAIR]
-            k = qkv[r, D + j * PAIR : D + (j + 1) * PAIR]
-            v = qkv[r, 2 * D + j * PAIR : 2 * D + (j + 1) * PAIR]
-            y = 0.0
-            for h in range(2):
-                s = jnp.where(keys, dot_nt(q * masks[h], k) * SCALE, MASKED_SCORE)
-                y += dot_nn(softmax_rows(s).astype(BF16), v * masks[h])
-            ys[r, j * PAIR : (j + 1) * PAIR] += y * queries
+            cq, ck, cv = pair_cols(j)
+            ys[r, cq] += pair_forward(qkv[r, cq], qkv[r, ck], qkv[r, cv], bias, masks) * valid
 
     loop(per, frame)
     y_out[...] = ys[...].astype(BF16)
@@ -450,44 +490,79 @@
     row_blocks(rows, norm)
 
 
-def mlp_kernel(scal, m, dy, par, w1_load, w2_load, x3_out, dm_out, dw1, dw1_their, dw2, dw2_their, dup, es, das, mt):
+def mlp_kernel(
+    scal, m, dy, par, weights, x3_out, dm_out, dw1, dw1_their, dw2, dw2_their, dup,
+    w1, w2, w_sems, e, da, mt, up_buf, up_sems, down_buf, down_sems,
+):
+    rows = D // 4
+    steps = FF // D
+
+    def loads(i):
+        at = pl.multiple_of(i * D, 128)
+        out = [pltpu.make_async_copy(weights.at[:, pl.ds(at, D)], w1.at[i % 2], w_sems.at[i % 2, 4])]
+        for j in range(4):
+            src = weights.at[pl.ds(pl.multiple_of(i * rows, 16), rows), FF + j * D : FF + (j + 1) * D]
+            to = w2.at[i % 2, j * rows : (j + 1) * rows, :]
+            out.append(pltpu.make_async_copy(src, to, w_sems.at[i % 2, j]))
+        return out
+
+    for c in loads(0):
+        c.start()
     mt[...] = m[...].T
-    w1, w2 = w1_load.get(), w2_load.get()
-
-    def hidden(i):
-        c = block(i, D)
-        a = dot_nn(m[...], w1[:, c]) + par[pl.ds(U_1 + i, 1), :]
-        g = dot_nt(dy[...], w2[c, :])
-        value, slope = gelu_parts(a)
-        da = (g * slope).astype(BF16)
-        es[:, c] = value.astype(BF16)
-        das[:, c] = da
-        dup[pl.ds(i, 1), :] = jnp.sum(da.astype(F32), axis=0, keepdims=True)
-
-    loop(FF // D, hidden)
-    weight_grad(mt, das, scal, dw1, dw1_their)
-    rows = D // 4
-
-    def down(i):
-        value = dot_tn(es[:, block(i, D)], dy[...]).astype(BF16)
+    x3_out[...] = jnp.zeros_like(x3_out)
+    dm_out[...] = jnp.zeros_like(dm_out)
+
+    def up_copy(i, k, out):
+        to = out.at[:, pl.ds(pl.multiple_of(i % 2 * D + k * NB, NB), NB)]
+        return pltpu.make_async_copy(up_buf.at[k], to, up_sems.at[k])
+
+    def down_copy(i, j, out):
+        to = out.at[pl.ds(pl.multiple_of(i * rows, 16), rows), j % 2 * D : (j % 2 + 1) * D]
+        return pltpu.make_async_copy(down_buf.at[j], to, down_sems.at[j])
+
+    def step(i):
+        slot = i % 2
+        for c in loads(i):
+            c.wait()
+
+        @pl.when(i + 1 < steps)
+        def ahead():
+            for c in loads(i + 1):
+                c.start()
+
+        up_w, down_w = w1.at[slot], w2.at[slot]
+        for k in range(D // NB):
+            c = slice(k * NB, (k + 1) * NB)
+            a = dot_nn(m[...], up_w[:, c]) + par[pl.ds(U_1 + i, 1), c]
+            g = dot_nt(dy[...], down_w[c, :])
+            value, slope = gelu_parts(a)
+            low = (g * slope).astype(BF16)
+            e[:, c] = value.astype(BF16)
+            da[:, c] = low
+            dup[pl.ds(i, 1), c] = jnp.sum(low.astype(F32), axis=0, keepdims=True)
+        for k in range(D // NB):
+            c = slice(k * NB, (k + 1) * NB)
+            value = dot_nn(mt[...], da[:, c]).astype(BF16)
+            pl.when(i >= 1)(lambda k=k: up_copy(i - 1, k, dw1).wait())
+            up_buf[k] = value
+            pl.when(scal[C_AT] == i // 2)(lambda k=k: up_copy(i, k, dw1).start())
+            pl.when(scal[C_AT] != i // 2)(lambda k=k: up_copy(i, k, dw1_their).start())
+        value = dot_tn(e[...], dy[...]).astype(BF16)
         for j in range(4):
-            part, to = value[j * rows : (j + 1) * rows, :], slice(j % 2 * D, (j % 2 + 1) * D)
-
-            @pl.when(scal[C_AT] == j // 2)
-            def keep(part=part, to=to):
-                dw2[block(i, rows), to] = part
-
-            @pl.when(scal[C_AT] != j // 2)
-            def send(part=part, to=to):
-                dw2_their[block(i, rows), to] = part
-
-    loop(FF // D, down)
-
-    def outs(c):
-        x3_out[:, c] = dot_nn(es[...], w2[:, c])
-        dm_out[:, c] = dot_nt(das[...], w1[c, :])
-
-    col_blocks(D, outs)
+            pl.when(i >= 1)(lambda j=j: down_copy(i - 1, j, dw2).wait())
+            down_buf[j] = value[j * rows : (j + 1) * rows, :]
+            pl.when(scal[C_AT] == j // 2)(lambda j=j: down_copy(i, j, dw2).start())
+            pl.when(scal[C_AT] != j // 2)(lambda j=j: down_copy(i, j, dw2_their).start())
+        for k in range(D // NB):
+            c = slice(k * NB, (k + 1) * NB)
+            x3_out[:, c] += dot_nn(e[...], down_w[:, c])
+            dm_out[:, c] += dot_nt(da[...], up_w[c, :])
+
+    loop(steps, step)
+    for k in range(D // NB):
+        up_copy(steps - 1, k, dw1).wait()
+    for j in range(4):
+        down_copy(steps - 1, j, dw2).wait()
 
 
 def mlp_out_kernel(per, scal, x2, x3, dm, dy, y, par, w_load, dx2_out, dys_out, dw, dw_their, dvec, b0, b1, b2, b3, xs, yt):
@@ -529,34 +604,16 @@
 
 def space_back_kernel(per, scal, qkv, dy, dqkv_out, dvec, acc):
     rows = dy.shape[0]
-    whole, step, width = space_windows(rows, per)
     masks = head_masks()
     acc[...] = jnp.zeros_like(acc)
-    key = lax.broadcasted_iota(jnp.int32, (1, width), 1)
-    query = lax.broadcasted_iota(jnp.int32, (width, 1), 0)
 
     def frame(f):
-        r = pl.ds(pl.multiple_of(f * step, 16), width)
-        first = f * (whole - step)
-        keys = (key >= first) & (key < first + whole)
-        queries = ((query >= first) & (query < first + whole)).astype(F32)
+        r, bias, valid, _ = space_frame(f, rows, per)
         for j in range(PAIRS):
-            cq = slice(j * PAIR, (j + 1) * PAIR)
-            ck = slice(D + j * PAIR, D + (j + 1) * PAIR)
-            cv = slice(2 * D + j * PAIR, 2 * D + (j + 1) * PAIR)
-            q, k, v, g = qkv[r, cq], qkv[r, ck], qkv[r, cv], dy[r, cq]
-            dq = dk = dv = 0.0
-            for h in range(2):
-                qm, km, gm = q * masks[h], k * masks[h], g * masks[h]
-                s = jnp.where(keys, dot_nt(qm, k) * SCALE, MASKED_SCORE)
-                p = softmax_rows(s) * queries
-                dp = dot_nt(gm, v)
-                ds = (p * (dp - jnp.sum(p * dp, axis=-1, keepdims=True))).astype(BF16)
-                dq += dot_nn(ds, km)
-                dk += dot_tn(ds, qm)
-                dv += dot_tn(p.astype(BF16), gm)
-            acc[r, cq] += dq * SCALE
-            acc[r, ck] += dk * SCALE
+            cq, ck, cv = pair_cols(j)
+            dq, dk, dv = pair_backward(qkv[r, cq], qkv[r, ck], qkv[r, cv], dy[r, cq], bias, masks, valid)
+            acc[r, cq] += dq
+            acc[r, ck] += dk
             acc[r, cv] += dv
 
     loop(per, frame)
@@ -641,30 +698,15 @@
 
 
 def time_attn_back_kernel(slots, scal, qkv, dys, dqkv_out, dvec):
-    mask = time_mask(scal, slots)
-    masks = head_masks()
-
-    def group(rr):
+    def body(r, bias, masks):
         for j in range(PAIRS):
-            cq = slice(j * PAIR, (j + 1) * PAIR)
-            ck = slice(D + j * PAIR, D + (j + 1) * PAIR)
-            cv = slice(2 * D + j * PAIR, 2 * D + (j + 1) * PAIR)
-            q, k, v, g = qkv[rr, cq], qkv[rr, ck], qkv[rr, cv], dys[rr, cq]
-            dq = dk = dv = 0.0
-            for hh in range(2):
-                qm, km, gm = q * masks[hh], k * masks[hh], g * masks[hh]
-                s = jnp.where(mask, dot_nt(qm, k) * SCALE, MASKED_SCORE)
-                p = softmax_rows(s)
-                dp = dot_nt(gm, v)
-                ds = (p * (dp - jnp.sum(p * dp, axis=-1, keepdims=True))).astype(BF16)
-                dq += dot_nn(ds, km)
-                dk += dot_tn(ds, qm)
-                dv += dot_tn(p.astype(BF16), gm)
-            dqkv_out[rr, cq] = (dq * SCALE).astype(BF16)
-            dqkv_out[rr, ck] = (dk * SCALE).astype(BF16)
-            dqkv_out[rr, cv] = dv.astype(BF16)
-
-    row_blocks(dys.shape[0], group)
+            cq, ck, cv = pair_cols(j)
+            dq, dk, dv = pair_backward(qkv[r, cq], qkv[r, ck], qkv[r, cv], dys[r, cq], bias, masks)
+            dqkv_out[r, cq] = dq.astype(BF16)
+            dqkv_out[r, ck] = dk.astype(BF16)
+            dqkv_out[r, cv] = dv.astype(BF16)
+
+    time_windows(dys.shape[0], slots, scal, body)
     dvec[...] = jnp.zeros_like(dvec)
     dvec[0:1, :] = jnp.sum(dqkv_out[:, :D].astype(F32), axis=0, keepdims=True)
     dvec[1:2, :] = jnp.sum(dqkv_out[:, 2 * D :].astype(F32), axis=0, keepdims=True)
@@ -740,7 +782,7 @@
         + [pl.BlockSpec(memory_space=pl.ANY)] * len(after),
         out_specs=tuple(pl.BlockSpec((1, *out.shape[1:]), lambda i: (i, 0, 0)) for _ in range(2)),
         compiler_params=pltpu.CompilerParams(vmem_limit_bytes=SMALL_VMEM),
-        cost_estimate=cost(2),
+        cost_estimate=cost(20),
     )(scal, *mine, *other, *after)
 
 
@@ -750,7 +792,7 @@
     square = BETA_SECOND * square + (1.0 - BETA_SECOND) * grad * grad
     moment_hat = moment * (1.0 / (1.0 - BETA_FIRST**STEP))
     square_hat = square * (1.0 / (1.0 - BETA_SECOND**STEP))
-    fresh = weight - rate * (moment_hat / (jnp.sqrt(square_hat) + ADAM_EPSILON) + decay * weight)
+    fresh = weight * (1.0 - rate * decay) - (rate * moment_hat) * (1.0 / (jnp.sqrt(square_hat) + ADAM_EPSILON))
     return (fresh, moment, square)
 
 
@@ -809,6 +851,27 @@
     return lax.optimization_barrier((value, *others))[0]
 
 
+def pack_kernel(n, *refs):
+    out, at = refs[-1], 0
+    for src in refs[:n]:
+        for part in range(src.shape[0] if len(src.shape) == 3 else 1):
+            out[at] = src[part] if len(src.shape) == 3 else src[...]
+            at += 1
+
+
+def pack(arrays, *after):
+    vmem = pl.BlockSpec(memory_space=pltpu.VMEM)
+    return pl.pallas_call(
+        functools.partial(pack_kernel, len(arrays)),
+        out_shape=sds((sum(v.shape[0] if v.ndim == 3 else 1 for v in arrays), *arrays[0].shape[-2:]), BF16),
+        in_specs=[vmem] * len(arrays) + [pl.BlockSpec(memory_space=pl.ANY)] * len(after),
+        out_specs=vmem,
+        compiler_params=pltpu.CompilerParams(vmem_limit_bytes=SMALL_VMEM),
+        cost_estimate=cost(20),
+        name="pack",
+    )(*arrays, *after)
+
+
 def gather_lines(piece):
     near = next_plane(piece)
     return [near, far_plane(piece), far_plane(near)]
@@ -835,15 +898,15 @@
         self.send, self.keep = add_split(self.scal, A_AT, mine, other, self.packs, 2 * PIECE, after)
         self.received = first_side(self.send)
 
-    def step(self, sel, shape, rows, move, after):
+    def step(self, sel, shape, rows, move, after, gate=()):
         shape = (*shape, self.width)
         self.send, self.keep = add_split(
             self.scal, sel, [self.keep.reshape(shape)], [self.received.reshape(shape)], [(0, self.width)], rows, after
         )
-        self.received = move(self.send)
-
-    def side(self, *after):
-        self.step(B_AT, (4, 2, PIECE), PIECE, second_side, after)
+        self.received = move(once(self.send, *gate) if gate else self.send)
+
+    def side(self, *after, gate=()):
+        self.step(B_AT, (4, 2, PIECE), PIECE, second_side, after, gate)
 
     def plane(self, *after):
         self.step(PAIR_AT, (1, 2, 2 * PIECE), 2 * PIECE, far_plane, after)
@@ -851,74 +914,107 @@
     def pair(self, *after):
         self.step(ODD_AT, (1, 2, PIECE), PIECE, next_plane, after)
 
-    def total(self):
-        return (self.keep[0].astype(F32) + self.received[0].astype(F32)).astype(BF16)
-
-
-def adam_kernel(jobs, n_arrays, scal, factor, *refs):
+    def total(self, square, alone=0, *after):
+        vmem = pl.BlockSpec(memory_space=pltpu.VMEM)
+        return pl.pallas_call(
+            functools.partial(total_kernel, self.width - alone),
+            out_shape=(sds((PIECE, self.width), BF16), sds(square.shape, F32)),
+            in_specs=[pl.BlockSpec(memory_space=pltpu.SMEM), vmem, vmem, vmem]
+            + [pl.BlockSpec(memory_space=pl.ANY)] * len(after),
+            out_specs=(vmem, vmem),
+            compiler_params=pltpu.CompilerParams(vmem_limit_bytes=SMALL_VMEM),
+            cost_estimate=cost(20),
+        )(self.scal, self.keep.reshape(PIECE, -1), self.received.reshape(PIECE, -1), square, *after)
+
+
+def total_kernel(alone, scal, keep, received, before, *refs):
+    out, square = refs[-2:]
+    total = (keep[...].astype(F32) + received[...].astype(F32)).astype(BF16)
+    out[...] = total
+    total = total.astype(F32)
+    found = jnp.sum(total[:, :alone] * total[:, :alone])
+    if alone < total.shape[1]:
+        found += jnp.where(scal[C_AT] == 0, jnp.sum(total[:, alone:] * total[:, alone:]), 0.0)
+    square[...] = before[...] + found
+
+
+def adam_kernel(jobs, n_arrays, steps, scal, total_square, *refs):
+    ins, refs = refs[:9], refs[9:]
     arrays, refs = refs[:n_arrays], refs[n_arrays:]
-    ins, outs, grads, sems = refs[:9], refs[9:19], refs[19:22], refs[22]
-    step, scale = pl.program_id(0), factor[0]
-
-    @pl.when(step == 0)
-    def bring():
-        copies = []
-        for start, offset, width, to_grad, firsts in jobs:
-            for k in range(8):
-                half = scal[C_AT] if k < 4 else 1 - scal[C_AT]
-                quarter = scal[Q_AT + k] * PIECE
-                each = width // len(firsts)
-                for j, (low, high) in enumerate(firsts):
-                    src = arrays[start + k].at[:, offset + j * each : offset + (j + 1) * each]
-                    if to_grad == 1:
-                        rows = pl.ds(pl.multiple_of(low + half * (high - low) + quarter, 16), PIECE)
-                        to = grads[1].at[rows, :]
-                    else:
-                        rows = pl.ds(pl.multiple_of(quarter, 16), PIECE)
-                        to = grads[to_grad].at[rows, pl.ds(pl.multiple_of(low + half * (high - low), 128), each)]
-                    copies.append(pltpu.make_async_copy(src, to, sems.at[len(copies)]))
-        for c in copies:
-            c.start()
-        for c in copies:
-            c.wait()
-        g = grads[2][:, :LANES].astype(F32).T[: ins[6].shape[0], :]
-        fresh = adam_update(ins[6][...], g, ins[7][...], ins[8][...], 0.0, scale, LEARN_RATE_VEC)
-        for out, value in zip(outs[6:9], fresh):
-            out[...] = value
-        outs[9][...] = g[U_2 : U_2 + 1, :] * scale
-
-    for i, grad in enumerate(grads[:2]):
-        weight, moment, square = ins[3 * i : 3 * i + 3]
-        size = weight.shape[0]
-        g = grad[pl.ds(pl.multiple_of(step * size, 16), size), :].astype(F32)
-        fresh = adam_update(weight[...], g, moment[...], square[...], WEIGHT_DECAY, scale, LEARN_RATE)
-        for out, value in zip(outs[3 * i : 3 * i + 3], fresh):
-            out[...] = value
-
-
-def adam_all(scal, factor, arrays, jobs, blocks, wide, tall, vec):
-    anywhere = pl.BlockSpec(memory_space=pl.ANY)
-    smem = pl.BlockSpec(memory_space=pltpu.SMEM)
-    both = [*wide, *tall]
-    specs = [pl.BlockSpec((v.shape[0] // blocks, v.shape[1]), lambda i: (i, 0)) for v in both]
-    specs += [pl.BlockSpec(v.shape, lambda i: (0, 0)) for v in vec]
-    both = both + list(vec)
+    outs, grads, sems, buffers, out_sems = refs[:10], refs[10:13], refs[13], refs[14:16], refs[16]
+    scale = CLIP_NORM / jnp.maximum(jnp.sqrt(total_square[0:1, 0:1]), CLIP_NORM)
+    copies = []
+    for start, offset, width, to_grad, firsts in jobs:
+        for k in range(8):
+            half = scal[C_AT] if k < 4 else 1 - scal[C_AT]
+            quarter = scal[Q_AT + k] * PIECE
+            each = width // len(firsts)
+            for j, (low, high) in enumerate(firsts):
+                src = arrays[start + k].at[:, offset + j * each : offset + (j + 1) * each]
+                if to_grad == 1:
+                    rows = pl.ds(pl.multiple_of(low + half * (high - low) + quarter, 16), PIECE)
+                    to = grads[1].at[rows, :]
+                else:
+                    rows = pl.ds(pl.multiple_of(quarter, 16), PIECE)
+                    to = grads[to_grad].at[rows, pl.ds(pl.multiple_of(low + half * (high - low), 128), each)]
+                copies.append(pltpu.make_async_copy(src, to, sems.at[len(copies)]))
+    for c in copies:
+        c.start()
+    for c in copies:
+        c.wait()
+
+    def rows_of(i, which):
+        size = buffers[which].shape[2]
+        return pl.ds(pl.multiple_of(i * size, 16), size)
+
+    def copy_out(i, which, j):
+        to = outs[3 * which + j].at[rows_of(i, which), :]
+        return pltpu.make_async_copy(buffers[which].at[i % 2, j], to, out_sems.at[i % 2, which, j])
+
+    def step(i):
+        for which in range(2):
+            r = rows_of(i, which)
+            weight, moment, square = (v[r, :] for v in ins[3 * which : 3 * which + 3])
+            g = grads[which][r, :].astype(F32)
+            fresh = adam_update(weight, g, moment, square, WEIGHT_DECAY, scale, LEARN_RATE)
+            for j, value in enumerate(fresh):
+                pl.when(i >= 2)(lambda j=j: copy_out(i - 2, which, j).wait())
+                buffers[which][i % 2, j] = value
+                copy_out(i, which, j).start()
+
+    loop(steps, step)
+    g = grads[2][:, :LANES].astype(F32).T[: ins[6].shape[0], :]
+    fresh = adam_update(ins[6][...], g, ins[7][...], ins[8][...], 0.0, scale, LEARN_RATE_VEC)
+    for out, value in zip(outs[6:9], fresh):
+        out[...] = value
+    outs[9][...] = g[U_2 : U_2 + 1, :] * scale
+    for i in (steps - 2, steps - 1):
+        for which in range(2):
+            for j in range(3):
+                copy_out(i, which, j).wait()
+
+
+def adam_all(scal, total_square, arrays, jobs, steps, wide, tall, vec):
+    anywhere, vmem = pl.BlockSpec(memory_space=pl.ANY), pl.BlockSpec(memory_space=pltpu.VMEM)
+    both = [*wide, *tall, *vec]
     shard = vec[0].shape[1]
     return pl.pallas_call(
-        functools.partial(adam_kernel, jobs, len(arrays)),
-        grid=(blocks,),
+        functools.partial(adam_kernel, jobs, len(arrays), steps),
         out_shape=tuple(sds(v.shape, F32) for v in both) + (sds((1, shard), F32),),
-        in_specs=[smem, smem] + [anywhere] * len(arrays) + specs,
-        out_specs=(*specs, pl.BlockSpec((1, shard), lambda i: (0, 0))),
+        in_specs=[pl.BlockSpec(memory_space=pltpu.SMEM)] + [vmem] * (1 + len(both)) + [anywhere] * len(arrays),
+        out_specs=tuple([pl.BlockSpec(memory_space=pltpu.HBM)] * 6 + [vmem] * 4),
         scratch_shapes=[
             pltpu.VMEM(wide[0].shape, BF16),
             pltpu.VMEM(tall[0].shape, BF16),
             pltpu.VMEM((shard, 2 * LANES), BF16),
             pltpu.SemaphoreType.DMA((sum(8 * len(j[4]) for j in jobs),)),
+            pltpu.VMEM((2, 3, wide[0].shape[0] // steps, wide[0].shape[1]), F32),
+            pltpu.VMEM((2, 3, tall[0].shape[0] // steps, tall[0].shape[1]), F32),
+            pltpu.SemaphoreType.DMA((2, 2, 3)),
         ],
-        compiler_params=pltpu.CompilerParams(vmem_limit_bytes=VMEM_LIMIT),
+        compiler_params=pltpu.CompilerParams(vmem_limit_bytes=ADAM_VMEM),
         cost_estimate=cost(25),
-    )(scal, factor, *arrays, *both)
+    )(scal, total_square, *both, *arrays)
 
 
 def shards(
@@ -1002,23 +1098,26 @@
         peer_tokens = tm_permute(peer_tokens)
         piece_1 = half_of(*spans["ot"])
         piece_2 = jnp.concatenate([half_of(*spans[name]) for name in ("as", "os")], axis=1)
-        first_0 = jnp.stack(
-            once(lines_0, peer_tokens, low_in, low_out, vec_low, own_tokens, scal, piece_1, piece_2)
-        )
+        first_0 = pack(lines_0, piece_1, peer_tokens)
         side_0, far_0 = sides(first_0)
-        up_all, down_all = whole(low_in[:, 9 * D :], first_0), whole(low_out, first_0)
+        down_quarters = jnp.concatenate(jnp.split(low_out, 4, axis=0), axis=1)
+        hidden_part = jnp.concatenate([low_in[:, 9 * D :], down_quarters], axis=1)
         piece_1 = once(piece_1, first_0)
         near_1 = next_plane(piece_1)
-        both_0 = second_side(side_0)
-        lines_1 = lines(once(piece_1, far_0, near_1), once(near_1, far_0))
+        pair_1 = pack([piece_1, near_1])
+        far_pair_1 = far_plane(pair_1)
+        both_0 = second_side(once(side_0, own_tokens, scal, vec_low, piece_2, hidden_part, pair_1))
+        hidden = whole(hidden_part, first_0)
         group_0 = cores([first_0, side_0, far_0, both_0])
-        peer_cot = tm_permute(once(peer_cot, both_0))
-        first_1 = jnp.stack(once(lines_1, both_0))
+        first_1 = pack([near_1, far_pair_1], both_0)
         side_1, far_1 = sides(first_1)
-        near_2 = next_plane(once(piece_2, first_1))
+        piece_2 = once(piece_2, first_1)
+        near_2 = next_plane(piece_2)
+        pair_2 = pack([piece_2, near_2], first_1)
+        far_pair_2 = far_plane(pair_2)
+        after_in = (first_1, pair_2)
         w_at = Weight(3 * D, shard=low_in, blocks=[spans["at"]], pieces=group_0)
         w_vec = Weight(2 * LANES, shard=vec_low, blocks=[(0, 2 * LANES)], pieces=group_0, offset=3 * D // 2)
-        after_in = (first_1,)
     else:
         peer_tokens, peer_cot = tm_permute(peer_tokens), tm_permute(peer_cot)
 
@@ -1032,40 +1131,57 @@
         time_in_kernel, scal, [own_tokens, peer_tokens], [w_at, w_vec], [act, act, wide, par_out], [scr_tiled], after_in
     )
     if line:
+        first_2 = pack([near_2, far_pair_2], h_t)
         both_1 = second_side(once(side_1, h_t))
-        lines_2 = lines(once(piece_2, h_t, near_2), once(near_2, h_t))
-        after_attn = (near_2, side_1, peer_cot)
+        side_2, far_2 = sides(first_2)
+        after_attn = (first_2, side_1)
     (y_t,) = call(functools.partial(time_attn_kernel, slots), scal, [qkv_t], [], [act], [], after_attn)
     if line:
         group_1 = cores(once([first_1, side_1, far_1, both_1], y_t))
         w_ot = Weight(2 * D, shard=low_in, blocks=[spans["ot"]], pieces=group_1)
-        first_2 = jnp.stack(once(lines_2, y_t))
-        side_2, far_2 = sides(first_2)
-        after_mid = (first_2,)
+        both_2 = second_side(once(side_2, y_t))
+        after_mid = (side_2,)
     z_t, *x1 = call(time_mid_kernel, scal, [y_t, x, par], [w_ot], [act, blk, blk, blk, blk], [scr_tiled], after_mid)
     x1 = [pos_permute(v, r) for r, v in enumerate(x1)]
-    cot = call(cut_kernel, scal, [own_cot, peer_cot], [], [blk] * 4, [], (z_t,))
     if line:
-        both_2 = second_side(once(side_2, z_t))
-        group_2 = cores([first_2, side_2, far_2, both_2])
+        peer_cot = tm_permute(once(peer_cot, z_t))
+        group_2 = cores(once([first_2, side_2, far_2, both_2], *x1[1:]))
         w_as = Weight(3 * D, shard=low_in, blocks=[spans["as"]], pieces=group_2)
         w_os = Weight(D, shard=low_in, blocks=[spans["os"]], pieces=group_2, offset=3 * D // 2)
-        after_space = (cot[0],)
+        after_space = (peer_cot,)
 
     x1, h_s, qkv_s = call(space_in_kernel, scal, [*x1, par], [w_as], [act, act, wide], [scr], after_space)
-    cot = [pos_permute(once(v, h_s), r) for r, v in enumerate(cot)]
+    cot = call(cut_kernel, scal, [own_cot, peer_cot], [], [blk] * 4, [], (h_s,))
+    cot = [pos_permute(v, r) for r, v in enumerate(cot)]
     y_s, x2, m = call(
-        functools.partial(space_mid_kernel, per), scal, [qkv_s, x1, par], [w_os], [act, full, act], [scr]
+        functools.partial(space_mid_kernel, per), scal, [qkv_s, x1, par], [w_os], [act, full, act], [scr], (cot[0],)
     )
     (dy,) = call(cot_kernel, scal, cot, [], [act], [scr], (m,))
 
+    if not line:
+        down_all = down_all.reshape(4, 4, D // 4, D).transpose(0, 2, 1, 3).reshape(D, FF)
+        hidden = jnp.concatenate([up_all, down_all], axis=1)
+    buffers = [
+        pltpu.VMEM((2, D, D), BF16),
+        pltpu.VMEM((2, D, D), BF16),
+        pltpu.SemaphoreType.DMA((2, 5)),
+        scr_low,
+        scr_low,
+        scr_t,
+        pltpu.VMEM((D // NB, D, NB), BF16),
+        pltpu.SemaphoreType.DMA((D // NB,)),
+        pltpu.VMEM((4, D // 4, D), BF16),
+        pltpu.SemaphoreType.DMA((4,)),
+    ]
     x3, dm, g_1, g_1t, g_2, g_2t, v_u = call(
         mlp_kernel,
         scal,
         [m, dy, par],
-        [Weight(FF, whole=up_all), Weight(D, rows=FF, whole=down_all)],
+        [],
         [full, full, *halves(FF // 2), *halves(FF // 2), vec_out],
-        [scr_hidden, scr_hidden, scr_t],
+        buffers,
+        anywhere=(2, 3, 4, 5),
+        left=(hidden,),
     )
     if line:
         group_a = Group(scal, [(g_1, g_1t), (g_2, g_2t)])
@@ -1077,6 +1193,7 @@
         [full, act, *halves(D // 2), vec_out, blk, blk, blk, blk],
         [scr, scr_t],
     )
+    mine = (jnp.arange(clips, dtype=jnp.int32) == t)[:, None, None, None]
 
     wait = ()
     if line:
@@ -1103,7 +1220,7 @@
 
     if line:
         group_s = Group(scal, [(g_os, g_ost), (g_as, g_ast)])
-        group_a.side(*dx1[1:])
+        group_a.side(v_n, gate=dx1[1:])
         wait = (group_a.send,)
     dx1, dy_t, g_ot, g_ott, v_t = call(
         time_proj_kernel,
@@ -1123,13 +1240,11 @@
     dqkv_t, v_a = call(
         functools.partial(time_attn_back_kernel, slots), scal, [qkv_t, dy_t], [], [wide, vec_out], [], wait
     )
+    if line:
+        group_a.pair(v_a)
+        group_s.side(group_a.send)
     out_own, out_peer = call(join_kernel, scal, out, [], [sds((half, here, D), BF16)] * 2, [], (v_a,))
-    if line:
-        group_s.side(v_a)
-        group_a.pair(v_a)
-        wait = (group_s.send, group_a.send, out_own)
-    out_peer = tm_permute(out_peer)
-    mine = (jnp.arange(clips, dtype=jnp.int32) == t)[:, None, None, None]
+    wait = (group_s.send, out_own) if line else ()
     grad_own, grad_peer, g_at, g_att, g_vec, _ = call(
         time_out_kernel,
         scal,
@@ -1147,38 +1262,34 @@
     )
     if line:
         group_t = Group(scal, [(g_at, g_att), (g_vec, g_vec)])
-        group_t.chip()
-        group_s.plane(group_t.send)
-        sum_a = group_a.total()
-        group_t.side()
-        group_s.pair(group_t.send)
-        group_t.plane()
-        sum_s = group_s.total()
-        parts = spread_plane(once(sum_a, group_t.send)) + spread_plane(once(sum_s, group_t.send))
-        grad_peer = once(grad_peer, group_t.send)
-        block_out = once(jnp.where(mine, out_own[None], out_peer[None]), group_t.send)
-        group_t.pair()
-        sum_t = group_t.total()
-        sums = [sum_a, sum_s, sum_t]
-        parts = [*parts, *spread_plane(sum_t)]
-    else:
-        block_out = jnp.where(mine, out_own[None], out_peer[None])
+        square = jnp.zeros((8, LANES), F32)
+        sum_a, square = group_a.total(square, 0, g_vec)
+        group_s.plane(sum_a)
+        sides_a = sides(sum_a)
+        group_t.chip(group_s.send)
+        group_s.pair(*sides_a, group_t.send)
+        group_t.side(group_s.send)
+        parts_a = [sum_a, *sides_a, second_side(once(sides_a[0], group_t.send))]
+        sum_s, square = group_s.total(square, 0, *parts_a[3:])
+        group_t.plane(sum_s)
+        sides_s = sides(once(sum_s, group_t.send))
+        parts_a = cores(once(parts_a, group_t.send))
+        group_t.pair(*sides_s, *parts_a[4:])
+        parts_s = cores([sum_s, *sides_s, second_side(once(sides_s[0], group_t.send))])
+        parts = parts_a + parts_s
+        sum_t, square = group_t.total(square, LANES, *parts_s[4:])
+        parts_t = spread_plane(sum_t)
+        parts = parts + parts_t
+        out_peer, grad_peer = once(out_peer, parts_t[3]), once(grad_peer, parts_t[3])
+    out_peer = tm_permute(out_peer)
+    block_out = jnp.where(mine, out_own[None], out_peer[None])
     grad_peer = tm_permute(grad_peer).astype(F32)
     input_grad = jnp.where(mine, grad_own[None], grad_peer[None])
 
     if line:
-        square_sums = []
-        for total in sums[:-1]:
-            total = total.astype(F32)
-            square_sums.append(jnp.sum(total * total))
-        last = sums[-1].astype(F32)
-        vec_at = group_t.width - LANES
-        alone = jnp.where(core == 0, last[:, vec_at:], 0.0)
-        square_sums += [jnp.sum(last[:, :vec_at] * last[:, :vec_at]), jnp.sum(alone * alone)]
-        total_square = jnp.broadcast_to(sum(square_sums), (8, LANES))
         for move in (next_plane, far_plane, first_side, second_side, other_core):
-            total_square = total_square + move(total_square)
-        total_square = total_square[0, 0]
+            square = square + move(square)
+        total_square = square[0, 0]
     else:
         g_in = jnp.concatenate([g_at, g_att, g_ot, g_ott, g_as, g_ast, g_os, g_ost, g_1, g_1t], axis=1)
         g_out = jnp.concatenate([g_2, g_2t], axis=1).reshape(4, D // 4, 4, D).transpose(0, 2, 1, 3).reshape(FF, D)
@@ -1211,7 +1322,7 @@
             jobs.append((8, offset, width, 0, span(name)))
         jobs.append((16, *group_t.packs[0], 0, span("at")))
         jobs.append((16, *group_t.packs[1], 2, ((0, LANES),)))
-        fresh = adam_all(scal, factor.reshape(1), parts, jobs, 12, wide_in, tall_in, [v.T for v in vec_in])
+        fresh = adam_all(scal, square, parts, jobs, 12, wide_in, tall_in, [v.T for v in vec_in])
         *fresh, new_v, first_v, second_v, bias_down = fresh
         fresh += [new_v.T, first_v.T, second_v.T]
         bias_down_grad = bias_down.reshape(-1)

time: 554 us -> 500 us (0.903)
  Pallas kernels: 269 us -> 202 us
  waiting for transfers between devices: 125 us -> 136 us
  local copies, waits for them, and re-layouts: 29.8 us -> 40.5 us
  other arithmetic: 18.8 us -> 10.3 us
  starting transfers between devices: 82.7 us -> 89.7 us
    pallas_call x15, Pallas kernels: 224 us -> 166 us  [call(): pl.pallas_call(body, name=name, out_shape=tuple(outs), in_specs=[pl.Block...]
    unnamed x186 -> x162, local copies, waits for them, and re-layouts: 13.1 us -> 26.3 us
    ppermute x75 -> x73, waiting for transfers between devices: 88 us -> 99.2 us  [grid_permute(): return lax.ppermute(a, EVERY, pairs)]
    ppermute x4, waiting for transfers between devices: 7.85 us -> 0.23 us  [tm_permute(): return lax.ppermute(a, 'tm', [(i, n - 1 - i) for i in range(n)])]
    ppermute x12, waiting for transfers between devices: 28.9 us -> 36.3 us  [pos_permute(): return lax.ppermute(a, 'pos', [(i, i ^ r) for i in range(n)]) if r else a]
    ppermute x75 -> x73, starting transfers between devices: 69.2 us -> 76.4 us  [grid_permute(): return lax.ppermute(a, EVERY, pairs)]
    pallas_call x1 -> x9, Pallas kernels: 28.6 us -> 24 us  [the longest x1 21.3 us: adam_all(): pl.pallas_call(functools.partial(adam_kernel, jobs, len(arrays), steps),...]
  transfers between devices with their start and end apart: 93 -> 90, of which waited for: 30 -> 38; matrix products, arithmetic and copies ran while one was open for 6% -> 6% of each run, Pallas kernels for 31% -> 31%
where the time goes in v2:
time: 500 us; the launch traced here: 496 us
  Pallas kernels  202 us (40%)
  waiting for transfers between devices  136 us (27%)
  starting transfers between devices  89.7 us (18%)
  local copies, waits for them, and re-layouts  40.5 us (8%)
  between operations  17.7 us (4%)
  other arithmetic  10.3 us (2%)
    pallas_call x15, Pallas kernels, call(): pl.pallas_call(body, name=name, out_shape=tuple(outs), in_specs=[pl.Block...  166 us
    ppermute x73, waiting for transfers between devices, grid_permute(): return lax.ppermute(a, EVERY, pairs)  99.2 us
    ppermute x73, starting transfers between devices, grid_permute(): return lax.ppermute(a, EVERY, pairs)  76.4 us
    ppermute x12, waiting for transfers between devices, pos_permute(): return lax.ppermute(a, 'pos', [(i, i ^ r) for i in range(n)]) if r else a  36.3 us
    unnamed x162, local copies, waits for them, and re-layouts  26.3 us
    pallas_call x1, Pallas kernels, adam_all(): pl.pallas_call(functools.partial(adam_kernel, jobs, len(arrays), steps),...  21.3 us
    pallas_call x12, Pallas kernels, add_split(): pl.pallas_call(functools.partial(add_split_kernel, packs, len(after), sel...  11.8 us
  transfers between devices with their start and end apart: 90, of which 38 were waited for; matrix products, arithmetic and copies ran while one was open for 6% of the time, Pallas kernels for 31%

profile of v2, /device:TPU:0, one launch (start us, length us, event | category | flops | bytes accessed | tf_op | source)
XLA Modules:
  0.0 495.9 jit_solution(896599716443256853)
XLA Ops:
  9.4 3.1 collective-permute-start.1
  12.5 2.5 collective-permute-start.2
  14.9 2.3 dynamic-slice_bitcast_fusion.1
  18.8 5.4 %convert_element_type.26.refs_2_.refs_3_.refs_5_.refs_6_.refs_11_ = bf16[192,9984]{1,0:T(8,128)(2,1)} convert(f32[192,9984]{1,0:T(8,128)} %refs_0_.1) | non-fusion elementwise | flops 1916928 | bytes 11501568 | tf_op jit(solution)/shard_map/convert_element_type | solution.py:1052
  24.2 2.5 slice_dynamic-update-slice_fusion
  27.9 1.7 slice_dynamic-update-slice_fusion.4
  29.6 1.7 slice_dynamic-update-slice_fusion.3
  31.3 1.7 slice_dynamic-update-slice_fusion.2
  33.0 1.7 slice_dynamic-update-slice_fusion.1
  36.0 1.7 constant_dynamic-slice_fusion
  46.8 2.6 collective-permute-done.6.refs_1_.refs_0_
  49.4 9.0 %collective-permute-done.4.refs_4_.refs_13_ = bf16[3,48,1280]{2,1,0:T(8,128)(2,1)S(1)} collective-permute-done((bf16[3,48,1280]{2,1,0:T(8,128)(2,1)S(1)}, bf16[3,48,1280]{2,1,0:T(8,128)(2,1)S(1)}, u32[]{:S(2)}, u32[]{:S(2)}) %collective-permute-start.4) | collective-permute-done | bytes 368672 | tf_op jit(solution)/shard_map/ppermute | solution.py:820
  60.4 6.5 %collective-permute-done.12.refs_1_ = bf16[2,48,768]{2,1,0:T(8,128)(2,1)S(1)} collective-permute-done((bf16[2,48,768]{2,1,0:T(8,128)(2,1)S(1)}, bf16[2,48,768]{2,1,0:T(8,128)(2,1)S(1)}, u32[]{:S(2)}, u32[]{:S(2)}) %collective-permute-start.12) | collective-permute-done | bytes 147488 | tf_op jit(solution)/shard_map/ppermute | solution.py:820
  67.6 2.2 collective-permute-done.5.refs_5_.refs_14_
  70.4 8.3 %collective-permute-done.13.refs_1_.refs_0_ = bf16[48,1536]{1,0:T(8,128)(2,1)S(1)} collective-permute-done((bf16[48,1536]{1,0:T(8,128)(2,1)S(1)}, bf16[48,1536]{1,0:T(8,128)(2,1)S(1)}, u32[]{:S(2)}, u32[]{:S(2)}) %collective-permute-start.13) | collective-permute-done | bytes 147488 | tf_op jit(solution)/shard_map/ppermute | solution.py:820
  79.0 2.2 copy-done
  81.2 9.7 %time_in.1 = (bf16[784,768]{1,0:T(8,128)(2,1)S(1)}, bf16[784,768]{1,0:T(8,128)(2,1)S(1)}, bf16[784,2304]{1,0:T(8,128)(2,1)S(1)}, f32[24,768]{1,0:T(8,128)S(1)}) custom-call(s32[17]{0:T(128)S(1)} %stack.68.scal_ref.scal, bf16[8,49,768]{2,1,0:T(8,128)(2,1)S(1)} %bitcast.74, bf16[8,49,768]{2,1,0:T(8,128)(2,1)S(1)} %copy.48.refs_4_.refs_1_, ...), custom_call_target="tpu_custom_call" | custom-call | tf_op jit(solution)/shard_map/time_in/pallas_call | solution.py:232
  92.0 2.0 collective-permute-start.17
  94.0 6.2 %time_attn.1.refs_0_.refs_4_ = bf16[784,768]{1,0:T(8,128)(2,1)S(1)} custom-call(s32[17]{0:T(128)S(1)} %stack.68.scal_ref.scal, bf16[784,2304]{1,0:T(8,128)(2,1)S(1)} %get-tuple-element.143.refs_0_, bf16[3,48,1536]{2,1,0:T(8,128)(2,1)S(1)} %pack.9.refs_1_.refs_6_.refs_4_.refs_7_, bf16[3,48,768]{2,1,0:T(8,128)(2,1)S(1)} %collective-permute-done.15.refs_2_.refs_5_.refs_8_), custom_call_target="tpu_custom_call" | custom-call | tf_op jit(solution)/shard_map/time_attn/pallas_call | solution.py:232
  100.5 2.1 collective-permute-start.19
  105.2 5.4 %time_mid.1 = (bf16[784,768]{1,0:T(8,128)(2,1)S(1)}, bf16[4,49,768]{2,1,0:T(8,128)(2,1)S(1)}, bf16[4,49,768]{2,1,0:T(8,128)(2,1)S(1)}, bf16[4,49,768]{2,1,0:T(8,128)(2,1)S(1)}, bf16[4,49,768]{2,1,0:T(8,128)(2,1)S(1)}) custom-call(s32[17]{0:T(128)S(1)} %stack.68.scal_ref.scal, bf16[784,768]{1,0:T(8,128)(2,1)S(1)} %time_attn.1.refs_0_.refs_4_, ...), custom_call_target="tpu_custom_call" | custom-call | tf_op jit(solution)/shard_map/time_mid/pallas_call | solution.py:232
  113.8 5.3 %collective-permute-done.26.refs_8_.refs_6_.refs_9_ = bf16[3,48,1536]{2,1,0:T(8,128)(2,1)S(1)} collective-permute-done((bf16[3,48,1536]{2,1,0:T(8,128)(2,1)S(1)}, bf16[3,48,1536]{2,1,0:T(8,128)(2,1)S(1)}, u32[]{:S(2)}, u32[]{:S(2)}) %collective-permute-start.26) | collective-permute-done | bytes 442400 | tf_op jit(solution)/shard_map/ppermute | solution.py:820
  119.0 2.2 collective-permute-start.32
  121.3 19.7 %collective-permute-done.24.refs_2_ = bf16[4,49,768]{2,1,0:T(8,128)(2,1)S(1)} collective-permute-done((bf16[4,49,768]{2,1,0:T(8,128)(2,1)S(1)}, bf16[4,49,768]{2,1,0:T(8,128)(2,1)S(1)}, u32[]{:S(2)}, u32[]{:S(2)}) %collective-permute-start.24) | collective-permute-done | bytes 301088 | tf_op jit(solution)/shard_map/ppermute | solution.py:805
  142.5 2.0 collective-permute-start.28
  147.8 7.8 %space_in.1 = (bf16[784,768]{1,0:T(8,128)(2,1)S(1)}, bf16[784,768]{1,0:T(8,128)(2,1)S(1)}, bf16[784,2304]{1,0:T(8,128)(2,1)S(1)}) custom-call(s32[17]{0:T(128)S(1)} %stack.68.scal_ref.scal, bf16[4,49,768]{2,1,0:T(8,128)(2,1)S(1)} %get-tuple-element.152.refs_0_, bf16[4,49,768]{2,1,0:T(8,128)(2,1)S(1)} %collective-permute-done.23.refs_1_, ...), custom_call_target="tpu_custom_call" | custom-call | tf_op jit(solution)/shard_map/space_in/pallas_call | solution.py:232
  158.5 11.9 %space_mid.1 = (bf16[784,768]{1,0:T(8,128)(2,1)S(1)}, f32[784,768]{1,0:T(8,128)S(1)}, bf16[784,768]{1,0:T(8,128)(2,1)S(1)}) custom-call(s32[17]{0:T(128)S(1)} %stack.68.scal_ref.scal, bf16[784,2304]{1,0:T(8,128)(2,1)S(1)} %get-tuple-element.163.refs_0_, bf16[784,768]{1,0:T(8,128)(2,1)S(1)} %get-tuple-element.164.refs_1_.refs_2_, ...), custom_call_target="tpu_custom_call" | custom-call | tf_op jit(solution)/shard_map/space_mid/pallas_call | solution.py:232
  176.8 3.7 copy-done.6
  183.1 45.8 %mlp.1 = (f32[784,768]{1,0:T(8,128)S(1)}, f32[784,768]{1,0:T(8,128)S(1)}, bf16[768,1536]{1,0:T(8,128)(2,1)S(1)}, bf16[768,1536]{1,0:T(8,128)(2,1)S(1)}, bf16[768...) custom-call(s32[17]{0:T(128)S(1)} %stack.68.scal_ref.scal, ...), custom_call_target="tpu_custom_call" | custom-call | tf_op jit(solution)/shard_map/mlp/pallas_call | solution.py:232
  229.7 8.1 %mlp_out.1 = (f32[784,768]{1,0:T(8,128)S(1)}, bf16[784,768]{1,0:T(8,128)(2,1)S(1)}, bf16[768,384]{1,0:T(8,128)(2,1)S(1)}, bf16[768,384]{1,0:T(8,128)(2,1)S(1)}, ...) custom-call(s32[17]{0:T(128)S(1)} %stack.68.scal_ref.scal, ...), custom_call_target="tpu_custom_call" | custom-call | tf_op jit(solution)/shard_map/mlp_out/pallas_call | solution.py:232
  237.9 1.9 shard_map.219
  241.3 16.5 %space_back.1 = (bf16[784,2304]{1,0:T(8,128)(2,1)S(1)}, f32[8,768]{1,0:T(8,128)S(1)}) custom-call(s32[17]{0:T(128)S(1)} %stack.68.scal_ref.scal, bf16[784,2304]{1,0:T(8,128)(2,1)S(1)} %copy-done.3, bf16[784,768]{1,0:T(8,128)(2,1)S(1)} %get-tuple-element.177.refs_1_, bf16[4,96,3072]{2,1,0:T(8,128)(2,1)S(1)} %get-tuple-element.183.refs_2_), custom_call_target="tpu_custom_call" | custom-call | tf_op jit(solution)/shard_map/space_back/pallas_call | solution.py:232
  257.8 13.7 %space_out.1 = (bf16[768,1152]{1,0:T(8,128)(2,1)S(1)}, bf16[768,1152]{1,0:T(8,128)(2,1)S(1)}, f32[8,768]{1,0:T(8,128)S(1)}, bf16[4,49,768]{2,1,0:T(8,128)(2,1)S(...) custom-call(s32[17]{0:T(128)S(1)} %stack.68.scal_ref.scal, ...), custom_call_target="tpu_custom_call" | custom-call | tf_op jit(solution)/shard_map/space_out/pallas_call | solution.py:232
  274.8 7.8 %collective-permute-done.39.refs_2_ = bf16[4,49,768]{2,1,0:T(8,128)(2,1)S(1)} collective-permute-done((bf16[4,49,768]{2,1,0:T(8,128)(2,1)S(1)}, bf16[4,49,768]{2,1,0:T(8,128)(2,1)S(1)}, u32[]{:S(2)}, u32[]{:S(2)}) %collective-permute-start.39) | collective-permute-done | bytes 301088 | tf_op jit(solution)/shard_map/ppermute | solution.py:805
  282.6 6.5 %collective-permute-done.40.refs_3_ = bf16[4,49,768]{2,1,0:T(8,128)(2,1)S(1)} collective-permute-done((bf16[4,49,768]{2,1,0:T(8,128)(2,1)S(1)}, bf16[4,49,768]{2,1,0:T(8,128)(2,1)S(1)}, u32[]{:S(2)}, u32[]{:S(2)}) %collective-permute-start.40) | collective-permute-done | bytes 301088 | tf_op jit(solution)/shard_map/ppermute | solution.py:805
  290.0 10.3 %time_proj.1 = (bf16[784,768]{1,0:T(8,128)(2,1)S(1)}, bf16[784,768]{1,0:T(8,128)(2,1)S(1)}, bf16[768,768]{1,0:T(8,128)(2,1)S(1)}, bf16[768,768]{1,0:T(8,128)(2,1)S(1)}, f32[8,768]{1,0:T(8,128)S(1)}) custom-call(s32[17]{0:T(128)S(1)} %stack.68.scal_ref.scal, bf16[4,49,768]{2,1,0:T(8,128)(2,1)S(1)} %get-tuple-element.186.refs_0_, ...), custom_call_target="tpu_custom_call" | custom-call | tf_op jit(solution)/shard_map/time_proj/pallas_call | solution.py:232
  302.1 4.7 collective-permute-done.48
  307.8 2.4 collective-permute-start.50
  313.2 13.5 %time_attn_back.1 = (bf16[784,2304]{1,0:T(8,128)(2,1)S(1)}, f32[8,768]{1,0:T(8,128)S(1)}) custom-call(s32[17]{0:T(128)S(1)} %stack.68.scal_ref.scal, bf16[784,2304]{1,0:T(8,128)(2,1)S(1)} %copy-done.5, bf16[784,768]{1,0:T(8,128)(2,1)S(1)} %get-tuple-element.201.refs_1_, bf16[4,96,2304]{2,1,0:T(8,128)(2,1)S(1)} %get-tuple-element.211.refs_2_), custom_call_target="tpu_custom_call" | custom-call | tf_op jit(solution)/shard_map/time_attn_back/pallas_call | solution.py:232
  328.5 10.8 %collective-permute-start.54 = (bf16[1,48,3072]{2,1,0:T(8,128)(2,1)S(1)}, bf16[1,48,3072]{2,1,0:T(8,128)(2,1)S(1)}, u32[]{:S(2)}, u32[]{:S(2)}) collective-permute-start(bf16[1,48,3072]{2,1,0:T(8,128)(2,1)S(1)} %get-tuple-element.221.refs_2_), channel_id=1, source_target_pairs={{0,8},{1,9},{2,10},{3,11},{4,12},{5,13},{6,14},{7,15},{8,0},{9,1},... | collective-permute-start | bytes 884744 | tf_op jit(solution)/shard_map/ppermute | solution.py:820
  340.4 2.1 collective-permute-start.53
  342.6 14.5 %time_out.1 = (f32[8,49,768]{2,1,0:T(8,128)S(1)}, bf16[8,49,768]{2,1,0:T(8,128)(2,1)S(1)}, bf16[768,1152]{1,0:T(8,128)(2,1)S(1)}, bf16[768,1152]{1,0:T(8,128)(2,...) custom-call(s32[17]{0:T(128)S(1)} %stack.68.scal_ref.scal, bf16[784,2304]{1,0:T(8,128)(2,1)S(1)} %get-tuple-element.215.refs_0_, ...), custom_call_target="tpu_custom_call" | custom-call | tf_op jit(solution)/shard_map/time_out/pallas_call | solution.py:232
  360.8 3.4 collective-permute-start.56
  367.7 7.6 %collective-permute-done.56 = bf16[1,96,2304]{2,1,0:T(8,128)(2,1)S(1)} collective-permute-done((bf16[1,96,2304]{2,1,0:T(8,128)(2,1)S(1)}, bf16[1,96,2304]{2,1,0:T(8,128)(2,1)S(1)}, u32[]{:S(2)}, u32[]{:S(2)}) %collective-permute-start.56) | collective-permute-done | bytes 442400 | tf_op jit(solution)/shard_map/ppermute | solution.py:820
  376.0 3.5 collective-permute-done.55
  381.2 6.4 %collective-permute-start.60 = (bf16[1,48,2304]{2,1,0:T(8,128)(2,1)S(1)}, bf16[1,48,2304]{2,1,0:T(8,128)(2,1)S(1)}, u32[]{:S(2)}, u32[]{:S(2)}) collective-permute-start(bf16[1,48,2304]{2,1,0:T(8,128)(2,1)S(1)} %get-tuple-element.233.refs_2_), channel_id=1, source_target_pairs={{0,8},{1,9},{2,10},{3,11},{4,12},{5,13},{6,14},{7,15},{8,0},{9,1},... | collective-permute-start | bytes 663560 | tf_op jit(solution)/shard_map/ppermute | solution.py:820
  388.9 4.9 collective-permute-done.60
  394.7 1.8 collective-permute-done.59
  397.1 1.6 collective-permute-start.63
  400.5 4.0 collective-permute-done.63.refs_2_.refs_18_
  404.7 2.0 collective-permute-start.62
  406.7 8.1 %collective-permute-done.62 = bf16[1,96,1280]{2,1,0:T(8,128)(2,1)S(1)} collective-permute-done((bf16[1,96,1280]{2,1,0:T(8,128)(2,1)S(1)}, bf16[1,96,1280]{2,1,0:T(8,128)(2,1)S(1)}, u32[]{:S(2)}, u32[]{:S(2)}) %collective-permute-start.62) | collective-permute-done | bytes 245792 | tf_op jit(solution)/shard_map/ppermute | solution.py:820
  417.2 4.2 collective-permute-done.73.refs_20_
  421.4 5.7 %collective-permute-start.69 = (bf16[1,48,1280]{2,1,0:T(8,128)(2,1)S(1)}, bf16[1,48,1280]{2,1,0:T(8,128)(2,1)S(1)}, u32[]{:S(2)}, u32[]{:S(2)}) collective-permute-start(bf16[1,48,1280]{2,1,0:T(8,128)(2,1)S(1)} %get-tuple-element.248), channel_id=1, source_target_pairs={{0,8},{1,9},{2,10},{3,11},{4,12},{5,13},{6,14},{7,15},{8,0},{9,1},... | collective-permute-start | bytes 368648 | tf_op jit(solution)/shard_map/ppermute | solution.py:820
  427.1 4.0 collective-permute-done.69
  433.7 4.4 collective-permute-done.75.refs_26_
  440.4 2.1 collective-permute-done.79
  442.5 2.2 collective-permute-start.80
  445.7 2.2 collective-permute-done.80
  448.4 3.1 collective-permute-done.81
  452.8 2.4 collective-permute-done.82
  460.0 3.2 copy-done.67
  463.2 21.3 %shard_map.234 = (f32[192,9984]{1,0:T(8,128)}, f32[192,9984]{1,0:T(8,128)}, f32[192,9984]{1,0:T(8,128)}, f32[768,768]{1,0:T(8,128)}, f32[768,768]{1,0:T(8,128)},...) custom-call(s32[17]{0:T(128)S(1)} %stack.68.scal_ref.scal, ...), custom_call_target="tpu_custom_call" | custom-call | flops 24999999488 | tf_op jit(solution)/shard_map/pallas_call | solution.py:1001
  484.7 1.7 broadcast_select_fusion
  (354 shorter events, 86.9 us)
Async XLA Ops:
  7.2 169.6 %all-gather.2.cloned.1.call-start = ((), (), s32[]{:S(2)}) async-start(), calls=%async_computation | async-start | bytes 9732096 | tf_op jit(solution)/shard_map/all_gather | solution.py:1061
  9.4 25.3 %collective-permute-start.1 = (bf16[48,1280]{1,0:T(8,128)(2,1)S(1)}, bf16[48,1280]{1,0:T(8,128)(2,1)S(1)}, u32[]{:S(2)}, u32[]{:S(2)}) collective-permute-start(bf16[48,1280]{1,0:T(8,128)(2,1)S(1)} %pad_maximum_fusion.1), channel_id=1, source_target_pairs={{0,8},{1,9},{2,10},{3,11},{4,12},{5,13},{6,14},{7,15},{8,0},{9,1},... | collective-permute-start | bytes 368648 | tf_op jit(solution)/shard_map/ppermute | solution.py:820
  12.5 27.5 %collective-permute-start.2 = (bf16[48,1280]{1,0:T(8,128)(2,1)S(1)}, bf16[48,1280]{1,0:T(8,128)(2,1)S(1)}, u32[]{:S(2)}, u32[]{:S(2)}) collective-permute-start(bf16[48,1280]{1,0:T(8,128)(2,1)S(1)} %pad_maximum_fusion.1), channel_id=1, source_target_pairs={{0,24},{1,25},{2,26},{3,27},{4,28},{5,29},{6,30},{7,31},{8,16},{9,... | collective-permute-start | bytes 368648 | tf_op jit(solution)/shard_map/ppermute | solution.py:820
  17.3 21.4 %collective-permute-start = (bf16[8,49,768]{2,0,1:T(8,128)(2,1)}, bf16[8,49,768]{2,0,1:T(8,128)(2,1)}, u32[]{:S(2)}, u32[]{:S(2)}) collective-permute-start(bf16[8,49,768]{2,0,1:T(8,128)(2,1)} %get-tuple-element.271), channel_id=1, source_target_pairs={{0,4},{4,0},{1,5},{5,1},{2,6},{6,2},{3,7},{7,3},{8,12},{12,8},{9,1... | collective-permute-start | bytes 1806344 | tf_op jit(solution)/shard_map/ppermute | solution.py:810
  46.2 12.2 %collective-permute-start.4 = (bf16[3,48,1280]{2,1,0:T(8,128)(2,1)S(1)}, bf16[3,48,1280]{2,1,0:T(8,128)(2,1)S(1)}, u32[]{:S(2)}, u32[]{:S(2)}) collective-permute-start(bf16[3,48,1280]{2,1,0:T(8,128)(2,1)S(1)} %pack.5.refs_3_.refs_12_), channel_id=1, source_target_pairs={{0,4},{1,3},{2,6},{3,1},{4,0},{5,7},{6,2},{7,5},{8,12},{9,11},{10,... | collective-permute-start | bytes 1105928 | tf_op jit(solution)/shard_map/ppermute | solution.py:820
  58.4 8.5 %collective-permute-start.7 = (bf16[3,48,1280]{2,1,0:T(8,128)(2,1)S(1)}, bf16[3,48,1280]{2,1,0:T(8,128)(2,1)S(1)}, u32[]{:S(2)}, u32[]{:S(2)}) collective-permute-start(bf16[3,48,1280]{2,1,0:T(8,128)(2,1)S(1)} %collective-permute-done.4.refs_4_.refs_13_), channel_id=1, source_target_pairs={{0,2},{1,5},{2,0},{3,7},{4,6},{5,1},{6,4},{7,3},{8,10},{9,13},{10,... | collective-permute-start | bytes 1105928 | tf_op jit(solution)/shard_map/ppermute | solution.py:820
  60.0 9.9 %collective-permute-start.5 = (bf16[3,48,1280]{2,1,0:T(8,128)(2,1)S(1)}, bf16[3,48,1280]{2,1,0:T(8,128)(2,1)S(1)}, u32[]{:S(2)}, u32[]{:S(2)}) collective-permute-start(bf16[3,48,1280]{2,1,0:T(8,128)(2,1)S(1)} %pack.5.refs_3_.refs_12_), channel_id=1, source_target_pairs={{0,2},{1,5},{2,0},{3,7},{4,6},{5,1},{6,4},{7,3},{8,10},{9,13},{10,... | collective-permute-start | bytes 1105928 | tf_op jit(solution)/shard_map/ppermute | solution.py:820
  66.9 11.7 %collective-permute-start.13 = (bf16[48,1536]{1,0:T(8,128)(2,1)S(1)}, bf16[48,1536]{1,0:T(8,128)(2,1)S(1)}, u32[]{:S(2)}, u32[]{:S(2)}) collective-permute-start(bf16[48,1536]{1,0:T(8,128)(2,1)S(1)} %pad_maximum_fusion.refs_0_), channel_id=1, source_target_pairs={{0,8},{1,9},{2,10},{3,11},{4,12},{5,13},{6,14},{7,15},{8,0},{9,1},... | collective-permute-start | bytes 442376 | tf_op jit(solution)/shard_map/ppermute | solution.py:820
  67.0 11.7 %collective-permute-start.8 = (bf16[3,48,1280]{2,1,0:T(8,128)(2,1)S(1)}, bf16[3,48,1280]{2,1,0:T(8,128)(2,1)S(1)}, u32[]{:S(2)}, u32[]{:S(2)}) collective-permute-start(bf16[3,48,1280]{2,1,0:T(8,128)(2,1)S(1)} %pack.5.refs_3_.refs_12_), channel_id=1, source_target_pairs={{0,1},{1,0},{2,3},{3,2},{4,5},{5,4},{6,7},{7,6},{8,9},{9,8},{10,11... | collective-permute-start | bytes 1105928 | tf_op jit(solution)/shard_map/ppermute | solution.py:820
  67.1 11.8 %collective-permute-start.9 = (bf16[3,48,1280]{2,1,0:T(8,128)(2,1)S(1)}, bf16[3,48,1280]{2,1,0:T(8,128)(2,1)S(1)}, u32[]{:S(2)}, u32[]{:S(2)}) collective-permute-start(bf16[3,48,1280]{2,1,0:T(8,128)(2,1)S(1)} %collective-permute-done.4.refs_4_.refs_13_), channel_id=1, source_target_pairs={{0,1},{1,0},{2,3},{3,2},{4,5},{5,4},{6,7},{7,6},{8,9},{9,8},{10,11... | collective-permute-start | bytes 1105928 | tf_op jit(solution)/shard_map/ppermute | solution.py:820
  69.8 9.0 %collective-permute-start.10 = (bf16[3,48,1280]{2,1,0:T(8,128)(2,1)S(1)}, bf16[3,48,1280]{2,1,0:T(8,128)(2,1)S(1)}, u32[]{:S(2)}, u32[]{:S(2)}) collective-permute-start(bf16[3,48,1280]{2,1,0:T(8,128)(2,1)S(1)} %collective-permute-done.5.refs_5_.refs_14_), channel_id=1, source_target_pairs={{0,1},{1,0},{2,3},{3,2},{4,5},{5,4},{6,7},{7,6},{8,9},{9,8},{10,11... | collective-permute-start | bytes 1105928 | tf_op jit(solution)/shard_map/ppermute | solution.py:820
  69.9 9.1 %collective-permute-start.11 = (bf16[3,48,1280]{2,1,0:T(8,128)(2,1)S(1)}, bf16[3,48,1280]{2,1,0:T(8,128)(2,1)S(1)}, u32[]{:S(2)}, u32[]{:S(2)}) collective-permute-start(bf16[3,48,1280]{2,1,0:T(8,128)(2,1)S(1)} %collective-permute-done.7.refs_2_.refs_6_.refs_15_), channel_id=1, source_target_pairs={{0,1},{1,0},{2,3},{3,2},{4,5},{5,4},{6,7},{7,6},{8,9},{9,8},{10,11... | collective-permute-start | bytes 1105928 | tf_op jit(solution)/shard_map/ppermute | solution.py:820
  78.7 12.3 %collective-permute-start.14 = (bf16[2,48,1536]{2,1,0:T(8,128)(2,1)S(1)}, bf16[2,48,1536]{2,1,0:T(8,128)(2,1)S(1)}, u32[]{:S(2)}, u32[]{:S(2)}) collective-permute-start(bf16[2,48,1536]{2,1,0:T(8,128)(2,1)S(1)} %pack.8.refs_21_), channel_id=1, source_target_pairs={{0,24},{1,25},{2,26},{3,27},{4,28},{5,29},{6,30},{7,31},{8,16},{9,... | collective-permute-start | bytes 884744 | tf_op jit(solution)/shard_map/ppermute | solution.py:820
  78.8 13.2 %collective-permute-start.15 = (bf16[3,48,768]{2,1,0:T(8,128)(2,1)S(1)}, bf16[3,48,768]{2,1,0:T(8,128)(2,1)S(1)}, u32[]{:S(2)}, u32[]{:S(2)}) collective-permute-start(bf16[3,48,768]{2,1,0:T(8,128)(2,1)S(1)} %pack.7.refs_2_.refs_20_.refs_4_.refs_7_), channel_id=1, source_target_pairs={{0,4},{1,3},{2,6},{3,1},{4,0},{5,7},{6,2},{7,5},{8,12},{9,11},{10,... | collective-permute-start | bytes 663560 | tf_op jit(solution)/shard_map/ppermute | solution.py:820
  92.0 10.6 %collective-permute-start.22 = (bf16[3,48,1536]{2,1,0:T(8,128)(2,1)S(1)}, bf16[3,48,1536]{2,1,0:T(8,128)(2,1)S(1)}, u32[]{:S(2)}, u32[]{:S(2)}) collective-permute-start(bf16[3,48,1536]{2,1,0:T(8,128)(2,1)S(1)} %pack.9.refs_1_.refs_6_.refs_4_.refs_7_), channel_id=1, source_target_pairs={{0,4},{1,3},{2,6},{3,1},{4,0},{5,7},{6,2},{7,5},{8,12},{9,11},{10,... | collective-permute-start | bytes 1327112 | tf_op jit(solution)/shard_map/ppermute | solution.py:820
  92.0 8.3 %collective-permute-start.17 = (bf16[3,48,768]{2,1,0:T(8,128)(2,1)S(1)}, bf16[3,48,768]{2,1,0:T(8,128)(2,1)S(1)}, u32[]{:S(2)}, u32[]{:S(2)}) collective-permute-start(bf16[3,48,768]{2,1,0:T(8,128)(2,1)S(1)} %collective-permute-done.15.refs_2_.refs_5_.refs_8_), channel_id=1, source_target_pairs={{0,2},{1,5},{2,0},{3,7},{4,6},{5,1},{6,4},{7,3},{8,10},{9,13},{10,... | collective-permute-start | bytes 663560 | tf_op jit(solution)/shard_map/ppermute | solution.py:820
  100.3 18.7 %collective-permute-start.26 = (bf16[3,48,1536]{2,1,0:T(8,128)(2,1)S(1)}, bf16[3,48,1536]{2,1,0:T(8,128)(2,1)S(1)}, u32[]{:S(2)}, u32[]{:S(2)}) collective-permute-start(bf16[3,48,1536]{2,1,0:T(8,128)(2,1)S(1)} %pack.9.refs_1_.refs_6_.refs_4_.refs_7_), channel_id=1, source_target_pairs={{0,2},{1,5},{2,0},{3,7},{4,6},{5,1},{6,4},{7,3},{8,10},{9,13},{10,... | collective-permute-start | bytes 1327112 | tf_op jit(solution)/shard_map/ppermute | solution.py:820
  103.1 39.4 %collective-permute-start.27 = (bf16[3,48,1536]{2,1,0:T(8,128)(2,1)S(1)}, bf16[3,48,1536]{2,1,0:T(8,128)(2,1)S(1)}, u32[]{:S(2)}, u32[]{:S(2)}) collective-permute-start(bf16[3,48,1536]{2,1,0:T(8,128)(2,1)S(1)} %collective-permute-done.22.refs_12_.refs_7_.refs_5_.refs_8_), channel_id=1, source_target_pairs={{0,2},{1,5},{2,0},{3,7},{4,6},{5,1},{6,4},{7,3},{8,10},{9,13},{10,... | collective-permute-start | bytes 1327112 | tf_op jit(solution)/shard_map/ppermute | solution.py:820
  111.8 9.5 %collective-permute-start.23 = (bf16[4,49,768]{2,1,0:T(8,128)(2,1)S(1)}, bf16[4,49,768]{2,1,0:T(8,128)(2,1)S(1)}, u32[]{:S(2)}, u32[]{:S(2)}) collective-permute-start(bf16[4,49,768]{2,1,0:T(8,128)(2,1)S(1)} %get-tuple-element.153), channel_id=1, source_target_pairs={{0,1},{1,0},{2,3},{3,2},{4,5},{5,4},{6,7},{7,6},{8,9},{9,8},{10,11... | collective-permute-start | bytes 903176 | tf_op jit(solution)/shard_map/ppermute | solution.py:805
  112.2 28.8 %collective-permute-start.24 = (bf16[4,49,768]{2,1,0:T(8,128)(2,1)S(1)}, bf16[4,49,768]{2,1,0:T(8,128)(2,1)S(1)}, u32[]{:S(2)}, u32[]{:S(2)}) collective-permute-start(bf16[4,49,768]{2,1,0:T(8,128)(2,1)S(1)} %get-tuple-element.154), channel_id=1, source_target_pairs={{0,2},{1,3},{2,0},{3,1},{4,6},{5,7},{6,4},{7,5},{8,10},{9,11},{10,... | collective-permute-start | bytes 903176 | tf_op jit(solution)/shard_map/ppermute | solution.py:805
  112.2 30.3 %collective-permute-start.25 = (bf16[4,49,768]{2,1,0:T(8,128)(2,1)S(1)}, bf16[4,49,768]{2,1,0:T(8,128)(2,1)S(1)}, u32[]{:S(2)}, u32[]{:S(2)}) collective-permute-start(bf16[4,49,768]{2,1,0:T(8,128)(2,1)S(1)} %get-tuple-element.155), channel_id=1, source_target_pairs={{0,3},{1,2},{2,1},{3,0},{4,7},{5,6},{6,5},{7,4},{8,11},{9,10},{10,... | collective-permute-start | bytes 903176 | tf_op jit(solution)/shard_map/ppermute | solution.py:805
  119.0 26.1 %collective-permute-start.32 = (bf16[8,49,768]{2,0,1:T(8,128)(2,1)S(1)}, bf16[8,49,768]{2,0,1:T(8,128)(2,1)S(1)}, u32[]{:S(2)}, u32[]{:S(2)}) collective-permute-start(bf16[8,49,768]{2,0,1:T(8,128)(2,1)S(1)} %get-tuple-element.162), channel_id=1, source_target_pairs={{0,4},{4,0},{1,5},{5,1},{2,6},{6,2},{3,7},{7,3},{8,12},{12,8},{9,1... | collective-permute-start | bytes 1806344 | tf_op jit(solution)/shard_map/ppermute | solution.py:810
  156.7 16.2 %collective-permute-start.33 = (bf16[4,49,768]{2,1,0:T(8,128)(2,1)S(1)}, bf16[4,49,768]{2,1,0:T(8,128)(2,1)S(1)}, u32[]{:S(2)}, u32[]{:S(2)}) collective-permute-start(bf16[4,49,768]{2,1,0:T(8,128)(2,1)S(1)} %get-tuple-element.169), channel_id=1, source_target_pairs={{0,1},{1,0},{2,3},{3,2},{4,5},{5,4},{6,7},{7,6},{8,9},{9,8},{10,11... | collective-permute-start | bytes 903176 | tf_op jit(solution)/shard_map/ppermute | solution.py:805
  157.0 15.8 %collective-permute-start.34 = (bf16[4,49,768]{2,1,0:T(8,128)(2,1)S(1)}, bf16[4,49,768]{2,1,0:T(8,128)(2,1)S(1)}, u32[]{:S(2)}, u32[]{:S(2)}) collective-permute-start(bf16[4,49,768]{2,1,0:T(8,128)(2,1)S(1)} %get-tuple-element.170), channel_id=1, source_target_pairs={{0,2},{1,3},{2,0},{3,1},{4,6},{5,7},{6,4},{7,5},{8,10},{9,11},{10,... | collective-permute-start | bytes 903176 | tf_op jit(solution)/shard_map/ppermute | solution.py:805
  157.3 16.4 %collective-permute-start.35 = (bf16[4,49,768]{2,1,0:T(8,128)(2,1)S(1)}, bf16[4,49,768]{2,1,0:T(8,128)(2,1)S(1)}, u32[]{:S(2)}, u32[]{:S(2)}) collective-permute-start(bf16[4,49,768]{2,1,0:T(8,128)(2,1)S(1)} %get-tuple-element.171), channel_id=1, source_target_pairs={{0,3},{1,2},{2,1},{3,0},{4,7},{5,6},{6,5},{7,4},{8,11},{9,10},{10,... | collective-permute-start | bytes 903176 | tf_op jit(solution)/shard_map/ppermute | solution.py:805
  228.9 8.9 %collective-permute-start.36 = (bf16[768,1536]{1,0:T(8,128)(2,1)S(1)}, bf16[768,1536]{1,0:T(8,128)(2,1)S(1)}, u32[]{:S(2)}, u32[]{:S(2)}) collective-permute-start(bf16[768,1536]{1,0:T(8,128)(2,1)S(1)} %get-tuple-element.180), channel_id=1, source_target_pairs={{0,1},{1,0},{2,3},{3,2},{4,5},{5,4},{6,7},{7,6},{8,9},{9,8},{10,11... | collective-permute-start | bytes 7077896 | tf_op jit(solution)/shard_map/ppermute | solution.py:820
  239.8 33.7 %collective-permute-start.41 = (bf16[4,96,3072]{2,1,0:T(8,128)(2,1)S(1)}, bf16[4,96,3072]{2,1,0:T(8,128)(2,1)S(1)}, u32[]{:S(2)}, u32[]{:S(2)}) collective-permute-start(bf16[4,96,3072]{2,1,0:T(8,128)(2,1)S(1)} %get-tuple-element.183.refs_2_), channel_id=1, source_target_pairs={{0,4},{1,3},{2,6},{3,1},{4,0},{5,7},{6,2},{7,5},{8,12},{9,11},{10,... | collective-permute-start | bytes 7077896 | tf_op jit(solution)/shard_map/ppermute | solution.py:820
  271.6 10.9 %collective-permute-start.39 = (bf16[4,49,768]{2,1,0:T(8,128)(2,1)S(1)}, bf16[4,49,768]{2,1,0:T(8,128)(2,1)S(1)}, u32[]{:S(2)}, u32[]{:S(2)}) collective-permute-start(bf16[4,49,768]{2,1,0:T(8,128)(2,1)S(1)} %get-tuple-element.188), channel_id=1, source_target_pairs={{0,2},{1,3},{2,0},{3,1},{4,6},{5,7},{6,4},{7,5},{8,10},{9,11},{10,... | collective-permute-start | bytes 903176 | tf_op jit(solution)/shard_map/ppermute | solution.py:805
  272.3 16.7 %collective-permute-start.40 = (bf16[4,49,768]{2,1,0:T(8,128)(2,1)S(1)}, bf16[4,49,768]{2,1,0:T(8,128)(2,1)S(1)}, u32[]{:S(2)}, u32[]{:S(2)}) collective-permute-start(bf16[4,49,768]{2,1,0:T(8,128)(2,1)S(1)} %get-tuple-element.189), channel_id=1, source_target_pairs={{0,3},{1,2},{2,1},{3,0},{4,7},{5,6},{6,5},{7,4},{8,11},{9,10},{10,... | collective-permute-start | bytes 903176 | tf_op jit(solution)/shard_map/ppermute | solution.py:805
  289.0 17.8 %collective-permute-start.48 = (bf16[4,48,3072]{2,1,0:T(8,128)(2,1)S(1)}, bf16[4,48,3072]{2,1,0:T(8,128)(2,1)S(1)}, u32[]{:S(2)}, u32[]{:S(2)}) collective-permute-start(bf16[4,48,3072]{2,1,0:T(8,128)(2,1)S(1)} %get-tuple-element.209.refs_15_), channel_id=1, source_target_pairs={{0,2},{1,5},{2,0},{3,7},{4,6},{5,1},{6,4},{7,3},{8,10},{9,13},{10,... | collective-permute-start | bytes 3538952 | tf_op jit(solution)/shard_map/ppermute | solution.py:820
  289.4 18.2 %collective-permute-start.45 = (bf16[768,384]{1,0:T(8,128)(2,1)S(1)}, bf16[768,384]{1,0:T(8,128)(2,1)S(1)}, u32[]{:S(2)}, u32[]{:S(2)}) collective-permute-start(bf16[768,384]{1,0:T(8,128)(2,1)S(1)} %get-tuple-element.205), channel_id=1, source_target_pairs={{0,1},{1,0},{2,3},{3,2},{4,5},{5,4},{6,7},{7,6},{8,9},{9,8},{10,11... | collective-permute-start | bytes 1769480 | tf_op jit(solution)/shard_map/ppermute | solution.py:820
  289.6 18.2 %collective-permute-start.46 = (bf16[768,1152]{1,0:T(8,128)(2,1)S(1)}, bf16[768,1152]{1,0:T(8,128)(2,1)S(1)}, u32[]{:S(2)}, u32[]{:S(2)}) collective-permute-start(bf16[768,1152]{1,0:T(8,128)(2,1)S(1)} %get-tuple-element.206), channel_id=1, source_target_pairs={{0,1},{1,0},{2,3},{3,2},{4,5},{5,4},{6,7},{7,6},{8,9},{9,8},{10,11... | collective-permute-start | bytes 5308424 | tf_op jit(solution)/shard_map/ppermute | solution.py:820
  300.3 9.8 %collective-permute-start.47 = (bf16[768,768]{1,0:T(8,128)(2,1)S(1)}, bf16[768,768]{1,0:T(8,128)(2,1)S(1)}, u32[]{:S(2)}, u32[]{:S(2)}) collective-permute-start(bf16[768,768]{1,0:T(8,128)(2,1)S(1)} %get-tuple-element.207), channel_id=1, source_target_pairs={{0,1},{1,0},{2,3},{3,2},{4,5},{5,4},{6,7},{7,6},{8,9},{9,8},{10,11... | collective-permute-start | bytes 3538952 | tf_op jit(solution)/shard_map/ppermute | solution.py:820
  300.5 26.2 %collective-permute-start.44 = (bf16[4,49,768]{2,1,0:T(8,128)(2,1)S(1)}, bf16[4,49,768]{2,1,0:T(8,128)(2,1)S(1)}, u32[]{:S(2)}, u32[]{:S(2)}) collective-permute-start(bf16[4,49,768]{2,1,0:T(8,128)(2,1)S(1)} %get-tuple-element.200), channel_id=1, source_target_pairs={{0,3},{1,2},{2,1},{3,0},{4,7},{5,6},{6,5},{7,4},{8,11},{9,10},{10,... | collective-permute-start | bytes 903176 | tf_op jit(solution)/shard_map/ppermute | solution.py:805
  306.9 19.9 %collective-permute-start.43 = (bf16[4,49,768]{2,1,0:T(8,128)(2,1)S(1)}, bf16[4,49,768]{2,1,0:T(8,128)(2,1)S(1)}, u32[]{:S(2)}, u32[]{:S(2)}) collective-permute-start(bf16[4,49,768]{2,1,0:T(8,128)(2,1)S(1)} %get-tuple-element.198), channel_id=1, source_target_pairs={{0,2},{1,3},{2,0},{3,1},{4,6},{5,7},{6,4},{7,5},{8,10},{9,11},{10,... | collective-permute-start | bytes 903176 | tf_op jit(solution)/shard_map/ppermute | solution.py:805
  307.7 19.1 %collective-permute-start.42 = (bf16[4,49,768]{2,1,0:T(8,128)(2,1)S(1)}, bf16[4,49,768]{2,1,0:T(8,128)(2,1)S(1)}, u32[]{:S(2)}, u32[]{:S(2)}) collective-permute-start(bf16[4,49,768]{2,1,0:T(8,128)(2,1)S(1)} %get-tuple-element.196), channel_id=1, source_target_pairs={{0,1},{1,0},{2,3},{3,2},{4,5},{5,4},{6,7},{7,6},{8,9},{9,8},{10,11... | collective-permute-start | bytes 903176 | tf_op jit(solution)/shard_map/ppermute | solution.py:805
  307.8 20.0 %collective-permute-start.50 = (bf16[1,96,3072]{2,1,0:T(8,128)(2,1)S(1)}, bf16[1,96,3072]{2,1,0:T(8,128)(2,1)S(1)}, u32[]{:S(2)}, u32[]{:S(2)}) collective-permute-start(bf16[1,96,3072]{2,1,0:T(8,128)(2,1)S(1)} %get-tuple-element.210.refs_6_), channel_id=1, source_target_pairs={{0,24},{1,25},{2,26},{3,27},{4,28},{5,29},{6,30},{7,31},{8,16},{9,... | collective-permute-start | bytes 1769480 | tf_op jit(solution)/shard_map/ppermute | solution.py:820
  311.6 27.6 %collective-permute-start.49 = (bf16[4,96,2304]{2,1,0:T(8,128)(2,1)S(1)}, bf16[4,96,2304]{2,1,0:T(8,128)(2,1)S(1)}, u32[]{:S(2)}, u32[]{:S(2)}) collective-permute-start(bf16[4,96,2304]{2,1,0:T(8,128)(2,1)S(1)} %get-tuple-element.211.refs_2_), channel_id=1, source_target_pairs={{0,4},{1,3},{2,6},{3,1},{4,0},{5,7},{6,2},{7,5},{8,12},{9,11},{10,... | collective-permute-start | bytes 5308424 | tf_op jit(solution)/shard_map/ppermute | solution.py:820
  328.5 28.7 %collective-permute-start.54 = (bf16[1,48,3072]{2,1,0:T(8,128)(2,1)S(1)}, bf16[1,48,3072]{2,1,0:T(8,128)(2,1)S(1)}, u32[]{:S(2)}, u32[]{:S(2)}) collective-permute-start(bf16[1,48,3072]{2,1,0:T(8,128)(2,1)S(1)} %get-tuple-element.221.refs_2_), channel_id=1, source_target_pairs={{0,8},{1,9},{2,10},{3,11},{4,12},{5,13},{6,14},{7,15},{8,0},{9,1},... | collective-permute-start | bytes 884744 | tf_op jit(solution)/shard_map/ppermute | solution.py:820
  340.4 19.5 %collective-permute-start.53 = (bf16[4,48,2304]{2,1,0:T(8,128)(2,1)S(1)}, bf16[4,48,2304]{2,1,0:T(8,128)(2,1)S(1)}, u32[]{:S(2)}, u32[]{:S(2)}) collective-permute-start(bf16[4,48,2304]{2,1,0:T(8,128)(2,1)S(1)} %get-tuple-element.222.refs_20_), channel_id=1, source_target_pairs={{0,2},{1,5},{2,0},{3,7},{4,6},{5,1},{6,4},{7,3},{8,10},{9,13},{10,... | collective-permute-start | bytes 2654216 | tf_op jit(solution)/shard_map/ppermute | solution.py:820
  358.2 9.6 %collective-permute-start.57 = (bf16[48,3072]{1,0:T(8,128)(2,1)S(1)}, bf16[48,3072]{1,0:T(8,128)(2,1)S(1)}, u32[]{:S(2)}, u32[]{:S(2)}) collective-permute-start(bf16[48,3072]{1,0:T(8,128)(2,1)S(1)} %get-tuple-element.243.refs_2_.refs_9_), channel_id=1, source_target_pairs={{0,4},{1,3},{2,6},{3,1},{4,0},{5,7},{6,2},{7,5},{8,12},{9,11},{10,... | collective-permute-start | bytes 884744 | tf_op jit(solution)/shard_map/ppermute | solution.py:820
  358.7 9.0 %collective-permute-start.58 = (bf16[48,3072]{1,0:T(8,128)(2,1)S(1)}, bf16[48,3072]{1,0:T(8,128)(2,1)S(1)}, u32[]{:S(2)}, u32[]{:S(2)}) collective-permute-start(bf16[48,3072]{1,0:T(8,128)(2,1)S(1)} %get-tuple-element.243.refs_2_.refs_9_), channel_id=1, source_target_pairs={{0,2},{1,5},{2,0},{3,7},{4,6},{5,1},{6,4},{7,3},{8,10},{9,13},{10,... | collective-permute-start | bytes 884744 | tf_op jit(solution)/shard_map/ppermute | solution.py:820
  360.8 14.5 %collective-permute-start.56 = (bf16[1,96,2304]{2,1,0:T(8,128)(2,1)S(1)}, bf16[1,96,2304]{2,1,0:T(8,128)(2,1)S(1)}, u32[]{:S(2)}, u32[]{:S(2)}) collective-permute-start(bf16[1,96,2304]{2,1,0:T(8,128)(2,1)S(1)} %get-tuple-element.229.refs_4_), channel_id=1, source_target_pairs={{0,24},{1,25},{2,26},{3,27},{4,28},{5,29},{6,30},{7,31},{8,16},{9,... | collective-permute-start | bytes 1327112 | tf_op jit(solution)/shard_map/ppermute | solution.py:820
  365.3 14.2 %collective-permute-start.55 = (bf16[4,96,1280]{2,1,0:T(8,128)(2,1)S(1)}, bf16[4,96,1280]{2,1,0:T(8,128)(2,1)S(1)}, u32[]{:S(2)}, u32[]{:S(2)}) collective-permute-start(bf16[4,96,1280]{2,1,0:T(8,128)(2,1)S(1)} %get-tuple-element.231.refs_4_), channel_id=1, source_target_pairs={{0,4},{1,3},{2,6},{3,1},{4,0},{5,7},{6,2},{7,5},{8,12},{9,11},{10,... | collective-permute-start | bytes 2949128 | tf_op jit(solution)/shard_map/ppermute | solution.py:820
  380.4 13.4 %collective-permute-start.61 = (bf16[48,3072]{1,0:T(8,128)(2,1)S(1)}, bf16[48,3072]{1,0:T(8,128)(2,1)S(1)}, u32[]{:S(2)}, u32[]{:S(2)}) collective-permute-start(bf16[48,3072]{1,0:T(8,128)(2,1)S(1)} %collective-permute-done.57.refs_2_.refs_10_), channel_id=1, source_target_pairs={{0,2},{1,5},{2,0},{3,7},{4,6},{5,1},{6,4},{7,3},{8,10},{9,13},{10,... | collective-permute-start | bytes 884744 | tf_op jit(solution)/shard_map/ppermute | solution.py:820
  381.2 12.6 %collective-permute-start.60 = (bf16[1,48,2304]{2,1,0:T(8,128)(2,1)S(1)}, bf16[1,48,2304]{2,1,0:T(8,128)(2,1)S(1)}, u32[]{:S(2)}, u32[]{:S(2)}) collective-permute-start(bf16[1,48,2304]{2,1,0:T(8,128)(2,1)S(1)} %get-tuple-element.233.refs_2_), channel_id=1, source_target_pairs={{0,8},{1,9},{2,10},{3,11},{4,12},{5,13},{6,14},{7,15},{8,0},{9,1},... | collective-permute-start | bytes 663560 | tf_op jit(solution)/shard_map/ppermute | solution.py:820
  387.6 8.8 %collective-permute-start.59 = (bf16[4,48,1280]{2,1,0:T(8,128)(2,1)S(1)}, bf16[4,48,1280]{2,1,0:T(8,128)(2,1)S(1)}, u32[]{:S(2)}, u32[]{:S(2)}) collective-permute-start(bf16[4,48,1280]{2,1,0:T(8,128)(2,1)S(1)} %get-tuple-element.235), channel_id=1, source_target_pairs={{0,2},{1,5},{2,0},{3,7},{4,6},{5,1},{6,4},{7,3},{8,10},{9,13},{10,... | collective-permute-start | bytes 1474568 | tf_op jit(solution)/shard_map/ppermute | solution.py:820
  400.0 14.7 %collective-permute-start.65 = (bf16[48,3072]{1,0:T(8,128)(2,1)S(1)}, bf16[48,3072]{1,0:T(8,128)(2,1)S(1)}, u32[]{:S(2)}, u32[]{:S(2)}) collective-permute-start(bf16[48,3072]{1,0:T(8,128)(2,1)S(1)} %get-tuple-element.243.refs_2_.refs_9_), channel_id=1, source_target_pairs={{0,1},{1,0},{2,3},{3,2},{4,5},{5,4},{6,7},{7,6},{8,9},{9,8},{10,11... | collective-permute-start | bytes 884744 | tf_op jit(solution)/shard_map/ppermute | solution.py:820
  400.0 14.7 %collective-permute-start.66 = (bf16[48,3072]{1,0:T(8,128)(2,1)S(1)}, bf16[48,3072]{1,0:T(8,128)(2,1)S(1)}, u32[]{:S(2)}, u32[]{:S(2)}) collective-permute-start(bf16[48,3072]{1,0:T(8,128)(2,1)S(1)} %collective-permute-done.57.refs_2_.refs_10_), channel_id=1, source_target_pairs={{0,1},{1,0},{2,3},{3,2},{4,5},{5,4},{6,7},{7,6},{8,9},{9,8},{10,11... | collective-permute-start | bytes 884744 | tf_op jit(solution)/shard_map/ppermute | solution.py:820
  400.5 14.2 %collective-permute-start.67 = (bf16[48,3072]{1,0:T(8,128)(2,1)S(1)}, bf16[48,3072]{1,0:T(8,128)(2,1)S(1)}, u32[]{:S(2)}, u32[]{:S(2)}) collective-permute-start(bf16[48,3072]{1,0:T(8,128)(2,1)S(1)} %collective-permute-done.58.refs_3_.refs_11_), channel_id=1, source_target_pairs={{0,1},{1,0},{2,3},{3,2},{4,5},{5,4},{6,7},{7,6},{8,9},{9,8},{10,11... | collective-permute-start | bytes 884744 | tf_op jit(solution)/shard_map/ppermute | solution.py:820
  404.5 10.3 %collective-permute-start.68 = (bf16[48,3072]{1,0:T(8,128)(2,1)S(1)}, bf16[48,3072]{1,0:T(8,128)(2,1)S(1)}, u32[]{:S(2)}, u32[]{:S(2)}) collective-permute-start(bf16[48,3072]{1,0:T(8,128)(2,1)S(1)} %collective-permute-done.61.refs_0_.refs_12_), channel_id=1, source_target_pairs={{0,1},{1,0},{2,3},{3,2},{4,5},{5,4},{6,7},{7,6},{8,9},{9,8},{10,11... | collective-permute-start | bytes 884744 | tf_op jit(solution)/shard_map/ppermute | solution.py:820
  404.7 10.1 %collective-permute-start.62 = (bf16[1,96,1280]{2,1,0:T(8,128)(2,1)S(1)}, bf16[1,96,1280]{2,1,0:T(8,128)(2,1)S(1)}, u32[]{:S(2)}, u32[]{:S(2)}) collective-permute-start(bf16[1,96,1280]{2,1,0:T(8,128)(2,1)S(1)} %get-tuple-element.241), channel_id=1, source_target_pairs={{0,24},{1,25},{2,26},{3,27},{4,28},{5,29},{6,30},{7,31},{8,16},{9,... | collective-permute-start | bytes 737288 | tf_op jit(solution)/shard_map/ppermute | solution.py:820
  416.7 10.4 %collective-permute-start.70 = (bf16[48,2304]{1,0:T(8,128)(2,1)S(1)}, bf16[48,2304]{1,0:T(8,128)(2,1)S(1)}, u32[]{:S(2)}, u32[]{:S(2)}) collective-permute-start(bf16[48,2304]{1,0:T(8,128)(2,1)S(1)} %get-tuple-element.242.refs_2_.refs_17_), channel_id=1, source_target_pairs={{0,1},{1,0},{2,3},{3,2},{4,5},{5,4},{6,7},{7,6},{8,9},{9,8},{10,11... | collective-permute-start | bytes 663560 | tf_op jit(solution)/shard_map/ppermute | solution.py:820
  416.7 14.4 %collective-permute-start.71 = (bf16[48,2304]{1,0:T(8,128)(2,1)S(1)}, bf16[48,2304]{1,0:T(8,128)(2,1)S(1)}, u32[]{:S(2)}, u32[]{:S(2)}) collective-permute-start(bf16[48,2304]{1,0:T(8,128)(2,1)S(1)} %collective-permute-done.63.refs_2_.refs_18_), channel_id=1, source_target_pairs={{0,1},{1,0},{2,3},{3,2},{4,5},{5,4},{6,7},{7,6},{8,9},{9,8},{10,11... | collective-permute-start | bytes 663560 | tf_op jit(solution)/shard_map/ppermute | solution.py:820
  417.2 13.9 %collective-permute-start.72 = (bf16[48,2304]{1,0:T(8,128)(2,1)S(1)}, bf16[48,2304]{1,0:T(8,128)(2,1)S(1)}, u32[]{:S(2)}, u32[]{:S(2)}) collective-permute-start(bf16[48,2304]{1,0:T(8,128)(2,1)S(1)} %collective-permute-done.64.refs_3_.refs_19_), channel_id=1, source_target_pairs={{0,1},{1,0},{2,3},{3,2},{4,5},{5,4},{6,7},{7,6},{8,9},{9,8},{10,11... | collective-permute-start | bytes 663560 | tf_op jit(solution)/shard_map/ppermute | solution.py:820
  421.4 9.7 %collective-permute-start.74 = (bf16[48,2304]{1,0:T(8,128)(2,1)S(1)}, bf16[48,2304]{1,0:T(8,128)(2,1)S(1)}, u32[]{:S(2)}, u32[]{:S(2)}) collective-permute-start(bf16[48,2304]{1,0:T(8,128)(2,1)S(1)} %collective-permute-done.73.refs_20_), channel_id=1, source_target_pairs={{0,1},{1,0},{2,3},{3,2},{4,5},{5,4},{6,7},{7,6},{8,9},{9,8},{10,11... | collective-permute-start | bytes 663560 | tf_op jit(solution)/shard_map/ppermute | solution.py:820
  421.4 9.7 %collective-permute-start.69 = (bf16[1,48,1280]{2,1,0:T(8,128)(2,1)S(1)}, bf16[1,48,1280]{2,1,0:T(8,128)(2,1)S(1)}, u32[]{:S(2)}, u32[]{:S(2)}) collective-permute-start(bf16[1,48,1280]{2,1,0:T(8,128)(2,1)S(1)} %get-tuple-element.248), channel_id=1, source_target_pairs={{0,8},{1,9},{2,10},{3,11},{4,12},{5,13},{6,14},{7,15},{8,0},{9,1},... | collective-permute-start | bytes 368648 | tf_op jit(solution)/shard_map/ppermute | solution.py:820
  432.5 12.7 %collective-permute-start.84 = (bf16[48,1280]{1,0:T(8,128)(2,1)S(1)}, bf16[48,1280]{1,0:T(8,128)(2,1)S(1)}, u32[]{:S(2)}, u32[]{:S(2)}) collective-permute-start(bf16[48,1280]{1,0:T(8,128)(2,1)S(1)} %get-tuple-element.251.refs_25_), channel_id=1, source_target_pairs={{0,2},{1,5},{2,0},{3,7},{4,6},{5,1},{6,4},{7,3},{8,10},{9,13},{10,... | collective-permute-start | bytes 368648 | tf_op jit(solution)/shard_map/ppermute | solution.py:820
  444.7 13.6 %collective-permute-start.85 = (bf16[48,1280]{1,0:T(8,128)(2,1)S(1)}, bf16[48,1280]{1,0:T(8,128)(2,1)S(1)}, u32[]{:S(2)}, u32[]{:S(2)}) collective-permute-start(bf16[48,1280]{1,0:T(8,128)(2,1)S(1)} %get-tuple-element.251.refs_25_), channel_id=1, source_target_pairs={{0,1},{1,0},{2,3},{3,2},{4,5},{5,4},{6,7},{7,6},{8,9},{9,8},{10,11... | collective-permute-start | bytes 368648 | tf_op jit(solution)/shard_map/ppermute | solution.py:820
  444.7 15.2 %collective-permute-start.86 = (bf16[48,1280]{1,0:T(8,128)(2,1)S(1)}, bf16[48,1280]{1,0:T(8,128)(2,1)S(1)}, u32[]{:S(2)}, u32[]{:S(2)}) collective-permute-start(bf16[48,1280]{1,0:T(8,128)(2,1)S(1)} %collective-permute-done.75.refs_26_), channel_id=1, source_target_pairs={{0,1},{1,0},{2,3},{3,2},{4,5},{5,4},{6,7},{7,6},{8,9},{9,8},{10,11... | collective-permute-start | bytes 368648 | tf_op jit(solution)/shard_map/ppermute | solution.py:820
  445.2 14.7 %collective-permute-start.87 = (bf16[48,1280]{1,0:T(8,128)(2,1)S(1)}, bf16[48,1280]{1,0:T(8,128)(2,1)S(1)}, u32[]{:S(2)}, u32[]{:S(2)}) collective-permute-start(bf16[48,1280]{1,0:T(8,128)(2,1)S(1)} %collective-permute-done.84.refs_27_), channel_id=1, source_target_pairs={{0,1},{1,0},{2,3},{3,2},{4,5},{5,4},{6,7},{7,6},{8,9},{9,8},{10,11... | collective-permute-start | bytes 368648 | tf_op jit(solution)/shard_map/ppermute | solution.py:820
  445.2 14.7 %collective-permute-start.88 = (bf16[48,1280]{1,0:T(8,128)(2,1)S(1)}, bf16[48,1280]{1,0:T(8,128)(2,1)S(1)}, u32[]{:S(2)}, u32[]{:S(2)}) collective-permute-start(bf16[48,1280]{1,0:T(8,128)(2,1)S(1)} %collective-permute-done.76.refs_28_), channel_id=1, source_target_pairs={{0,1},{1,0},{2,3},{3,2},{4,5},{5,4},{6,7},{7,6},{8,9},{9,8},{10,11... | collective-permute-start | bytes 368648 | tf_op jit(solution)/shard_map/ppermute | solution.py:820
  457.6 26.9 %collective-permute-start.78 = (bf16[8,49,768]{2,0,1:T(8,128)(2,1)S(1)}, bf16[8,49,768]{2,0,1:T(8,128)(2,1)S(1)}, u32[]{:S(2)}, u32[]{:S(2)}) collective-permute-start(bf16[8,49,768]{2,0,1:T(8,128)(2,1)S(1)} %copy.55), channel_id=1, source_target_pairs={{0,4},{4,0},{1,5},{5,1},{2,6},{6,2},{3,7},{7,3},{8,12},{12,8},{9,1... | collective-permute-start | bytes 1806344 | tf_op jit(solution)/shard_map/ppermute | solution.py:810
  458.3 28.2 %collective-permute-start.77 = (bf16[8,49,768]{2,0,1:T(8,128)(2,1)S(1)}, bf16[8,49,768]{2,0,1:T(8,128)(2,1)S(1)}, u32[]{:S(2)}, u32[]{:S(2)}) collective-permute-start(bf16[8,49,768]{2,0,1:T(8,128)(2,1)S(1)} %copy.53), channel_id=1, source_target_pairs={{0,4},{4,0},{1,5},{5,1},{2,6},{6,2},{3,7},{7,3},{8,12},{12,8},{9,1... | collective-permute-start | bytes 1806344 | tf_op jit(solution)/shard_map/ppermute | solution.py:810
  (105 other events, 1149.8 us)
Sparse Core Ops, SparseCore 0:
  41.6 101.7 all-gather.1

commit v3 on v2

--- a/solution.py
+++ b/solution.py
@@ -1095,19 +1095,23 @@
         piece_0 = jnp.concatenate([half_of(*spans["at"]), vec_quarter], axis=1)
         near_0 = next_plane(piece_0)
         lines_0 = lines(piece_0, near_0)
+        part = D // 4 // (tm * n_pos)
+        up_rows = lax.dynamic_slice(weight_in, ((t * n_pos + p) * part, 9 * D), (part, FF))
+        down_rows = lax.dynamic_slice(
+            weight_out.reshape(4, D // 4, D), (0, (t * n_pos + p) * part, 0), (4, part, D)
+        )
+        hidden = jnp.concatenate([up_rows, *down_rows], axis=1).astype(BF16)
+        hidden = lax.all_gather(once(hidden, near_0), EVERY, axis=0, tiled=True)
         peer_tokens = tm_permute(peer_tokens)
         piece_1 = half_of(*spans["ot"])
         piece_2 = jnp.concatenate([half_of(*spans[name]) for name in ("as", "os")], axis=1)
         first_0 = pack(lines_0, piece_1, peer_tokens)
         side_0, far_0 = sides(first_0)
-        down_quarters = jnp.concatenate(jnp.split(low_out, 4, axis=0), axis=1)
-        hidden_part = jnp.concatenate([low_in[:, 9 * D :], down_quarters], axis=1)
         piece_1 = once(piece_1, first_0)
         near_1 = next_plane(piece_1)
         pair_1 = pack([piece_1, near_1])
         far_pair_1 = far_plane(pair_1)
-        both_0 = second_side(once(side_0, own_tokens, scal, vec_low, piece_2, hidden_part, pair_1))
-        hidden = whole(hidden_part, first_0)
+        both_0 = second_side(once(side_0, own_tokens, scal, vec_low, piece_2, pair_1))
         group_0 = cores([first_0, side_0, far_0, both_0])
         first_1 = pack([near_1, far_pair_1], both_0)
         side_1, far_1 = sides(first_1)
@@ -1241,8 +1245,7 @@
         functools.partial(time_attn_back_kernel, slots), scal, [qkv_t, dy_t], [], [wide, vec_out], [], wait
     )
     if line:
-        group_a.pair(v_a)
-        group_s.side(group_a.send)
+        group_s.side(v_a)
     out_own, out_peer = call(join_kernel, scal, out, [], [sds((half, here, D), BF16)] * 2, [], (v_a,))
     wait = (group_s.send, out_own) if line else ()
     grad_own, grad_peer, g_at, g_att, g_vec, _ = call(
@@ -1263,23 +1266,22 @@
     if line:
         group_t = Group(scal, [(g_at, g_att), (g_vec, g_vec)])
         square = jnp.zeros((8, LANES), F32)
-        sum_a, square = group_a.total(square, 0, g_vec)
-        group_s.plane(sum_a)
+        group_a.pair(g_vec)
+        group_s.plane(group_a.send)
+        group_t.chip(group_s.send)
+        group_t.side()
+        sum_a, square = group_a.total(square, 0, group_t.send)
         sides_a = sides(sum_a)
-        group_t.chip(group_s.send)
-        group_s.pair(*sides_a, group_t.send)
-        group_t.side(group_s.send)
+        group_s.pair(sum_a)
+        group_t.plane(group_s.send)
+        sum_s, square = group_s.total(square, 0, group_t.send)
         parts_a = [sum_a, *sides_a, second_side(once(sides_a[0], group_t.send))]
-        sum_s, square = group_s.total(square, 0, *parts_a[3:])
-        group_t.plane(sum_s)
-        sides_s = sides(once(sum_s, group_t.send))
-        parts_a = cores(once(parts_a, group_t.send))
-        group_t.pair(*sides_s, *parts_a[4:])
-        parts_s = cores([sum_s, *sides_s, second_side(once(sides_s[0], group_t.send))])
-        parts = parts_a + parts_s
-        sum_t, square = group_t.total(square, LANES, *parts_s[4:])
+        group_t.pair(sum_s)
+        sides_s = sides(sum_s)
+        parts_s = [sum_s, *sides_s, second_side(once(sides_s[0], group_t.send))]
+        sum_t, square = group_t.total(square, LANES, *parts_a, *sides_s)
         parts_t = spread_plane(sum_t)
-        parts = parts + parts_t
+        parts = [*cores(parts_a), *cores(parts_s), *parts_t]
         out_peer, grad_peer = once(out_peer, parts_t[3]), once(grad_peer, parts_t[3])
     out_peer = tm_permute(out_peer)
     block_out = jnp.where(mine, out_own[None], out_peer[None])
@@ -1287,8 +1289,11 @@
     input_grad = jnp.where(mine, grad_own[None], grad_peer[None])
 
     if line:
-        for move in (next_plane, far_plane, first_side, second_side, other_core):
-            square = square + move(square)
+        square = square + next_plane(square)
+        square = square + far_plane(once(square, *parts_t[1:3]))
+        square = square + first_side(square)
+        square = square + second_side(once(square, parts_t[3]))
+        square = square + other_core(square)
         total_square = square[0, 0]
     else:
         g_in = jnp.concatenate([g_at, g_att, g_ot, g_ott, g_as, g_ast, g_os, g_ost, g_1, g_1t], axis=1)

time: 500 us -> 461 us (0.922)
  waiting for transfers between devices: 136 us -> 119 us
  local copies, waits for them, and re-layouts: 40.5 us -> 24 us
  other arithmetic: 10.3 us -> 4.85 us
    ppermute x73, waiting for transfers between devices: 99.2 us -> 80.8 us  [grid_permute(): return lax.ppermute(a, EVERY, pairs)]
    unnamed x162 -> x164, local copies, waits for them, and re-layouts: 26.3 us -> 16.4 us
    ppermute x4, waiting for transfers between devices: 0.23 us -> 8.01 us  [tm_permute(): return lax.ppermute(a, 'tm', [(i, n - 1 - i) for i in range(n)])]
    ppermute x12, waiting for transfers between devices: 36.3 us -> 30 us  [pos_permute(): return lax.ppermute(a, 'pos', [(i, i ^ r) for i in range(n)]) if r else a]
    convert_element_type x2 -> x1, other arithmetic: 6.58 us -> 0.38 us  [shards(): low_in, low_out = (weight_in.astype(BF16), weight_out.astype(BF16))]
  transfers between devices with their start and end apart: 90 -> 90, of which waited for: 38 -> 37; matrix products, arithmetic and copies ran while one was open for 6% -> 2% of each run, Pallas kernels for 31% -> 33%
where the time goes in v3:
time: 461 us; the launch traced here: 458 us
  Pallas kernels  202 us (44%)
  waiting for transfers between devices  119 us (26%)
  starting transfers between devices  90.2 us (20%)
  local copies, waits for them, and re-layouts  24 us (5%)
  between operations  17.8 us (4%)
  other arithmetic  4.85 us (1%)
    pallas_call x15, Pallas kernels, call(): pl.pallas_call(body, name=name, out_shape=tuple(outs), in_specs=[pl.Block...  166 us
    ppermute x73, waiting for transfers between devices, grid_permute(): return lax.ppermute(a, EVERY, pairs)  80.8 us
    ppermute x73, starting transfers between devices, grid_permute(): return lax.ppermute(a, EVERY, pairs)  77.6 us
    ppermute x12, waiting for transfers between devices, pos_permute(): return lax.ppermute(a, 'pos', [(i, i ^ r) for i in range(n)]) if r else a  30 us
    pallas_call x1, Pallas kernels, adam_all(): pl.pallas_call(functools.partial(adam_kernel, jobs, len(arrays), steps),...  21.3 us
    unnamed x164, local copies, waits for them, and re-layouts  16.4 us
    pallas_call x12, Pallas kernels, add_split(): pl.pallas_call(functools.partial(add_split_kernel, packs, len(after), sel...  11.8 us
  transfers between devices with their start and end apart: 90, of which 37 were waited for; matrix products, arithmetic and copies ran while one was open for 2% of the time, Pallas kernels for 33%

profile of v3, /device:TPU:0, one launch (start us, length us, event | category | flops | bytes accessed | tf_op | source)
XLA Modules:
  0.0 457.7 jit_solution(17324475066131596059)
XLA Ops:
  10.1 3.0 collective-permute-start.1
  15.2 1.5 collective-permute-done.1.refs_0_
  16.8 1.8 collective-permute-start
  18.6 3.6 collective-permute-start.2
  26.0 7.7 %collective-permute-done = bf16[8,49,768]{2,0,1:T(8,128)(2,1)S(1)} collective-permute-done((bf16[8,49,768]{2,0,1:T(8,128)(2,1)S(1)}, bf16[8,49,768]{2,0,1:T(8,128)(2,1)S(1)}, u32[]{:S(2)}, u32[]{:S(2)}) %collective-permute-start) | collective-permute-done | bytes 602144 | tf_op jit(solution)/shard_map/ppermute | solution.py:810
  35.4 1.6 collective-permute-start.4
  37.0 2.5 collective-permute-done.6.refs_1_.refs_0_
  39.6 4.7 %collective-permute-done.4.refs_4_.refs_13_ = bf16[3,48,1280]{2,1,0:T(8,128)(2,1)S(1)} collective-permute-done((bf16[3,48,1280]{2,1,0:T(8,128)(2,1)S(1)}, bf16[3,48,1280]{2,1,0:T(8,128)(2,1)S(1)}, u32[]{:S(2)}, u32[]{:S(2)}) %collective-permute-start.4) | collective-permute-done | bytes 368672 | tf_op jit(solution)/shard_map/ppermute | solution.py:820
  44.3 1.5 collective-permute-start.7
  45.8 2.5 collective-permute-start.12
  48.7 8.4 %collective-permute-done.12.refs_1_ = bf16[2,48,768]{2,1,0:T(8,128)(2,1)S(1)} collective-permute-done((bf16[2,48,768]{2,1,0:T(8,128)(2,1)S(1)}, bf16[2,48,768]{2,1,0:T(8,128)(2,1)S(1)}, u32[]{:S(2)}, u32[]{:S(2)}) %collective-permute-start.12) | collective-permute-done | bytes 147488 | tf_op jit(solution)/shard_map/ppermute | solution.py:820
  57.1 1.8 collective-permute-start.13
  60.5 5.4 %collective-permute-done.13.refs_1_.refs_0_ = bf16[48,1536]{1,0:T(8,128)(2,1)S(1)} collective-permute-done((bf16[48,1536]{1,0:T(8,128)(2,1)S(1)}, bf16[48,1536]{1,0:T(8,128)(2,1)S(1)}, u32[]{:S(2)}, u32[]{:S(2)}) %collective-permute-start.13) | collective-permute-done | bytes 147488 | tf_op jit(solution)/shard_map/ppermute | solution.py:820
  65.9 2.9 collective-permute-start.14
  69.2 2.8 collective-permute-start.15
  72.2 9.7 %time_in.1 = (bf16[784,768]{1,0:T(8,128)(2,1)S(1)}, bf16[784,768]{1,0:T(8,128)(2,1)S(1)}, bf16[784,2304]{1,0:T(8,128)(2,1)S(1)}, f32[24,768]{1,0:T(8,128)S(1)}) custom-call(s32[17]{0:T(128)S(1)} %stack.68.scal_ref.scal, bf16[8,49,768]{2,1,0:T(8,128)(2,1)S(1)} %bitcast.93, bf16[8,49,768]{2,1,0:T(8,128)(2,1)S(1)} %copy.48.refs_4_.refs_1_, ...), custom_call_target="tpu_custom_call" | custom-call | tf_op jit(solution)/shard_map/time_in/pallas_call | solution.py:232
  85.1 6.2 %time_attn.1.refs_0_.refs_4_ = bf16[784,768]{1,0:T(8,128)(2,1)S(1)} custom-call(s32[17]{0:T(128)S(1)} %stack.68.scal_ref.scal, bf16[784,2304]{1,0:T(8,128)(2,1)S(1)} %get-tuple-element.140.refs_0_, bf16[3,48,1536]{2,1,0:T(8,128)(2,1)S(1)} %pack.9.refs_1_.refs_6_.refs_4_.refs_7_, bf16[3,48,768]{2,1,0:T(8,128)(2,1)S(1)} %collective-permute-done.15.refs_2_.refs_5_.refs_8_), custom_call_target="tpu_custom_call" | custom-call | tf_op jit(solution)/shard_map/time_attn/pallas_call | solution.py:232
  91.3 2.6 collective-permute-done.16.refs_6_.refs_9_
  93.9 7.1 %collective-permute-done.17.refs_7_.refs_10_ = bf16[3,48,768]{2,1,0:T(8,128)(2,1)S(1)} collective-permute-done((bf16[3,48,768]{2,1,0:T(8,128)(2,1)S(1)}, bf16[3,48,768]{2,1,0:T(8,128)(2,1)S(1)}, u32[]{:S(2)}, u32[]{:S(2)}) %collective-permute-start.17) | collective-permute-done | bytes 221216 | tf_op jit(solution)/shard_map/ppermute | solution.py:820
  104.8 5.4 %time_mid.1 = (bf16[784,768]{1,0:T(8,128)(2,1)S(1)}, bf16[4,49,768]{2,1,0:T(8,128)(2,1)S(1)}, bf16[4,49,768]{2,1,0:T(8,128)(2,1)S(1)}, bf16[4,49,768]{2,1,0:T(8,128)(2,1)S(1)}, bf16[4,49,768]{2,1,0:T(8,128)(2,1)S(1)}) custom-call(s32[17]{0:T(128)S(1)} %stack.68.scal_ref.scal, bf16[784,768]{1,0:T(8,128)(2,1)S(1)} %time_attn.1.refs_0_.refs_4_, ...), custom_call_target="tpu_custom_call" | custom-call | tf_op jit(solution)/shard_map/time_mid/pallas_call | solution.py:232
  113.4 8.6 %collective-permute-done.24.refs_2_ = bf16[4,49,768]{2,1,0:T(8,128)(2,1)S(1)} collective-permute-done((bf16[4,49,768]{2,1,0:T(8,128)(2,1)S(1)}, bf16[4,49,768]{2,1,0:T(8,128)(2,1)S(1)}, u32[]{:S(2)}, u32[]{:S(2)}) %collective-permute-start.24) | collective-permute-done | bytes 301088 | tf_op jit(solution)/shard_map/ppermute | solution.py:805
  122.0 6.3 %collective-permute-done.25.refs_3_ = bf16[4,49,768]{2,1,0:T(8,128)(2,1)S(1)} collective-permute-done((bf16[4,49,768]{2,1,0:T(8,128)(2,1)S(1)}, bf16[4,49,768]{2,1,0:T(8,128)(2,1)S(1)}, u32[]{:S(2)}, u32[]{:S(2)}) %collective-permute-start.25) | collective-permute-done | bytes 301088 | tf_op jit(solution)/shard_map/ppermute | solution.py:805
  132.0 7.8 %space_in.1 = (bf16[784,768]{1,0:T(8,128)(2,1)S(1)}, bf16[784,768]{1,0:T(8,128)(2,1)S(1)}, bf16[784,2304]{1,0:T(8,128)(2,1)S(1)}) custom-call(s32[17]{0:T(128)S(1)} %stack.68.scal_ref.scal, bf16[4,49,768]{2,1,0:T(8,128)(2,1)S(1)} %get-tuple-element.149.refs_0_, bf16[4,49,768]{2,1,0:T(8,128)(2,1)S(1)} %collective-permute-done.23.refs_1_, ...), custom_call_target="tpu_custom_call" | custom-call | tf_op jit(solution)/shard_map/space_in/pallas_call | solution.py:232
  142.7 11.9 %space_mid.1 = (bf16[784,768]{1,0:T(8,128)(2,1)S(1)}, f32[784,768]{1,0:T(8,128)S(1)}, bf16[784,768]{1,0:T(8,128)(2,1)S(1)}) custom-call(s32[17]{0:T(128)S(1)} %stack.68.scal_ref.scal, bf16[784,2304]{1,0:T(8,128)(2,1)S(1)} %get-tuple-element.160.refs_0_, bf16[784,768]{1,0:T(8,128)(2,1)S(1)} %get-tuple-element.161.refs_1_.refs_2_, ...), custom_call_target="tpu_custom_call" | custom-call | tf_op jit(solution)/shard_map/space_mid/pallas_call | solution.py:232
  154.6 1.4 copy-done.35
  160.9 3.7 copy-done.6
  167.2 45.8 %mlp.1 = (f32[784,768]{1,0:T(8,128)S(1)}, f32[784,768]{1,0:T(8,128)S(1)}, bf16[768,1536]{1,0:T(8,128)(2,1)S(1)}, bf16[768,1536]{1,0:T(8,128)(2,1)S(1)}, bf16[768...) custom-call(s32[17]{0:T(128)S(1)} %stack.68.scal_ref.scal, ...), custom_call_target="tpu_custom_call" | custom-call | tf_op jit(solution)/shard_map/mlp/pallas_call | solution.py:232
  213.9 8.1 %mlp_out.1 = (f32[784,768]{1,0:T(8,128)S(1)}, bf16[784,768]{1,0:T(8,128)(2,1)S(1)}, bf16[768,384]{1,0:T(8,128)(2,1)S(1)}, bf16[768,384]{1,0:T(8,128)(2,1)S(1)}, ...) custom-call(s32[17]{0:T(128)S(1)} %stack.68.scal_ref.scal, ...), custom_call_target="tpu_custom_call" | custom-call | tf_op jit(solution)/shard_map/mlp_out/pallas_call | solution.py:232
  222.0 1.9 shard_map.219
  223.9 1.8 collective-permute-start.41
  225.7 16.5 %space_back.1 = (bf16[784,2304]{1,0:T(8,128)(2,1)S(1)}, f32[8,768]{1,0:T(8,128)S(1)}) custom-call(s32[17]{0:T(128)S(1)} %stack.68.scal_ref.scal, bf16[784,2304]{1,0:T(8,128)(2,1)S(1)} %copy-done.3, bf16[784,768]{1,0:T(8,128)(2,1)S(1)} %get-tuple-element.174.refs_1_, bf16[4,96,3072]{2,1,0:T(8,128)(2,1)S(1)} %get-tuple-element.180.refs_2_), custom_call_target="tpu_custom_call" | custom-call | tf_op jit(solution)/shard_map/space_back/pallas_call | solution.py:232
  242.3 13.7 %space_out.1 = (bf16[768,1152]{1,0:T(8,128)(2,1)S(1)}, bf16[768,1152]{1,0:T(8,128)(2,1)S(1)}, f32[8,768]{1,0:T(8,128)S(1)}, bf16[4,49,768]{2,1,0:T(8,128)(2,1)S(...) custom-call(s32[17]{0:T(128)S(1)} %stack.68.scal_ref.scal, ...), custom_call_target="tpu_custom_call" | custom-call | tf_op jit(solution)/shard_map/space_out/pallas_call | solution.py:232
  259.2 7.8 %collective-permute-done.39.refs_2_ = bf16[4,49,768]{2,1,0:T(8,128)(2,1)S(1)} collective-permute-done((bf16[4,49,768]{2,1,0:T(8,128)(2,1)S(1)}, bf16[4,49,768]{2,1,0:T(8,128)(2,1)S(1)}, u32[]{:S(2)}, u32[]{:S(2)}) %collective-permute-start.39) | collective-permute-done | bytes 301088 | tf_op jit(solution)/shard_map/ppermute | solution.py:805
  267.0 6.5 %collective-permute-done.40.refs_3_ = bf16[4,49,768]{2,1,0:T(8,128)(2,1)S(1)} collective-permute-done((bf16[4,49,768]{2,1,0:T(8,128)(2,1)S(1)}, bf16[4,49,768]{2,1,0:T(8,128)(2,1)S(1)}, u32[]{:S(2)}, u32[]{:S(2)}) %collective-permute-start.40) | collective-permute-done | bytes 301088 | tf_op jit(solution)/shard_map/ppermute | solution.py:805
  274.9 10.3 %time_proj.1 = (bf16[784,768]{1,0:T(8,128)(2,1)S(1)}, bf16[784,768]{1,0:T(8,128)(2,1)S(1)}, bf16[768,768]{1,0:T(8,128)(2,1)S(1)}, bf16[768,768]{1,0:T(8,128)(2,1)S(1)}, f32[8,768]{1,0:T(8,128)S(1)}) custom-call(s32[17]{0:T(128)S(1)} %stack.68.scal_ref.scal, bf16[4,49,768]{2,1,0:T(8,128)(2,1)S(1)} %get-tuple-element.183.refs_0_, ...), custom_call_target="tpu_custom_call" | custom-call | tf_op jit(solution)/shard_map/time_proj/pallas_call | solution.py:232
  286.6 4.3 collective-permute-done.48
  293.0 1.5 shard_map.222
  295.2 13.5 %time_attn_back.1 = (bf16[784,2304]{1,0:T(8,128)(2,1)S(1)}, f32[8,768]{1,0:T(8,128)S(1)}) custom-call(s32[17]{0:T(128)S(1)} %stack.68.scal_ref.scal, bf16[784,2304]{1,0:T(8,128)(2,1)S(1)} %copy-done.5, bf16[784,768]{1,0:T(8,128)(2,1)S(1)} %get-tuple-element.198.refs_1_, bf16[4,96,2304]{2,1,0:T(8,128)(2,1)S(1)} %get-tuple-element.208.refs_2_), custom_call_target="tpu_custom_call" | custom-call | tf_op jit(solution)/shard_map/time_attn_back/pallas_call | solution.py:232
  309.8 7.3 %collective-permute-done.49 = bf16[4,96,2304]{2,1,0:T(8,128)(2,1)S(1)} collective-permute-done((bf16[4,96,2304]{2,1,0:T(8,128)(2,1)S(1)}, bf16[4,96,2304]{2,1,0:T(8,128)(2,1)S(1)}, u32[]{:S(2)}, u32[]{:S(2)}) %collective-permute-start.49) | collective-permute-done | bytes 1769504 | tf_op jit(solution)/shard_map/ppermute | solution.py:820
  318.2 2.1 collective-permute-start.52
  320.4 14.5 %time_out.1 = (f32[8,49,768]{2,1,0:T(8,128)S(1)}, bf16[8,49,768]{2,1,0:T(8,128)(2,1)S(1)}, bf16[768,1152]{1,0:T(8,128)(2,1)S(1)}, bf16[768,1152]{1,0:T(8,128)(2,...) custom-call(s32[17]{0:T(128)S(1)} %stack.68.scal_ref.scal, bf16[784,2304]{1,0:T(8,128)(2,1)S(1)} %get-tuple-element.212.refs_0_, ...), custom_call_target="tpu_custom_call" | custom-call | tf_op jit(solution)/shard_map/time_out/pallas_call | solution.py:232
  334.9 7.1 %collective-permute-start.50 = (bf16[768,1152]{1,0:T(8,128)(2,1)S(1)}, bf16[768,1152]{1,0:T(8,128)(2,1)S(1)}, u32[]{:S(2)}, u32[]{:S(2)}) collective-permute-start(bf16[768,1152]{1,0:T(8,128)(2,1)S(1)} %get-tuple-element.220), channel_id=1, source_target_pairs={{0,1},{1,0},{2,3},{3,2},{4,5},{5,4},{6,7},{7,6},{8,9},{9,8},{10,11... | collective-permute-start | bytes 5308424 | tf_op jit(solution)/shard_map/ppermute | solution.py:820
  343.6 2.1 collective-permute-done.51
  347.4 3.3 collective-permute-start.57
  350.7 10.2 %collective-permute-done.54 = bf16[4,96,1280]{2,1,0:T(8,128)(2,1)S(1)} collective-permute-done((bf16[4,96,1280]{2,1,0:T(8,128)(2,1)S(1)}, bf16[4,96,1280]{2,1,0:T(8,128)(2,1)S(1)}, u32[]{:S(2)}, u32[]{:S(2)}) %collective-permute-start.54) | collective-permute-done | bytes 983072 | tf_op jit(solution)/shard_map/ppermute | solution.py:820
  362.9 6.7 %collective-permute-start.61 = (bf16[48,3072]{1,0:T(8,128)(2,1)S(1)}, bf16[48,3072]{1,0:T(8,128)(2,1)S(1)}, u32[]{:S(2)}, u32[]{:S(2)}) collective-permute-start(bf16[48,3072]{1,0:T(8,128)(2,1)S(1)} %get-tuple-element.231.refs_2_.refs_0_.refs_9_), channel_id=1, source_target_pairs={{0,4},{1,3},{2,6},{3,1},{4,0},{5,7},{6,2},{7,5},{8,12},{9,11},{10,... | collective-permute-start | bytes 884744 | tf_op jit(solution)/shard_map/ppermute | solution.py:820
  370.8 3.0 collective-permute-start.59
  375.5 4.0 collective-permute-done.59
  380.4 1.4 collective-permute-start.64
  382.1 1.8 collective-permute-start.63
  383.8 1.8 collective-permute-done.58
  386.3 3.0 collective-permute-start.60
  393.1 2.1 collective-permute-start.70
  395.1 1.6 collective-permute-done.70
  398.8 2.8 collective-permute-done.71.refs_27_
  402.3 2.3 collective-permute-start.72
  404.6 3.1 collective-permute-done.72
  407.7 1.8 collective-permute-start.73
  409.5 1.9 collective-permute-done.73
  413.3 2.3 collective-permute-done.74
  419.5 1.8 collective-permute-start.69
  421.7 3.2 copy-done.65
  424.9 21.3 %shard_map.234 = (f32[192,9984]{1,0:T(8,128)}, f32[192,9984]{1,0:T(8,128)}, f32[192,9984]{1,0:T(8,128)}, f32[768,768]{1,0:T(8,128)}, f32[768,768]{1,0:T(8,128)},...) custom-call(s32[17]{0:T(128)S(1)} %stack.68.scal_ref.scal, ...), custom_call_target="tpu_custom_call" | custom-call | flops 24999999488 | tf_op jit(solution)/shard_map/pallas_call | solution.py:1001
  446.3 1.7 broadcast_select_fusion
  (356 shorter events, 71.5 us)
Async XLA Ops:
  7.2 153.7 %all-gather.2.cloned.1.call-start = ((), (), s32[]{:S(2)}) async-start(), calls=%async_computation | async-start | bytes 9732096 | tf_op jit(solution)/shard_map/all_gather | solution.py:1104
  10.1 6.6 %collective-permute-start.1 = (bf16[48,1280]{1,0:T(8,128)(2,1)}, bf16[48,1280]{1,0:T(8,128)(2,1)S(1)}, u32[]{:S(2)}, u32[]{:S(2)}) collective-permute-start(bf16[48,1280]{1,0:T(8,128)(2,1)} %pad_maximum_fusion.1), channel_id=1, source_target_pairs={{0,8},{1,9},{2,10},{3,11},{4,12},{5,13},{6,14},{7,15},{8,0},{9,1},... | collective-permute-start | bytes 368648 | tf_op jit(solution)/shard_map/ppermute | solution.py:820
  16.8 16.9 %collective-permute-start = (bf16[8,49,768]{2,0,1:T(8,128)(2,1)S(1)}, bf16[8,49,768]{2,0,1:T(8,128)(2,1)S(1)}, u32[]{:S(2)}, u32[]{:S(2)}) collective-permute-start(bf16[8,49,768]{2,0,1:T(8,128)(2,1)S(1)} %get-tuple-element.265), channel_id=1, source_target_pairs={{0,4},{4,0},{1,5},{5,1},{2,6},{6,2},{3,7},{7,3},{8,12},{12,8},{9,1... | collective-permute-start | bytes 1806344 | tf_op jit(solution)/shard_map/ppermute | solution.py:810
  18.6 15.3 %collective-permute-start.2 = (bf16[48,1280]{1,0:T(8,128)(2,1)}, bf16[48,1280]{1,0:T(8,128)(2,1)S(1)}, u32[]{:S(2)}, u32[]{:S(2)}) collective-permute-start(bf16[48,1280]{1,0:T(8,128)(2,1)} %pad_maximum_fusion.1), channel_id=1, source_target_pairs={{0,24},{1,25},{2,26},{3,27},{4,28},{5,29},{6,30},{7,31},{8,16},{9,... | collective-permute-start | bytes 368648 | tf_op jit(solution)/shard_map/ppermute | solution.py:820
  25.7 8.7 %collective-permute-start.3 = (bf16[48,1280]{1,0:T(8,128)(2,1)S(1)}, bf16[48,1280]{1,0:T(8,128)(2,1)S(1)}, u32[]{:S(2)}, u32[]{:S(2)}) collective-permute-start(bf16[48,1280]{1,0:T(8,128)(2,1)S(1)} %collective-permute-done.1.refs_0_), channel_id=1, source_target_pairs={{0,24},{1,25},{2,26},{3,27},{4,28},{5,29},{6,30},{7,31},{8,16},{9,... | collective-permute-start | bytes 368648 | tf_op jit(solution)/shard_map/ppermute | solution.py:820
  35.4 8.9 %collective-permute-start.4 = (bf16[3,48,1280]{2,1,0:T(8,128)(2,1)S(1)}, bf16[3,48,1280]{2,1,0:T(8,128)(2,1)S(1)}, u32[]{:S(2)}, u32[]{:S(2)}) collective-permute-start(bf16[3,48,1280]{2,1,0:T(8,128)(2,1)S(1)} %pack.5.refs_3_.refs_12_), channel_id=1, source_target_pairs={{0,4},{1,3},{2,6},{3,1},{4,0},{5,7},{6,2},{7,5},{8,12},{9,11},{10,... | collective-permute-start | bytes 1105928 | tf_op jit(solution)/shard_map/ppermute | solution.py:820
  44.3 12.7 %collective-permute-start.7 = (bf16[3,48,1280]{2,1,0:T(8,128)(2,1)S(1)}, bf16[3,48,1280]{2,1,0:T(8,128)(2,1)S(1)}, u32[]{:S(2)}, u32[]{:S(2)}) collective-permute-start(bf16[3,48,1280]{2,1,0:T(8,128)(2,1)S(1)} %collective-permute-done.4.refs_4_.refs_13_), channel_id=1, source_target_pairs={{0,2},{1,5},{2,0},{3,7},{4,6},{5,1},{6,4},{7,3},{8,10},{9,13},{10,... | collective-permute-start | bytes 1105928 | tf_op jit(solution)/shard_map/ppermute | solution.py:820
  45.8 11.2 %collective-permute-start.12 = (bf16[2,48,768]{2,1,0:T(8,128)(2,1)S(1)}, bf16[2,48,768]{2,1,0:T(8,128)(2,1)S(1)}, u32[]{:S(2)}, u32[]{:S(2)}) collective-permute-start(bf16[2,48,768]{2,1,0:T(8,128)(2,1)S(1)} %pack.6), channel_id=1, source_target_pairs={{0,24},{1,25},{2,26},{3,27},{4,28},{5,29},{6,30},{7,31},{8,16},{9,... | collective-permute-start | bytes 442376 | tf_op jit(solution)/shard_map/ppermute | solution.py:820
  48.3 11.7 %collective-permute-start.5 = (bf16[3,48,1280]{2,1,0:T(8,128)(2,1)S(1)}, bf16[3,48,1280]{2,1,0:T(8,128)(2,1)S(1)}, u32[]{:S(2)}, u32[]{:S(2)}) collective-permute-start(bf16[3,48,1280]{2,1,0:T(8,128)(2,1)S(1)} %pack.5.refs_3_.refs_12_), channel_id=1, source_target_pairs={{0,2},{1,5},{2,0},{3,7},{4,6},{5,1},{6,4},{7,3},{8,10},{9,13},{10,... | collective-permute-start | bytes 1105928 | tf_op jit(solution)/shard_map/ppermute | solution.py:820
  57.1 8.8 %collective-permute-start.13 = (bf16[48,1536]{1,0:T(8,128)(2,1)S(1)}, bf16[48,1536]{1,0:T(8,128)(2,1)S(1)}, u32[]{:S(2)}, u32[]{:S(2)}) collective-permute-start(bf16[48,1536]{1,0:T(8,128)(2,1)S(1)} %pad_maximum_fusion.refs_0_), channel_id=1, source_target_pairs={{0,8},{1,9},{2,10},{3,11},{4,12},{5,13},{6,14},{7,15},{8,0},{9,1},... | collective-permute-start | bytes 442376 | tf_op jit(solution)/shard_map/ppermute | solution.py:820
  58.9 10.3 %collective-permute-start.8 = (bf16[3,48,1280]{2,1,0:T(8,128)(2,1)S(1)}, bf16[3,48,1280]{2,1,0:T(8,128)(2,1)S(1)}, u32[]{:S(2)}, u32[]{:S(2)}) collective-permute-start(bf16[3,48,1280]{2,1,0:T(8,128)(2,1)S(1)} %pack.5.refs_3_.refs_12_), channel_id=1, source_target_pairs={{0,1},{1,0},{2,3},{3,2},{4,5},{5,4},{6,7},{7,6},{8,9},{9,8},{10,11... | collective-permute-start | bytes 1105928 | tf_op jit(solution)/shard_map/ppermute | solution.py:820
  58.9 13.1 %collective-permute-start.9 = (bf16[3,48,1280]{2,1,0:T(8,128)(2,1)S(1)}, bf16[3,48,1280]{2,1,0:T(8,128)(2,1)S(1)}, u32[]{:S(2)}, u32[]{:S(2)}) collective-permute-start(bf16[3,48,1280]{2,1,0:T(8,128)(2,1)S(1)} %collective-permute-done.4.refs_4_.refs_13_), channel_id=1, source_target_pairs={{0,1},{1,0},{2,3},{3,2},{4,5},{5,4},{6,7},{7,6},{8,9},{9,8},{10,11... | collective-permute-start | bytes 1105928 | tf_op jit(solution)/shard_map/ppermute | solution.py:820
  60.0 12.1 %collective-permute-start.10 = (bf16[3,48,1280]{2,1,0:T(8,128)(2,1)S(1)}, bf16[3,48,1280]{2,1,0:T(8,128)(2,1)S(1)}, u32[]{:S(2)}, u32[]{:S(2)}) collective-permute-start(bf16[3,48,1280]{2,1,0:T(8,128)(2,1)S(1)} %collective-permute-done.5.refs_5_.refs_14_), channel_id=1, source_target_pairs={{0,1},{1,0},{2,3},{3,2},{4,5},{5,4},{6,7},{7,6},{8,9},{9,8},{10,11... | collective-permute-start | bytes 1105928 | tf_op jit(solution)/shard_map/ppermute | solution.py:820
  60.0 12.1 %collective-permute-start.11 = (bf16[3,48,1280]{2,1,0:T(8,128)(2,1)S(1)}, bf16[3,48,1280]{2,1,0:T(8,128)(2,1)S(1)}, u32[]{:S(2)}, u32[]{:S(2)}) collective-permute-start(bf16[3,48,1280]{2,1,0:T(8,128)(2,1)S(1)} %collective-permute-done.7.refs_2_.refs_6_.refs_15_), channel_id=1, source_target_pairs={{0,1},{1,0},{2,3},{3,2},{4,5},{5,4},{6,7},{7,6},{8,9},{9,8},{10,11... | collective-permute-start | bytes 1105928 | tf_op jit(solution)/shard_map/ppermute | solution.py:820
  65.9 16.1 %collective-permute-start.14 = (bf16[2,48,1536]{2,1,0:T(8,128)(2,1)S(1)}, bf16[2,48,1536]{2,1,0:T(8,128)(2,1)S(1)}, u32[]{:S(2)}, u32[]{:S(2)}) collective-permute-start(bf16[2,48,1536]{2,1,0:T(8,128)(2,1)S(1)} %pack.8.refs_21_), channel_id=1, source_target_pairs={{0,24},{1,25},{2,26},{3,27},{4,28},{5,29},{6,30},{7,31},{8,16},{9,... | collective-permute-start | bytes 884744 | tf_op jit(solution)/shard_map/ppermute | solution.py:820
  69.2 14.7 %collective-permute-start.15 = (bf16[3,48,768]{2,1,0:T(8,128)(2,1)S(1)}, bf16[3,48,768]{2,1,0:T(8,128)(2,1)S(1)}, u32[]{:S(2)}, u32[]{:S(2)}) collective-permute-start(bf16[3,48,768]{2,1,0:T(8,128)(2,1)S(1)} %pack.7.refs_2_.refs_20_.refs_4_.refs_7_), channel_id=1, source_target_pairs={{0,4},{1,3},{2,6},{3,1},{4,0},{5,7},{6,2},{7,5},{8,12},{9,11},{10,... | collective-permute-start | bytes 663560 | tf_op jit(solution)/shard_map/ppermute | solution.py:820
  83.0 20.0 %collective-permute-start.22 = (bf16[3,48,1536]{2,1,0:T(8,128)(2,1)S(1)}, bf16[3,48,1536]{2,1,0:T(8,128)(2,1)S(1)}, u32[]{:S(2)}, u32[]{:S(2)}) collective-permute-start(bf16[3,48,1536]{2,1,0:T(8,128)(2,1)S(1)} %pack.9.refs_1_.refs_6_.refs_4_.refs_7_), channel_id=1, source_target_pairs={{0,4},{1,3},{2,6},{3,1},{4,0},{5,7},{6,2},{7,5},{8,12},{9,11},{10,... | collective-permute-start | bytes 1327112 | tf_op jit(solution)/shard_map/ppermute | solution.py:820
  83.0 10.9 %collective-permute-start.16 = (bf16[3,48,768]{2,1,0:T(8,128)(2,1)S(1)}, bf16[3,48,768]{2,1,0:T(8,128)(2,1)S(1)}, u32[]{:S(2)}, u32[]{:S(2)}) collective-permute-start(bf16[3,48,768]{2,1,0:T(8,128)(2,1)S(1)} %pack.7.refs_2_.refs_20_.refs_4_.refs_7_), channel_id=1, source_target_pairs={{0,2},{1,5},{2,0},{3,7},{4,6},{5,1},{6,4},{7,3},{8,10},{9,13},{10,... | collective-permute-start | bytes 663560 | tf_op jit(solution)/shard_map/ppermute | solution.py:820
  83.9 17.1 %collective-permute-start.17 = (bf16[3,48,768]{2,1,0:T(8,128)(2,1)S(1)}, bf16[3,48,768]{2,1,0:T(8,128)(2,1)S(1)}, u32[]{:S(2)}, u32[]{:S(2)}) collective-permute-start(bf16[3,48,768]{2,1,0:T(8,128)(2,1)S(1)} %collective-permute-done.15.refs_2_.refs_5_.refs_8_), channel_id=1, source_target_pairs={{0,2},{1,5},{2,0},{3,7},{4,6},{5,1},{6,4},{7,3},{8,10},{9,13},{10,... | collective-permute-start | bytes 663560 | tf_op jit(solution)/shard_map/ppermute | solution.py:820
  101.0 11.3 %collective-permute-start.26 = (bf16[3,48,1536]{2,1,0:T(8,128)(2,1)S(1)}, bf16[3,48,1536]{2,1,0:T(8,128)(2,1)S(1)}, u32[]{:S(2)}, u32[]{:S(2)}) collective-permute-start(bf16[3,48,1536]{2,1,0:T(8,128)(2,1)S(1)} %pack.9.refs_1_.refs_6_.refs_4_.refs_7_), channel_id=1, source_target_pairs={{0,2},{1,5},{2,0},{3,7},{4,6},{5,1},{6,4},{7,3},{8,10},{9,13},{10,... | collective-permute-start | bytes 1327112 | tf_op jit(solution)/shard_map/ppermute | solution.py:820
  103.5 24.7 %collective-permute-start.27 = (bf16[3,48,1536]{2,1,0:T(8,128)(2,1)S(1)}, bf16[3,48,1536]{2,1,0:T(8,128)(2,1)S(1)}, u32[]{:S(2)}, u32[]{:S(2)}) collective-permute-start(bf16[3,48,1536]{2,1,0:T(8,128)(2,1)S(1)} %collective-permute-done.22.refs_12_.refs_7_.refs_5_.refs_8_), channel_id=1, source_target_pairs={{0,2},{1,5},{2,0},{3,7},{4,6},{5,1},{6,4},{7,3},{8,10},{9,13},{10,... | collective-permute-start | bytes 1327112 | tf_op jit(solution)/shard_map/ppermute | solution.py:820
  110.7 11.3 %collective-permute-start.24 = (bf16[4,49,768]{2,1,0:T(8,128)(2,1)S(1)}, bf16[4,49,768]{2,1,0:T(8,128)(2,1)S(1)}, u32[]{:S(2)}, u32[]{:S(2)}) collective-permute-start(bf16[4,49,768]{2,1,0:T(8,128)(2,1)S(1)} %get-tuple-element.151), channel_id=1, source_target_pairs={{0,2},{1,3},{2,0},{3,1},{4,6},{5,7},{6,4},{7,5},{8,10},{9,11},{10,... | collective-permute-start | bytes 903176 | tf_op jit(solution)/shard_map/ppermute | solution.py:805
  111.6 16.7 %collective-permute-start.25 = (bf16[4,49,768]{2,1,0:T(8,128)(2,1)S(1)}, bf16[4,49,768]{2,1,0:T(8,128)(2,1)S(1)}, u32[]{:S(2)}, u32[]{:S(2)}) collective-permute-start(bf16[4,49,768]{2,1,0:T(8,128)(2,1)S(1)} %get-tuple-element.152), channel_id=1, source_target_pairs={{0,3},{1,2},{2,1},{3,0},{4,7},{5,6},{6,5},{7,4},{8,11},{9,10},{10,... | collective-permute-start | bytes 903176 | tf_op jit(solution)/shard_map/ppermute | solution.py:805
  112.4 17.0 %collective-permute-start.32 = (bf16[8,49,768]{2,0,1:T(8,128)(2,1)S(1)}, bf16[8,49,768]{2,0,1:T(8,128)(2,1)S(1)}, u32[]{:S(2)}, u32[]{:S(2)}) collective-permute-start(bf16[8,49,768]{2,0,1:T(8,128)(2,1)S(1)} %get-tuple-element.159), channel_id=1, source_target_pairs={{0,4},{4,0},{1,5},{5,1},{2,6},{6,2},{3,7},{7,3},{8,12},{12,8},{9,1... | collective-permute-start | bytes 1806344 | tf_op jit(solution)/shard_map/ppermute | solution.py:810
  140.8 16.2 %collective-permute-start.33 = (bf16[4,49,768]{2,1,0:T(8,128)(2,1)S(1)}, bf16[4,49,768]{2,1,0:T(8,128)(2,1)S(1)}, u32[]{:S(2)}, u32[]{:S(2)}) collective-permute-start(bf16[4,49,768]{2,1,0:T(8,128)(2,1)S(1)} %get-tuple-element.166), channel_id=1, source_target_pairs={{0,1},{1,0},{2,3},{3,2},{4,5},{5,4},{6,7},{7,6},{8,9},{9,8},{10,11... | collective-permute-start | bytes 903176 | tf_op jit(solution)/shard_map/ppermute | solution.py:805
  141.2 15.8 %collective-permute-start.34 = (bf16[4,49,768]{2,1,0:T(8,128)(2,1)S(1)}, bf16[4,49,768]{2,1,0:T(8,128)(2,1)S(1)}, u32[]{:S(2)}, u32[]{:S(2)}) collective-permute-start(bf16[4,49,768]{2,1,0:T(8,128)(2,1)S(1)} %get-tuple-element.167), channel_id=1, source_target_pairs={{0,2},{1,3},{2,0},{3,1},{4,6},{5,7},{6,4},{7,5},{8,10},{9,11},{10,... | collective-permute-start | bytes 903176 | tf_op jit(solution)/shard_map/ppermute | solution.py:805
  142.1 15.8 %collective-permute-start.35 = (bf16[4,49,768]{2,1,0:T(8,128)(2,1)S(1)}, bf16[4,49,768]{2,1,0:T(8,128)(2,1)S(1)}, u32[]{:S(2)}, u32[]{:S(2)}) collective-permute-start(bf16[4,49,768]{2,1,0:T(8,128)(2,1)S(1)} %get-tuple-element.168), channel_id=1, source_target_pairs={{0,3},{1,2},{2,1},{3,0},{4,7},{5,6},{6,5},{7,4},{8,11},{9,10},{10,... | collective-permute-start | bytes 903176 | tf_op jit(solution)/shard_map/ppermute | solution.py:805
  213.1 8.9 %collective-permute-start.36 = (bf16[768,1536]{1,0:T(8,128)(2,1)S(1)}, bf16[768,1536]{1,0:T(8,128)(2,1)S(1)}, u32[]{:S(2)}, u32[]{:S(2)}) collective-permute-start(bf16[768,1536]{1,0:T(8,128)(2,1)S(1)} %get-tuple-element.177), channel_id=1, source_target_pairs={{0,1},{1,0},{2,3},{3,2},{4,5},{5,4},{6,7},{7,6},{8,9},{9,8},{10,11... | collective-permute-start | bytes 7077896 | tf_op jit(solution)/shard_map/ppermute | solution.py:820
  213.8 8.2 %collective-permute-start.37 = (bf16[768,1536]{1,0:T(8,128)(2,1)S(1)}, bf16[768,1536]{1,0:T(8,128)(2,1)S(1)}, u32[]{:S(2)}, u32[]{:S(2)}) collective-permute-start(bf16[768,1536]{1,0:T(8,128)(2,1)S(1)} %get-tuple-element.178), channel_id=1, source_target_pairs={{0,1},{1,0},{2,3},{3,2},{4,5},{5,4},{6,7},{7,6},{8,9},{9,8},{10,11... | collective-permute-start | bytes 7077896 | tf_op jit(solution)/shard_map/ppermute | solution.py:820
  223.9 34.0 %collective-permute-start.41 = (bf16[4,96,3072]{2,1,0:T(8,128)(2,1)S(1)}, bf16[4,96,3072]{2,1,0:T(8,128)(2,1)S(1)}, u32[]{:S(2)}, u32[]{:S(2)}) collective-permute-start(bf16[4,96,3072]{2,1,0:T(8,128)(2,1)S(1)} %get-tuple-element.180.refs_2_), channel_id=1, source_target_pairs={{0,4},{1,3},{2,6},{3,1},{4,0},{5,7},{6,2},{7,5},{8,12},{9,11},{10,... | collective-permute-start | bytes 7077896 | tf_op jit(solution)/shard_map/ppermute | solution.py:820
  256.1 10.9 %collective-permute-start.39 = (bf16[4,49,768]{2,1,0:T(8,128)(2,1)S(1)}, bf16[4,49,768]{2,1,0:T(8,128)(2,1)S(1)}, u32[]{:S(2)}, u32[]{:S(2)}) collective-permute-start(bf16[4,49,768]{2,1,0:T(8,128)(2,1)S(1)} %get-tuple-element.185), channel_id=1, source_target_pairs={{0,2},{1,3},{2,0},{3,1},{4,6},{5,7},{6,4},{7,5},{8,10},{9,11},{10,... | collective-permute-start | bytes 903176 | tf_op jit(solution)/shard_map/ppermute | solution.py:805
  257.0 16.4 %collective-permute-start.40 = (bf16[4,49,768]{2,1,0:T(8,128)(2,1)S(1)}, bf16[4,49,768]{2,1,0:T(8,128)(2,1)S(1)}, u32[]{:S(2)}, u32[]{:S(2)}) collective-permute-start(bf16[4,49,768]{2,1,0:T(8,128)(2,1)S(1)} %get-tuple-element.186), channel_id=1, source_target_pairs={{0,3},{1,2},{2,1},{3,0},{4,7},{5,6},{6,5},{7,4},{8,11},{9,10},{10,... | collective-permute-start | bytes 903176 | tf_op jit(solution)/shard_map/ppermute | solution.py:805
  273.5 17.4 %collective-permute-start.48 = (bf16[4,48,3072]{2,1,0:T(8,128)(2,1)S(1)}, bf16[4,48,3072]{2,1,0:T(8,128)(2,1)S(1)}, u32[]{:S(2)}, u32[]{:S(2)}) collective-permute-start(bf16[4,48,3072]{2,1,0:T(8,128)(2,1)S(1)} %get-tuple-element.206.refs_15_), channel_id=1, source_target_pairs={{0,2},{1,5},{2,0},{3,7},{4,6},{5,1},{6,4},{7,3},{8,10},{9,13},{10,... | collective-permute-start | bytes 3538952 | tf_op jit(solution)/shard_map/ppermute | solution.py:820
  274.4 18.0 %collective-permute-start.45 = (bf16[768,384]{1,0:T(8,128)(2,1)S(1)}, bf16[768,384]{1,0:T(8,128)(2,1)S(1)}, u32[]{:S(2)}, u32[]{:S(2)}) collective-permute-start(bf16[768,384]{1,0:T(8,128)(2,1)S(1)} %get-tuple-element.202), channel_id=1, source_target_pairs={{0,1},{1,0},{2,3},{3,2},{4,5},{5,4},{6,7},{7,6},{8,9},{9,8},{10,11... | collective-permute-start | bytes 1769480 | tf_op jit(solution)/shard_map/ppermute | solution.py:820
  274.4 18.1 %collective-permute-start.46 = (bf16[768,1152]{1,0:T(8,128)(2,1)S(1)}, bf16[768,1152]{1,0:T(8,128)(2,1)S(1)}, u32[]{:S(2)}, u32[]{:S(2)}) collective-permute-start(bf16[768,1152]{1,0:T(8,128)(2,1)S(1)} %get-tuple-element.203), channel_id=1, source_target_pairs={{0,1},{1,0},{2,3},{3,2},{4,5},{5,4},{6,7},{7,6},{8,9},{9,8},{10,11... | collective-permute-start | bytes 5308424 | tf_op jit(solution)/shard_map/ppermute | solution.py:820
  285.2 7.8 %collective-permute-start.47 = (bf16[768,768]{1,0:T(8,128)(2,1)S(1)}, bf16[768,768]{1,0:T(8,128)(2,1)S(1)}, u32[]{:S(2)}, u32[]{:S(2)}) collective-permute-start(bf16[768,768]{1,0:T(8,128)(2,1)S(1)} %get-tuple-element.204), channel_id=1, source_target_pairs={{0,1},{1,0},{2,3},{3,2},{4,5},{5,4},{6,7},{7,6},{8,9},{9,8},{10,11... | collective-permute-start | bytes 3538952 | tf_op jit(solution)/shard_map/ppermute | solution.py:820
  285.3 23.4 %collective-permute-start.44 = (bf16[4,49,768]{2,1,0:T(8,128)(2,1)S(1)}, bf16[4,49,768]{2,1,0:T(8,128)(2,1)S(1)}, u32[]{:S(2)}, u32[]{:S(2)}) collective-permute-start(bf16[4,49,768]{2,1,0:T(8,128)(2,1)S(1)} %get-tuple-element.197), channel_id=1, source_target_pairs={{0,3},{1,2},{2,1},{3,0},{4,7},{5,6},{6,5},{7,4},{8,11},{9,10},{10,... | collective-permute-start | bytes 903176 | tf_op jit(solution)/shard_map/ppermute | solution.py:805
  290.9 17.9 %collective-permute-start.43 = (bf16[4,49,768]{2,1,0:T(8,128)(2,1)S(1)}, bf16[4,49,768]{2,1,0:T(8,128)(2,1)S(1)}, u32[]{:S(2)}, u32[]{:S(2)}) collective-permute-start(bf16[4,49,768]{2,1,0:T(8,128)(2,1)S(1)} %get-tuple-element.195), channel_id=1, source_target_pairs={{0,2},{1,3},{2,0},{3,1},{4,6},{5,7},{6,4},{7,5},{8,10},{9,11},{10,... | collective-permute-start | bytes 903176 | tf_op jit(solution)/shard_map/ppermute | solution.py:805
  292.4 16.4 %collective-permute-start.42 = (bf16[4,49,768]{2,1,0:T(8,128)(2,1)S(1)}, bf16[4,49,768]{2,1,0:T(8,128)(2,1)S(1)}, u32[]{:S(2)}, u32[]{:S(2)}) collective-permute-start(bf16[4,49,768]{2,1,0:T(8,128)(2,1)S(1)} %get-tuple-element.193), channel_id=1, source_target_pairs={{0,1},{1,0},{2,3},{3,2},{4,5},{5,4},{6,7},{7,6},{8,9},{9,8},{10,11... | collective-permute-start | bytes 903176 | tf_op jit(solution)/shard_map/ppermute | solution.py:805
  292.5 49.6 %collective-permute-start.53 = (bf16[1,96,3072]{2,1,0:T(8,128)(2,1)S(1)}, bf16[1,96,3072]{2,1,0:T(8,128)(2,1)S(1)}, u32[]{:S(2)}, u32[]{:S(2)}) collective-permute-start(bf16[1,96,3072]{2,1,0:T(8,128)(2,1)S(1)} %get-tuple-element.207.refs_6_), channel_id=1, source_target_pairs={{0,24},{1,25},{2,26},{3,27},{4,28},{5,29},{6,30},{7,31},{8,16},{9,... | collective-permute-start | bytes 1769480 | tf_op jit(solution)/shard_map/ppermute | solution.py:820
  294.5 22.6 %collective-permute-start.49 = (bf16[4,96,2304]{2,1,0:T(8,128)(2,1)S(1)}, bf16[4,96,2304]{2,1,0:T(8,128)(2,1)S(1)}, u32[]{:S(2)}, u32[]{:S(2)}) collective-permute-start(bf16[4,96,2304]{2,1,0:T(8,128)(2,1)S(1)} %get-tuple-element.208.refs_2_), channel_id=1, source_target_pairs={{0,4},{1,3},{2,6},{3,1},{4,0},{5,7},{6,2},{7,5},{8,12},{9,11},{10,... | collective-permute-start | bytes 5308424 | tf_op jit(solution)/shard_map/ppermute | solution.py:820
  318.2 24.6 %collective-permute-start.52 = (bf16[4,48,2304]{2,1,0:T(8,128)(2,1)S(1)}, bf16[4,48,2304]{2,1,0:T(8,128)(2,1)S(1)}, u32[]{:S(2)}, u32[]{:S(2)}) collective-permute-start(bf16[4,48,2304]{2,1,0:T(8,128)(2,1)S(1)} %get-tuple-element.217.refs_20_), channel_id=1, source_target_pairs={{0,2},{1,5},{2,0},{3,7},{4,6},{5,1},{6,4},{7,3},{8,10},{9,13},{10,... | collective-permute-start | bytes 2654216 | tf_op jit(solution)/shard_map/ppermute | solution.py:820
  334.9 10.7 %collective-permute-start.50 = (bf16[768,1152]{1,0:T(8,128)(2,1)S(1)}, bf16[768,1152]{1,0:T(8,128)(2,1)S(1)}, u32[]{:S(2)}, u32[]{:S(2)}) collective-permute-start(bf16[768,1152]{1,0:T(8,128)(2,1)S(1)} %get-tuple-element.220), channel_id=1, source_target_pairs={{0,1},{1,0},{2,3},{3,2},{4,5},{5,4},{6,7},{7,6},{8,9},{9,8},{10,11... | collective-permute-start | bytes 5308424 | tf_op jit(solution)/shard_map/ppermute | solution.py:820
  346.8 14.2 %collective-permute-start.54 = (bf16[4,96,1280]{2,1,0:T(8,128)(2,1)S(1)}, bf16[4,96,1280]{2,1,0:T(8,128)(2,1)S(1)}, u32[]{:S(2)}, u32[]{:S(2)}) collective-permute-start(bf16[4,96,1280]{2,1,0:T(8,128)(2,1)S(1)} %get-tuple-element.226), channel_id=1, source_target_pairs={{0,4},{1,3},{2,6},{3,1},{4,0},{5,7},{6,2},{7,5},{8,12},{9,11},{10,... | collective-permute-start | bytes 2949128 | tf_op jit(solution)/shard_map/ppermute | solution.py:820
  347.4 14.5 %collective-permute-start.57 = (bf16[1,48,3072]{2,1,0:T(8,128)(2,1)S(1)}, bf16[1,48,3072]{2,1,0:T(8,128)(2,1)S(1)}, u32[]{:S(2)}, u32[]{:S(2)}) collective-permute-start(bf16[1,48,3072]{2,1,0:T(8,128)(2,1)S(1)} %get-tuple-element.223.refs_2_), channel_id=1, source_target_pairs={{0,8},{1,9},{2,10},{3,11},{4,12},{5,13},{6,14},{7,15},{8,0},{9,1},... | collective-permute-start | bytes 884744 | tf_op jit(solution)/shard_map/ppermute | solution.py:820
  350.7 19.4 %collective-permute-start.56 = (bf16[1,96,2304]{2,1,0:T(8,128)(2,1)S(1)}, bf16[1,96,2304]{2,1,0:T(8,128)(2,1)S(1)}, u32[]{:S(2)}, u32[]{:S(2)}) collective-permute-start(bf16[1,96,2304]{2,1,0:T(8,128)(2,1)S(1)} %get-tuple-element.224.refs_4_), channel_id=1, source_target_pairs={{0,24},{1,25},{2,26},{3,27},{4,28},{5,29},{6,30},{7,31},{8,16},{9,... | collective-permute-start | bytes 1327112 | tf_op jit(solution)/shard_map/ppermute | solution.py:820
  361.8 11.9 %collective-permute-start.55 = (bf16[4,48,1280]{2,1,0:T(8,128)(2,1)S(1)}, bf16[4,48,1280]{2,1,0:T(8,128)(2,1)S(1)}, u32[]{:S(2)}, u32[]{:S(2)}) collective-permute-start(bf16[4,48,1280]{2,1,0:T(8,128)(2,1)S(1)} %get-tuple-element.228.refs_0_), channel_id=1, source_target_pairs={{0,2},{1,5},{2,0},{3,7},{4,6},{5,1},{6,4},{7,3},{8,10},{9,13},{10,... | collective-permute-start | bytes 1474568 | tf_op jit(solution)/shard_map/ppermute | solution.py:820
  362.9 19.2 %collective-permute-start.61 = (bf16[48,3072]{1,0:T(8,128)(2,1)S(1)}, bf16[48,3072]{1,0:T(8,128)(2,1)S(1)}, u32[]{:S(2)}, u32[]{:S(2)}) collective-permute-start(bf16[48,3072]{1,0:T(8,128)(2,1)S(1)} %get-tuple-element.231.refs_2_.refs_0_.refs_9_), channel_id=1, source_target_pairs={{0,4},{1,3},{2,6},{3,1},{4,0},{5,7},{6,2},{7,5},{8,12},{9,11},{10,... | collective-permute-start | bytes 884744 | tf_op jit(solution)/shard_map/ppermute | solution.py:820
  369.6 19.6 %collective-permute-start.62 = (bf16[48,3072]{1,0:T(8,128)(2,1)S(1)}, bf16[48,3072]{1,0:T(8,128)(2,1)S(1)}, u32[]{:S(2)}, u32[]{:S(2)}) collective-permute-start(bf16[48,3072]{1,0:T(8,128)(2,1)S(1)} %get-tuple-element.231.refs_2_.refs_0_.refs_9_), channel_id=1, source_target_pairs={{0,2},{1,5},{2,0},{3,7},{4,6},{5,1},{6,4},{7,3},{8,10},{9,13},{10,... | collective-permute-start | bytes 884744 | tf_op jit(solution)/shard_map/ppermute | solution.py:820
  370.8 8.8 %collective-permute-start.59 = (bf16[1,48,2304]{2,1,0:T(8,128)(2,1)S(1)}, bf16[1,48,2304]{2,1,0:T(8,128)(2,1)S(1)}, u32[]{:S(2)}, u32[]{:S(2)}) collective-permute-start(bf16[1,48,2304]{2,1,0:T(8,128)(2,1)S(1)} %get-tuple-element.232.refs_2_), channel_id=1, source_target_pairs={{0,8},{1,9},{2,10},{3,11},{4,12},{5,13},{6,14},{7,15},{8,0},{9,1},... | collective-permute-start | bytes 663560 | tf_op jit(solution)/shard_map/ppermute | solution.py:820
  374.4 11.3 %collective-permute-start.58 = (bf16[1,96,1280]{2,1,0:T(8,128)(2,1)S(1)}, bf16[1,96,1280]{2,1,0:T(8,128)(2,1)S(1)}, u32[]{:S(2)}, u32[]{:S(2)}) collective-permute-start(bf16[1,96,1280]{2,1,0:T(8,128)(2,1)S(1)} %get-tuple-element.234.refs_0_), channel_id=1, source_target_pairs={{0,24},{1,25},{2,26},{3,27},{4,28},{5,29},{6,30},{7,31},{8,16},{9,... | collective-permute-start | bytes 737288 | tf_op jit(solution)/shard_map/ppermute | solution.py:820
  380.4 8.9 %collective-permute-start.64 = (bf16[48,2304]{1,0:T(8,128)(2,1)S(1)}, bf16[48,2304]{1,0:T(8,128)(2,1)S(1)}, u32[]{:S(2)}, u32[]{:S(2)}) collective-permute-start(bf16[48,2304]{1,0:T(8,128)(2,1)S(1)} %get-tuple-element.237.refs_2_.refs_17_), channel_id=1, source_target_pairs={{0,4},{1,3},{2,6},{3,1},{4,0},{5,7},{6,2},{7,5},{8,12},{9,11},{10,... | collective-permute-start | bytes 663560 | tf_op jit(solution)/shard_map/ppermute | solution.py:820
  381.8 8.0 %collective-permute-start.65 = (bf16[48,2304]{1,0:T(8,128)(2,1)S(1)}, bf16[48,2304]{1,0:T(8,128)(2,1)S(1)}, u32[]{:S(2)}, u32[]{:S(2)}) collective-permute-start(bf16[48,2304]{1,0:T(8,128)(2,1)S(1)} %get-tuple-element.237.refs_2_.refs_17_), channel_id=1, source_target_pairs={{0,2},{1,5},{2,0},{3,7},{4,6},{5,1},{6,4},{7,3},{8,10},{9,13},{10,... | collective-permute-start | bytes 663560 | tf_op jit(solution)/shard_map/ppermute | solution.py:820
  382.1 8.8 %collective-permute-start.63 = (bf16[48,3072]{1,0:T(8,128)(2,1)S(1)}, bf16[48,3072]{1,0:T(8,128)(2,1)S(1)}, u32[]{:S(2)}, u32[]{:S(2)}) collective-permute-start(bf16[48,3072]{1,0:T(8,128)(2,1)S(1)} %collective-permute-done.61.refs_1_.refs_10_), channel_id=1, source_target_pairs={{0,2},{1,5},{2,0},{3,7},{4,6},{5,1},{6,4},{7,3},{8,10},{9,13},{10,... | collective-permute-start | bytes 884744 | tf_op jit(solution)/shard_map/ppermute | solution.py:820
  389.3 13.0 %collective-permute-start.77 = (bf16[48,3072]{1,0:T(8,128)(2,1)S(1)}, bf16[48,3072]{1,0:T(8,128)(2,1)S(1)}, u32[]{:S(2)}, u32[]{:S(2)}) collective-permute-start(bf16[48,3072]{1,0:T(8,128)(2,1)S(1)} %collective-permute-done.61.refs_1_.refs_10_), channel_id=1, source_target_pairs={{0,1},{1,0},{2,3},{3,2},{4,5},{5,4},{6,7},{7,6},{8,9},{9,8},{10,11... | collective-permute-start | bytes 884744 | tf_op jit(solution)/shard_map/ppermute | solution.py:820
  389.8 14.8 %collective-permute-start.78 = (bf16[48,3072]{1,0:T(8,128)(2,1)S(1)}, bf16[48,3072]{1,0:T(8,128)(2,1)S(1)}, u32[]{:S(2)}, u32[]{:S(2)}) collective-permute-start(bf16[48,3072]{1,0:T(8,128)(2,1)S(1)} %collective-permute-done.62.refs_2_.refs_11_), channel_id=1, source_target_pairs={{0,1},{1,0},{2,3},{3,2},{4,5},{5,4},{6,7},{7,6},{8,9},{9,8},{10,11... | collective-permute-start | bytes 884744 | tf_op jit(solution)/shard_map/ppermute | solution.py:820
  393.0 14.7 %collective-permute-start.81 = (bf16[48,2304]{1,0:T(8,128)(2,1)S(1)}, bf16[48,2304]{1,0:T(8,128)(2,1)S(1)}, u32[]{:S(2)}, u32[]{:S(2)}) collective-permute-start(bf16[48,2304]{1,0:T(8,128)(2,1)S(1)} %get-tuple-element.237.refs_2_.refs_17_), channel_id=1, source_target_pairs={{0,1},{1,0},{2,3},{3,2},{4,5},{5,4},{6,7},{7,6},{8,9},{9,8},{10,11... | collective-permute-start | bytes 663560 | tf_op jit(solution)/shard_map/ppermute | solution.py:820
  397.8 14.1 %collective-permute-start.80 = (bf16[48,2304]{1,0:T(8,128)(2,1)S(1)}, bf16[48,2304]{1,0:T(8,128)(2,1)S(1)}, u32[]{:S(2)}, u32[]{:S(2)}) collective-permute-start(bf16[48,2304]{1,0:T(8,128)(2,1)S(1)} %collective-permute-done.64.refs_4_.refs_18_), channel_id=1, source_target_pairs={{0,2},{1,5},{2,0},{3,7},{4,6},{5,1},{6,4},{7,3},{8,10},{9,13},{10,... | collective-permute-start | bytes 663560 | tf_op jit(solution)/shard_map/ppermute | solution.py:820
  401.6 9.8 %collective-permute-start.67 = (bf16[48,1280]{1,0:T(8,128)(2,1)S(1)}, bf16[48,1280]{1,0:T(8,128)(2,1)S(1)}, u32[]{:S(2)}, u32[]{:S(2)}) collective-permute-start(bf16[48,1280]{1,0:T(8,128)(2,1)S(1)} %collective-permute-done.66.refs_26_), channel_id=1, source_target_pairs={{0,2},{1,5},{2,0},{3,7},{4,6},{5,1},{6,4},{7,3},{8,10},{9,13},{10,... | collective-permute-start | bytes 368648 | tf_op jit(solution)/shard_map/ppermute | solution.py:820
  404.6 11.0 %collective-permute-start.82 = (bf16[48,2304]{1,0:T(8,128)(2,1)S(1)}, bf16[48,2304]{1,0:T(8,128)(2,1)S(1)}, u32[]{:S(2)}, u32[]{:S(2)}) collective-permute-start(bf16[48,2304]{1,0:T(8,128)(2,1)S(1)} %collective-permute-done.64.refs_4_.refs_18_), channel_id=1, source_target_pairs={{0,1},{1,0},{2,3},{3,2},{4,5},{5,4},{6,7},{7,6},{8,9},{9,8},{10,11... | collective-permute-start | bytes 663560 | tf_op jit(solution)/shard_map/ppermute | solution.py:820
  407.7 8.3 %collective-permute-start.83 = (bf16[48,2304]{1,0:T(8,128)(2,1)S(1)}, bf16[48,2304]{1,0:T(8,128)(2,1)S(1)}, u32[]{:S(2)}, u32[]{:S(2)}) collective-permute-start(bf16[48,2304]{1,0:T(8,128)(2,1)S(1)} %collective-permute-done.65.refs_5_.refs_19_), channel_id=1, source_target_pairs={{0,1},{1,0},{2,3},{3,2},{4,5},{5,4},{6,7},{7,6},{8,9},{9,8},{10,11... | collective-permute-start | bytes 663560 | tf_op jit(solution)/shard_map/ppermute | solution.py:820
  411.4 8.1 %collective-permute-start.79 = (bf16[48,3072]{1,0:T(8,128)(2,1)S(1)}, bf16[48,3072]{1,0:T(8,128)(2,1)S(1)}, u32[]{:S(2)}, u32[]{:S(2)}) collective-permute-start(bf16[48,3072]{1,0:T(8,128)(2,1)S(1)} %collective-permute-done.63.refs_3_.refs_12_), channel_id=1, source_target_pairs={{0,1},{1,0},{2,3},{3,2},{4,5},{5,4},{6,7},{7,6},{8,9},{9,8},{10,11... | collective-permute-start | bytes 884744 | tf_op jit(solution)/shard_map/ppermute | solution.py:820
  419.5 26.7 %collective-permute-start.69 = (bf16[8,49,768]{2,0,1:T(8,128)(2,1)S(1)}, bf16[8,49,768]{2,0,1:T(8,128)(2,1)S(1)}, u32[]{:S(2)}, u32[]{:S(2)}) collective-permute-start(bf16[8,49,768]{2,0,1:T(8,128)(2,1)S(1)} %copy.55), channel_id=1, source_target_pairs={{0,4},{4,0},{1,5},{5,1},{2,6},{6,2},{3,7},{7,3},{8,12},{12,8},{9,1... | collective-permute-start | bytes 1806344 | tf_op jit(solution)/shard_map/ppermute | solution.py:810
  421.3 27.0 %collective-permute-start.68 = (bf16[8,49,768]{2,0,1:T(8,128)(2,1)S(1)}, bf16[8,49,768]{2,0,1:T(8,128)(2,1)S(1)}, u32[]{:S(2)}, u32[]{:S(2)}) collective-permute-start(bf16[8,49,768]{2,0,1:T(8,128)(2,1)S(1)} %copy.53), channel_id=1, source_target_pairs={{0,4},{4,0},{1,5},{5,1},{2,6},{6,2},{3,7},{7,3},{8,12},{12,8},{9,1... | collective-permute-start | bytes 1806344 | tf_op jit(solution)/shard_map/ppermute | solution.py:810
  (106 other events, 1289.7 us)
Sparse Core Ops, SparseCore 0:
  16.8 103.6 all-gather.1

commit v4 on v3

--- a/solution.py
+++ b/solution.py
@@ -1290,8 +1290,8 @@
 
     if line:
         square = square + next_plane(square)
-        square = square + far_plane(once(square, *parts_t[1:3]))
-        square = square + first_side(square)
+        square = square + far_plane(square)
+        square = square + first_side(once(square, *parts_t[1:3]))
         square = square + second_side(once(square, parts_t[3]))
         square = square + other_core(square)
         total_square = square[0, 0]

time: 461 us -> 459 us (level)
  transfers between devices with their start and end apart: 90 -> 90, of which waited for: 37 -> 35; matrix products, arithmetic and copies ran while one was open for 2% -> 2% of each run, Pallas kernels for 33% -> 34%
where the time goes in v4:
time: 459 us; the launch traced here: 455 us
  Pallas kernels  202 us (44%)
  waiting for transfers between devices  116 us (25%)
  starting transfers between devices  90.9 us (20%)
  local copies, waits for them, and re-layouts  24 us (5%)
  between operations  17.8 us (4%)
  other arithmetic  4.85 us (1%)
    pallas_call x15, Pallas kernels, call(): pl.pallas_call(body, name=name, out_shape=tuple(outs), in_specs=[pl.Block...  166 us
    ppermute x73, starting transfers between devices, grid_permute(): return lax.ppermute(a, EVERY, pairs)  78.3 us
    ppermute x73, waiting for transfers between devices, grid_permute(): return lax.ppermute(a, EVERY, pairs)  77.7 us
    ppermute x12, waiting for transfers between devices, pos_permute(): return lax.ppermute(a, 'pos', [(i, i ^ r) for i in range(n)]) if r else a  30 us
    pallas_call x1, Pallas kernels, adam_all(): pl.pallas_call(functools.partial(adam_kernel, jobs, len(arrays), steps),...  21.3 us
    unnamed x164, local copies, waits for them, and re-layouts  16.4 us
    pallas_call x12, Pallas kernels, add_split(): pl.pallas_call(functools.partial(add_split_kernel, packs, len(after), sel...  11.8 us
  transfers between devices with their start and end apart: 90, of which 35 were waited for; matrix products, arithmetic and copies ran while one was open for 2% of the time, Pallas kernels for 34%

profile of v4, /device:TPU:0, one launch (start us, length us, event | category | flops | bytes accessed | tf_op | source)
XLA Modules:
  0.0 455.3 jit_solution(4926306825424323788)
XLA Ops:
  10.1 3.0 collective-permute-start.1
  15.2 1.5 collective-permute-done.1.refs_0_
  16.8 1.8 collective-permute-start
  18.6 3.6 collective-permute-start.2
  26.0 7.7 %collective-permute-done = bf16[8,49,768]{2,0,1:T(8,128)(2,1)S(1)} collective-permute-done((bf16[8,49,768]{2,0,1:T(8,128)(2,1)S(1)}, bf16[8,49,768]{2,0,1:T(8,128)(2,1)S(1)}, u32[]{:S(2)}, u32[]{:S(2)}) %collective-permute-start) | collective-permute-done | bytes 602144 | tf_op jit(solution)/shard_map/ppermute | solution.py:810
  35.4 1.6 collective-permute-start.4
  37.0 2.5 collective-permute-done.6.refs_1_.refs_0_
  39.6 4.7 %collective-permute-done.4.refs_4_.refs_13_ = bf16[3,48,1280]{2,1,0:T(8,128)(2,1)S(1)} collective-permute-done((bf16[3,48,1280]{2,1,0:T(8,128)(2,1)S(1)}, bf16[3,48,1280]{2,1,0:T(8,128)(2,1)S(1)}, u32[]{:S(2)}, u32[]{:S(2)}) %collective-permute-start.4) | collective-permute-done | bytes 368672 | tf_op jit(solution)/shard_map/ppermute | solution.py:820
  44.3 1.5 collective-permute-start.7
  45.8 2.5 collective-permute-start.12
  48.7 8.4 %collective-permute-done.12.refs_1_ = bf16[2,48,768]{2,1,0:T(8,128)(2,1)S(1)} collective-permute-done((bf16[2,48,768]{2,1,0:T(8,128)(2,1)S(1)}, bf16[2,48,768]{2,1,0:T(8,128)(2,1)S(1)}, u32[]{:S(2)}, u32[]{:S(2)}) %collective-permute-start.12) | collective-permute-done | bytes 147488 | tf_op jit(solution)/shard_map/ppermute | solution.py:820
  57.1 1.8 collective-permute-start.13
  60.5 5.4 %collective-permute-done.13.refs_1_.refs_0_ = bf16[48,1536]{1,0:T(8,128)(2,1)S(1)} collective-permute-done((bf16[48,1536]{1,0:T(8,128)(2,1)S(1)}, bf16[48,1536]{1,0:T(8,128)(2,1)S(1)}, u32[]{:S(2)}, u32[]{:S(2)}) %collective-permute-start.13) | collective-permute-done | bytes 147488 | tf_op jit(solution)/shard_map/ppermute | solution.py:820
  65.9 2.9 collective-permute-start.14
  69.2 2.8 collective-permute-start.15
  72.2 9.7 %time_in.1 = (bf16[784,768]{1,0:T(8,128)(2,1)S(1)}, bf16[784,768]{1,0:T(8,128)(2,1)S(1)}, bf16[784,2304]{1,0:T(8,128)(2,1)S(1)}, f32[24,768]{1,0:T(8,128)S(1)}) custom-call(s32[17]{0:T(128)S(1)} %stack.68.scal_ref.scal, bf16[8,49,768]{2,1,0:T(8,128)(2,1)S(1)} %bitcast.93, bf16[8,49,768]{2,1,0:T(8,128)(2,1)S(1)} %copy.48.refs_4_.refs_1_, ...), custom_call_target="tpu_custom_call" | custom-call | tf_op jit(solution)/shard_map/time_in/pallas_call | solution.py:232
  85.1 6.2 %time_attn.1.refs_0_.refs_4_ = bf16[784,768]{1,0:T(8,128)(2,1)S(1)} custom-call(s32[17]{0:T(128)S(1)} %stack.68.scal_ref.scal, bf16[784,2304]{1,0:T(8,128)(2,1)S(1)} %get-tuple-element.140.refs_0_, bf16[3,48,1536]{2,1,0:T(8,128)(2,1)S(1)} %pack.9.refs_1_.refs_6_.refs_4_.refs_7_, bf16[3,48,768]{2,1,0:T(8,128)(2,1)S(1)} %collective-permute-done.15.refs_2_.refs_5_.refs_8_), custom_call_target="tpu_custom_call" | custom-call | tf_op jit(solution)/shard_map/time_attn/pallas_call | solution.py:232
  91.3 2.6 collective-permute-done.16.refs_6_.refs_9_
  93.9 7.1 %collective-permute-done.17.refs_7_.refs_10_ = bf16[3,48,768]{2,1,0:T(8,128)(2,1)S(1)} collective-permute-done((bf16[3,48,768]{2,1,0:T(8,128)(2,1)S(1)}, bf16[3,48,768]{2,1,0:T(8,128)(2,1)S(1)}, u32[]{:S(2)}, u32[]{:S(2)}) %collective-permute-start.17) | collective-permute-done | bytes 221216 | tf_op jit(solution)/shard_map/ppermute | solution.py:820
  101.7 1.3 collective-permute-start.19
  104.8 5.4 %time_mid.1 = (bf16[784,768]{1,0:T(8,128)(2,1)S(1)}, bf16[4,49,768]{2,1,0:T(8,128)(2,1)S(1)}, bf16[4,49,768]{2,1,0:T(8,128)(2,1)S(1)}, bf16[4,49,768]{2,1,0:T(8,128)(2,1)S(1)}, bf16[4,49,768]{2,1,0:T(8,128)(2,1)S(1)}) custom-call(s32[17]{0:T(128)S(1)} %stack.68.scal_ref.scal, bf16[784,768]{1,0:T(8,128)(2,1)S(1)} %time_attn.1.refs_0_.refs_4_, ...), custom_call_target="tpu_custom_call" | custom-call | tf_op jit(solution)/shard_map/time_mid/pallas_call | solution.py:232
  113.4 8.6 %collective-permute-done.24.refs_2_ = bf16[4,49,768]{2,1,0:T(8,128)(2,1)S(1)} collective-permute-done((bf16[4,49,768]{2,1,0:T(8,128)(2,1)S(1)}, bf16[4,49,768]{2,1,0:T(8,128)(2,1)S(1)}, u32[]{:S(2)}, u32[]{:S(2)}) %collective-permute-start.24) | collective-permute-done | bytes 301088 | tf_op jit(solution)/shard_map/ppermute | solution.py:805
  122.0 6.3 %collective-permute-done.25.refs_3_ = bf16[4,49,768]{2,1,0:T(8,128)(2,1)S(1)} collective-permute-done((bf16[4,49,768]{2,1,0:T(8,128)(2,1)S(1)}, bf16[4,49,768]{2,1,0:T(8,128)(2,1)S(1)}, u32[]{:S(2)}, u32[]{:S(2)}) %collective-permute-start.25) | collective-permute-done | bytes 301088 | tf_op jit(solution)/shard_map/ppermute | solution.py:805
  132.0 7.8 %space_in.1 = (bf16[784,768]{1,0:T(8,128)(2,1)S(1)}, bf16[784,768]{1,0:T(8,128)(2,1)S(1)}, bf16[784,2304]{1,0:T(8,128)(2,1)S(1)}) custom-call(s32[17]{0:T(128)S(1)} %stack.68.scal_ref.scal, bf16[4,49,768]{2,1,0:T(8,128)(2,1)S(1)} %get-tuple-element.149.refs_0_, bf16[4,49,768]{2,1,0:T(8,128)(2,1)S(1)} %collective-permute-done.23.refs_1_, ...), custom_call_target="tpu_custom_call" | custom-call | tf_op jit(solution)/shard_map/space_in/pallas_call | solution.py:232
  142.7 11.9 %space_mid.1 = (bf16[784,768]{1,0:T(8,128)(2,1)S(1)}, f32[784,768]{1,0:T(8,128)S(1)}, bf16[784,768]{1,0:T(8,128)(2,1)S(1)}) custom-call(s32[17]{0:T(128)S(1)} %stack.68.scal_ref.scal, bf16[784,2304]{1,0:T(8,128)(2,1)S(1)} %get-tuple-element.160.refs_0_, bf16[784,768]{1,0:T(8,128)(2,1)S(1)} %get-tuple-element.161.refs_1_.refs_2_, ...), custom_call_target="tpu_custom_call" | custom-call | tf_op jit(solution)/shard_map/space_mid/pallas_call | solution.py:232
  154.6 1.4 copy-done.35
  160.9 3.7 copy-done.6
  167.2 45.8 %mlp.1 = (f32[784,768]{1,0:T(8,128)S(1)}, f32[784,768]{1,0:T(8,128)S(1)}, bf16[768,1536]{1,0:T(8,128)(2,1)S(1)}, bf16[768,1536]{1,0:T(8,128)(2,1)S(1)}, bf16[768...) custom-call(s32[17]{0:T(128)S(1)} %stack.68.scal_ref.scal, ...), custom_call_target="tpu_custom_call" | custom-call | tf_op jit(solution)/shard_map/mlp/pallas_call | solution.py:232
  213.9 8.1 %mlp_out.1 = (f32[784,768]{1,0:T(8,128)S(1)}, bf16[784,768]{1,0:T(8,128)(2,1)S(1)}, bf16[768,384]{1,0:T(8,128)(2,1)S(1)}, bf16[768,384]{1,0:T(8,128)(2,1)S(1)}, ...) custom-call(s32[17]{0:T(128)S(1)} %stack.68.scal_ref.scal, ...), custom_call_target="tpu_custom_call" | custom-call | tf_op jit(solution)/shard_map/mlp_out/pallas_call | solution.py:232
  222.0 1.9 shard_map.219
  223.9 1.8 collective-permute-start.41
  225.7 16.5 %space_back.1 = (bf16[784,2304]{1,0:T(8,128)(2,1)S(1)}, f32[8,768]{1,0:T(8,128)S(1)}) custom-call(s32[17]{0:T(128)S(1)} %stack.68.scal_ref.scal, bf16[784,2304]{1,0:T(8,128)(2,1)S(1)} %copy-done.3, bf16[784,768]{1,0:T(8,128)(2,1)S(1)} %get-tuple-element.174.refs_1_, bf16[4,96,3072]{2,1,0:T(8,128)(2,1)S(1)} %get-tuple-element.180.refs_2_), custom_call_target="tpu_custom_call" | custom-call | tf_op jit(solution)/shard_map/space_back/pallas_call | solution.py:232
  242.3 13.7 %space_out.1 = (bf16[768,1152]{1,0:T(8,128)(2,1)S(1)}, bf16[768,1152]{1,0:T(8,128)(2,1)S(1)}, f32[8,768]{1,0:T(8,128)S(1)}, bf16[4,49,768]{2,1,0:T(8,128)(2,1)S(...) custom-call(s32[17]{0:T(128)S(1)} %stack.68.scal_ref.scal, ...), custom_call_target="tpu_custom_call" | custom-call | tf_op jit(solution)/shard_map/space_out/pallas_call | solution.py:232
  259.2 7.8 %collective-permute-done.39.refs_2_ = bf16[4,49,768]{2,1,0:T(8,128)(2,1)S(1)} collective-permute-done((bf16[4,49,768]{2,1,0:T(8,128)(2,1)S(1)}, bf16[4,49,768]{2,1,0:T(8,128)(2,1)S(1)}, u32[]{:S(2)}, u32[]{:S(2)}) %collective-permute-start.39) | collective-permute-done | bytes 301088 | tf_op jit(solution)/shard_map/ppermute | solution.py:805
  267.0 6.5 %collective-permute-done.40.refs_3_ = bf16[4,49,768]{2,1,0:T(8,128)(2,1)S(1)} collective-permute-done((bf16[4,49,768]{2,1,0:T(8,128)(2,1)S(1)}, bf16[4,49,768]{2,1,0:T(8,128)(2,1)S(1)}, u32[]{:S(2)}, u32[]{:S(2)}) %collective-permute-start.40) | collective-permute-done | bytes 301088 | tf_op jit(solution)/shard_map/ppermute | solution.py:805
  274.9 10.3 %time_proj.1 = (bf16[784,768]{1,0:T(8,128)(2,1)S(1)}, bf16[784,768]{1,0:T(8,128)(2,1)S(1)}, bf16[768,768]{1,0:T(8,128)(2,1)S(1)}, bf16[768,768]{1,0:T(8,128)(2,1)S(1)}, f32[8,768]{1,0:T(8,128)S(1)}) custom-call(s32[17]{0:T(128)S(1)} %stack.68.scal_ref.scal, bf16[4,49,768]{2,1,0:T(8,128)(2,1)S(1)} %get-tuple-element.183.refs_0_, ...), custom_call_target="tpu_custom_call" | custom-call | tf_op jit(solution)/shard_map/time_proj/pallas_call | solution.py:232
  286.6 4.3 collective-permute-done.48
  293.0 1.5 shard_map.222
  295.2 13.5 %time_attn_back.1 = (bf16[784,2304]{1,0:T(8,128)(2,1)S(1)}, f32[8,768]{1,0:T(8,128)S(1)}) custom-call(s32[17]{0:T(128)S(1)} %stack.68.scal_ref.scal, bf16[784,2304]{1,0:T(8,128)(2,1)S(1)} %copy-done.5, bf16[784,768]{1,0:T(8,128)(2,1)S(1)} %get-tuple-element.198.refs_1_, bf16[4,96,2304]{2,1,0:T(8,128)(2,1)S(1)} %get-tuple-element.208.refs_2_), custom_call_target="tpu_custom_call" | custom-call | tf_op jit(solution)/shard_map/time_attn_back/pallas_call | solution.py:232
  309.8 7.3 %collective-permute-done.49 = bf16[4,96,2304]{2,1,0:T(8,128)(2,1)S(1)} collective-permute-done((bf16[4,96,2304]{2,1,0:T(8,128)(2,1)S(1)}, bf16[4,96,2304]{2,1,0:T(8,128)(2,1)S(1)}, u32[]{:S(2)}, u32[]{:S(2)}) %collective-permute-start.49) | collective-permute-done | bytes 1769504 | tf_op jit(solution)/shard_map/ppermute | solution.py:820
  318.2 2.1 collective-permute-start.52
  320.4 14.5 %time_out.1 = (f32[8,49,768]{2,1,0:T(8,128)S(1)}, bf16[8,49,768]{2,1,0:T(8,128)(2,1)S(1)}, bf16[768,1152]{1,0:T(8,128)(2,1)S(1)}, bf16[768,1152]{1,0:T(8,128)(2,...) custom-call(s32[17]{0:T(128)S(1)} %stack.68.scal_ref.scal, bf16[784,2304]{1,0:T(8,128)(2,1)S(1)} %get-tuple-element.212.refs_0_, ...), custom_call_target="tpu_custom_call" | custom-call | tf_op jit(solution)/shard_map/time_out/pallas_call | solution.py:232
  334.9 7.1 %collective-permute-start.50 = (bf16[768,1152]{1,0:T(8,128)(2,1)S(1)}, bf16[768,1152]{1,0:T(8,128)(2,1)S(1)}, u32[]{:S(2)}, u32[]{:S(2)}) collective-permute-start(bf16[768,1152]{1,0:T(8,128)(2,1)S(1)} %get-tuple-element.220), channel_id=1, source_target_pairs={{0,1},{1,0},{2,3},{3,2},{4,5},{5,4},{6,7},{7,6},{8,9},{9,8},{10,11... | collective-permute-start | bytes 5308424 | tf_op jit(solution)/shard_map/ppermute | solution.py:820
  343.6 2.1 collective-permute-done.51
  347.4 3.3 collective-permute-start.57
  350.7 10.2 %collective-permute-done.54 = bf16[4,96,1280]{2,1,0:T(8,128)(2,1)S(1)} collective-permute-done((bf16[4,96,1280]{2,1,0:T(8,128)(2,1)S(1)}, bf16[4,96,1280]{2,1,0:T(8,128)(2,1)S(1)}, u32[]{:S(2)}, u32[]{:S(2)}) %collective-permute-start.54) | collective-permute-done | bytes 983072 | tf_op jit(solution)/shard_map/ppermute | solution.py:820
  362.9 6.7 %collective-permute-start.61 = (bf16[48,3072]{1,0:T(8,128)(2,1)S(1)}, bf16[48,3072]{1,0:T(8,128)(2,1)S(1)}, u32[]{:S(2)}, u32[]{:S(2)}) collective-permute-start(bf16[48,3072]{1,0:T(8,128)(2,1)S(1)} %get-tuple-element.231.refs_2_.refs_0_.refs_9_), channel_id=1, source_target_pairs={{0,4},{1,3},{2,6},{3,1},{4,0},{5,7},{6,2},{7,5},{8,12},{9,11},{10,... | collective-permute-start | bytes 884744 | tf_op jit(solution)/shard_map/ppermute | solution.py:820
  370.8 3.0 collective-permute-start.59
  375.5 4.0 collective-permute-done.59
  380.4 1.4 collective-permute-start.64
  382.1 1.8 collective-permute-start.63
  383.8 1.8 collective-permute-done.58
  386.3 3.0 collective-permute-start.60
  393.8 2.1 collective-permute-start.70
  395.9 1.6 collective-permute-done.70
  399.5 2.2 collective-permute-start.71
  401.7 3.2 collective-permute-done.71
  405.4 1.7 collective-permute-start.73
  407.1 1.9 collective-permute-done.73
  410.8 2.4 collective-permute-done.74
  417.1 1.8 collective-permute-start.69
  419.3 3.2 copy-done.65
  422.5 21.3 %shard_map.234 = (f32[192,9984]{1,0:T(8,128)}, f32[192,9984]{1,0:T(8,128)}, f32[192,9984]{1,0:T(8,128)}, f32[768,768]{1,0:T(8,128)}, f32[768,768]{1,0:T(8,128)},...) custom-call(s32[17]{0:T(128)S(1)} %stack.68.scal_ref.scal, ...), custom_call_target="tpu_custom_call" | custom-call | flops 24999999488 | tf_op jit(solution)/shard_map/pallas_call | solution.py:1001
  444.0 1.7 broadcast_select_fusion
  (356 shorter events, 70.7 us)
Async XLA Ops:
  7.2 153.7 %all-gather.2.cloned.1.call-start = ((), (), s32[]{:S(2)}) async-start(), calls=%async_computation | async-start | bytes 9732096 | tf_op jit(solution)/shard_map/all_gather | solution.py:1104
  10.1 6.6 %collective-permute-start.1 = (bf16[48,1280]{1,0:T(8,128)(2,1)}, bf16[48,1280]{1,0:T(8,128)(2,1)S(1)}, u32[]{:S(2)}, u32[]{:S(2)}) collective-permute-start(bf16[48,1280]{1,0:T(8,128)(2,1)} %pad_maximum_fusion.1), channel_id=1, source_target_pairs={{0,8},{1,9},{2,10},{3,11},{4,12},{5,13},{6,14},{7,15},{8,0},{9,1},... | collective-permute-start | bytes 368648 | tf_op jit(solution)/shard_map/ppermute | solution.py:820
  16.8 16.9 %collective-permute-start = (bf16[8,49,768]{2,0,1:T(8,128)(2,1)S(1)}, bf16[8,49,768]{2,0,1:T(8,128)(2,1)S(1)}, u32[]{:S(2)}, u32[]{:S(2)}) collective-permute-start(bf16[8,49,768]{2,0,1:T(8,128)(2,1)S(1)} %get-tuple-element.265), channel_id=1, source_target_pairs={{0,4},{4,0},{1,5},{5,1},{2,6},{6,2},{3,7},{7,3},{8,12},{12,8},{9,1... | collective-permute-start | bytes 1806344 | tf_op jit(solution)/shard_map/ppermute | solution.py:810
  18.6 15.3 %collective-permute-start.2 = (bf16[48,1280]{1,0:T(8,128)(2,1)}, bf16[48,1280]{1,0:T(8,128)(2,1)S(1)}, u32[]{:S(2)}, u32[]{:S(2)}) collective-permute-start(bf16[48,1280]{1,0:T(8,128)(2,1)} %pad_maximum_fusion.1), channel_id=1, source_target_pairs={{0,24},{1,25},{2,26},{3,27},{4,28},{5,29},{6,30},{7,31},{8,16},{9,... | collective-permute-start | bytes 368648 | tf_op jit(solution)/shard_map/ppermute | solution.py:820
  25.7 8.7 %collective-permute-start.3 = (bf16[48,1280]{1,0:T(8,128)(2,1)S(1)}, bf16[48,1280]{1,0:T(8,128)(2,1)S(1)}, u32[]{:S(2)}, u32[]{:S(2)}) collective-permute-start(bf16[48,1280]{1,0:T(8,128)(2,1)S(1)} %collective-permute-done.1.refs_0_), channel_id=1, source_target_pairs={{0,24},{1,25},{2,26},{3,27},{4,28},{5,29},{6,30},{7,31},{8,16},{9,... | collective-permute-start | bytes 368648 | tf_op jit(solution)/shard_map/ppermute | solution.py:820
  35.4 8.9 %collective-permute-start.4 = (bf16[3,48,1280]{2,1,0:T(8,128)(2,1)S(1)}, bf16[3,48,1280]{2,1,0:T(8,128)(2,1)S(1)}, u32[]{:S(2)}, u32[]{:S(2)}) collective-permute-start(bf16[3,48,1280]{2,1,0:T(8,128)(2,1)S(1)} %pack.5.refs_3_.refs_12_), channel_id=1, source_target_pairs={{0,4},{1,3},{2,6},{3,1},{4,0},{5,7},{6,2},{7,5},{8,12},{9,11},{10,... | collective-permute-start | bytes 1105928 | tf_op jit(solution)/shard_map/ppermute | solution.py:820
  44.3 12.7 %collective-permute-start.7 = (bf16[3,48,1280]{2,1,0:T(8,128)(2,1)S(1)}, bf16[3,48,1280]{2,1,0:T(8,128)(2,1)S(1)}, u32[]{:S(2)}, u32[]{:S(2)}) collective-permute-start(bf16[3,48,1280]{2,1,0:T(8,128)(2,1)S(1)} %collective-permute-done.4.refs_4_.refs_13_), channel_id=1, source_target_pairs={{0,2},{1,5},{2,0},{3,7},{4,6},{5,1},{6,4},{7,3},{8,10},{9,13},{10,... | collective-permute-start | bytes 1105928 | tf_op jit(solution)/shard_map/ppermute | solution.py:820
  45.8 11.2 %collective-permute-start.12 = (bf16[2,48,768]{2,1,0:T(8,128)(2,1)S(1)}, bf16[2,48,768]{2,1,0:T(8,128)(2,1)S(1)}, u32[]{:S(2)}, u32[]{:S(2)}) collective-permute-start(bf16[2,48,768]{2,1,0:T(8,128)(2,1)S(1)} %pack.6), channel_id=1, source_target_pairs={{0,24},{1,25},{2,26},{3,27},{4,28},{5,29},{6,30},{7,31},{8,16},{9,... | collective-permute-start | bytes 442376 | tf_op jit(solution)/shard_map/ppermute | solution.py:820
  48.3 11.7 %collective-permute-start.5 = (bf16[3,48,1280]{2,1,0:T(8,128)(2,1)S(1)}, bf16[3,48,1280]{2,1,0:T(8,128)(2,1)S(1)}, u32[]{:S(2)}, u32[]{:S(2)}) collective-permute-start(bf16[3,48,1280]{2,1,0:T(8,128)(2,1)S(1)} %pack.5.refs_3_.refs_12_), channel_id=1, source_target_pairs={{0,2},{1,5},{2,0},{3,7},{4,6},{5,1},{6,4},{7,3},{8,10},{9,13},{10,... | collective-permute-start | bytes 1105928 | tf_op jit(solution)/shard_map/ppermute | solution.py:820
  57.1 8.8 %collective-permute-start.13 = (bf16[48,1536]{1,0:T(8,128)(2,1)S(1)}, bf16[48,1536]{1,0:T(8,128)(2,1)S(1)}, u32[]{:S(2)}, u32[]{:S(2)}) collective-permute-start(bf16[48,1536]{1,0:T(8,128)(2,1)S(1)} %pad_maximum_fusion.refs_0_), channel_id=1, source_target_pairs={{0,8},{1,9},{2,10},{3,11},{4,12},{5,13},{6,14},{7,15},{8,0},{9,1},... | collective-permute-start | bytes 442376 | tf_op jit(solution)/shard_map/ppermute | solution.py:820
  58.9 10.3 %collective-permute-start.8 = (bf16[3,48,1280]{2,1,0:T(8,128)(2,1)S(1)}, bf16[3,48,1280]{2,1,0:T(8,128)(2,1)S(1)}, u32[]{:S(2)}, u32[]{:S(2)}) collective-permute-start(bf16[3,48,1280]{2,1,0:T(8,128)(2,1)S(1)} %pack.5.refs_3_.refs_12_), channel_id=1, source_target_pairs={{0,1},{1,0},{2,3},{3,2},{4,5},{5,4},{6,7},{7,6},{8,9},{9,8},{10,11... | collective-permute-start | bytes 1105928 | tf_op jit(solution)/shard_map/ppermute | solution.py:820
  58.9 13.1 %collective-permute-start.9 = (bf16[3,48,1280]{2,1,0:T(8,128)(2,1)S(1)}, bf16[3,48,1280]{2,1,0:T(8,128)(2,1)S(1)}, u32[]{:S(2)}, u32[]{:S(2)}) collective-permute-start(bf16[3,48,1280]{2,1,0:T(8,128)(2,1)S(1)} %collective-permute-done.4.refs_4_.refs_13_), channel_id=1, source_target_pairs={{0,1},{1,0},{2,3},{3,2},{4,5},{5,4},{6,7},{7,6},{8,9},{9,8},{10,11... | collective-permute-start | bytes 1105928 | tf_op jit(solution)/shard_map/ppermute | solution.py:820
  60.0 12.1 %collective-permute-start.10 = (bf16[3,48,1280]{2,1,0:T(8,128)(2,1)S(1)}, bf16[3,48,1280]{2,1,0:T(8,128)(2,1)S(1)}, u32[]{:S(2)}, u32[]{:S(2)}) collective-permute-start(bf16[3,48,1280]{2,1,0:T(8,128)(2,1)S(1)} %collective-permute-done.5.refs_5_.refs_14_), channel_id=1, source_target_pairs={{0,1},{1,0},{2,3},{3,2},{4,5},{5,4},{6,7},{7,6},{8,9},{9,8},{10,11... | collective-permute-start | bytes 1105928 | tf_op jit(solution)/shard_map/ppermute | solution.py:820
  60.0 12.1 %collective-permute-start.11 = (bf16[3,48,1280]{2,1,0:T(8,128)(2,1)S(1)}, bf16[3,48,1280]{2,1,0:T(8,128)(2,1)S(1)}, u32[]{:S(2)}, u32[]{:S(2)}) collective-permute-start(bf16[3,48,1280]{2,1,0:T(8,128)(2,1)S(1)} %collective-permute-done.7.refs_2_.refs_6_.refs_15_), channel_id=1, source_target_pairs={{0,1},{1,0},{2,3},{3,2},{4,5},{5,4},{6,7},{7,6},{8,9},{9,8},{10,11... | collective-permute-start | bytes 1105928 | tf_op jit(solution)/shard_map/ppermute | solution.py:820
  65.9 16.1 %collective-permute-start.14 = (bf16[2,48,1536]{2,1,0:T(8,128)(2,1)S(1)}, bf16[2,48,1536]{2,1,0:T(8,128)(2,1)S(1)}, u32[]{:S(2)}, u32[]{:S(2)}) collective-permute-start(bf16[2,48,1536]{2,1,0:T(8,128)(2,1)S(1)} %pack.8.refs_21_), channel_id=1, source_target_pairs={{0,24},{1,25},{2,26},{3,27},{4,28},{5,29},{6,30},{7,31},{8,16},{9,... | collective-permute-start | bytes 884744 | tf_op jit(solution)/shard_map/ppermute | solution.py:820
  69.2 14.7 %collective-permute-start.15 = (bf16[3,48,768]{2,1,0:T(8,128)(2,1)S(1)}, bf16[3,48,768]{2,1,0:T(8,128)(2,1)S(1)}, u32[]{:S(2)}, u32[]{:S(2)}) collective-permute-start(bf16[3,48,768]{2,1,0:T(8,128)(2,1)S(1)} %pack.7.refs_2_.refs_20_.refs_4_.refs_7_), channel_id=1, source_target_pairs={{0,4},{1,3},{2,6},{3,1},{4,0},{5,7},{6,2},{7,5},{8,12},{9,11},{10,... | collective-permute-start | bytes 663560 | tf_op jit(solution)/shard_map/ppermute | solution.py:820
  83.0 20.0 %collective-permute-start.22 = (bf16[3,48,1536]{2,1,0:T(8,128)(2,1)S(1)}, bf16[3,48,1536]{2,1,0:T(8,128)(2,1)S(1)}, u32[]{:S(2)}, u32[]{:S(2)}) collective-permute-start(bf16[3,48,1536]{2,1,0:T(8,128)(2,1)S(1)} %pack.9.refs_1_.refs_6_.refs_4_.refs_7_), channel_id=1, source_target_pairs={{0,4},{1,3},{2,6},{3,1},{4,0},{5,7},{6,2},{7,5},{8,12},{9,11},{10,... | collective-permute-start | bytes 1327112 | tf_op jit(solution)/shard_map/ppermute | solution.py:820
  83.0 10.9 %collective-permute-start.16 = (bf16[3,48,768]{2,1,0:T(8,128)(2,1)S(1)}, bf16[3,48,768]{2,1,0:T(8,128)(2,1)S(1)}, u32[]{:S(2)}, u32[]{:S(2)}) collective-permute-start(bf16[3,48,768]{2,1,0:T(8,128)(2,1)S(1)} %pack.7.refs_2_.refs_20_.refs_4_.refs_7_), channel_id=1, source_target_pairs={{0,2},{1,5},{2,0},{3,7},{4,6},{5,1},{6,4},{7,3},{8,10},{9,13},{10,... | collective-permute-start | bytes 663560 | tf_op jit(solution)/shard_map/ppermute | solution.py:820
  83.9 17.1 %collective-permute-start.17 = (bf16[3,48,768]{2,1,0:T(8,128)(2,1)S(1)}, bf16[3,48,768]{2,1,0:T(8,128)(2,1)S(1)}, u32[]{:S(2)}, u32[]{:S(2)}) collective-permute-start(bf16[3,48,768]{2,1,0:T(8,128)(2,1)S(1)} %collective-permute-done.15.refs_2_.refs_5_.refs_8_), channel_id=1, source_target_pairs={{0,2},{1,5},{2,0},{3,7},{4,6},{5,1},{6,4},{7,3},{8,10},{9,13},{10,... | collective-permute-start | bytes 663560 | tf_op jit(solution)/shard_map/ppermute | solution.py:820
  101.0 11.3 %collective-permute-start.26 = (bf16[3,48,1536]{2,1,0:T(8,128)(2,1)S(1)}, bf16[3,48,1536]{2,1,0:T(8,128)(2,1)S(1)}, u32[]{:S(2)}, u32[]{:S(2)}) collective-permute-start(bf16[3,48,1536]{2,1,0:T(8,128)(2,1)S(1)} %pack.9.refs_1_.refs_6_.refs_4_.refs_7_), channel_id=1, source_target_pairs={{0,2},{1,5},{2,0},{3,7},{4,6},{5,1},{6,4},{7,3},{8,10},{9,13},{10,... | collective-permute-start | bytes 1327112 | tf_op jit(solution)/shard_map/ppermute | solution.py:820
  103.5 24.7 %collective-permute-start.27 = (bf16[3,48,1536]{2,1,0:T(8,128)(2,1)S(1)}, bf16[3,48,1536]{2,1,0:T(8,128)(2,1)S(1)}, u32[]{:S(2)}, u32[]{:S(2)}) collective-permute-start(bf16[3,48,1536]{2,1,0:T(8,128)(2,1)S(1)} %collective-permute-done.22.refs_12_.refs_7_.refs_5_.refs_8_), channel_id=1, source_target_pairs={{0,2},{1,5},{2,0},{3,7},{4,6},{5,1},{6,4},{7,3},{8,10},{9,13},{10,... | collective-permute-start | bytes 1327112 | tf_op jit(solution)/shard_map/ppermute | solution.py:820
  110.7 11.3 %collective-permute-start.24 = (bf16[4,49,768]{2,1,0:T(8,128)(2,1)S(1)}, bf16[4,49,768]{2,1,0:T(8,128)(2,1)S(1)}, u32[]{:S(2)}, u32[]{:S(2)}) collective-permute-start(bf16[4,49,768]{2,1,0:T(8,128)(2,1)S(1)} %get-tuple-element.151), channel_id=1, source_target_pairs={{0,2},{1,3},{2,0},{3,1},{4,6},{5,7},{6,4},{7,5},{8,10},{9,11},{10,... | collective-permute-start | bytes 903176 | tf_op jit(solution)/shard_map/ppermute | solution.py:805
  111.6 16.7 %collective-permute-start.25 = (bf16[4,49,768]{2,1,0:T(8,128)(2,1)S(1)}, bf16[4,49,768]{2,1,0:T(8,128)(2,1)S(1)}, u32[]{:S(2)}, u32[]{:S(2)}) collective-permute-start(bf16[4,49,768]{2,1,0:T(8,128)(2,1)S(1)} %get-tuple-element.152), channel_id=1, source_target_pairs={{0,3},{1,2},{2,1},{3,0},{4,7},{5,6},{6,5},{7,4},{8,11},{9,10},{10,... | collective-permute-start | bytes 903176 | tf_op jit(solution)/shard_map/ppermute | solution.py:805
  112.4 17.0 %collective-permute-start.32 = (bf16[8,49,768]{2,0,1:T(8,128)(2,1)S(1)}, bf16[8,49,768]{2,0,1:T(8,128)(2,1)S(1)}, u32[]{:S(2)}, u32[]{:S(2)}) collective-permute-start(bf16[8,49,768]{2,0,1:T(8,128)(2,1)S(1)} %get-tuple-element.159), channel_id=1, source_target_pairs={{0,4},{4,0},{1,5},{5,1},{2,6},{6,2},{3,7},{7,3},{8,12},{12,8},{9,1... | collective-permute-start | bytes 1806344 | tf_op jit(solution)/shard_map/ppermute | solution.py:810
  140.8 16.2 %collective-permute-start.33 = (bf16[4,49,768]{2,1,0:T(8,128)(2,1)S(1)}, bf16[4,49,768]{2,1,0:T(8,128)(2,1)S(1)}, u32[]{:S(2)}, u32[]{:S(2)}) collective-permute-start(bf16[4,49,768]{2,1,0:T(8,128)(2,1)S(1)} %get-tuple-element.166), channel_id=1, source_target_pairs={{0,1},{1,0},{2,3},{3,2},{4,5},{5,4},{6,7},{7,6},{8,9},{9,8},{10,11... | collective-permute-start | bytes 903176 | tf_op jit(solution)/shard_map/ppermute | solution.py:805
  141.2 15.8 %collective-permute-start.34 = (bf16[4,49,768]{2,1,0:T(8,128)(2,1)S(1)}, bf16[4,49,768]{2,1,0:T(8,128)(2,1)S(1)}, u32[]{:S(2)}, u32[]{:S(2)}) collective-permute-start(bf16[4,49,768]{2,1,0:T(8,128)(2,1)S(1)} %get-tuple-element.167), channel_id=1, source_target_pairs={{0,2},{1,3},{2,0},{3,1},{4,6},{5,7},{6,4},{7,5},{8,10},{9,11},{10,... | collective-permute-start | bytes 903176 | tf_op jit(solution)/shard_map/ppermute | solution.py:805
  142.1 15.8 %collective-permute-start.35 = (bf16[4,49,768]{2,1,0:T(8,128)(2,1)S(1)}, bf16[4,49,768]{2,1,0:T(8,128)(2,1)S(1)}, u32[]{:S(2)}, u32[]{:S(2)}) collective-permute-start(bf16[4,49,768]{2,1,0:T(8,128)(2,1)S(1)} %get-tuple-element.168), channel_id=1, source_target_pairs={{0,3},{1,2},{2,1},{3,0},{4,7},{5,6},{6,5},{7,4},{8,11},{9,10},{10,... | collective-permute-start | bytes 903176 | tf_op jit(solution)/shard_map/ppermute | solution.py:805
  213.1 8.9 %collective-permute-start.36 = (bf16[768,1536]{1,0:T(8,128)(2,1)S(1)}, bf16[768,1536]{1,0:T(8,128)(2,1)S(1)}, u32[]{:S(2)}, u32[]{:S(2)}) collective-permute-start(bf16[768,1536]{1,0:T(8,128)(2,1)S(1)} %get-tuple-element.177), channel_id=1, source_target_pairs={{0,1},{1,0},{2,3},{3,2},{4,5},{5,4},{6,7},{7,6},{8,9},{9,8},{10,11... | collective-permute-start | bytes 7077896 | tf_op jit(solution)/shard_map/ppermute | solution.py:820
  213.8 8.2 %collective-permute-start.37 = (bf16[768,1536]{1,0:T(8,128)(2,1)S(1)}, bf16[768,1536]{1,0:T(8,128)(2,1)S(1)}, u32[]{:S(2)}, u32[]{:S(2)}) collective-permute-start(bf16[768,1536]{1,0:T(8,128)(2,1)S(1)} %get-tuple-element.178), channel_id=1, source_target_pairs={{0,1},{1,0},{2,3},{3,2},{4,5},{5,4},{6,7},{7,6},{8,9},{9,8},{10,11... | collective-permute-start | bytes 7077896 | tf_op jit(solution)/shard_map/ppermute | solution.py:820
  223.9 34.0 %collective-permute-start.41 = (bf16[4,96,3072]{2,1,0:T(8,128)(2,1)S(1)}, bf16[4,96,3072]{2,1,0:T(8,128)(2,1)S(1)}, u32[]{:S(2)}, u32[]{:S(2)}) collective-permute-start(bf16[4,96,3072]{2,1,0:T(8,128)(2,1)S(1)} %get-tuple-element.180.refs_2_), channel_id=1, source_target_pairs={{0,4},{1,3},{2,6},{3,1},{4,0},{5,7},{6,2},{7,5},{8,12},{9,11},{10,... | collective-permute-start | bytes 7077896 | tf_op jit(solution)/shard_map/ppermute | solution.py:820
  256.1 10.9 %collective-permute-start.39 = (bf16[4,49,768]{2,1,0:T(8,128)(2,1)S(1)}, bf16[4,49,768]{2,1,0:T(8,128)(2,1)S(1)}, u32[]{:S(2)}, u32[]{:S(2)}) collective-permute-start(bf16[4,49,768]{2,1,0:T(8,128)(2,1)S(1)} %get-tuple-element.185), channel_id=1, source_target_pairs={{0,2},{1,3},{2,0},{3,1},{4,6},{5,7},{6,4},{7,5},{8,10},{9,11},{10,... | collective-permute-start | bytes 903176 | tf_op jit(solution)/shard_map/ppermute | solution.py:805
  257.0 16.4 %collective-permute-start.40 = (bf16[4,49,768]{2,1,0:T(8,128)(2,1)S(1)}, bf16[4,49,768]{2,1,0:T(8,128)(2,1)S(1)}, u32[]{:S(2)}, u32[]{:S(2)}) collective-permute-start(bf16[4,49,768]{2,1,0:T(8,128)(2,1)S(1)} %get-tuple-element.186), channel_id=1, source_target_pairs={{0,3},{1,2},{2,1},{3,0},{4,7},{5,6},{6,5},{7,4},{8,11},{9,10},{10,... | collective-permute-start | bytes 903176 | tf_op jit(solution)/shard_map/ppermute | solution.py:805
  273.5 17.4 %collective-permute-start.48 = (bf16[4,48,3072]{2,1,0:T(8,128)(2,1)S(1)}, bf16[4,48,3072]{2,1,0:T(8,128)(2,1)S(1)}, u32[]{:S(2)}, u32[]{:S(2)}) collective-permute-start(bf16[4,48,3072]{2,1,0:T(8,128)(2,1)S(1)} %get-tuple-element.206.refs_15_), channel_id=1, source_target_pairs={{0,2},{1,5},{2,0},{3,7},{4,6},{5,1},{6,4},{7,3},{8,10},{9,13},{10,... | collective-permute-start | bytes 3538952 | tf_op jit(solution)/shard_map/ppermute | solution.py:820
  274.4 18.0 %collective-permute-start.45 = (bf16[768,384]{1,0:T(8,128)(2,1)S(1)}, bf16[768,384]{1,0:T(8,128)(2,1)S(1)}, u32[]{:S(2)}, u32[]{:S(2)}) collective-permute-start(bf16[768,384]{1,0:T(8,128)(2,1)S(1)} %get-tuple-element.202), channel_id=1, source_target_pairs={{0,1},{1,0},{2,3},{3,2},{4,5},{5,4},{6,7},{7,6},{8,9},{9,8},{10,11... | collective-permute-start | bytes 1769480 | tf_op jit(solution)/shard_map/ppermute | solution.py:820
  274.4 18.1 %collective-permute-start.46 = (bf16[768,1152]{1,0:T(8,128)(2,1)S(1)}, bf16[768,1152]{1,0:T(8,128)(2,1)S(1)}, u32[]{:S(2)}, u32[]{:S(2)}) collective-permute-start(bf16[768,1152]{1,0:T(8,128)(2,1)S(1)} %get-tuple-element.203), channel_id=1, source_target_pairs={{0,1},{1,0},{2,3},{3,2},{4,5},{5,4},{6,7},{7,6},{8,9},{9,8},{10,11... | collective-permute-start | bytes 5308424 | tf_op jit(solution)/shard_map/ppermute | solution.py:820
  285.2 7.8 %collective-permute-start.47 = (bf16[768,768]{1,0:T(8,128)(2,1)S(1)}, bf16[768,768]{1,0:T(8,128)(2,1)S(1)}, u32[]{:S(2)}, u32[]{:S(2)}) collective-permute-start(bf16[768,768]{1,0:T(8,128)(2,1)S(1)} %get-tuple-element.204), channel_id=1, source_target_pairs={{0,1},{1,0},{2,3},{3,2},{4,5},{5,4},{6,7},{7,6},{8,9},{9,8},{10,11... | collective-permute-start | bytes 3538952 | tf_op jit(solution)/shard_map/ppermute | solution.py:820
  285.3 23.4 %collective-permute-start.44 = (bf16[4,49,768]{2,1,0:T(8,128)(2,1)S(1)}, bf16[4,49,768]{2,1,0:T(8,128)(2,1)S(1)}, u32[]{:S(2)}, u32[]{:S(2)}) collective-permute-start(bf16[4,49,768]{2,1,0:T(8,128)(2,1)S(1)} %get-tuple-element.197), channel_id=1, source_target_pairs={{0,3},{1,2},{2,1},{3,0},{4,7},{5,6},{6,5},{7,4},{8,11},{9,10},{10,... | collective-permute-start | bytes 903176 | tf_op jit(solution)/shard_map/ppermute | solution.py:805
  290.9 17.9 %collective-permute-start.43 = (bf16[4,49,768]{2,1,0:T(8,128)(2,1)S(1)}, bf16[4,49,768]{2,1,0:T(8,128)(2,1)S(1)}, u32[]{:S(2)}, u32[]{:S(2)}) collective-permute-start(bf16[4,49,768]{2,1,0:T(8,128)(2,1)S(1)} %get-tuple-element.195), channel_id=1, source_target_pairs={{0,2},{1,3},{2,0},{3,1},{4,6},{5,7},{6,4},{7,5},{8,10},{9,11},{10,... | collective-permute-start | bytes 903176 | tf_op jit(solution)/shard_map/ppermute | solution.py:805
  292.4 16.4 %collective-permute-start.42 = (bf16[4,49,768]{2,1,0:T(8,128)(2,1)S(1)}, bf16[4,49,768]{2,1,0:T(8,128)(2,1)S(1)}, u32[]{:S(2)}, u32[]{:S(2)}) collective-permute-start(bf16[4,49,768]{2,1,0:T(8,128)(2,1)S(1)} %get-tuple-element.193), channel_id=1, source_target_pairs={{0,1},{1,0},{2,3},{3,2},{4,5},{5,4},{6,7},{7,6},{8,9},{9,8},{10,11... | collective-permute-start | bytes 903176 | tf_op jit(solution)/shard_map/ppermute | solution.py:805
  292.5 49.6 %collective-permute-start.53 = (bf16[1,96,3072]{2,1,0:T(8,128)(2,1)S(1)}, bf16[1,96,3072]{2,1,0:T(8,128)(2,1)S(1)}, u32[]{:S(2)}, u32[]{:S(2)}) collective-permute-start(bf16[1,96,3072]{2,1,0:T(8,128)(2,1)S(1)} %get-tuple-element.207.refs_6_), channel_id=1, source_target_pairs={{0,24},{1,25},{2,26},{3,27},{4,28},{5,29},{6,30},{7,31},{8,16},{9,... | collective-permute-start | bytes 1769480 | tf_op jit(solution)/shard_map/ppermute | solution.py:820
  294.5 22.6 %collective-permute-start.49 = (bf16[4,96,2304]{2,1,0:T(8,128)(2,1)S(1)}, bf16[4,96,2304]{2,1,0:T(8,128)(2,1)S(1)}, u32[]{:S(2)}, u32[]{:S(2)}) collective-permute-start(bf16[4,96,2304]{2,1,0:T(8,128)(2,1)S(1)} %get-tuple-element.208.refs_2_), channel_id=1, source_target_pairs={{0,4},{1,3},{2,6},{3,1},{4,0},{5,7},{6,2},{7,5},{8,12},{9,11},{10,... | collective-permute-start | bytes 5308424 | tf_op jit(solution)/shard_map/ppermute | solution.py:820
  318.2 24.6 %collective-permute-start.52 = (bf16[4,48,2304]{2,1,0:T(8,128)(2,1)S(1)}, bf16[4,48,2304]{2,1,0:T(8,128)(2,1)S(1)}, u32[]{:S(2)}, u32[]{:S(2)}) collective-permute-start(bf16[4,48,2304]{2,1,0:T(8,128)(2,1)S(1)} %get-tuple-element.217.refs_20_), channel_id=1, source_target_pairs={{0,2},{1,5},{2,0},{3,7},{4,6},{5,1},{6,4},{7,3},{8,10},{9,13},{10,... | collective-permute-start | bytes 2654216 | tf_op jit(solution)/shard_map/ppermute | solution.py:820
  334.9 10.7 %collective-permute-start.50 = (bf16[768,1152]{1,0:T(8,128)(2,1)S(1)}, bf16[768,1152]{1,0:T(8,128)(2,1)S(1)}, u32[]{:S(2)}, u32[]{:S(2)}) collective-permute-start(bf16[768,1152]{1,0:T(8,128)(2,1)S(1)} %get-tuple-element.220), channel_id=1, source_target_pairs={{0,1},{1,0},{2,3},{3,2},{4,5},{5,4},{6,7},{7,6},{8,9},{9,8},{10,11... | collective-permute-start | bytes 5308424 | tf_op jit(solution)/shard_map/ppermute | solution.py:820
  346.8 14.2 %collective-permute-start.54 = (bf16[4,96,1280]{2,1,0:T(8,128)(2,1)S(1)}, bf16[4,96,1280]{2,1,0:T(8,128)(2,1)S(1)}, u32[]{:S(2)}, u32[]{:S(2)}) collective-permute-start(bf16[4,96,1280]{2,1,0:T(8,128)(2,1)S(1)} %get-tuple-element.226), channel_id=1, source_target_pairs={{0,4},{1,3},{2,6},{3,1},{4,0},{5,7},{6,2},{7,5},{8,12},{9,11},{10,... | collective-permute-start | bytes 2949128 | tf_op jit(solution)/shard_map/ppermute | solution.py:820
  347.4 14.5 %collective-permute-start.57 = (bf16[1,48,3072]{2,1,0:T(8,128)(2,1)S(1)}, bf16[1,48,3072]{2,1,0:T(8,128)(2,1)S(1)}, u32[]{:S(2)}, u32[]{:S(2)}) collective-permute-start(bf16[1,48,3072]{2,1,0:T(8,128)(2,1)S(1)} %get-tuple-element.223.refs_2_), channel_id=1, source_target_pairs={{0,8},{1,9},{2,10},{3,11},{4,12},{5,13},{6,14},{7,15},{8,0},{9,1},... | collective-permute-start | bytes 884744 | tf_op jit(solution)/shard_map/ppermute | solution.py:820
  350.7 19.4 %collective-permute-start.56 = (bf16[1,96,2304]{2,1,0:T(8,128)(2,1)S(1)}, bf16[1,96,2304]{2,1,0:T(8,128)(2,1)S(1)}, u32[]{:S(2)}, u32[]{:S(2)}) collective-permute-start(bf16[1,96,2304]{2,1,0:T(8,128)(2,1)S(1)} %get-tuple-element.224.refs_4_), channel_id=1, source_target_pairs={{0,24},{1,25},{2,26},{3,27},{4,28},{5,29},{6,30},{7,31},{8,16},{9,... | collective-permute-start | bytes 1327112 | tf_op jit(solution)/shard_map/ppermute | solution.py:820
  361.8 11.9 %collective-permute-start.55 = (bf16[4,48,1280]{2,1,0:T(8,128)(2,1)S(1)}, bf16[4,48,1280]{2,1,0:T(8,128)(2,1)S(1)}, u32[]{:S(2)}, u32[]{:S(2)}) collective-permute-start(bf16[4,48,1280]{2,1,0:T(8,128)(2,1)S(1)} %get-tuple-element.228.refs_0_), channel_id=1, source_target_pairs={{0,2},{1,5},{2,0},{3,7},{4,6},{5,1},{6,4},{7,3},{8,10},{9,13},{10,... | collective-permute-start | bytes 1474568 | tf_op jit(solution)/shard_map/ppermute | solution.py:820
  362.9 19.2 %collective-permute-start.61 = (bf16[48,3072]{1,0:T(8,128)(2,1)S(1)}, bf16[48,3072]{1,0:T(8,128)(2,1)S(1)}, u32[]{:S(2)}, u32[]{:S(2)}) collective-permute-start(bf16[48,3072]{1,0:T(8,128)(2,1)S(1)} %get-tuple-element.231.refs_2_.refs_0_.refs_9_), channel_id=1, source_target_pairs={{0,4},{1,3},{2,6},{3,1},{4,0},{5,7},{6,2},{7,5},{8,12},{9,11},{10,... | collective-permute-start | bytes 884744 | tf_op jit(solution)/shard_map/ppermute | solution.py:820
  369.6 19.6 %collective-permute-start.62 = (bf16[48,3072]{1,0:T(8,128)(2,1)S(1)}, bf16[48,3072]{1,0:T(8,128)(2,1)S(1)}, u32[]{:S(2)}, u32[]{:S(2)}) collective-permute-start(bf16[48,3072]{1,0:T(8,128)(2,1)S(1)} %get-tuple-element.231.refs_2_.refs_0_.refs_9_), channel_id=1, source_target_pairs={{0,2},{1,5},{2,0},{3,7},{4,6},{5,1},{6,4},{7,3},{8,10},{9,13},{10,... | collective-permute-start | bytes 884744 | tf_op jit(solution)/shard_map/ppermute | solution.py:820
  370.8 8.8 %collective-permute-start.59 = (bf16[1,48,2304]{2,1,0:T(8,128)(2,1)S(1)}, bf16[1,48,2304]{2,1,0:T(8,128)(2,1)S(1)}, u32[]{:S(2)}, u32[]{:S(2)}) collective-permute-start(bf16[1,48,2304]{2,1,0:T(8,128)(2,1)S(1)} %get-tuple-element.232.refs_2_), channel_id=1, source_target_pairs={{0,8},{1,9},{2,10},{3,11},{4,12},{5,13},{6,14},{7,15},{8,0},{9,1},... | collective-permute-start | bytes 663560 | tf_op jit(solution)/shard_map/ppermute | solution.py:820
  374.4 11.3 %collective-permute-start.58 = (bf16[1,96,1280]{2,1,0:T(8,128)(2,1)S(1)}, bf16[1,96,1280]{2,1,0:T(8,128)(2,1)S(1)}, u32[]{:S(2)}, u32[]{:S(2)}) collective-permute-start(bf16[1,96,1280]{2,1,0:T(8,128)(2,1)S(1)} %get-tuple-element.234.refs_0_), channel_id=1, source_target_pairs={{0,24},{1,25},{2,26},{3,27},{4,28},{5,29},{6,30},{7,31},{8,16},{9,... | collective-permute-start | bytes 737288 | tf_op jit(solution)/shard_map/ppermute | solution.py:820
  380.4 8.9 %collective-permute-start.64 = (bf16[48,2304]{1,0:T(8,128)(2,1)S(1)}, bf16[48,2304]{1,0:T(8,128)(2,1)S(1)}, u32[]{:S(2)}, u32[]{:S(2)}) collective-permute-start(bf16[48,2304]{1,0:T(8,128)(2,1)S(1)} %get-tuple-element.237.refs_2_.refs_17_), channel_id=1, source_target_pairs={{0,4},{1,3},{2,6},{3,1},{4,0},{5,7},{6,2},{7,5},{8,12},{9,11},{10,... | collective-permute-start | bytes 663560 | tf_op jit(solution)/shard_map/ppermute | solution.py:820
  381.8 8.0 %collective-permute-start.65 = (bf16[48,2304]{1,0:T(8,128)(2,1)S(1)}, bf16[48,2304]{1,0:T(8,128)(2,1)S(1)}, u32[]{:S(2)}, u32[]{:S(2)}) collective-permute-start(bf16[48,2304]{1,0:T(8,128)(2,1)S(1)} %get-tuple-element.237.refs_2_.refs_17_), channel_id=1, source_target_pairs={{0,2},{1,5},{2,0},{3,7},{4,6},{5,1},{6,4},{7,3},{8,10},{9,13},{10,... | collective-permute-start | bytes 663560 | tf_op jit(solution)/shard_map/ppermute | solution.py:820
  382.1 8.8 %collective-permute-start.63 = (bf16[48,3072]{1,0:T(8,128)(2,1)S(1)}, bf16[48,3072]{1,0:T(8,128)(2,1)S(1)}, u32[]{:S(2)}, u32[]{:S(2)}) collective-permute-start(bf16[48,3072]{1,0:T(8,128)(2,1)S(1)} %collective-permute-done.61.refs_1_.refs_10_), channel_id=1, source_target_pairs={{0,2},{1,5},{2,0},{3,7},{4,6},{5,1},{6,4},{7,3},{8,10},{9,13},{10,... | collective-permute-start | bytes 884744 | tf_op jit(solution)/shard_map/ppermute | solution.py:820
  389.8 9.7 %collective-permute-start.78 = (bf16[48,3072]{1,0:T(8,128)(2,1)S(1)}, bf16[48,3072]{1,0:T(8,128)(2,1)S(1)}, u32[]{:S(2)}, u32[]{:S(2)}) collective-permute-start(bf16[48,3072]{1,0:T(8,128)(2,1)S(1)} %collective-permute-done.62.refs_2_.refs_11_), channel_id=1, source_target_pairs={{0,1},{1,0},{2,3},{3,2},{4,5},{5,4},{6,7},{7,6},{8,9},{9,8},{10,11... | collective-permute-start | bytes 884744 | tf_op jit(solution)/shard_map/ppermute | solution.py:820
  390.9 14.5 %collective-permute-start.81 = (bf16[48,2304]{1,0:T(8,128)(2,1)S(1)}, bf16[48,2304]{1,0:T(8,128)(2,1)S(1)}, u32[]{:S(2)}, u32[]{:S(2)}) collective-permute-start(bf16[48,2304]{1,0:T(8,128)(2,1)S(1)} %get-tuple-element.237.refs_2_.refs_17_), channel_id=1, source_target_pairs={{0,1},{1,0},{2,3},{3,2},{4,5},{5,4},{6,7},{7,6},{8,9},{9,8},{10,11... | collective-permute-start | bytes 663560 | tf_op jit(solution)/shard_map/ppermute | solution.py:820
  393.0 11.9 %collective-permute-start.72 = (bf16[48,1280]{1,0:T(8,128)(2,1)S(1)}, bf16[48,1280]{1,0:T(8,128)(2,1)S(1)}, u32[]{:S(2)}, u32[]{:S(2)}) collective-permute-start(bf16[48,1280]{1,0:T(8,128)(2,1)S(1)} %get-tuple-element.242.refs_25_), channel_id=1, source_target_pairs={{0,2},{1,5},{2,0},{3,7},{4,6},{5,1},{6,4},{7,3},{8,10},{9,13},{10,... | collective-permute-start | bytes 368648 | tf_op jit(solution)/shard_map/ppermute | solution.py:820
  397.4 12.1 %collective-permute-start.80 = (bf16[48,2304]{1,0:T(8,128)(2,1)S(1)}, bf16[48,2304]{1,0:T(8,128)(2,1)S(1)}, u32[]{:S(2)}, u32[]{:S(2)}) collective-permute-start(bf16[48,2304]{1,0:T(8,128)(2,1)S(1)} %collective-permute-done.64.refs_4_.refs_18_), channel_id=1, source_target_pairs={{0,2},{1,5},{2,0},{3,7},{4,6},{5,1},{6,4},{7,3},{8,10},{9,13},{10,... | collective-permute-start | bytes 663560 | tf_op jit(solution)/shard_map/ppermute | solution.py:820
  398.7 10.3 %collective-permute-start.67 = (bf16[48,1280]{1,0:T(8,128)(2,1)S(1)}, bf16[48,1280]{1,0:T(8,128)(2,1)S(1)}, u32[]{:S(2)}, u32[]{:S(2)}) collective-permute-start(bf16[48,1280]{1,0:T(8,128)(2,1)S(1)} %collective-permute-done.66.refs_26_), channel_id=1, source_target_pairs={{0,2},{1,5},{2,0},{3,7},{4,6},{5,1},{6,4},{7,3},{8,10},{9,13},{10,... | collective-permute-start | bytes 368648 | tf_op jit(solution)/shard_map/ppermute | solution.py:820
  404.9 8.3 %collective-permute-start.82 = (bf16[48,2304]{1,0:T(8,128)(2,1)S(1)}, bf16[48,2304]{1,0:T(8,128)(2,1)S(1)}, u32[]{:S(2)}, u32[]{:S(2)}) collective-permute-start(bf16[48,2304]{1,0:T(8,128)(2,1)S(1)} %collective-permute-done.64.refs_4_.refs_18_), channel_id=1, source_target_pairs={{0,1},{1,0},{2,3},{3,2},{4,5},{5,4},{6,7},{7,6},{8,9},{9,8},{10,11... | collective-permute-start | bytes 663560 | tf_op jit(solution)/shard_map/ppermute | solution.py:820
  404.9 8.8 %collective-permute-start.83 = (bf16[48,2304]{1,0:T(8,128)(2,1)S(1)}, bf16[48,2304]{1,0:T(8,128)(2,1)S(1)}, u32[]{:S(2)}, u32[]{:S(2)}) collective-permute-start(bf16[48,2304]{1,0:T(8,128)(2,1)S(1)} %collective-permute-done.65.refs_5_.refs_19_), channel_id=1, source_target_pairs={{0,1},{1,0},{2,3},{3,2},{4,5},{5,4},{6,7},{7,6},{8,9},{9,8},{10,11... | collective-permute-start | bytes 663560 | tf_op jit(solution)/shard_map/ppermute | solution.py:820
  409.0 8.1 %collective-permute-start.79 = (bf16[48,3072]{1,0:T(8,128)(2,1)S(1)}, bf16[48,3072]{1,0:T(8,128)(2,1)S(1)}, u32[]{:S(2)}, u32[]{:S(2)}) collective-permute-start(bf16[48,3072]{1,0:T(8,128)(2,1)S(1)} %collective-permute-done.63.refs_3_.refs_12_), channel_id=1, source_target_pairs={{0,1},{1,0},{2,3},{3,2},{4,5},{5,4},{6,7},{7,6},{8,9},{9,8},{10,11... | collective-permute-start | bytes 884744 | tf_op jit(solution)/shard_map/ppermute | solution.py:820
  417.1 26.7 %collective-permute-start.69 = (bf16[8,49,768]{2,0,1:T(8,128)(2,1)S(1)}, bf16[8,49,768]{2,0,1:T(8,128)(2,1)S(1)}, u32[]{:S(2)}, u32[]{:S(2)}) collective-permute-start(bf16[8,49,768]{2,0,1:T(8,128)(2,1)S(1)} %copy.55), channel_id=1, source_target_pairs={{0,4},{4,0},{1,5},{5,1},{2,6},{6,2},{3,7},{7,3},{8,12},{12,8},{9,1... | collective-permute-start | bytes 1806344 | tf_op jit(solution)/shard_map/ppermute | solution.py:810
  418.9 27.0 %collective-permute-start.68 = (bf16[8,49,768]{2,0,1:T(8,128)(2,1)S(1)}, bf16[8,49,768]{2,0,1:T(8,128)(2,1)S(1)}, u32[]{:S(2)}, u32[]{:S(2)}) collective-permute-start(bf16[8,49,768]{2,0,1:T(8,128)(2,1)S(1)} %copy.53), channel_id=1, source_target_pairs={{0,4},{4,0},{1,5},{5,1},{2,6},{6,2},{3,7},{7,3},{8,12},{12,8},{9,1... | collective-permute-start | bytes 1806344 | tf_op jit(solution)/shard_map/ppermute | solution.py:810
  (106 other events, 1278.1 us)
Sparse Core Ops, SparseCore 0:
  16.8 103.6 all-gather.1
